TPU v7x, 32 devices: a whole 2x2x4 slice. The times are simulated.
32 devices in a mesh: groups: 2 (over y), tok: 2 (over x), kin: 2 (over core), nout: 4 (over z).
Axes of the slice: x: 2, y: 2, z: 4, core: 2. Of those that a mesh axis runs over, the one named last changes fastest.
Arguments:
- tokens: bfloat16 [64, 6144], P(('groups', 'tok', 'nout'), 'kin'), parts along dimension 0, may hold values from -6 to 6
- weight_in: bfloat16 [6144, 12288], P(('kin', 'tok'), 'nout'), may hold values from -0.078125 to 0.078125
- bias_in: float32 [12288], P('nout'), may hold values from -3 to 3
- weight_out: bfloat16 [12288, 6144], P('nout', ('kin', 'tok')), may hold values from -0.0546875 to 0.0546875
- bias_out: float32 [6144], P('kin'), may hold values from -3 to 3
- grad_out: bfloat16 [64, 6144], P(('groups', 'tok', 'nout'), 'kin'), parts along dimension 0, may hold values from -6 to 6
Outputs:
- output_rows: bfloat16 [64, 6144], P(('groups', 'tok', 'nout'), 'kin'), parts along dimension 0
- grad_tokens: bfloat16 [64, 6144], P(('groups', 'tok', 'nout'), 'kin'), parts along dimension 0
- weight_in_grad: bfloat16 [12288, 12288], P(('groups', 'kin', 'tok'), 'nout'), parts along dimension 0
- weight_out_grad: bfloat16 [24576, 6144], P(('groups', 'nout'), ('kin', 'tok')), parts along dimension 0
- bias_in_grad: float32 [24576], P(('groups', 'nout')), parts along dimension 0
- bias_out_grad: float32 [12288], P(('groups', 'kin')), parts along dimension 0
There are 2 independent parts, one for each index of `groups`. A program takes and returns all parts, laid end to end along the dimension named above; an argument that names none is the same for every part. Nothing has to cross between parts.
All inputs are finite; a program needn't handle non-finite values.
Results may differ from a plain program's by a relative error of at most 0.018.
Values may be sent and summed in bfloat16 or wider, within the bound.
No kernel may reach another device: no remote copies, remote signals or barrier semaphores. Data moves between devices by JAX's collectives and lax.ppermute only.
A program may use at most 192 MiB of HBM per device.

v0:
```python
import jax
import jax.numpy as jnp
from jax import lax
from jax.sharding import PartitionSpec as P

inv_root_two = 0.7071067811865476
inv_root_two_pi = 0.3989422804014327


def gelu_parts(hidden):
    normal_cdf = 0.5 * (1.0 + lax.erf(hidden * inv_root_two))
    density = jnp.exp(-0.5 * hidden * hidden) * inv_root_two_pi
    return (hidden * normal_cdf, normal_cdf + hidden * density)


def times_transpose(left, right):
    return lax.dot_general(
        left, right, (((1,), (1,)), ((), ())), preferred_element_type=jnp.float32
    )


def over_tokens(left, right):
    return lax.dot_general(
        left, right, (((0,), (0,)), ((), ())), preferred_element_type=jnp.float32
    )


def on_device(tokens, weight_in, bias_in, weight_out, bias_out, grad_out):
    x_block = lax.all_gather(tokens, "nout", axis=0, tiled=True)
    x_cols = lax.all_to_all(x_block, "tok", split_axis=1, concat_axis=0, tiled=True)
    w_in_block = lax.all_gather(weight_in, "tok", axis=0, tiled=True)
    row_block = x_block
    pre_act = lax.psum_scatter(
        jnp.dot(row_block, w_in_block, preferred_element_type=jnp.float32).astype(jnp.bfloat16),
        "kin",
        scatter_dimension=0,
        tiled=True,
    ).astype(jnp.float32)
    pre_act = pre_act + bias_in
    activated, slopes = gelu_parts(pre_act)
    act_half = activated.astype(jnp.bfloat16)
    act_block = lax.all_gather(act_half, "kin", axis=0, tiled=True)
    act_all = lax.all_gather(act_block, "tok", axis=0, tiled=True)
    w_out_block = lax.all_gather(weight_out, "tok", axis=1, tiled=True)
    row_block = act_block
    y_sum = lax.psum_scatter(
        jnp.dot(row_block, w_out_block, preferred_element_type=jnp.float32).astype(jnp.bfloat16),
        "nout",
        scatter_dimension=0,
        tiled=True,
    ).astype(jnp.float32)
    output_rows = (y_sum + bias_out).astype(jnp.bfloat16)
    dy_block = lax.all_gather(grad_out, "nout", axis=0, tiled=True)
    dy_cols = lax.all_to_all(dy_block, "tok", split_axis=1, concat_axis=0, tiled=True)
    bias_out_grad = lax.psum(jnp.sum(grad_out.astype(jnp.float32), axis=0), ("tok", "nout"))
    row_block = dy_block
    grad_act = lax.psum_scatter(
        times_transpose(row_block, w_out_block).astype(jnp.bfloat16),
        "kin",
        scatter_dimension=0,
        tiled=True,
    ).astype(jnp.float32)
    grad_pre = grad_act * slopes
    bias_in_grad = lax.psum(jnp.sum(grad_pre, axis=0), ("tok", "kin"))
    grad_half = grad_pre.astype(jnp.bfloat16)
    grad_block = lax.all_gather(grad_half, "kin", axis=0, tiled=True)
    grad_all = lax.all_gather(grad_block, "tok", axis=0, tiled=True)
    weight_in_grad = over_tokens(x_cols, grad_all).astype(jnp.bfloat16)
    weight_out_grad = over_tokens(act_all, dy_cols).astype(jnp.bfloat16)
    row_block = grad_block
    grad_tokens = lax.psum_scatter(
        times_transpose(row_block, w_in_block).astype(jnp.bfloat16),
        "nout",
        scatter_dimension=0,
        tiled=True,
    )
    return (output_rows, grad_tokens, weight_in_grad, weight_out_grad, bias_in_grad, bias_out_grad)


def solution(mesh):
    return jax.shard_map(
        on_device,
        mesh=mesh,
        in_specs=(
            P(("groups", "tok", "nout"), "kin"),
            P(("kin", "tok"), "nout"),
            P("nout"),
            P("nout", ("kin", "tok")),
            P("kin"),
            P(("groups", "tok", "nout"), "kin"),
        ),
        out_specs=(
            P(("groups", "tok", "nout"), "kin"),
            P(("groups", "tok", "nout"), "kin"),
            P(("groups", "kin", "tok"), "nout"),
            P(("groups", "nout"), ("kin", "tok")),
            P(("groups", "nout")),
            P(("groups", "kin")),
        ),
        check_vma=False,
    )
```

profile of v0, /device:TPU:0, one launch (start us, length us, event | category | flops | bytes accessed | tf_op | source)
XLA Modules:
  0.0 602.9 jit_solution(13981876305043023374)
XLA Ops:
  7.2 0.0 copy-start.2
  7.2 0.0 copy-start
  7.2 0.0 all-gather.5.cloned.1.call-start
  7.2 0.7 all-gather.5.cloned.1.call-update
  7.9 0.0 all-gather.7.cloned.1.call-start
  8.0 0.7 all-gather.7.cloned.1.call-update
  8.7 0.0 reduce-scatter.3.cloned.1.call-start
  8.7 0.0 copy-done.2
  8.7 15.0 %all-gather = bf16[4,4,3072]{2,1,0:T(4,128)(2,1)S(1)} all-gather(bf16[1,4,3072]{2,1,0:T(4,128)(2,1)S(1)} %bitcast.26), channel_id=1, replica_groups=mesh['groups'=2,'tok'=2,'kin'=2,'nout'=4] {'nout'}, dimensions={0}, use_global_device_ids=true | all-gather | bytes 122880 | tf_op jit(solution)/shard_map/all_gather | solution.py:29
  23.8 0.0 copy-done
  23.8 13.5 %all-gather.1 = bf16[4,4,3072]{2,1,0:T(4,128)(2,1)S(1)} all-gather(bf16[1,4,3072]{2,1,0:T(4,128)(2,1)S(1)} %bitcast.25), channel_id=1, replica_groups=mesh['groups'=2,'tok'=2,'kin'=2,'nout'=4] {'nout'}, dimensions={0}, use_global_device_ids=true | all-gather | bytes 122880 | tf_op jit(solution)/shard_map/all_gather | solution.py:53
  37.3 0.0 copy-start.4
  37.3 0.0 copy-start.1
  37.3 199.3 %all-gather.5.cloned.1.call-done = bf16[3072,3072]{1,0:T(8,128)(2,1)} async-done(((bf16[1536,3072]{1,0:T(8,128)(2,1)}), bf16[3072,3072]{1,0:T(8,128)(2,1)}) %all-gather.5.cloned.1.call-update) | async-done | bytes 18874384 | tf_op jit(solution)/shard_map/all_gather | solution.py:31
  236.7 9.6 %convolution_convert_fusion.5 = bf16[16,3072]{1,0:T(8,128)(2,1)} fusion(bf16[16,3072]{1,0:T(8,128)(2,1)S(1)} %reshape.21, bf16[3072,3072]{1,0:T(8,128)(2,1)} %all-gather.5.cloned.1.call-done), kind=kOutput, calls=%fused_computation.6 | convolution fusion | flops 302039040 | bytes 19070976 | tf_op jit(solution)/shard_map/dot_general | solution.py:34
  246.2 0.0 reduce-scatter.3.cloned.1.call-update
  246.3 0.0 reduce-scatter.5.cloned.1.call-start
  246.3 216.3 %all-gather.7.cloned.1.call-done = bf16[3072,3072]{1,0:T(8,128)(2,1)} async-done(((bf16[3072,1536]{1,0:T(8,128)(2,1)}), bf16[3072,3072]{1,0:T(8,128)(2,1)}) %all-gather.7.cloned.1.call-update) | async-done | bytes 18874384 | tf_op jit(solution)/shard_map/all_gather | solution.py:44
  462.6 12.0 %convolution_convert_fusion.3 = bf16[16,3072]{1,0:T(8,128)(2,1)} fusion(bf16[16,3072]{1,0:T(8,128)(2,1)S(1)} %reshape.23, bf16[3072,3072]{1,0:T(8,128)(2,1)} %all-gather.7.cloned.1.call-done), kind=kOutput, calls=%fused_computation.4 | convolution fusion | flops 302039040 | bytes 19070976 | tf_op jit(solution)/shard_map/dot_general | solution.py:17
  474.6 0.0 reduce-scatter.5.cloned.1.call-update
  474.6 0.6 copy.17
  475.3 3.3 all-to-all-start
  478.6 0.0 all-reduce.5.cloned.1.call-start
  478.7 0.6 copy.18
  479.4 0.0 copy-done.4
  479.4 0.6 dynamic-slice
  480.7 37.7 %psum.15 = f32[3072]{0:T(1024)} all-reduce(f32[3072]{0:T(1024)S(1)} %convert_reduce_fusion), channel_id=1, replica_groups=mesh['groups'=2,'tok'=2,'kin'=2,'nout'=4] {'tok','nout'}, use_global_device_ids=true, to_apply=%region_7.0 | all-reduce | flops 3072 | bytes 24576 | tf_op jit(solution)/shard_map/psum | solution.py:55
  518.4 0.0 reduce-scatter.3.cloned.1.call-done
  518.4 0.0 reduce-scatter.5.cloned.1.call-done
  518.4 0.0 copy-done.1
  518.4 0.9 fusion.6
  519.3 0.9 fusion.7
  520.2 1.9 all_gather.29
  522.1 2.0 all_gather.26
  524.1 12.0 %convolution_convert_fusion.2 = bf16[16,3072]{1,0:T(8,128)(2,1)} fusion(bf16[16,3072]{1,0:T(8,128)(2,1)S(1)} %all_gather.29, bf16[3072,3072]{1,0:T(8,128)(2,1)} %all-gather.5.cloned.1.call-done), kind=kOutput, calls=%fused_computation.3 | convolution fusion | flops 302039040 | bytes 19070976 | tf_op jit(solution)/shard_map/dot_general | solution.py:17
  536.1 9.6 %convolution_convert_fusion.4 = bf16[16,3072]{1,0:T(8,128)(2,1)} fusion(bf16[16,3072]{1,0:T(8,128)(2,1)S(1)} %all_gather.26, bf16[3072,3072]{1,0:T(8,128)(2,1)} %all-gather.7.cloned.1.call-done), kind=kOutput, calls=%fused_computation.5 | convolution fusion | flops 302039040 | bytes 19070976 | tf_op jit(solution)/shard_map/dot_general | solution.py:47
  545.6 0.0 all-reduce.5.cloned.1.call-update
  545.7 5.5 all_gather.30
  551.2 0.0 all-to-all-done
  551.2 3.3 all-to-all-start.1
  554.5 5.1 fusion
  559.6 0.0 copy-start.3
  559.6 5.4 all_gather.31
  565.0 0.0 all-to-all-done.1
  565.0 5.2 convolution_convert_fusion
  570.2 12.6 %copy.19 = bf16[1536,3072]{1,0:T(8,128)(2,1)} copy(bf16[1536,3072]{0,1:T(8,128)(2,1)} %fusion) | data formatting | bytes 18874368
  582.8 10.7 %psum.14 = f32[3072]{0:T(1024)} all-reduce(f32[3072]{0:T(1024)S(1)} %get-tuple-element.32), channel_id=1, replica_groups=mesh['groups'=2,'tok'=2,'kin'=2,'nout'=4] {'tok','kin'}, use_global_device_ids=true, to_apply=%region_5.0 | all-reduce | flops 3072 | bytes 24576 | tf_op jit(solution)/shard_map/psum | solution.py:64
  593.5 0.0 all-reduce.5.cloned.1.call-done
  593.5 1.4 constant_dynamic-slice_fusion
  594.9 0.0 copy-done.3
  594.9 1.4 add_convert_fusion
  (5 shorter events, 0.2 us)
Async XLA Ops:
  7.2 1.6 copy-start.2
  7.2 16.6 %copy-start = (bf16[4,3072]{1,0:T(4,128)(2,1)S(1)}, bf16[4,3072]{1,0:T(4,128)(2,1)}, u32[]{:S(2)}) copy-start(bf16[4,3072]{1,0:T(4,128)(2,1)} %param.11) | copy-start | bytes 73732
  7.2 229.5 %all-gather.5.cloned.1.call-start = ((), (), s32[]{:S(2)}) async-start(), calls=%async_computation.4 | async-start | bytes 28311552 | tf_op jit(solution)/shard_map/all_gather | solution.py:31
  7.9 454.7 %all-gather.7.cloned.1.call-start = ((), (), s32[]{:S(2)}) async-start(), calls=%async_computation.6 | async-start | bytes 28311552 | tf_op jit(solution)/shard_map/all_gather | solution.py:44
  8.7 509.7 %reduce-scatter.3.cloned.1.call-start = ((), (), s32[]{:S(2)}) async-start(), calls=%async_computation.5 | async-start | bytes 147456 | tf_op jit(solution)/shard_map/reduce_scatter | solution.py:33
  37.3 442.1 %copy-start.4 = (u32[32]{0:T(128)S(1)}, u32[32]{0:T(128)}, u32[]{:S(2)}) copy-start(u32[32]{0:T(128)} %constant.16) | copy-start | bytes 388
  37.3 481.1 %copy-start.1 = (f32[3072]{0:T(1024)S(1)}, f32[3072]{0:T(1024)}, u32[]{:S(2)}) copy-start(f32[3072]{0:T(1024)} %param.8) | copy-start | bytes 36868
  246.3 272.1 %reduce-scatter.5.cloned.1.call-start = ((), (), s32[]{:S(2)}) async-start(), calls=%async_computation.7 | async-start | bytes 147456 | tf_op jit(solution)/shard_map/reduce_scatter | solution.py:57
  475.3 75.9 %all-to-all-start = ((bf16[16,2,1536]{2,0,1:T(8,128)(2,1)}), bf16[16,2,1536]{2,0,1:T(8,128)(2,1)S(1)}, u32[]{:S(2)}, u32[]{:S(2)}) async-start(bf16[16,2,1536]{2,0,1:T(8,128)(2,1)} %copy.17), calls=%async_computation.2 | async-start | bytes 196608 | tf_op jit(solution)/shard_map/all_to_all | solution.py:30
  478.6 114.9 %all-reduce.5.cloned.1.call-start = ((), (), s32[]{:S(2)}) async-start(), calls=%async_computation.8 | async-start | bytes 393216
  551.2 13.8 %all-to-all-start.1 = ((bf16[16,2,1536]{2,0,1:T(8,128)(2,1)}), bf16[16,2,1536]{2,0,1:T(8,128)(2,1)S(1)}, u32[]{:S(2)}, u32[]{:S(2)}) async-start(bf16[16,2,1536]{2,0,1:T(8,128)(2,1)} %copy.18), calls=%async_computation.3 | async-start | bytes 196608 | tf_op jit(solution)/shard_map/all_to_all | solution.py:54
  559.6 35.3 %copy-start.3 = (f32[3072]{0:T(1024)S(1)}, f32[3072]{0:T(1024)}, u32[]{:S(2)}) copy-start(f32[3072]{0:T(1024)} %param.10) | copy-start | bytes 36868
Sparse Core Ops, SparseCore 0:
  9.6 227.0 all-gather.4
  238.2 224.3 all-gather.6
  465.4 7.4 reduce-scatter.2
  475.5 8.6 reduce-scatter.4
  545.8 32.4 all-reduce.4
where the time goes:
time: 604 us; the launch traced here: 603 us
  waiting for transfers between devices  417 us (69%)
  blocking collectives  91.8 us (15%)
  matrix products  53.3 us (9%)
  local copies, waits for them, and re-layouts  16 us (3%)
  between operations  14.5 us (2%)
  starting transfers between devices  6.87 us (1%)
    all_gather x1, waiting for transfers between devices, on_device(): w_out_block = lax.all_gather(weight_out, 'tok', axis=1, tiled=True)  216 us
    all_gather x1, waiting for transfers between devices, on_device(): w_in_block = lax.all_gather(weight_in, 'tok', axis=0, tiled=True)  199 us
    psum x1, blocking collectives, on_device(): lax.psum(jnp.sum(grad_out.astype(jnp.float32), axis=0), ('tok', 'nout'))  37.7 us
    dot_general x2, matrix products, times_transpose(): lax.dot_general(left, right, (((1,), (1,)), ((), ())), preferred_element_...  24 us
    all_gather x1, blocking collectives, on_device(): x_block = lax.all_gather(tokens, 'nout', axis=0, tiled=True)  15 us
    unnamed x15, local copies, waits for them, and re-layouts  14.7 us
    all_gather x1, blocking collectives, on_device(): dy_block = lax.all_gather(grad_out, 'nout', axis=0, tiled=True)  13.5 us
  transfers between devices with their start and end apart: 7, of which 2 were waited for; matrix products, arithmetic and copies ran while one was open for 12% of the time, Pallas kernels for 0%

commit v1 on v0

v1 whole, which is shorter than its diff:
```python
import jax
import jax.numpy as jnp
from jax import lax
from jax.sharding import PartitionSpec as P

inv_root_two = 0.7071067811865476
inv_root_two_pi = 0.3989422804014327


def gelu_parts(hidden):
    normal_cdf = 0.5 * (1.0 + lax.erf(hidden * inv_root_two))
    density = jnp.exp(-0.5 * hidden * hidden) * inv_root_two_pi
    return (hidden * normal_cdf, normal_cdf + hidden * density)


def dot(left, right, left_dim, right_dim):
    return lax.dot_general(
        left, right, (((left_dim,), (right_dim,)), ((), ())), preferred_element_type=jnp.float32
    )


def exchange(chunks, axes):
    return lax.all_to_all(chunks, axes, split_axis=0, concat_axis=0, tiled=True)


def make(mesh):
    nt, nk, nn = mesh.shape["tok"], mesh.shape["kin"], mesh.shape["nout"]
    spread, square = nt * nn, nk * nt

    def on_device(tokens, weight_in, bias_in, weight_out, bias_out, grad_out):
        rows, cols = tokens.shape
        wide, hid = weight_in.shape
        part = hid // square
        pair = 2 * rows
        total = pair * spread

        mine = jnp.concatenate([tokens, grad_out], axis=0)
        by_owner = mine.reshape(pair, nt, wide).transpose(1, 0, 2)
        chunks = jnp.broadcast_to(by_owner[:, None], (nt, nn, pair, wide))
        mixed = exchange(chunks.reshape(spread, pair, wide), ("tok", "nout")).reshape(total, wide)
        is_fwd = (lax.broadcasted_iota(jnp.int32, (total, 1), 0) % pair) < rows

        col_sums = jnp.sum(jnp.where(is_fwd, 0.0, mixed.astype(jnp.float32)), axis=0)
        bias_out_grad = lax.all_gather(col_sums, "tok", axis=0, tiled=True)

        partial = jnp.where(is_fwd, dot(mixed, weight_in, 1, 0), dot(mixed, weight_out, 1, 1))
        partial = partial.astype(jnp.bfloat16).reshape(total, square, part).transpose(1, 0, 2)
        got = exchange(partial, ("kin", "tok"))
        summed = jnp.sum(got.astype(jnp.float32), axis=0).reshape(spread, 2, rows, part)
        at = lax.axis_index(("kin", "tok"))
        pre_act = summed[:, 0] + lax.dynamic_slice_in_dim(bias_in, at * part, part)
        activated, slopes = gelu_parts(pre_act)
        grad_pre = summed[:, 1] * slopes
        both = jnp.stack([activated, grad_pre], axis=1).astype(jnp.bfloat16).reshape(total, part)
        both = exchange(jnp.broadcast_to(both[None], (square, total, part)), ("kin", "tok"))
        both = both.transpose(1, 0, 2).reshape(total, hid)

        split = both.reshape(spread, 2, rows, hid)
        act = split[:, 0].reshape(spread * rows, hid)
        grad_half = split[:, 1].reshape(spread * rows, hid)
        split = mixed.reshape(spread, 2, rows, wide)
        x_cols = split[:, 0].reshape(spread * rows, wide)
        dy_cols = split[:, 1].reshape(spread * rows, wide)
        bias_in_grad = jnp.sum(grad_half.astype(jnp.float32), axis=0)

        block = jnp.stack(
            [
                dot(act, weight_out, 1, 0).reshape(spread, rows, wide),
                dot(grad_half, weight_in, 1, 1).reshape(spread, rows, wide),
            ],
            axis=1,
        )
        block = block.astype(jnp.bfloat16).reshape(spread, pair, wide)
        back = exchange(block, ("tok", "nout")).reshape(nt, nn, pair, wide)
        weight_in_grad = dot(x_cols, grad_half, 0, 0).astype(jnp.bfloat16)
        weight_out_grad = dot(act, dy_cols, 0, 0).astype(jnp.bfloat16)
        final = jnp.sum(back.astype(jnp.float32), axis=1).transpose(1, 0, 2).reshape(pair, cols)
        output_rows = (final[:rows] + bias_out).astype(jnp.bfloat16)
        grad_tokens = final[rows:].astype(jnp.bfloat16)
        return (output_rows, grad_tokens, weight_in_grad, weight_out_grad, bias_in_grad, bias_out_grad)

    return on_device


def solution(mesh):
    return jax.shard_map(
        make(mesh),
        mesh=mesh,
        in_specs=(
            P(("groups", "tok", "nout"), "kin"),
            P(("kin", "tok"), "nout"),
            P("nout"),
            P("nout", ("kin", "tok")),
            P("kin"),
            P(("groups", "tok", "nout"), "kin"),
        ),
        out_specs=(
            P(("groups", "tok", "nout"), "kin"),
            P(("groups", "tok", "nout"), "kin"),
            P(("groups", "kin", "tok"), "nout"),
            P(("groups", "nout"), ("kin", "tok")),
            P(("groups", "nout")),
            P(("groups", "kin")),
        ),
        check_vma=False,
    )
```

time: 604 us -> 81.4 us (0.13)
  waiting for transfers between devices: 417 us -> 15.3 us
  blocking collectives: 91.8 us -> 7.44 us
  matrix products: 53.3 us -> 30.7 us
  between operations: 14.5 us -> 0.8 us
  starting transfers between devices: 6.87 us -> 17.6 us
  local copies, waits for them, and re-layouts: 16 us -> 6.56 us
    all_gather x2 -> x0, waiting for transfers between devices: 416 us -> none  [the longest x1 216 us: on_device(): w_out_block = lax.all_gather(weight_out, 'tok', axis=1, tiled=True)]
    psum x2 -> x0, blocking collectives: 48.4 us -> none  [the longest x1 37.7 us: on_device(): lax.psum(jnp.sum(grad_out.astype(jnp.float32), axis=0), ('tok', 'nout'))]
    all_gather x6 -> x1, blocking collectives: 43.4 us -> 7.44 us  [on_device(): bias_out_grad = lax.all_gather(col_sums, 'tok', axis=0, tiled=True)]
    dot_general x6, matrix products: 53.3 us -> 30.7 us  [dot(): lax.dot_general(left, right, (((left_dim,), (right_dim,)), ((), ())), pre...]
    all_to_all x2 -> x4, waiting for transfers between devices: 0.01 us -> 15.3 us  [exchange(): return lax.all_to_all(chunks, axes, split_axis=0, concat_axis=0, tiled=True)]
    unnamed x15 -> x6, local copies, waits for them, and re-layouts: 14.7 us -> 1.39 us
    all_to_all x2 -> x4, starting transfers between devices: 6.67 us -> 17.6 us  [exchange(): return lax.all_to_all(chunks, axes, split_axis=0, concat_axis=0, tiled=True)]
  transfers between devices with their start and end apart: 7 -> 4, of which waited for: 2 -> 2; matrix products, arithmetic and copies ran while one was open for 12% -> 15% of each run, Pallas kernels for 0% -> 0%
where the time goes in v1:
time: 81.4 us; the launch traced here: 80.8 us
  matrix products  30.7 us (38%)
  starting transfers between devices  17.6 us (22%)
  waiting for transfers between devices  15.3 us (19%)
  blocking collectives  7.44 us (9%)
  local copies, waits for them, and re-layouts  6.56 us (8%)
  other arithmetic  2.41 us (3%)
    dot_general x6, matrix products, dot(): lax.dot_general(left, right, (((left_dim,), (right_dim,)), ((), ())), pre...  30.7 us
    all_to_all x4, starting transfers between devices, exchange(): return lax.all_to_all(chunks, axes, split_axis=0, concat_axis=0, tiled=True)  17.6 us
    all_to_all x4, waiting for transfers between devices, exchange(): return lax.all_to_all(chunks, axes, split_axis=0, concat_axis=0, tiled=True)  15.3 us
    all_gather x1, blocking collectives, on_device(): bias_out_grad = lax.all_gather(col_sums, 'tok', axis=0, tiled=True)  7.44 us
  transfers between devices with their start and end apart: 4, of which 2 were waited for; matrix products, arithmetic and copies ran while one was open for 15% of the time, Pallas kernels for 0%

profile of v1, /device:TPU:0, one launch (start us, length us, event | category | flops | bytes accessed | tf_op | source)
XLA Modules:
  0.0 80.8 jit_solution(14736334049109159310)
XLA Ops:
  0.6 0.8 pad_maximum_fusion.2
  1.4 0.7 broadcast_in_dim.34
  2.1 7.3 %all-to-all-start = ((bf16[8,8,1536]{2,1,0:T(8,128)(2,1)}), bf16[8,8,1536]{2,1,0:T(8,128)(2,1)S(1)}, u32[]{:S(2)}, u32[]{:S(2)}) async-start(bf16[8,8,1536]{2,1,0:T(8,128)(2,1)} %bitcast.2), calls=%async_computation | async-start | bytes 393216 | tf_op jit(solution)/shard_map/all_to_all | solution.py:23
  9.4 8.7 %all-to-all-done = bf16[8,8,1536]{2,1,0:T(8,128)(2,1)S(1)} async-done(((bf16[8,8,1536]{2,1,0:T(8,128)(2,1)}), bf16[8,8,1536]{2,1,0:T(8,128)(2,1)S(1)}, u32[]{:S(2)}, u32[]{:S(2)}) %all-to-all-start) | async-done | bytes 196640 | tf_op jit(solution)/shard_map/all_to_all | solution.py:23
  18.1 0.0 copy-start
  18.1 5.6 %fusion.20 = bf16[64,3072]{1,0:T(8,128)(2,1)S(1)} fusion(bf16[1536,3072]{1,0:T(8,128)(2,1)} %param.7, bf16[8,8,1536]{2,1,0:T(8,128)(2,1)S(1)} %all-to-all-done), kind=kOutput, calls=%fused_computation.22 | convolution fusion | flops 603979776 | bytes 10027008 | tf_op jit(solution)/shard_map/dot_general | solution.py:17
  23.7 0.8 copy-done
  24.5 2.9 %fusion.4 = bf16[64,3072]{1,0:T(8,128)(2,1)S(1)} fusion(bf16[64,3072]{1,0:T(8,128)(2,1)S(1)} %fusion.20, bf16[3072,1536]{1,0:T(8,128)(2,1)S(1)} %copy-done, pred[64]{0:T(512)(128)(4,1)S(1)} %fusion.34, bf16[8,8,1536]{2,1,0:T(8,128)(2,1)S(1)} %all-to-all-done), kind=kOutput, calls=%fused_computation.7 | convolution fusion | flops 604176384 | bytes 10420288 | tf_op jit(solution)/shard_map/dot_general | solution.py:17
  27.4 0.8 copy.73
  28.2 3.5 %all-to-all-start.1 = ((bf16[4,64,768]{2,1,0:T(8,128)(2,1)}), bf16[4,64,768]{2,1,0:T(8,128)(2,1)S(1)}, u32[]{:S(2)}, u32[]{:S(2)}) async-start(bf16[4,64,768]{2,1,0:T(8,128)(2,1)} %bitcast.64), calls=%async_computation.1 | async-start | bytes 786432 | tf_op jit(solution)/shard_map/all_to_all | solution.py:23
  31.6 0.8 dynamic_slice.3
  32.4 6.6 %all-to-all-done.1 = bf16[4,64,768]{2,1,0:T(8,128)(2,1)S(1)} async-done(((bf16[4,64,768]{2,1,0:T(8,128)(2,1)}), bf16[4,64,768]{2,1,0:T(8,128)(2,1)S(1)}, u32[]{:S(2)}, u32[]{:S(2)}) %all-to-all-start.1) | async-done | bytes 393248 | tf_op jit(solution)/shard_map/all_to_all | solution.py:23
  39.0 0.1 convert_reduce_fusion
  39.1 0.1 reshape.95
  39.2 0.1 multiply_convert_fusion
  39.4 0.8 broadcast_in_dim.35
  40.1 3.5 %all-to-all-start.2 = ((bf16[4,64,768]{2,1,0:T(8,128)(2,1)}), bf16[4,64,768]{2,1,0:T(8,128)(2,1)S(1)}, u32[]{:S(2)}, u32[]{:S(2)}) async-start(bf16[4,64,768]{2,1,0:T(8,128)(2,1)} %broadcast_in_dim.35), calls=%async_computation.2 | async-start | bytes 786432 | tf_op jit(solution)/shard_map/all_to_all | solution.py:23
  43.6 0.1 select_reduce_fusion
  43.8 7.4 %all-gather = f32[2,1,1536]{2,1,0:T(1,128)S(1)} all-gather(f32[1,1,1536]{2,1,0:T(1,128)S(1)} %reshape.101), channel_id=1, replica_groups=mesh['groups'=2,'tok'=2,'kin'=2,'nout'=4] {'tok'}, dimensions={0}, use_global_device_ids=true | all-gather | bytes 18432 | tf_op jit(solution)/shard_map/all_gather | solution.py:44
  51.2 0.1 copy.42
  51.3 0.0 all-to-all-done.2
  51.3 0.3 copy.38
  51.6 0.1 reshape_reshape.6
  51.7 0.1 fusion.35
  51.9 5.3 %fusion.14 = bf16[8,1,4,1536]{3,0,2,1:T(8,128)(2,1)S(1)} fusion(bf16[3072,1536]{1,0:T(8,128)(2,1)} %param.9, bf16[8,1,4,3072]{3,2,1,0:T(4,128)(2,1)S(1)} %get-tuple-element.6), kind=kOutput, calls=%fused_computation.11 | convolution fusion | flops 302039040 | bytes 9732096 | tf_op jit(solution)/shard_map/dot_general | solution.py:17
  57.2 6.5 %fusion.11 = bf16[8,1,4,1536]{3,0,2,1:T(8,128)(2,1)S(1)} fusion(bf16[1536,3072]{1,0:T(8,128)(2,1)} %param.7, bf16[8,1,4,3072]{3,2,1,0:T(4,128)(2,1)S(1)} %get-tuple-element.7), kind=kOutput, calls=%fused_computation.10 | convolution fusion | flops 302039040 | bytes 9732096 | tf_op jit(solution)/shard_map/dot_general | solution.py:17
  63.7 0.7 copy.41
  64.4 3.4 %all-to-all-start.3 = ((bf16[8,8,1536]{2,1,0:T(8,128)(2,1)}), bf16[8,8,1536]{2,1,0:T(8,128)(2,1)S(1)}, u32[]{:S(2)}, u32[]{:S(2)}) async-start(bf16[8,8,1536]{2,1,0:T(8,128)(2,1)} %copy.41), calls=%async_computation.3 | async-start | bytes 393216 | tf_op jit(solution)/shard_map/all_to_all | solution.py:23
  67.8 5.2 %bitcast_convert_fusion.1 = bf16[1536,3072]{1,0:T(8,128)(2,1)} fusion(bf16[8,1,4,3072]{3,2,1,0:T(4,128)(2,1)S(1)} %get-tuple-element.7, bf16[8,2,4,1536]{3,0,2,1:T(8,128)(2,1)S(1)} %bitcast.70), kind=kOutput, calls=%fused_computation.1 | convolution fusion | flops 306708480 | bytes 9732096 | tf_op jit(solution)/shard_map/dot_general | solution.py:17
  73.0 0.0 copy-start.1
  73.0 5.2 %bitcast_convert_fusion = bf16[3072,1536]{1,0:T(8,128)(2,1)} fusion(bf16[8,1,4,3072]{3,2,1,0:T(4,128)(2,1)S(1)} %get-tuple-element.6, bf16[8,2,4,1536]{3,0,2,1:T(8,128)(2,1)S(1)} %bitcast.71), kind=kOutput, calls=%fused_computation | convolution fusion | flops 306708480 | bytes 9732096 | tf_op jit(solution)/shard_map/dot_general | solution.py:17
  78.2 0.7 convert_reduce_fusion.2
  78.9 0.0 all-to-all-done.3
  78.9 0.6 slice.51
  79.5 0.0 copy-done.1
  79.5 0.6 add_convert_fusion
  80.2 0.6 copy.75
  (10 shorter events, 0.2 us)
Async XLA Ops:
  2.1 16.0 %all-to-all-start = ((bf16[8,8,1536]{2,1,0:T(8,128)(2,1)}), bf16[8,8,1536]{2,1,0:T(8,128)(2,1)S(1)}, u32[]{:S(2)}, u32[]{:S(2)}) async-start(bf16[8,8,1536]{2,1,0:T(8,128)(2,1)} %bitcast.2), calls=%async_computation | async-start | bytes 393216 | tf_op jit(solution)/shard_map/all_to_all | solution.py:23
  18.1 6.4 %copy-start = (bf16[3072,1536]{1,0:T(8,128)(2,1)S(1)}, bf16[3072,1536]{1,0:T(8,128)(2,1)}, u32[]{:S(2)}) copy-start(bf16[3072,1536]{1,0:T(8,128)(2,1)} %param.9) | copy-start | bytes 28311556
  28.2 10.9 %all-to-all-start.1 = ((bf16[4,64,768]{2,1,0:T(8,128)(2,1)}), bf16[4,64,768]{2,1,0:T(8,128)(2,1)S(1)}, u32[]{:S(2)}, u32[]{:S(2)}) async-start(bf16[4,64,768]{2,1,0:T(8,128)(2,1)} %bitcast.64), calls=%async_computation.1 | async-start | bytes 786432 | tf_op jit(solution)/shard_map/all_to_all | solution.py:23
  40.1 11.1 %all-to-all-start.2 = ((bf16[4,64,768]{2,1,0:T(8,128)(2,1)}), bf16[4,64,768]{2,1,0:T(8,128)(2,1)S(1)}, u32[]{:S(2)}, u32[]{:S(2)}) async-start(bf16[4,64,768]{2,1,0:T(8,128)(2,1)} %broadcast_in_dim.35), calls=%async_computation.2 | async-start | bytes 786432 | tf_op jit(solution)/shard_map/all_to_all | solution.py:23
  64.4 14.4 %all-to-all-start.3 = ((bf16[8,8,1536]{2,1,0:T(8,128)(2,1)}), bf16[8,8,1536]{2,1,0:T(8,128)(2,1)S(1)}, u32[]{:S(2)}, u32[]{:S(2)}) async-start(bf16[8,8,1536]{2,1,0:T(8,128)(2,1)} %copy.41), calls=%async_computation.3 | async-start | bytes 393216 | tf_op jit(solution)/shard_map/all_to_all | solution.py:23
  73.0 6.5 %copy-start.1 = (f32[3072]{0:T(1024)S(1)}, f32[3072]{0:T(1024)}, u32[]{:S(2)}) copy-start(f32[3072]{0:T(1024)} %param.10) | copy-start | bytes 36868

commit v2 on v1

--- a/solution.py
+++ b/solution.py
@@ -19,8 +19,23 @@
     )
 
 
-def exchange(chunks, axes):
-    return lax.all_to_all(chunks, axes, split_axis=0, concat_axis=0, tiled=True)
+def exchange(chunks, axes, sizes):
+    count = chunks.shape[0]
+    if count > 8:
+        return lax.all_to_all(chunks, axes, split_axis=0, concat_axis=0, tiled=True)
+    me = lax.axis_index(axes)
+    got = [lax.dynamic_index_in_dim(chunks, me, 0, keepdims=False)]
+    in_order = tuple(name for name in ("tok", "kin", "nout") if name in axes)
+
+    def place(i):
+        low, high = i % sizes[1], i // sizes[1]
+        return i if in_order == axes else low * sizes[0] + high
+
+    for apart in range(1, count):
+        sent = lax.dynamic_index_in_dim(chunks, me ^ apart, 0, keepdims=False)
+        pairs = [(place(i), place(i ^ apart)) for i in range(count)]
+        got.append(lax.ppermute(sent, in_order, pairs))
+    return jnp.take(jnp.stack(got), me ^ jnp.arange(count), axis=0, mode="clip")
 
 
 def make(mesh):
@@ -37,7 +52,7 @@
         mine = jnp.concatenate([tokens, grad_out], axis=0)
         by_owner = mine.reshape(pair, nt, wide).transpose(1, 0, 2)
         chunks = jnp.broadcast_to(by_owner[:, None], (nt, nn, pair, wide))
-        mixed = exchange(chunks.reshape(spread, pair, wide), ("tok", "nout")).reshape(total, wide)
+        mixed = exchange(chunks.reshape(spread, pair, wide), ("tok", "nout"), (nt, nn)).reshape(total, wide)
         is_fwd = (lax.broadcasted_iota(jnp.int32, (total, 1), 0) % pair) < rows
 
         col_sums = jnp.sum(jnp.where(is_fwd, 0.0, mixed.astype(jnp.float32)), axis=0)
@@ -45,14 +60,14 @@
 
         partial = jnp.where(is_fwd, dot(mixed, weight_in, 1, 0), dot(mixed, weight_out, 1, 1))
         partial = partial.astype(jnp.bfloat16).reshape(total, square, part).transpose(1, 0, 2)
-        got = exchange(partial, ("kin", "tok"))
+        got = exchange(partial, ("kin", "tok"), (nk, nt))
         summed = jnp.sum(got.astype(jnp.float32), axis=0).reshape(spread, 2, rows, part)
         at = lax.axis_index(("kin", "tok"))
         pre_act = summed[:, 0] + lax.dynamic_slice_in_dim(bias_in, at * part, part)
         activated, slopes = gelu_parts(pre_act)
         grad_pre = summed[:, 1] * slopes
         both = jnp.stack([activated, grad_pre], axis=1).astype(jnp.bfloat16).reshape(total, part)
-        both = exchange(jnp.broadcast_to(both[None], (square, total, part)), ("kin", "tok"))
+        both = exchange(jnp.broadcast_to(both[None], (square, total, part)), ("kin", "tok"), (nk, nt))
         both = both.transpose(1, 0, 2).reshape(total, hid)
 
         split = both.reshape(spread, 2, rows, hid)
@@ -71,7 +86,7 @@
             axis=1,
         )
         block = block.astype(jnp.bfloat16).reshape(spread, pair, wide)
-        back = exchange(block, ("tok", "nout")).reshape(nt, nn, pair, wide)
+        back = exchange(block, ("tok", "nout"), (nt, nn)).reshape(nt, nn, pair, wide)
         weight_in_grad = dot(x_cols, grad_half, 0, 0).astype(jnp.bfloat16)
         weight_out_grad = dot(act, dy_cols, 0, 0).astype(jnp.bfloat16)
         final = jnp.sum(back.astype(jnp.float32), axis=1).transpose(1, 0, 2).reshape(pair, cols)

time: 81.4 us -> 90.4 us (1.11)
  starting transfers between devices: 17.6 us -> 30.9 us
  matrix products: 30.7 us -> 27.4 us
  blocking collectives: 7.44 us -> 5.11 us
    ppermute x0 -> x20, starting transfers between devices: none -> 30.9 us  [exchange(): got.append(lax.ppermute(sent, in_order, pairs))]
    all_to_all x4 -> x0, starting transfers between devices: 17.6 us -> none  [exchange(): return lax.all_to_all(chunks, axes, split_axis=0, concat_axis=0, tiled=True)]
    ppermute x0 -> x20, waiting for transfers between devices: none -> 16.1 us  [exchange(): got.append(lax.ppermute(sent, in_order, pairs))]
    all_to_all x4 -> x0, waiting for transfers between devices: 15.3 us -> none  [exchange(): return lax.all_to_all(chunks, axes, split_axis=0, concat_axis=0, tiled=True)]
    dot_general x6, matrix products: 30.7 us -> 27.4 us  [dot(): lax.dot_general(left, right, (((left_dim,), (right_dim,)), ((), ())), pre...]
    all_gather x1, blocking collectives: 7.44 us -> 5.11 us  [on_device(): bias_out_grad = lax.all_gather(col_sums, 'tok', axis=0, tiled=True)]
    gather x0 -> x5, local copies, waits for them, and re-layouts: none -> 2.33 us  [exchange(): return jnp.take(jnp.stack(got), me ^ jnp.arange(count), axis=0, mode='clip')]
  transfers between devices with their start and end apart: 4 -> 20, of which waited for: 2 -> 7; matrix products, arithmetic and copies ran while one was open for 15% -> 1% of each run, Pallas kernels for 0% -> 0%
where the time goes in v2:
time: 90.4 us; the launch traced here: 90.2 us
  starting transfers between devices  30.9 us (34%)
  matrix products  27.4 us (30%)
  waiting for transfers between devices  16.1 us (18%)
  local copies, waits for them, and re-layouts  6.9 us (8%)
  blocking collectives  5.11 us (6%)
  other arithmetic  2.54 us (3%)
  between operations  1.22 us (1%)
    ppermute x20, starting transfers between devices, exchange(): got.append(lax.ppermute(sent, in_order, pairs))  30.9 us
    dot_general x6, matrix products, dot(): lax.dot_general(left, right, (((left_dim,), (right_dim,)), ((), ())), pre...  27.4 us
    ppermute x20, waiting for transfers between devices, exchange(): got.append(lax.ppermute(sent, in_order, pairs))  16.1 us
    all_gather x1, blocking collectives, on_device(): bias_out_grad = lax.all_gather(col_sums, 'tok', axis=0, tiled=True)  5.11 us
    gather x5, local copies, waits for them, and re-layouts, exchange(): return jnp.take(jnp.stack(got), me ^ jnp.arange(count), axis=0, mode='clip')  2.33 us
  transfers between devices with their start and end apart: 20, of which 7 were waited for; matrix products, arithmetic and copies ran while one was open for 1% of the time, Pallas kernels for 0%

profile of v2, /device:TPU:0, one launch (start us, length us, event | category | flops | bytes accessed | tf_op | source)
XLA Modules:
  0.0 90.2 jit_solution(17134881429735345764)
XLA Ops:
  0.7 0.8 pad_maximum_fusion.3
  1.5 6.0 %collective-permute-start.6 = (bf16[8,1536]{1,0:T(8,128)(2,1)S(1)}, bf16[8,1536]{1,0:T(8,128)(2,1)S(1)}, u32[]{:S(2)}, u32[]{:S(2)}) collective-permute-start(bf16[8,1536]{1,0:T(8,128)(2,1)S(1)} %get-tuple-element.22), channel_id=1, source_target_pairs={{0,11},{1,10},{2,9},{3,8},{8,3},{9,2},{10,1},{11,0},{4,15},{5,14},... | collective-permute-start | bytes 73736 | tf_op jit(solution)/shard_map/ppermute | solution.py:37
  7.6 1.7 %collective-permute-start.4 = (bf16[8,1536]{1,0:T(8,128)(2,1)S(1)}, bf16[8,1536]{1,0:T(8,128)(2,1)S(1)}, u32[]{:S(2)}, u32[]{:S(2)}) collective-permute-start(bf16[8,1536]{1,0:T(8,128)(2,1)S(1)} %get-tuple-element.24), channel_id=1, source_target_pairs={{0,9},{1,8},{2,11},{3,10},{8,1},{9,0},{10,3},{11,2},{4,13},{5,12},... | collective-permute-start | bytes 73736 | tf_op jit(solution)/shard_map/ppermute | solution.py:37
  9.3 0.4 collective-permute-start.3
  9.7 1.4 %collective-permute-start = (bf16[8,1536]{1,0:T(8,128)(2,1)S(1)}, bf16[8,1536]{1,0:T(8,128)(2,1)S(1)}, u32[]{:S(2)}, u32[]{:S(2)}) collective-permute-start(bf16[8,1536]{1,0:T(8,128)(2,1)S(1)} %get-tuple-element.28), channel_id=1, source_target_pairs={{0,1},{1,0},{2,3},{3,2},{8,9},{9,8},{10,11},{11,10},{4,5},{5,4},{6... | collective-permute-start | bytes 73736 | tf_op jit(solution)/shard_map/ppermute | solution.py:37
  11.1 0.8 dynamic_slice.72
  11.9 1.6 %collective-permute-done = bf16[8,1536]{1,0:T(8,128)(2,1)S(1)} collective-permute-done((bf16[8,1536]{1,0:T(8,128)(2,1)S(1)}, bf16[8,1536]{1,0:T(8,128)(2,1)S(1)}, u32[]{:S(2)}, u32[]{:S(2)}) %collective-permute-start) | collective-permute-done | bytes 24608 | tf_op jit(solution)/shard_map/ppermute | solution.py:37
  13.5 2.3 %collective-permute-start.1 = (bf16[8,1536]{1,0:T(8,128)(2,1)S(1)}, bf16[8,1536]{1,0:T(8,128)(2,1)S(1)}, u32[]{:S(2)}, u32[]{:S(2)}) collective-permute-start(bf16[8,1536]{1,0:T(8,128)(2,1)S(1)} %get-tuple-element.27), channel_id=1, source_target_pairs={{0,2},{1,3},{2,0},{3,1},{8,10},{9,11},{10,8},{11,9},{4,6},{5,7},{6... | collective-permute-start | bytes 73736 | tf_op jit(solution)/shard_map/ppermute | solution.py:37
  15.8 2.4 %collective-permute-done.1 = bf16[8,1536]{1,0:T(8,128)(2,1)S(1)} collective-permute-done((bf16[8,1536]{1,0:T(8,128)(2,1)S(1)}, bf16[8,1536]{1,0:T(8,128)(2,1)S(1)}, u32[]{:S(2)}, u32[]{:S(2)}) %collective-permute-start.1) | collective-permute-done | bytes 24608 | tf_op jit(solution)/shard_map/ppermute | solution.py:37
  18.2 3.7 %collective-permute-start.2 = (bf16[8,1536]{1,0:T(8,128)(2,1)S(1)}, bf16[8,1536]{1,0:T(8,128)(2,1)S(1)}, u32[]{:S(2)}, u32[]{:S(2)}) collective-permute-start(bf16[8,1536]{1,0:T(8,128)(2,1)S(1)} %get-tuple-element.26), channel_id=1, source_target_pairs={{0,3},{1,2},{2,1},{3,0},{8,11},{9,10},{10,9},{11,8},{4,7},{5,6},{6... | collective-permute-start | bytes 73736 | tf_op jit(solution)/shard_map/ppermute | solution.py:37
  22.0 1.9 %collective-permute-done.2 = bf16[8,1536]{1,0:T(8,128)(2,1)S(1)} collective-permute-done((bf16[8,1536]{1,0:T(8,128)(2,1)S(1)}, bf16[8,1536]{1,0:T(8,128)(2,1)S(1)}, u32[]{:S(2)}, u32[]{:S(2)}) %collective-permute-start.2) | collective-permute-done | bytes 24608 | tf_op jit(solution)/shard_map/ppermute | solution.py:37
  23.9 0.0 collective-permute-done.4
  23.9 0.0 collective-permute-done.6
  23.9 0.6 gather_fusion
  24.5 0.0 copy-start
  24.5 6.8 %fusion.19 = bf16[64,3072]{1,0:T(8,128)(2,1)S(1)} fusion(bf16[3072,1536]{1,0:T(8,128)(2,1)} %param.9, bf16[8,8,1536]{2,1,0:T(8,128)(2,1)S(1)} %gather_fusion), kind=kOutput, calls=%fused_computation.27 | convolution fusion | flops 603979776 | bytes 10027008 | tf_op jit(solution)/shard_map/dot_general | solution.py:17
  31.3 1.8 %fusion.4 = bf16[64,3072]{1,0:T(8,128)(2,1)S(1)} fusion(bf16[64,3072]{1,0:T(8,128)(2,1)S(1)} %fusion.19, bf16[1536,3072]{1,0:T(8,128)(2,1)S(1)} %copy-done, pred[64]{0:T(512)(128)(4,1)S(1)} %fusion.34, bf16[8,8,1536]{2,1,0:T(8,128)(2,1)S(1)} %gather_fusion), kind=kOutput, calls=%fused_computation.11 | convolution fusion | flops 604176384 | bytes 10420288 | tf_op jit(solution)/shard_map/dot_general | solution.py:17
  33.1 0.3 reshape.124
  33.3 0.8 constant_dynamic-slice_fusion.11
  34.2 0.1 collective-permute-start.9
  34.3 1.7 %collective-permute-start.7 = (bf16[64,768]{1,0:T(8,128)(2,1)S(1)}, bf16[64,768]{1,0:T(8,128)(2,1)S(1)}, u32[]{:S(2)}, u32[]{:S(2)}) collective-permute-start(bf16[64,768]{1,0:T(8,128)(2,1)S(1)} %bitcast.162), channel_id=1, source_target_pairs={{0,8},{8,0},{4,12},{12,4},{1,9},{9,1},{5,13},{13,5},{2,10},{10,2},... | collective-permute-start | bytes 294920 | tf_op jit(solution)/shard_map/ppermute | solution.py:37
  36.0 0.2 collective-permute-start.8
  36.2 0.1 copy.94
  36.3 2.9 %collective-permute-done.9 = bf16[64,768]{1,0:T(8,128)(2,1)S(1)} collective-permute-done((bf16[64,768]{1,0:T(8,128)(2,1)S(1)}, bf16[64,768]{1,0:T(8,128)(2,1)S(1)}, u32[]{:S(2)}, u32[]{:S(2)}) %collective-permute-start.9) | collective-permute-done | bytes 98336 | tf_op jit(solution)/shard_map/ppermute | solution.py:37
  39.2 2.3 %collective-permute-done.7 = bf16[64,768]{1,0:T(8,128)(2,1)S(1)} collective-permute-done((bf16[64,768]{1,0:T(8,128)(2,1)S(1)}, bf16[64,768]{1,0:T(8,128)(2,1)S(1)}, u32[]{:S(2)}, u32[]{:S(2)}) %collective-permute-start.7) | collective-permute-done | bytes 98336 | tf_op jit(solution)/shard_map/ppermute | solution.py:37
  41.5 0.0 collective-permute-done.8
  41.5 0.1 pad_maximum_fusion
  41.6 0.0 slice-start
  41.6 0.6 gather_fusion.1
  42.2 0.1 convert_reduce_fusion
  42.2 0.1 reshape.125
  42.3 0.1 fusion.29
  42.5 0.1 collective-permute-start.12
  42.6 0.2 collective-permute-start.11
  42.8 1.9 %collective-permute-start.10 = (bf16[64,768]{1,0:T(8,128)(2,1)S(1)}, bf16[64,768]{1,0:T(8,128)(2,1)S(1)}, u32[]{:S(2)}, u32[]{:S(2)}) collective-permute-start(bf16[64,768]{1,0:T(8,128)(2,1)S(1)} %convert_element_type.59), channel_id=1, source_target_pairs={{0,8},{8,0},{4,12},{12,4},{1,9},{9,1},{5,13},{13,5},{2,10},{10,2},... | collective-permute-start | bytes 294920 | tf_op jit(solution)/shard_map/ppermute | solution.py:37
  44.7 0.1 select_reduce_fusion
  44.8 5.1 %all-gather = f32[2,1,1536]{2,1,0:T(1,128)S(1)} all-gather(f32[1,1,1536]{2,1,0:T(1,128)S(1)} %reshape.163), channel_id=1, replica_groups=mesh['groups'=2,'tok'=2,'kin'=2,'nout'=4] {'tok'}, dimensions={0}, use_global_device_ids=true | all-gather | bytes 18432 | tf_op jit(solution)/shard_map/all_gather | solution.py:59
  50.0 0.0 collective-permute-done.12
  50.0 0.0 collective-permute-done.11
  50.0 0.1 pad_maximum_fusion.1
  50.1 0.6 gather_fusion.2
  50.6 0.3 copy.83
  50.9 0.1 reshape_reshape.6
  51.1 0.0 slice-start.1
  51.1 0.1 fusion.35
  51.3 0.7 convert_reduce_fusion.2
  51.9 6.9 %fusion.11 = bf16[8,1,4,1536]{3,0,2,1:T(8,128)(2,1)S(1)} fusion(bf16[1536,3072]{1,0:T(8,128)(2,1)} %param.7, bf16[8,1,4,3072]{3,2,1,0:T(4,128)(2,1)S(1)} %get-tuple-element.7), kind=kOutput, calls=%fused_computation.14 | convolution fusion | flops 302039040 | bytes 9732096 | tf_op jit(solution)/shard_map/dot_general | solution.py:17
  58.9 1.6 %fusion.14 = bf16[8,1,4,1536]{3,0,2,1:T(8,128)(2,1)S(1)} fusion(bf16[3072,1536]{1,0:T(8,128)(2,1)S(1)} %bitcast.144, bf16[8,1,4,3072]{3,2,1,0:T(4,128)(2,1)S(1)} %get-tuple-element.6), kind=kOutput, calls=%fused_computation.15 | convolution fusion | flops 302039040 | bytes 9732096 | tf_op jit(solution)/shard_map/dot_general | solution.py:17
  60.5 5.2 %bitcast_convert_fusion.1 = bf16[1536,3072]{1,0:T(8,128)(2,1)} fusion(bf16[8,1,4,3072]{3,2,1,0:T(4,128)(2,1)S(1)} %get-tuple-element.7, bf16[8,2,4,1536]{3,0,2,1:T(8,128)(2,1)S(1)} %bitcast.151), kind=kOutput, calls=%fused_computation.5 | convolution fusion | flops 306708480 | bytes 9732096 | tf_op jit(solution)/shard_map/dot_general | solution.py:17
  65.7 5.2 %bitcast_convert_fusion = bf16[3072,1536]{1,0:T(8,128)(2,1)} fusion(bf16[8,1,4,3072]{3,2,1,0:T(4,128)(2,1)S(1)} %get-tuple-element.6, bf16[8,2,4,1536]{3,0,2,1:T(8,128)(2,1)S(1)} %bitcast.152), kind=kOutput, calls=%fused_computation.4 | convolution fusion | flops 306708480 | bytes 9732096 | tf_op jit(solution)/shard_map/dot_general | solution.py:17
  70.9 0.5 constant_dynamic-slice_fusion
  71.4 0.1 collective-permute-start.13
  71.5 4.3 %collective-permute-start.14 = (bf16[8,1536]{1,0:T(8,128)(2,1)S(1)}, bf16[8,1536]{1,0:T(8,128)(2,1)S(1)}, u32[]{:S(2)}, u32[]{:S(2)}) collective-permute-start(bf16[8,1536]{1,0:T(8,128)(2,1)S(1)} %bitcast.171), channel_id=1, source_target_pairs={{0,2},{1,3},{2,0},{3,1},{8,10},{9,11},{10,8},{11,9},{4,6},{5,7},{6... | collective-permute-start | bytes 73736 | tf_op jit(solution)/shard_map/ppermute | solution.py:37
  75.8 0.1 collective-permute-start.15
  75.9 0.1 collective-permute-start.16
  76.0 1.8 %collective-permute-start.17 = (bf16[8,1536]{1,0:T(8,128)(2,1)S(1)}, bf16[8,1536]{1,0:T(8,128)(2,1)S(1)}, u32[]{:S(2)}, u32[]{:S(2)}) collective-permute-start(bf16[8,1536]{1,0:T(8,128)(2,1)S(1)} %bitcast.166), channel_id=1, source_target_pairs={{0,9},{1,8},{2,11},{3,10},{8,1},{9,0},{10,3},{11,2},{4,13},{5,12},... | collective-permute-start | bytes 73736 | tf_op jit(solution)/shard_map/ppermute | solution.py:37
  77.8 3.3 %collective-permute-start.18 = (bf16[8,1536]{1,0:T(8,128)(2,1)S(1)}, bf16[8,1536]{1,0:T(8,128)(2,1)S(1)}, u32[]{:S(2)}, u32[]{:S(2)}) collective-permute-start(bf16[8,1536]{1,0:T(8,128)(2,1)S(1)} %bitcast.170), channel_id=1, source_target_pairs={{0,10},{1,11},{2,8},{3,9},{8,2},{9,3},{10,0},{11,1},{4,14},{5,15},... | collective-permute-start | bytes 73736 | tf_op jit(solution)/shard_map/ppermute | solution.py:37
  81.2 1.6 %collective-permute-start.19 = (bf16[8,1536]{1,0:T(8,128)(2,1)S(1)}, bf16[8,1536]{1,0:T(8,128)(2,1)S(1)}, u32[]{:S(2)}, u32[]{:S(2)}) collective-permute-start(bf16[8,1536]{1,0:T(8,128)(2,1)S(1)} %bitcast.169), channel_id=1, source_target_pairs={{0,11},{1,10},{2,9},{3,8},{8,3},{9,2},{10,1},{11,0},{4,15},{5,14},... | collective-permute-start | bytes 73736 | tf_op jit(solution)/shard_map/ppermute | solution.py:37
  82.8 0.8 collective-permute-done.18
  83.6 4.1 %collective-permute-done.19 = bf16[8,1536]{1,0:T(8,128)(2,1)S(1)} collective-permute-done((bf16[8,1536]{1,0:T(8,128)(2,1)S(1)}, bf16[8,1536]{1,0:T(8,128)(2,1)S(1)}, u32[]{:S(2)}, u32[]{:S(2)}) %collective-permute-start.19) | collective-permute-done | bytes 24608 | tf_op jit(solution)/shard_map/ppermute | solution.py:37
  87.7 0.6 gather_fusion.3
  88.3 0.6 slice.59
  88.9 0.6 add_convert_fusion
  89.6 0.6 copy.173
  (60 shorter events, 0.5 us)
Async XLA Ops:
  1.5 22.4 %collective-permute-start.6 = (bf16[8,1536]{1,0:T(8,128)(2,1)S(1)}, bf16[8,1536]{1,0:T(8,128)(2,1)S(1)}, u32[]{:S(2)}, u32[]{:S(2)}) collective-permute-start(bf16[8,1536]{1,0:T(8,128)(2,1)S(1)} %get-tuple-element.22), channel_id=1, source_target_pairs={{0,11},{1,10},{2,9},{3,8},{8,3},{9,2},{10,1},{11,0},{4,15},{5,14},... | collective-permute-start | bytes 73736 | tf_op jit(solution)/shard_map/ppermute | solution.py:37
  7.6 16.3 %collective-permute-start.5 = (bf16[8,1536]{1,0:T(8,128)(2,1)S(1)}, bf16[8,1536]{1,0:T(8,128)(2,1)S(1)}, u32[]{:S(2)}, u32[]{:S(2)}) collective-permute-start(bf16[8,1536]{1,0:T(8,128)(2,1)S(1)} %get-tuple-element.23), channel_id=1, source_target_pairs={{0,10},{1,11},{2,8},{3,9},{8,2},{9,3},{10,0},{11,1},{4,14},{5,15},... | collective-permute-start | bytes 73736 | tf_op jit(solution)/shard_map/ppermute | solution.py:37
  7.6 16.3 %collective-permute-start.4 = (bf16[8,1536]{1,0:T(8,128)(2,1)S(1)}, bf16[8,1536]{1,0:T(8,128)(2,1)S(1)}, u32[]{:S(2)}, u32[]{:S(2)}) collective-permute-start(bf16[8,1536]{1,0:T(8,128)(2,1)S(1)} %get-tuple-element.24), channel_id=1, source_target_pairs={{0,9},{1,8},{2,11},{3,10},{8,1},{9,0},{10,3},{11,2},{4,13},{5,12},... | collective-permute-start | bytes 73736 | tf_op jit(solution)/shard_map/ppermute | solution.py:37
  9.3 14.6 %collective-permute-start.3 = (bf16[8,1536]{1,0:T(8,128)(2,1)S(1)}, bf16[8,1536]{1,0:T(8,128)(2,1)S(1)}, u32[]{:S(2)}, u32[]{:S(2)}) collective-permute-start(bf16[8,1536]{1,0:T(8,128)(2,1)S(1)} %get-tuple-element.25), channel_id=1, source_target_pairs={{0,8},{1,9},{2,10},{3,11},{8,0},{9,1},{10,2},{11,3},{4,12},{5,13},... | collective-permute-start | bytes 73736 | tf_op jit(solution)/shard_map/ppermute | solution.py:37
  9.7 3.8 %collective-permute-start = (bf16[8,1536]{1,0:T(8,128)(2,1)S(1)}, bf16[8,1536]{1,0:T(8,128)(2,1)S(1)}, u32[]{:S(2)}, u32[]{:S(2)}) collective-permute-start(bf16[8,1536]{1,0:T(8,128)(2,1)S(1)} %get-tuple-element.28), channel_id=1, source_target_pairs={{0,1},{1,0},{2,3},{3,2},{8,9},{9,8},{10,11},{11,10},{4,5},{5,4},{6... | collective-permute-start | bytes 73736 | tf_op jit(solution)/shard_map/ppermute | solution.py:37
  13.5 4.7 %collective-permute-start.1 = (bf16[8,1536]{1,0:T(8,128)(2,1)S(1)}, bf16[8,1536]{1,0:T(8,128)(2,1)S(1)}, u32[]{:S(2)}, u32[]{:S(2)}) collective-permute-start(bf16[8,1536]{1,0:T(8,128)(2,1)S(1)} %get-tuple-element.27), channel_id=1, source_target_pairs={{0,2},{1,3},{2,0},{3,1},{8,10},{9,11},{10,8},{11,9},{4,6},{5,7},{6... | collective-permute-start | bytes 73736 | tf_op jit(solution)/shard_map/ppermute | solution.py:37
  18.2 5.6 %collective-permute-start.2 = (bf16[8,1536]{1,0:T(8,128)(2,1)S(1)}, bf16[8,1536]{1,0:T(8,128)(2,1)S(1)}, u32[]{:S(2)}, u32[]{:S(2)}) collective-permute-start(bf16[8,1536]{1,0:T(8,128)(2,1)S(1)} %get-tuple-element.26), channel_id=1, source_target_pairs={{0,3},{1,2},{2,1},{3,0},{8,11},{9,10},{10,9},{11,8},{4,7},{5,6},{6... | collective-permute-start | bytes 73736 | tf_op jit(solution)/shard_map/ppermute | solution.py:37
  24.5 6.8 %copy-start = (bf16[1536,3072]{1,0:T(8,128)(2,1)S(1)}, bf16[1536,3072]{1,0:T(8,128)(2,1)}, u32[]{:S(2)}) copy-start(bf16[1536,3072]{1,0:T(8,128)(2,1)} %param.7) | copy-start | bytes 28311556
  34.2 5.0 %collective-permute-start.9 = (bf16[64,768]{1,0:T(8,128)(2,1)S(1)}, bf16[64,768]{1,0:T(8,128)(2,1)S(1)}, u32[]{:S(2)}, u32[]{:S(2)}) collective-permute-start(bf16[64,768]{1,0:T(8,128)(2,1)S(1)} %bitcast.163), channel_id=1, source_target_pairs={{0,12},{8,4},{4,8},{12,0},{1,13},{9,5},{5,9},{13,1},{2,14},{10,6},... | collective-permute-start | bytes 294920 | tf_op jit(solution)/shard_map/ppermute | solution.py:37
  34.3 7.2 %collective-permute-start.7 = (bf16[64,768]{1,0:T(8,128)(2,1)S(1)}, bf16[64,768]{1,0:T(8,128)(2,1)S(1)}, u32[]{:S(2)}, u32[]{:S(2)}) collective-permute-start(bf16[64,768]{1,0:T(8,128)(2,1)S(1)} %bitcast.162), channel_id=1, source_target_pairs={{0,8},{8,0},{4,12},{12,4},{1,9},{9,1},{5,13},{13,5},{2,10},{10,2},... | collective-permute-start | bytes 294920 | tf_op jit(solution)/shard_map/ppermute | solution.py:37
  36.0 5.5 %collective-permute-start.8 = (bf16[64,768]{1,0:T(8,128)(2,1)S(1)}, bf16[64,768]{1,0:T(8,128)(2,1)S(1)}, u32[]{:S(2)}, u32[]{:S(2)}) collective-permute-start(bf16[64,768]{1,0:T(8,128)(2,1)S(1)} %bitcast.161), channel_id=1, source_target_pairs={{0,4},{8,12},{4,0},{12,8},{1,5},{9,13},{5,1},{13,9},{2,6},{10,14},... | collective-permute-start | bytes 294920 | tf_op jit(solution)/shard_map/ppermute | solution.py:37
  41.6 17.3 %slice-start = ((s8[9437184]{0:T(1024)(128)(4,1)}), s8[1048576]{0:T(1024)(128)(4,1)S(1)}, s32[]{:S(2)}) async-start(s8[9437184]{0:T(1024)(128)(4,1)} %bitcast.143), calls=%async_computation | async-start | bytes 2097152
  42.5 7.5 %collective-permute-start.12 = (bf16[64,768]{1,0:T(8,128)(2,1)S(1)}, bf16[64,768]{1,0:T(8,128)(2,1)S(1)}, u32[]{:S(2)}, u32[]{:S(2)}) collective-permute-start(bf16[64,768]{1,0:T(8,128)(2,1)S(1)} %convert_element_type.59), channel_id=1, source_target_pairs={{0,12},{8,4},{4,8},{12,0},{1,13},{9,5},{5,9},{13,1},{2,14},{10,6},... | collective-permute-start | bytes 294920 | tf_op jit(solution)/shard_map/ppermute | solution.py:37
  42.6 7.4 %collective-permute-start.11 = (bf16[64,768]{1,0:T(8,128)(2,1)S(1)}, bf16[64,768]{1,0:T(8,128)(2,1)S(1)}, u32[]{:S(2)}, u32[]{:S(2)}) collective-permute-start(bf16[64,768]{1,0:T(8,128)(2,1)S(1)} %convert_element_type.59), channel_id=1, source_target_pairs={{0,4},{8,12},{4,0},{12,8},{1,5},{9,13},{5,1},{13,9},{2,6},{10,14},... | collective-permute-start | bytes 294920 | tf_op jit(solution)/shard_map/ppermute | solution.py:37
  42.8 7.2 %collective-permute-start.10 = (bf16[64,768]{1,0:T(8,128)(2,1)S(1)}, bf16[64,768]{1,0:T(8,128)(2,1)S(1)}, u32[]{:S(2)}, u32[]{:S(2)}) collective-permute-start(bf16[64,768]{1,0:T(8,128)(2,1)S(1)} %convert_element_type.59), channel_id=1, source_target_pairs={{0,8},{8,0},{4,12},{12,4},{1,9},{9,1},{5,13},{13,5},{2,10},{10,2},... | collective-permute-start | bytes 294920 | tf_op jit(solution)/shard_map/ppermute | solution.py:37
  51.1 7.8 %slice-start.1 = ((s8[9437184]{0:T(1024)(128)(4,1)}), s8[4194304]{0:T(1024)(128)(4,1)S(1)}, s32[]{:S(2)}) async-start(s8[9437184]{0:T(1024)(128)(4,1)} %bitcast.143), calls=%async_computation.1 | async-start | bytes 8388608
  51.9 6.9 %slice-start.2 = ((s8[9437184]{0:T(1024)(128)(4,1)}), s8[4194304]{0:T(1024)(128)(4,1)S(1)}, s32[]{:S(2)}) async-start(s8[9437184]{0:T(1024)(128)(4,1)} %bitcast.143), calls=%async_computation.2 | async-start | bytes 8388608
  65.7 23.3 %copy-start.1 = (f32[3072]{0:T(1024)S(1)}, f32[3072]{0:T(1024)}, u32[]{:S(2)}) copy-start(f32[3072]{0:T(1024)} %param.10) | copy-start | bytes 36868
  71.4 6.4 %collective-permute-start.13 = (bf16[8,1536]{1,0:T(8,128)(2,1)S(1)}, bf16[8,1536]{1,0:T(8,128)(2,1)S(1)}, u32[]{:S(2)}, u32[]{:S(2)}) collective-permute-start(bf16[8,1536]{1,0:T(8,128)(2,1)S(1)} %bitcast.172), channel_id=1, source_target_pairs={{0,1},{1,0},{2,3},{3,2},{8,9},{9,8},{10,11},{11,10},{4,5},{5,4},{6... | collective-permute-start | bytes 73736 | tf_op jit(solution)/shard_map/ppermute | solution.py:37
  71.5 9.7 %collective-permute-start.14 = (bf16[8,1536]{1,0:T(8,128)(2,1)S(1)}, bf16[8,1536]{1,0:T(8,128)(2,1)S(1)}, u32[]{:S(2)}, u32[]{:S(2)}) collective-permute-start(bf16[8,1536]{1,0:T(8,128)(2,1)S(1)} %bitcast.171), channel_id=1, source_target_pairs={{0,2},{1,3},{2,0},{3,1},{8,10},{9,11},{10,8},{11,9},{4,6},{5,7},{6... | collective-permute-start | bytes 73736 | tf_op jit(solution)/shard_map/ppermute | solution.py:37
  75.8 7.0 %collective-permute-start.15 = (bf16[8,1536]{1,0:T(8,128)(2,1)S(1)}, bf16[8,1536]{1,0:T(8,128)(2,1)S(1)}, u32[]{:S(2)}, u32[]{:S(2)}) collective-permute-start(bf16[8,1536]{1,0:T(8,128)(2,1)S(1)} %bitcast.168), channel_id=1, source_target_pairs={{0,3},{1,2},{2,1},{3,0},{8,11},{9,10},{10,9},{11,8},{4,7},{5,6},{6... | collective-permute-start | bytes 73736 | tf_op jit(solution)/shard_map/ppermute | solution.py:37
  75.9 6.9 %collective-permute-start.16 = (bf16[8,1536]{1,0:T(8,128)(2,1)S(1)}, bf16[8,1536]{1,0:T(8,128)(2,1)S(1)}, u32[]{:S(2)}, u32[]{:S(2)}) collective-permute-start(bf16[8,1536]{1,0:T(8,128)(2,1)S(1)} %bitcast.167), channel_id=1, source_target_pairs={{0,8},{1,9},{2,10},{3,11},{8,0},{9,1},{10,2},{11,3},{4,12},{5,13},... | collective-permute-start | bytes 73736 | tf_op jit(solution)/shard_map/ppermute | solution.py:37
  76.0 6.8 %collective-permute-start.17 = (bf16[8,1536]{1,0:T(8,128)(2,1)S(1)}, bf16[8,1536]{1,0:T(8,128)(2,1)S(1)}, u32[]{:S(2)}, u32[]{:S(2)}) collective-permute-start(bf16[8,1536]{1,0:T(8,128)(2,1)S(1)} %bitcast.166), channel_id=1, source_target_pairs={{0,9},{1,8},{2,11},{3,10},{8,1},{9,0},{10,3},{11,2},{4,13},{5,12},... | collective-permute-start | bytes 73736 | tf_op jit(solution)/shard_map/ppermute | solution.py:37
  77.8 5.8 %collective-permute-start.18 = (bf16[8,1536]{1,0:T(8,128)(2,1)S(1)}, bf16[8,1536]{1,0:T(8,128)(2,1)S(1)}, u32[]{:S(2)}, u32[]{:S(2)}) collective-permute-start(bf16[8,1536]{1,0:T(8,128)(2,1)S(1)} %bitcast.170), channel_id=1, source_target_pairs={{0,10},{1,11},{2,8},{3,9},{8,2},{9,3},{10,0},{11,1},{4,14},{5,15},... | collective-permute-start | bytes 73736 | tf_op jit(solution)/shard_map/ppermute | solution.py:37
  81.2 6.5 %collective-permute-start.19 = (bf16[8,1536]{1,0:T(8,128)(2,1)S(1)}, bf16[8,1536]{1,0:T(8,128)(2,1)S(1)}, u32[]{:S(2)}, u32[]{:S(2)}) collective-permute-start(bf16[8,1536]{1,0:T(8,128)(2,1)S(1)} %bitcast.169), channel_id=1, source_target_pairs={{0,11},{1,10},{2,9},{3,8},{8,3},{9,2},{10,1},{11,0},{4,15},{5,14},... | collective-permute-start | bytes 73736 | tf_op jit(solution)/shard_map/ppermute | solution.py:37

commit v3 on v1

--- a/solution.py
+++ b/solution.py
@@ -1,6 +1,8 @@
 import jax
 import jax.numpy as jnp
 from jax import lax
+from jax.experimental import pallas as pl
+from jax.experimental.pallas import tpu as pltpu
 from jax.sharding import PartitionSpec as P
 
 inv_root_two = 0.7071067811865476
@@ -19,41 +21,82 @@
     )
 
 
-def exchange(chunks, axes):
-    return lax.all_to_all(chunks, axes, split_axis=0, concat_axis=0, tiled=True)
+def load_body(*refs):
+    count = (len(refs) - 1) // 2
+    sems = refs[-1]
+    copies = [
+        pltpu.make_async_copy(refs[i], refs[count + i], sems.at[i]) for i in range(count)
+    ]
+    for copy in copies:
+        copy.start()
+    for copy in copies:
+        copy.wait()
+
+
+def load_weights(*weights):
+    size = sum(w.size * w.dtype.itemsize for w in weights)
+    return pl.pallas_call(
+        load_body,
+        out_shape=[pltpu.VMEM(w.shape, w.dtype) for w in weights],
+        in_specs=[pl.BlockSpec(memory_space=pl.ANY)] * len(weights),
+        out_specs=[pl.BlockSpec(memory_space=pltpu.VMEM)] * len(weights),
+        scratch_shapes=[pltpu.SemaphoreType.DMA((len(weights),))],
+        cost_estimate=pl.CostEstimate(flops=0, bytes_accessed=2 * size, transcendentals=0),
+        compiler_params=pltpu.CompilerParams(vmem_limit_bytes=1 << 20),
+        name="load_weights",
+    )(*weights)
 
 
 def make(mesh):
     nt, nk, nn = mesh.shape["tok"], mesh.shape["kin"], mesh.shape["nout"]
-    spread, square = nt * nn, nk * nt
+    spread = nt * nn
+    swap = [(0, 1), (1, 0)]
 
     def on_device(tokens, weight_in, bias_in, weight_out, bias_out, grad_out):
         rows, cols = tokens.shape
         wide, hid = weight_in.shape
-        part = hid // square
+        half = hid // nk
         pair = 2 * rows
         total = pair * spread
+        core = lax.axis_index("kin")
 
         mine = jnp.concatenate([tokens, grad_out], axis=0)
         by_owner = mine.reshape(pair, nt, wide).transpose(1, 0, 2)
         chunks = jnp.broadcast_to(by_owner[:, None], (nt, nn, pair, wide))
-        mixed = exchange(chunks.reshape(spread, pair, wide), ("tok", "nout")).reshape(total, wide)
+        chunks = chunks.reshape(spread, pair, wide)
+        mixed = lax.all_to_all(chunks, ("tok", "nout"), split_axis=0, concat_axis=0, tiled=True)
+        mixed = mixed.reshape(total, wide)
+        w_in, w_out = load_weights(weight_in, weight_out)
         is_fwd = (lax.broadcasted_iota(jnp.int32, (total, 1), 0) % pair) < rows
 
         col_sums = jnp.sum(jnp.where(is_fwd, 0.0, mixed.astype(jnp.float32)), axis=0)
-        bias_out_grad = lax.all_gather(col_sums, "tok", axis=0, tiled=True)
 
-        partial = jnp.where(is_fwd, dot(mixed, weight_in, 1, 0), dot(mixed, weight_out, 1, 1))
-        partial = partial.astype(jnp.bfloat16).reshape(total, square, part).transpose(1, 0, 2)
-        got = exchange(partial, ("kin", "tok"))
-        summed = jnp.sum(got.astype(jnp.float32), axis=0).reshape(spread, 2, rows, part)
-        at = lax.axis_index(("kin", "tok"))
-        pre_act = summed[:, 0] + lax.dynamic_slice_in_dim(bias_in, at * part, part)
+        partial = jnp.where(is_fwd, dot(mixed, w_in, 1, 0), dot(mixed, w_out, 1, 1))
+        partial = partial.astype(jnp.bfloat16)
+        own = lax.dynamic_slice_in_dim(partial, core * half, half, 1)
+        sent = lax.dynamic_slice_in_dim(partial, (1 - core) * half, half, 1)
+        own = own.astype(jnp.float32) + lax.ppermute(sent, "kin", swap).astype(jnp.float32)
+        own = own.astype(jnp.bfloat16)
+        if nt == 2:
+            other = lax.ppermute(own, "tok", swap)
+            summed = own.astype(jnp.float32) + other.astype(jnp.float32)
+            other_sums = lax.ppermute(col_sums, "tok", swap)
+            first = lax.axis_index("tok") == 0
+            bias_out_grad = jnp.concatenate(
+                [jnp.where(first, col_sums, other_sums), jnp.where(first, other_sums, col_sums)]
+            )
+        else:
+            summed = jnp.sum(lax.all_gather(own, "tok", axis=0).astype(jnp.float32), axis=0)
+            bias_out_grad = lax.all_gather(col_sums, "tok", axis=0, tiled=True)
+        summed = summed.reshape(spread, 2, rows, half)
+        pre_act = summed[:, 0] + lax.dynamic_slice_in_dim(bias_in, core * half, half)
         activated, slopes = gelu_parts(pre_act)
         grad_pre = summed[:, 1] * slopes
-        both = jnp.stack([activated, grad_pre], axis=1).astype(jnp.bfloat16).reshape(total, part)
-        both = exchange(jnp.broadcast_to(both[None], (square, total, part)), ("kin", "tok"))
-        both = both.transpose(1, 0, 2).reshape(total, hid)
+        both = jnp.stack([activated, grad_pre], axis=1).astype(jnp.bfloat16).reshape(total, half)
+        far = lax.ppermute(both, "kin", swap)
+        low = jnp.where(core == 0, both, far)
+        high = jnp.where(core == 0, far, both)
+        both = jnp.concatenate([low, high], axis=1)
 
         split = both.reshape(spread, 2, rows, hid)
         act = split[:, 0].reshape(spread * rows, hid)
@@ -65,13 +108,14 @@
 
         block = jnp.stack(
             [
-                dot(act, weight_out, 1, 0).reshape(spread, rows, wide),
-                dot(grad_half, weight_in, 1, 1).reshape(spread, rows, wide),
+                dot(act, w_out, 1, 0).reshape(spread, rows, wide),
+                dot(grad_half, w_in, 1, 1).reshape(spread, rows, wide),
             ],
             axis=1,
         )
         block = block.astype(jnp.bfloat16).reshape(spread, pair, wide)
-        back = exchange(block, ("tok", "nout")).reshape(nt, nn, pair, wide)
+        back = lax.all_to_all(block, ("tok", "nout"), split_axis=0, concat_axis=0, tiled=True)
+        back = back.reshape(nt, nn, pair, wide)
         weight_in_grad = dot(x_cols, grad_half, 0, 0).astype(jnp.bfloat16)
         weight_out_grad = dot(act, dy_cols, 0, 0).astype(jnp.bfloat16)
         final = jnp.sum(back.astype(jnp.float32), axis=1).transpose(1, 0, 2).reshape(pair, cols)

time: 81.4 us -> 73.9 us (0.908)
  local copies, waits for them, and re-layouts: 6.56 us -> 18.5 us
  waiting for transfers between devices: 15.3 us -> 7.12 us
  blocking collectives: 7.44 us -> 0 us
  matrix products: 30.7 us -> 27.1 us
  starting transfers between devices: 17.6 us -> 15.3 us
  Pallas kernels: 0 us -> 1.27 us
  other arithmetic: 2.41 us -> 3.25 us
    all_to_all x4 -> x2, waiting for transfers between devices: 15.3 us -> 0.01 us  [the longest x1 0.01 us: on_device(): lax.all_to_all(chunks, ('tok', 'nout'), split_axis=0, concat_axis=0, tile...]
    unnamed x6 -> x20, local copies, waits for them, and re-layouts: 1.39 us -> 15.6 us
    all_gather x1 -> x0, blocking collectives: 7.44 us -> none  [on_device(): bias_out_grad = lax.all_gather(col_sums, 'tok', axis=0, tiled=True)]
    ppermute x0 -> x4, waiting for transfers between devices: none -> 7.12 us  [the longest x1 4.99 us: on_device(): other = lax.ppermute(own, 'tok', swap)]
    all_to_all x4 -> x2, starting transfers between devices: 17.6 us -> 13 us  [the longest x1 7.25 us: on_device(): lax.all_to_all(chunks, ('tok', 'nout'), split_axis=0, concat_axis=0, tile...]
    dot_general x6, matrix products: 30.7 us -> 27.1 us  [dot(): lax.dot_general(left, right, (((left_dim,), (right_dim,)), ((), ())), pre...]
    ppermute x0 -> x4, starting transfers between devices: none -> 2.31 us  [the longest x1 2.1 us: on_device(): other = lax.ppermute(own, 'tok', swap)]
    pallas_call x0 -> x1, Pallas kernels: none -> 1.27 us  [load_weights(): pl.pallas_call(load_body, out_shape=[pltpu.VMEM(w.shape, w.dtype) for w i...]
  transfers between devices with their start and end apart: 4 -> 6, of which waited for: 2 -> 3; matrix products, arithmetic and copies ran while one was open for 15% -> 17% of each run, Pallas kernels for 0% -> 2%
where the time goes in v3:
time: 73.9 us; the launch traced here: 73.4 us
  matrix products  27.1 us (37%)
  local copies, waits for them, and re-layouts  18.5 us (25%)
  starting transfers between devices  15.3 us (21%)
  waiting for transfers between devices  7.12 us (10%)
  other arithmetic  3.25 us (4%)
  Pallas kernels  1.27 us (2%)
  between operations  0.91 us (1%)
    dot_general x6, matrix products, dot(): lax.dot_general(left, right, (((left_dim,), (right_dim,)), ((), ())), pre...  27.1 us
    unnamed x20, local copies, waits for them, and re-layouts  15.6 us
    all_to_all x1, starting transfers between devices, on_device(): lax.all_to_all(chunks, ('tok', 'nout'), split_axis=0, concat_axis=0, tile...  7.25 us
    all_to_all x1, starting transfers between devices, on_device(): lax.all_to_all(block, ('tok', 'nout'), split_axis=0, concat_axis=0, tiled...  5.71 us
    ppermute x1, waiting for transfers between devices, on_device(): other = lax.ppermute(own, 'tok', swap)  4.99 us
    ppermute x1, starting transfers between devices, on_device(): other = lax.ppermute(own, 'tok', swap)  2.1 us
  transfers between devices with their start and end apart: 6, of which 3 were waited for; matrix products, arithmetic and copies ran while one was open for 17% of the time, Pallas kernels for 2%

profile of v3, /device:TPU:0, one launch (start us, length us, event | category | flops | bytes accessed | tf_op | source)
XLA Modules:
  0.0 73.4 jit_solution(5161882059676360143)
XLA Ops:
  0.6 0.8 %pad_maximum_fusion.3 = bf16[8,3072]{1,0:T(8,128)(2,1)S(1)} fusion(bf16[4,3072]{1,0:T(4,128)(2,1)} %param.11, bf16[4,3072]{1,0:T(4,128)(2,1)} %param.6), kind=kLoop, calls=%fused_computation.43 | loop fusion | flops 98304 | bytes 98304 | tf_op jit(solution)/shard_map/concatenate | solution.py:63
  1.4 0.7 broadcast_in_dim.29
  2.1 7.3 %all-to-all-start = ((bf16[8,8,1536]{2,1,0:T(8,128)(2,1)}), bf16[8,8,1536]{2,1,0:T(8,128)(2,1)S(1)}, u32[]{:S(2)}, u32[]{:S(2)}) async-start(bf16[8,8,1536]{2,1,0:T(8,128)(2,1)} %bitcast.2), calls=%async_computation | async-start | bytes 393216 | tf_op jit(solution)/shard_map/all_to_all | solution.py:67
  9.4 0.0 copy-start.3
  9.4 3.7 %copy-done.3 = bf16[1536,3072]{1,0:T(8,128)(2,1)S(1)} copy-done((bf16[1536,3072]{1,0:T(8,128)(2,1)S(1)}, bf16[1536,3072]{1,0:T(8,128)(2,1)}, u32[]{:S(2)}) %copy-start.3) | copy-done | bytes 9437208
  13.1 0.0 copy-start.4
  13.1 3.7 %copy-done.4 = bf16[3072,1536]{1,0:T(8,128)(2,1)S(1)} copy-done((bf16[3072,1536]{1,0:T(8,128)(2,1)S(1)}, bf16[3072,1536]{1,0:T(8,128)(2,1)}, u32[]{:S(2)}) %copy-start.4) | copy-done | bytes 9437208
  16.7 1.3 %load_weights.1 = (bf16[1536,3072]{1,0:T(8,128)(2,1)S(1)}, bf16[3072,1536]{1,0:T(8,128)(2,1)S(1)}) custom-call(bf16[1536,3072]{1,0:T(8,128)(2,1)S(1)} %copy-done.3, bf16[3072,1536]{1,0:T(8,128)(2,1)S(1)} %copy-done.4), custom_call_target="tpu_custom_call" | custom-call | bytes 37748736 | tf_op jit(solution)/shard_map/load_weights/pallas_call | solution.py:38
  18.0 0.0 copy-start
  18.0 3.7 %copy-done = bf16[1536,3072]{1,0:T(8,128)(2,1)} copy-done((bf16[1536,3072]{1,0:T(8,128)(2,1)}, bf16[1536,3072]{1,0:T(8,128)(2,1)S(1)}, u32[]{:S(2)}) %copy-start) | copy-done | bytes 9437208
  21.8 0.0 copy-start.1
  21.8 3.7 %copy-done.1 = bf16[3072,1536]{1,0:T(8,128)(2,1)} copy-done((bf16[3072,1536]{1,0:T(8,128)(2,1)}, bf16[3072,1536]{1,0:T(8,128)(2,1)S(1)}, u32[]{:S(2)}) %copy-start.1) | copy-done | bytes 9437208
  25.5 0.0 all-to-all-done
  25.5 0.0 copy-start.2
  25.5 5.6 %fusion.26 = bf16[64,3072]{1,0:T(8,128)(2,1)S(1)} fusion(bf16[1536,3072]{1,0:T(8,128)(2,1)} %copy-done, bf16[8,8,1536]{2,1,0:T(8,128)(2,1)S(1)} %all-to-all-done), kind=kOutput, calls=%fused_computation.32 | convolution fusion | flops 603979776 | bytes 10027008 | tf_op jit(solution)/shard_map/dot_general | solution.py:19
  31.1 0.0 copy-start.6
  31.1 0.8 %copy-done.2 = bf16[3072,1536]{1,0:T(8,128)(2,1)S(1)} copy-done((bf16[3072,1536]{1,0:T(8,128)(2,1)S(1)}, bf16[3072,1536]{1,0:T(8,128)(2,1)}, u32[]{:S(2)}) %copy-start.2) | copy-done | bytes 9437208
  31.9 2.9 %fusion.4 = bf16[64,3072]{1,0:T(8,128)(2,1)S(1)} fusion(bf16[64,3072]{1,0:T(8,128)(2,1)S(1)} %fusion.26, bf16[3072,1536]{1,0:T(8,128)(2,1)S(1)} %copy-done.2, pred[64]{0:T(512)(128)(4,1)S(1)} %fusion.34, bf16[8,8,1536]{2,1,0:T(8,128)(2,1)S(1)} %all-to-all-done), kind=kOutput, calls=%fused_computation.7 | convolution fusion | flops 604176384 | bytes 10420288 | tf_op jit(solution)/shard_map/dot_general | solution.py:19
  34.8 0.1 collective-permute-start
  34.9 0.0 copy-done.6
  34.9 0.1 dynamic_slice.11
  35.0 1.3 %collective-permute-done = bf16[64,1536]{1,0:T(8,128)(2,1)S(1)} collective-permute-done((bf16[64,1536]{1,0:T(8,128)(2,1)S(1)}, bf16[64,1536]{1,0:T(8,128)(2,1)S(1)}, u32[]{:S(2)}, u32[]{:S(2)}) %collective-permute-start) | collective-permute-done | bytes 196640 | tf_op jit(solution)/shard_map/ppermute | solution.py:78
  36.4 0.1 add_convert_fusion
  36.4 2.1 %collective-permute-start.1 = (bf16[64,1536]{1,0:T(8,128)(2,1)S(1)}, bf16[64,1536]{1,0:T(8,128)(2,1)S(1)}, u32[]{:S(2)}, u32[]{:S(2)}) collective-permute-start(bf16[64,1536]{1,0:T(8,128)(2,1)S(1)} %add_convert_fusion), channel_id=1, source_target_pairs={{0,8},{8,0},{1,9},{9,1},{2,10},{10,2},{3,11},{11,3},{4,12},{12,4},... | collective-permute-start | bytes 589832 | tf_op jit(solution)/shard_map/ppermute | solution.py:81
  38.5 0.1 select_reduce_fusion
  38.7 0.1 collective-permute-start.3
  38.7 0.1 copy.34
  38.8 5.0 %collective-permute-done.1 = bf16[64,1536]{1,0:T(8,128)(2,1)S(1)} collective-permute-done((bf16[64,1536]{1,0:T(8,128)(2,1)S(1)}, bf16[64,1536]{1,0:T(8,128)(2,1)S(1)}, u32[]{:S(2)}, u32[]{:S(2)}) %collective-permute-start.1) | collective-permute-done | bytes 196640 | tf_op jit(solution)/shard_map/ppermute | solution.py:81
  43.8 0.0 slice-start
  43.8 0.1 reshape.91
  44.0 0.2 multiply_convert_fusion
  44.2 0.1 copy.30
  44.3 0.1 convert_element_type.61
  44.4 0.1 collective-permute-start.2
  44.5 0.0 collective-permute-done.3
  44.5 0.6 pad_maximum_fusion.4
  45.1 0.8 %collective-permute-done.2 = bf16[64,1536]{1,0:T(8,128)(2,1)S(1)} collective-permute-done((bf16[64,1536]{1,0:T(8,128)(2,1)S(1)}, bf16[64,1536]{1,0:T(8,128)(2,1)S(1)}, u32[]{:S(2)}, u32[]{:S(2)}) %collective-permute-start.2) | collective-permute-done | bytes 196640 | tf_op jit(solution)/shard_map/ppermute | solution.py:96
  45.9 0.1 reshape.92
  46.1 0.0 slice-start.1
  46.1 0.1 fusion.35
  46.3 0.0 slice-start.2
  46.3 6.6 %fusion.11 = bf16[8,1,4,1536]{3,0,2,1:T(8,128)(2,1)S(1)} fusion(bf16[1536,3072]{1,0:T(8,128)(2,1)} %copy-done, bf16[8,1,4,3072]{3,2,1,0:T(4,128)(2,1)S(1)} %get-tuple-element.11), kind=kOutput, calls=%fused_computation.10 | convolution fusion | flops 302039040 | bytes 9732096 | tf_op jit(solution)/shard_map/dot_general | solution.py:19
  52.9 0.0 slice-done
  52.9 0.0 slice-done.1
  53.0 0.0 slice-done.2
  53.0 1.6 %fusion.14 = bf16[8,1,4,1536]{3,0,2,1:T(8,128)(2,1)S(1)} fusion(bf16[3072,1536]{1,0:T(8,128)(2,1)S(1)} %bitcast.57, bf16[8,1,4,3072]{3,2,1,0:T(4,128)(2,1)S(1)} %get-tuple-element.10), kind=kOutput, calls=%fused_computation.11 | convolution fusion | flops 302039040 | bytes 9732096 | tf_op jit(solution)/shard_map/dot_general | solution.py:19
  54.6 0.8 %copy.33 = bf16[8,8,1536]{2,1,0:T(8,128)(2,1)} copy(bf16[8,8,1536]{2,0,1:T(8,128)(2,1)S(1)} %bitcast.58) | data formatting | bytes 393216 | tf_op jit(solution)/shard_map/convert_element_type | solution.py:116
  55.4 5.7 %all-to-all-start.1 = ((bf16[8,8,1536]{2,1,0:T(8,128)(2,1)}), bf16[8,8,1536]{2,1,0:T(8,128)(2,1)S(1)}, u32[]{:S(2)}, u32[]{:S(2)}) async-start(bf16[8,8,1536]{2,1,0:T(8,128)(2,1)} %copy.33), calls=%async_computation.1 | async-start | bytes 393216 | tf_op jit(solution)/shard_map/all_to_all | solution.py:117
  61.1 5.2 %bitcast_convert_fusion.1 = bf16[1536,3072]{1,0:T(8,128)(2,1)} fusion(bf16[8,1,4,3072]{3,2,1,0:T(4,128)(2,1)S(1)} %get-tuple-element.11, bf16[8,2,4,1536]{3,0,2,1:T(8,128)(2,1)S(1)} %bitcast.61), kind=kOutput, calls=%fused_computation.1 | convolution fusion | flops 306708480 | bytes 9732096 | tf_op jit(solution)/shard_map/dot_general | solution.py:19
  66.3 0.0 copy-start.5
  66.3 5.2 %bitcast_convert_fusion = bf16[3072,1536]{1,0:T(8,128)(2,1)} fusion(bf16[8,1,4,3072]{3,2,1,0:T(4,128)(2,1)S(1)} %get-tuple-element.10, bf16[8,2,4,1536]{3,0,2,1:T(8,128)(2,1)S(1)} %bitcast.62), kind=kOutput, calls=%fused_computation | convolution fusion | flops 306708480 | bytes 9732096 | tf_op jit(solution)/shard_map/dot_general | solution.py:19
  71.4 0.7 convert_reduce_fusion.1
  72.1 0.0 all-to-all-done.1
  72.2 0.6 slice.51
  72.8 0.0 copy-done.5
  72.8 0.6 add_convert_fusion.1
  (13 shorter events, 0.3 us)
Async XLA Ops:
  2.1 23.4 %all-to-all-start = ((bf16[8,8,1536]{2,1,0:T(8,128)(2,1)}), bf16[8,8,1536]{2,1,0:T(8,128)(2,1)S(1)}, u32[]{:S(2)}, u32[]{:S(2)}) async-start(bf16[8,8,1536]{2,1,0:T(8,128)(2,1)} %bitcast.2), calls=%async_computation | async-start | bytes 393216 | tf_op jit(solution)/shard_map/all_to_all | solution.py:67
  9.4 3.7 %copy-start.3 = (bf16[1536,3072]{1,0:T(8,128)(2,1)S(1)}, bf16[1536,3072]{1,0:T(8,128)(2,1)}, u32[]{:S(2)}) copy-start(bf16[1536,3072]{1,0:T(8,128)(2,1)} %refs_0_.1) | copy-start | bytes 28311556
  13.1 3.7 %copy-start.4 = (bf16[3072,1536]{1,0:T(8,128)(2,1)S(1)}, bf16[3072,1536]{1,0:T(8,128)(2,1)}, u32[]{:S(2)}) copy-start(bf16[3072,1536]{1,0:T(8,128)(2,1)} %refs_1_.1) | copy-start | bytes 28311556
  18.0 3.7 %copy-start = (bf16[1536,3072]{1,0:T(8,128)(2,1)}, bf16[1536,3072]{1,0:T(8,128)(2,1)S(1)}, u32[]{:S(2)}) copy-start(bf16[1536,3072]{1,0:T(8,128)(2,1)S(1)} %get-tuple-element.8) | copy-start | bytes 28311556
  21.8 3.7 %copy-start.1 = (bf16[3072,1536]{1,0:T(8,128)(2,1)}, bf16[3072,1536]{1,0:T(8,128)(2,1)S(1)}, u32[]{:S(2)}) copy-start(bf16[3072,1536]{1,0:T(8,128)(2,1)S(1)} %get-tuple-element.9) | copy-start | bytes 28311556
  25.5 6.4 %copy-start.2 = (bf16[3072,1536]{1,0:T(8,128)(2,1)S(1)}, bf16[3072,1536]{1,0:T(8,128)(2,1)}, u32[]{:S(2)}) copy-start(bf16[3072,1536]{1,0:T(8,128)(2,1)} %copy-done.1) | copy-start | bytes 28311556
  31.1 3.8 %copy-start.6 = (f32[3072]{0:T(1024)S(1)}, f32[3072]{0:T(1024)}, u32[]{:S(2)}) copy-start(f32[3072]{0:T(1024)} %param.8) | copy-start | bytes 36868
  34.8 1.5 %collective-permute-start = (bf16[64,1536]{1,0:T(8,128)(2,1)S(1)}, bf16[64,1536]{1,0:T(8,128)(2,1)S(1)}, u32[]{:S(2)}, u32[]{:S(2)}) collective-permute-start(bf16[64,1536]{1,0:T(8,128)(2,1)S(1)} %constant_dynamic-slice_fusion), channel_id=1, source_target_pairs={{0,4},{4,0},{1,5},{5,1},{2,6},{6,2},{3,7},{7,3},{8,12},{12,8},{9,1... | collective-permute-start | bytes 589832 | tf_op jit(solution)/shard_map/ppermute | solution.py:78
  36.4 7.4 %collective-permute-start.1 = (bf16[64,1536]{1,0:T(8,128)(2,1)S(1)}, bf16[64,1536]{1,0:T(8,128)(2,1)S(1)}, u32[]{:S(2)}, u32[]{:S(2)}) collective-permute-start(bf16[64,1536]{1,0:T(8,128)(2,1)S(1)} %add_convert_fusion), channel_id=1, source_target_pairs={{0,8},{8,0},{1,9},{9,1},{2,10},{10,2},{3,11},{11,3},{4,12},{12,4},... | collective-permute-start | bytes 589832 | tf_op jit(solution)/shard_map/ppermute | solution.py:81
  38.7 5.8 %collective-permute-start.3 = (f32[1536]{0:T(1024)S(1)}, f32[1536]{0:T(1024)S(1)}, u32[]{:S(2)}, u32[]{:S(2)}) collective-permute-start(f32[1536]{0:T(1024)S(1)} %select_reduce_fusion), channel_id=1, source_target_pairs={{0,8},{8,0},{1,9},{9,1},{2,10},{10,2},{3,11},{11,3},{4,12},{12,4},... | collective-permute-start | bytes 18440 | tf_op jit(solution)/shard_map/ppermute | solution.py:83
  43.8 9.1 %slice-start = ((s8[9437184]{0:T(1024)(128)(4,1)}), s8[1048576]{0:T(1024)(128)(4,1)S(1)}, s32[]{:S(2)}) async-start(s8[9437184]{0:T(1024)(128)(4,1)} %bitcast.56), calls=%async_computation.2 | async-start | bytes 2097152
  44.4 1.5 %collective-permute-start.2 = (bf16[64,1536]{1,0:T(8,128)(2,1)S(1)}, bf16[64,1536]{1,0:T(8,128)(2,1)S(1)}, u32[]{:S(2)}, u32[]{:S(2)}) collective-permute-start(bf16[64,1536]{1,0:T(8,128)(2,1)S(1)} %convert_element_type.61), channel_id=1, source_target_pairs={{0,4},{4,0},{1,5},{5,1},{2,6},{6,2},{3,7},{7,3},{8,12},{12,8},{9,1... | collective-permute-start | bytes 589832 | tf_op jit(solution)/shard_map/ppermute | solution.py:96
  46.1 6.8 %slice-start.1 = ((s8[9437184]{0:T(1024)(128)(4,1)}), s8[4194304]{0:T(1024)(128)(4,1)S(1)}, s32[]{:S(2)}) async-start(s8[9437184]{0:T(1024)(128)(4,1)} %bitcast.56), calls=%async_computation.3 | async-start | bytes 8388608
  46.3 6.7 %slice-start.2 = ((s8[9437184]{0:T(1024)(128)(4,1)}), s8[4194304]{0:T(1024)(128)(4,1)S(1)}, s32[]{:S(2)}) async-start(s8[9437184]{0:T(1024)(128)(4,1)} %bitcast.56), calls=%async_computation.4 | async-start | bytes 8388608
  55.4 16.8 %all-to-all-start.1 = ((bf16[8,8,1536]{2,1,0:T(8,128)(2,1)}), bf16[8,8,1536]{2,1,0:T(8,128)(2,1)S(1)}, u32[]{:S(2)}, u32[]{:S(2)}) async-start(bf16[8,8,1536]{2,1,0:T(8,128)(2,1)} %copy.33), calls=%async_computation.1 | async-start | bytes 393216 | tf_op jit(solution)/shard_map/all_to_all | solution.py:117
  66.3 6.5 %copy-start.5 = (f32[3072]{0:T(1024)S(1)}, f32[3072]{0:T(1024)}, u32[]{:S(2)}) copy-start(f32[3072]{0:T(1024)} %param.10) | copy-start | bytes 36868

commit v4 on v1

v4 whole, which is shorter than its diff:
```python
import functools

import jax
import jax.numpy as jnp
from jax import lax
from jax.experimental import pallas as pl
from jax.experimental.pallas import tpu as pltpu
from jax.sharding import PartitionSpec as P

inv_root_two = 0.7071067811865476
inv_root_two_pi = 0.3989422804014327

MIB = 1 << 20
whole = pl.BlockSpec(memory_space=pltpu.VMEM)


def gelu_parts(hidden):
    normal_cdf = 0.5 * (1.0 + lax.erf(hidden * inv_root_two))
    density = jnp.exp(-0.5 * hidden * hidden) * inv_root_two_pi
    return (hidden * normal_cdf, normal_cdf + hidden * density)


def dot(left, right, left_dim, right_dim):
    return lax.dot_general(
        left, right, (((left_dim,), (right_dim,)), ((), ())), preferred_element_type=jnp.float32
    )


def tile_of(size, most):
    return max(t for t in range(128, most + 1, 128) if size % t == 0)


def cost(flops, moved):
    return pl.CostEstimate(flops=flops, bytes_accessed=moved, transcendentals=0)


def call(body, name, outs, grant=4 * MIB, flops=0, moved=0, scratch=(), resident=True):
    shapes = [pltpu.VMEM(o.shape, o.dtype) if resident else o for o in outs]
    return functools.partial(
        pl.pallas_call,
        body,
        out_shape=shapes,
        out_specs=[whole] * len(outs),
        scratch_shapes=list(scratch),
        cost_estimate=cost(flops, moved),
        compiler_params=pltpu.CompilerParams(vmem_limit_bytes=grant),
        name=name,
    )


def kept(array):
    return pltpu.with_memory_space_constraint(array, pltpu.VMEM)


def in_hbm(array):
    return pltpu.with_memory_space_constraint(array, pltpu.HBM)


def forward_rows(shape, rows):
    return lax.rem(lax.broadcasted_iota(jnp.int32, shape, 0), 2 * rows) < rows


def ordered(core, own, far):
    return jnp.concatenate([jnp.where(core == 0, own, far), jnp.where(core == 0, far, own)], axis=0)


def load_body(in_hbm, out_hbm, after_ref, in_ref, out_ref, sems):
    first = pltpu.make_async_copy(in_hbm, in_ref, sems.at[0])
    second = pltpu.make_async_copy(out_hbm, out_ref, sems.at[1])
    first.start()
    second.start()
    first.wait()
    second.wait()


def pair_body(own_ref, got_ref, out_ref):
    out_ref[...] = ordered(lax.axis_index("tok"), own_ref[...], got_ref[...])


def partial_body(rows, tile, *refs):
    *piece_refs, w_in_ref, w_out_ref, own_ref, sent_ref, mixed_ref, sums_ref = refs
    mixed = jnp.concatenate([ref[...] for ref in piece_refs], axis=0)
    mixed_ref[...] = mixed
    total = mixed.shape[0]
    hid = w_in_ref.shape[1]
    core = lax.axis_index("kin")
    is_fwd = forward_rows((total, tile), rows)

    @pl.loop(0, hid // tile)
    def _(step):
        at = pl.ds(pl.multiple_of(step * tile, tile), tile)
        forward = dot(mixed, w_in_ref[:, at], 1, 0)
        backward = dot(mixed, w_out_ref[at, :], 1, 1)
        both = jnp.where(is_fwd, forward, backward)
        low, high = both[: total // 2], both[total // 2 :]
        own_ref[:, at] = jnp.where(core == 0, low, high).astype(jnp.bfloat16)
        sent_ref[:, at] = jnp.where(core == 0, high, low).astype(jnp.bfloat16)

    cotangents = jnp.where(forward_rows(mixed.shape, rows), 0.0, mixed.astype(jnp.float32))
    sums_ref[...] = jnp.sum(cotangents, axis=0, keepdims=True)


def add_body(left_ref, right_ref, out_ref):
    out_ref[...] = (
        left_ref[...].astype(jnp.float32) + right_ref[...].astype(jnp.float32)
    ).astype(jnp.bfloat16)


def gelu_body(rows, tile, bias_ref, *refs):
    *part_refs, out_ref = refs
    is_fwd = forward_rows((out_ref.shape[0], tile), rows)

    @pl.loop(0, out_ref.shape[1] // tile)
    def _(step):
        at = pl.ds(pl.multiple_of(step * tile, tile), tile)
        summed = sum(ref[:, at].astype(jnp.float32) for ref in part_refs)
        activated, slopes = gelu_parts(summed + bias_ref[:, at])
        grad_pre = summed * pltpu.roll(slopes, rows, 0)
        out_ref[:, at] = jnp.where(is_fwd, activated, grad_pre).astype(jnp.bfloat16)


def block_body(rows, tile, own_ref, far_ref, w_in_ref, w_out_ref, *out_refs):
    wide = w_in_ref.shape[0]
    both = ordered(lax.axis_index("kin"), own_ref[...], far_ref[...])
    is_fwd = forward_rows((both.shape[0], tile), rows)
    size = both.shape[0] // len(out_refs)

    @pl.loop(0, wide // tile)
    def _(step):
        at = pl.ds(pl.multiple_of(step * tile, tile), tile)
        forward = dot(both, w_out_ref[:, at], 1, 0)
        backward = dot(both, w_in_ref[at, :], 1, 1)
        terms = jnp.where(is_fwd, forward, backward).astype(jnp.bfloat16)
        for i, out_ref in enumerate(out_refs):
            out_ref[:, at] = terms[i * size : (i + 1) * size]


def split_body(rows, own_ref, far_ref, mixed_ref, act_ref, grad_ref, turned_ref, bias_ref):
    both = ordered(lax.axis_index("kin"), own_ref[...], far_ref[...]).astype(jnp.float32)
    is_fwd = forward_rows(both.shape, rows)
    zero = jnp.zeros_like(both)
    act_ref[...] = jnp.where(is_fwd, both, zero).astype(jnp.bfloat16)
    gradient = jnp.where(is_fwd, zero, both)
    grad_ref[...] = gradient.astype(jnp.bfloat16)
    bias_ref[...] = jnp.sum(gradient, axis=0, keepdims=True)
    mixed = mixed_ref[...].astype(jnp.float32)
    to_tokens = pltpu.roll(mixed, mixed.shape[0] - rows, 0)
    to_cotangents = pltpu.roll(mixed, rows, 0)
    is_fwd = forward_rows(mixed.shape, rows)
    turned_ref[...] = jnp.where(is_fwd, to_tokens, to_cotangents).astype(jnp.bfloat16)


def product_body(size, left_ref, right_ref, out_ref):
    at = pl.ds(pl.multiple_of(pl.program_id(0) * size, size), size)
    out_ref[...] = dot(left_ref[:, at], right_ref[...], 0, 0).astype(jnp.bfloat16)


def product(left, right, name, most):
    total, high = left.shape
    wide = right.shape[1]
    size = tile_of(high, most)
    return pl.pallas_call(
        functools.partial(product_body, size),
        grid=(high // size,),
        out_shape=jax.ShapeDtypeStruct((high, wide), jnp.bfloat16),
        in_specs=[whole] * 2,
        out_specs=pl.BlockSpec((size, wide), lambda i: (i, 0)),
        cost_estimate=cost(2 * total * wide * high, 2 * wide * high),
        compiler_params=pltpu.CompilerParams(vmem_limit_bytes=16 * MIB),
        name=name,
    )(kept(left), kept(right))


def sum_body(rows, bias_ref, *refs):
    *term_refs, own_ref, sent_ref = refs
    wide = own_ref.shape[1]
    me = lax.axis_index("tok")
    summed = sum(ref[...].astype(jnp.float32) for ref in term_refs)
    bias = jnp.where(me == 0, bias_ref[:, :wide], bias_ref[:, wide:])
    summed = summed + jnp.where(forward_rows(summed.shape, rows), bias, 0.0)
    low, high = summed[: 2 * rows], summed[2 * rows :]
    own_ref[...] = jnp.where(me == 0, low, high).astype(jnp.bfloat16)
    sent_ref[...] = jnp.where(me == 0, high, low).astype(jnp.bfloat16)


def final_body(rows, own_ref, got_ref, own_sums_ref, got_sums_ref, rows_ref, grad_ref, sums_ref):
    wide = own_ref.shape[1]
    me = lax.axis_index("tok")
    own, got = own_ref[...].astype(jnp.float32), got_ref[...].astype(jnp.float32)
    own_sums, got_sums = own_sums_ref[...], got_sums_ref[...]
    for i in range(2):
        at = pl.ds(i * wide, wide)
        part = jnp.where(me == i, own, got)
        rows_ref[:, at] = part[:rows].astype(jnp.bfloat16)
        grad_ref[:, at] = part[rows:].astype(jnp.bfloat16)
        sums_ref[:, at] = jnp.where(me == i, own_sums, got_sums)


def make(mesh):
    nt, nk, nn = mesh.shape["tok"], mesh.shape["kin"], mesh.shape["nout"]
    small = nt == 2 and nn <= 4
    spread = nt * nn
    swap = [(0, 1), (1, 0)]
    bf16, f32 = jnp.bfloat16, jnp.float32
    like = jax.ShapeDtypeStruct

    def across(array, shift):
        return lax.ppermute(array, "nout", [(i, i ^ shift) for i in range(nn)])

    def on_device(tokens, weight_in, bias_in, weight_out, bias_out, grad_out):
        rows, cols = tokens.shape
        wide, hid = weight_in.shape
        pair = 2 * rows
        total = pair * spread
        half = total // nk
        work = 4 * total * wide * hid

        mine = jnp.concatenate([tokens, grad_out], axis=0)
        if small:
            me = lax.axis_index("tok")
            own = lax.dynamic_slice_in_dim(mine, me * wide, wide, 1)
            sent = lax.dynamic_slice_in_dim(mine, (1 - me) * wide, wide, 1)
            got = lax.ppermute(sent, "tok", swap)
            (tiles,) = call(pair_body, "pair_tiles", [like((nt * pair, wide), bf16)])(
                in_specs=[whole] * 2
            )(kept(own), kept(got))
            pieces = [tiles] + [across(tiles, shift) for shift in range(1, nn)]
        else:
            chunks = mine.reshape(pair, nt, wide).transpose(1, 0, 2)
            tiles = lax.all_to_all(chunks, "tok", split_axis=0, concat_axis=0, tiled=True)
            tiles = tiles.reshape(nt * pair, wide)
            pieces = [lax.all_gather(tiles, "nout", axis=0, tiled=True)]

        w_in, w_out = call(
            load_body,
            "load_weights",
            [weight_in, weight_out],
            grant=MIB,
            moved=8 * wide * hid,
            scratch=[pltpu.SemaphoreType.DMA((2,))],
        )(in_specs=[pl.BlockSpec(memory_space=pltpu.HBM)] * 2 + [pl.BlockSpec(memory_space=pl.ANY)])(
            in_hbm(weight_in), in_hbm(weight_out), tiles
        )

        tile = tile_of(hid, 512)
        own, sent, mixed, sums = call(
            functools.partial(partial_body, rows, tile),
            "partial_sums",
            [like((half, hid), bf16)] * 2 + [like((total, wide), bf16), like((1, wide), f32)],
            grant=8 * MIB,
            flops=work,
        )(in_specs=[whole] * (len(pieces) + 2))(
            *[kept(piece) for piece in pieces], kept(w_in), kept(w_out)
        )
        got = lax.ppermute(sent, "kin", swap)
        (own,) = call(add_body, "add_cores", [like((half, hid), bf16)])(in_specs=[whole] * 2)(
            kept(own), kept(got)
        )
        if nt == 2:
            others = [lax.ppermute(own, "tok", swap)]
            own_others = [own] + others
        else:
            gathered = lax.all_gather(own, "tok", axis=0)
            own_others = [gathered[i] for i in range(nt)]
        (both,) = call(
            functools.partial(gelu_body, rows, tile), "gelu", [like((half, hid), bf16)]
        )(in_specs=[whole] * (nt + 1))(
            bias_in.reshape(1, hid), *[kept(part) for part in own_others]
        )
        far = lax.ppermute(both, "kin", swap)
        blocks = call(
            functools.partial(block_body, rows, tile_of(wide, 512)),
            "output_blocks",
            [like((total // len(pieces), wide), bf16)] * len(pieces),
            grant=8 * MIB,
            flops=work,
        )(in_specs=[whole] * 4)(kept(both), kept(far), kept(w_in), kept(w_out))

        act, grad, turned, bias_in_grad = call(
            functools.partial(split_body, rows),
            "split_rows",
            [like((total, hid), bf16)] * 2 + [like((total, wide), bf16), like((1, hid), f32)],
            grant=8 * MIB,
        )(in_specs=[whole] * 3)(kept(both), kept(far), kept(mixed))
        weight_in_grad = product(turned, grad, "weight_in_grad", 256)
        weight_out_grad = product(act, turned, "weight_out_grad", 512)

        if small:
            terms = [blocks[0]] + [across(blocks[shift], shift) for shift in range(1, nn)]
            own, sent = call(
                functools.partial(sum_body, rows), "sum_blocks", [like((pair, wide), bf16)] * 2
            )(in_specs=[whole] * (nn + 1))(
                bias_out.reshape(1, cols), *[kept(term) for term in terms]
            )
            got = lax.ppermute(sent, "tok", swap)
            got_sums = lax.ppermute(sums, "tok", swap)
            output_rows, grad_tokens, bias_out_grad = call(
                functools.partial(final_body, rows),
                "final_rows",
                [like((rows, cols), bf16)] * 2 + [like((1, cols), f32)],
                resident=False,
            )(in_specs=[whole] * 4)(kept(own), kept(got), kept(sums), kept(got_sums))
            bias_out_grad = bias_out_grad.reshape(cols)
        else:
            chunks = blocks[0].reshape(nn, nt * pair, wide)
            back = lax.all_to_all(chunks, "nout", split_axis=0, concat_axis=0, tiled=True)
            summed = jnp.sum(back.astype(f32), axis=0).reshape(nt, pair, wide)
            at = lax.axis_index("tok") * wide
            bias = lax.dynamic_slice_in_dim(bias_out, at, wide)
            summed = summed + jnp.where(jnp.arange(pair) < rows, 1.0, 0.0)[:, None] * bias
            summed = summed.astype(bf16)
            ends = lax.all_to_all(summed, "tok", split_axis=0, concat_axis=0, tiled=True)
            ends = ends.transpose(1, 0, 2).reshape(pair, cols)
            output_rows, grad_tokens = ends[:rows], ends[rows:]
            bias_out_grad = lax.all_gather(sums.reshape(wide), "tok", axis=0, tiled=True)
        return (
            output_rows,
            grad_tokens,
            weight_in_grad,
            weight_out_grad,
            bias_in_grad.reshape(hid),
            bias_out_grad,
        )

    return on_device


def solution(mesh):
    return jax.shard_map(
        make(mesh),
        mesh=mesh,
        in_specs=(
            P(("groups", "tok", "nout"), "kin"),
            P(("kin", "tok"), "nout"),
            P("nout"),
            P("nout", ("kin", "tok")),
            P("kin"),
            P(("groups", "tok", "nout"), "kin"),
        ),
        out_specs=(
            P(("groups", "tok", "nout"), "kin"),
            P(("groups", "tok", "nout"), "kin"),
            P(("groups", "kin", "tok"), "nout"),
            P(("groups", "nout"), ("kin", "tok")),
            P(("groups", "nout")),
            P(("groups", "kin")),
        ),
        check_vma=False,
    )
```

time: 81.4 us -> 58 us (0.71)
  matrix products: 30.7 us -> 0 us
  Pallas kernels: 0 us -> 29.6 us
  blocking collectives: 7.44 us -> 0 us
  waiting for transfers between devices: 15.3 us -> 8.5 us
  local copies, waits for them, and re-layouts: 6.56 us -> 0.61 us
  other arithmetic: 2.41 us -> 0.86 us
    dot_general x6 -> x0, matrix products: 30.7 us -> none  [dot(): lax.dot_general(left, right, (((left_dim,), (right_dim,)), ((), ())), pre...]
    pallas_call x0 -> x11, Pallas kernels: none -> 29.6 us  [the longest x2 11.6 us: product(): pl.pallas_call(functools.partial(product_body, size), grid=(high // size,...]
    all_to_all x4 -> x0, starting transfers between devices: 17.6 us -> none  [exchange(): return lax.all_to_all(chunks, axes, split_axis=0, concat_axis=0, tiled=True)]
    ppermute x0 -> x12, starting transfers between devices: none -> 17.3 us  [the longest x6 9.21 us: across(): return lax.ppermute(array, 'nout', [(i, i ^ shift) for i in range(nn)])]
    all_to_all x4 -> x0, waiting for transfers between devices: 15.3 us -> none  [exchange(): return lax.all_to_all(chunks, axes, split_axis=0, concat_axis=0, tiled=True)]
    ppermute x0 -> x12, waiting for transfers between devices: none -> 8.5 us  [the longest x1 5.24 us: on_device(): others = [lax.ppermute(own, 'tok', swap)]]
    all_gather x1 -> x0, blocking collectives: 7.44 us -> none  [on_device(): bias_out_grad = lax.all_gather(col_sums, 'tok', axis=0, tiled=True)]
    broadcast_in_dim x2 -> x0, local copies, waits for them, and re-layouts: 1.46 us -> none  [the longest x1 0.77 us: on_device(): jnp.broadcast_to(both[None], (square, total, part))]
  transfers between devices with their start and end apart: 4 -> 12, of which waited for: 2 -> 3; matrix products, arithmetic and copies ran while one was open for 15% -> 1% of each run, Pallas kernels for 0% -> 40%
where the time goes in v4:
time: 58 us; the launch traced here: 57.7 us
  Pallas kernels  29.6 us (51%)
  starting transfers between devices  17.3 us (30%)
  waiting for transfers between devices  8.5 us (15%)
  other arithmetic  0.86 us (1%)
  between operations  0.76 us (1%)
  local copies, waits for them, and re-layouts  0.61 us (1%)
    pallas_call x2, Pallas kernels, product(): pl.pallas_call(functools.partial(product_body, size), grid=(high // size,...  11.6 us
    ppermute x6, starting transfers between devices, across(): return lax.ppermute(array, 'nout', [(i, i ^ shift) for i in range(nn)])  9.21 us
    pallas_call x1, Pallas kernels, on_device(): call(load_body, 'load_weights', [weight_in, weight_out], grant=MIB, moved...  6.41 us
    pallas_call x1, Pallas kernels, on_device(): call(functools.partial(partial_body, rows, tile), 'partial_sums', [like((...  5.34 us
    ppermute x1, waiting for transfers between devices, on_device(): others = [lax.ppermute(own, 'tok', swap)]  5.24 us
    pallas_call x1, Pallas kernels, on_device(): call(functools.partial(block_body, rows, tile_of(wide, 512)), 'output_blo...  4.91 us
    ppermute x2, starting transfers between devices, on_device(): got = lax.ppermute(sent, 'tok', swap)  4.42 us
    ppermute x2, waiting for transfers between devices, on_device(): got = lax.ppermute(sent, 'tok', swap)  1.81 us
  transfers between devices with their start and end apart: 12, of which 3 were waited for; matrix products, arithmetic and copies ran while one was open for 1% of the time, Pallas kernels for 40%

profile of v4, /device:TPU:0, one launch (start us, length us, event | category | flops | bytes accessed | tf_op | source)
XLA Modules:
  0.0 57.7 jit_solution(16278783029324946284)
XLA Ops:
  0.6 0.9 %fusion = (bf16[8,1536]{1,0:T(8,128)(2,1)S(1)}, bf16[8,1536]{1,0:T(8,128)(2,1)S(1)}) fusion(s32[]{:T(128)S(6)} %select_n.7, bf16[4,3072]{1,0:T(4,128)(2,1)} %param.6, bf16[4,3072]{1,0:T(4,128)(2,1)} %param.11, s32[]{:T(128)S(6)} %select_n.6), kind=kLoop, calls=%fused_computation.4 | loop fusion | flops 98304 | bytes 98312 | tf_op jit(solution)/shard_map/concatenate | solution.py:218
  1.5 3.0 %collective-permute-start = (bf16[8,1536]{1,0:T(8,128)(2,1)S(1)}, bf16[8,1536]{1,0:T(8,128)(2,1)S(1)}, u32[]{:S(2)}, u32[]{:S(2)}) collective-permute-start(bf16[8,1536]{1,0:T(8,128)(2,1)S(1)} %get-tuple-element.44), channel_id=1, source_target_pairs={{0,8},{8,0},{1,9},{9,1},{2,10},{10,2},{3,11},{11,3},{4,12},{12,4},... | collective-permute-start | bytes 73736 | tf_op jit(solution)/shard_map/ppermute | solution.py:223
  4.5 1.8 %collective-permute-done.got_ref = bf16[8,1536]{1,0:T(8,128)(2,1)S(1)} collective-permute-done((bf16[8,1536]{1,0:T(8,128)(2,1)S(1)}, bf16[8,1536]{1,0:T(8,128)(2,1)S(1)}, u32[]{:S(2)}, u32[]{:S(2)}) %collective-permute-start) | collective-permute-done | bytes 24608 | tf_op jit(solution)/shard_map/ppermute | solution.py:223
  6.3 2.2 %collective-permute-start.1 = (bf16[16,1536]{1,0:T(8,128)(2,1)S(1)}, bf16[16,1536]{1,0:T(8,128)(2,1)S(1)}, u32[]{:S(2)}, u32[]{:S(2)}) collective-permute-start(bf16[16,1536]{1,0:T(8,128)(2,1)S(1)} %pair_tiles.1.after_ref.refs_0_), channel_id=1, source_target_pairs={{0,1},{1,0},{2,3},{3,2},{4,5},{5,4},{6,7},{7,6},{8,9},{9,8},{10,11... | collective-permute-start | bytes 147464 | tf_op jit(solution)/shard_map/ppermute | solution.py:208
  8.5 2.6 %collective-permute-start.2 = (bf16[16,1536]{1,0:T(8,128)(2,1)S(1)}, bf16[16,1536]{1,0:T(8,128)(2,1)S(1)}, u32[]{:S(2)}, u32[]{:S(2)}) collective-permute-start(bf16[16,1536]{1,0:T(8,128)(2,1)S(1)} %pair_tiles.1.after_ref.refs_0_), channel_id=1, source_target_pairs={{0,2},{1,3},{2,0},{3,1},{4,6},{5,7},{6,4},{7,5},{8,10},{9,11},{10,... | collective-permute-start | bytes 147464 | tf_op jit(solution)/shard_map/ppermute | solution.py:208
  11.1 0.0 collective-permute-start.3
  11.1 6.4 %load_weights.1 = (bf16[1536,3072]{1,0:T(8,128)(2,1)S(1)}, bf16[3072,1536]{1,0:T(8,128)(2,1)S(1)}) custom-call(bf16[1536,3072]{1,0:T(8,128)(2,1)} %in_hbm.1, bf16[3072,1536]{1,0:T(8,128)(2,1)} %out_hbm.1, bf16[16,1536]{1,0:T(8,128)(2,1)S(1)} %pair_tiles.1.after_ref.refs_0_), custom_call_target="tpu_custom_call" | custom-call | bytes 37748736 | tf_op jit(solution)/shard_map/load_weights/pallas_call | solution.py:234
  17.5 0.0 collective-permute-done.1.refs_1_
  17.5 0.0 collective-permute-done.2.refs_2_
  17.5 0.0 collective-permute-done.3.refs_3_
  17.5 0.0 copy-start.1
  17.6 5.3 %partial_sums.1 = (bf16[32,3072]{1,0:T(8,128)(2,1)S(1)}, bf16[32,3072]{1,0:T(8,128)(2,1)S(1)}, bf16[64,1536]{1,0:T(8,128)(2,1)S(1)}, f32[1,1536]{1,0:T(1,128)S(1)}) custom-call(bf16[16,1536]{1,0:T(8,128)(2,1)S(1)} %pair_tiles.1.after_ref.refs_0_, bf16[16,1536]{1,0:T(8,128)(2,1)S(1)} %collective-permute-done.1.refs_1_, ...), custom_call_target="tpu_custom_call" | custom-call | flops 1207959552 | tf_op jit(solution)/shard_map/partial_sums/pallas_call | solution.py:246
  22.9 0.1 collective-permute-start.4
  23.0 1.4 %collective-permute-done.4.right_ref = bf16[32,3072]{1,0:T(8,128)(2,1)S(1)} collective-permute-done((bf16[32,3072]{1,0:T(8,128)(2,1)S(1)}, bf16[32,3072]{1,0:T(8,128)(2,1)S(1)}, u32[]{:S(2)}, u32[]{:S(2)}) %collective-permute-start.4) | collective-permute-done | bytes 196640 | tf_op jit(solution)/shard_map/ppermute | solution.py:255
  24.4 1.8 %collective-permute-start.5 = (bf16[32,3072]{1,0:T(8,128)(2,1)S(1)}, bf16[32,3072]{1,0:T(8,128)(2,1)S(1)}, u32[]{:S(2)}, u32[]{:S(2)}) collective-permute-start(bf16[32,3072]{1,0:T(8,128)(2,1)S(1)} %add_cores.1.refs_0_), channel_id=1, source_target_pairs={{0,8},{8,0},{1,9},{9,1},{2,10},{10,2},{3,11},{11,3},{4,12},{12,4},... | collective-permute-start | bytes 589832 | tf_op jit(solution)/shard_map/ppermute | solution.py:260
  26.2 5.2 %collective-permute-done.5.refs_1_ = bf16[32,3072]{1,0:T(8,128)(2,1)S(1)} collective-permute-done((bf16[32,3072]{1,0:T(8,128)(2,1)S(1)}, bf16[32,3072]{1,0:T(8,128)(2,1)S(1)}, u32[]{:S(2)}, u32[]{:S(2)}) %collective-permute-start.5) | collective-permute-done | bytes 196640 | tf_op jit(solution)/shard_map/ppermute | solution.py:260
  31.5 0.0 copy-done.1
  31.5 0.3 gelu.1.own_ref
  31.8 0.1 collective-permute-start.6
  31.9 1.8 %collective-permute-start.11 = (f32[1,1536]{1,0:T(1,128)S(1)}, f32[1,1536]{1,0:T(1,128)S(1)}, u32[]{:S(2)}, u32[]{:S(2)}) collective-permute-start(f32[1,1536]{1,0:T(1,128)S(1)} %get-tuple-element.35.own_sums_ref), channel_id=1, source_target_pairs={{0,8},{8,0},{1,9},{9,1},{2,10},{10,2},{3,11},{11,3},{4,12},{12,4},... | collective-permute-start | bytes 18440 | tf_op jit(solution)/shard_map/ppermute | solution.py:296
  33.6 0.0 collective-permute-done.6.far_ref
  33.6 4.9 %output_blocks.1 = (bf16[16,1536]{1,0:T(8,128)(2,1)S(1)}, bf16[16,1536]{1,0:T(8,128)(2,1)S(1)}, bf16[16,1536]{1,0:T(8,128)(2,1)S(1)}, bf16[16,1536]{1,0:T(8,128)(2,1)S(1)}) custom-call(bf16[32,3072]{1,0:T(8,128)(2,1)S(1)} %gelu.1.own_ref, bf16[32,3072]{1,0:T(8,128)(2,1)S(1)} %collective-permute-done.6.far_ref, ...), custom_call_target="tpu_custom_call" | custom-call | flops 1207959552 | tf_op jit(solution)/shard_map/output_blocks/pallas_call | solution.py:271
  38.6 0.0 copy-start
  38.6 0.7 %collective-permute-start.7 = (bf16[16,1536]{1,0:T(8,128)(2,1)S(1)}, bf16[16,1536]{1,0:T(8,128)(2,1)S(1)}, u32[]{:S(2)}, u32[]{:S(2)}) collective-permute-start(bf16[16,1536]{1,0:T(8,128)(2,1)S(1)} %get-tuple-element.30), channel_id=1, source_target_pairs={{0,1},{1,0},{2,3},{3,2},{4,5},{5,4},{6,7},{7,6},{8,9},{9,8},{10,11... | collective-permute-start | bytes 147464 | tf_op jit(solution)/shard_map/ppermute | solution.py:208
  39.3 3.5 %collective-permute-start.8 = (bf16[16,1536]{1,0:T(8,128)(2,1)S(1)}, bf16[16,1536]{1,0:T(8,128)(2,1)S(1)}, u32[]{:S(2)}, u32[]{:S(2)}) collective-permute-start(bf16[16,1536]{1,0:T(8,128)(2,1)S(1)} %get-tuple-element.31), channel_id=1, source_target_pairs={{0,2},{1,3},{2,0},{3,1},{4,6},{5,7},{6,4},{7,5},{8,10},{9,11},{10,... | collective-permute-start | bytes 147464 | tf_op jit(solution)/shard_map/ppermute | solution.py:208
  42.8 0.2 collective-permute-start.9
  43.0 0.3 split_rows.1
  43.3 5.8 %weight_in_grad.1 = bf16[1536,3072]{1,0:T(8,128)(2,1)} custom-call(bf16[64,1536]{1,0:T(8,128)(2,1)S(1)} %get-tuple-element.39.left_ref.right_ref, bf16[64,3072]{1,0:T(8,128)(2,1)S(1)} %get-tuple-element.40.right_ref), custom_call_target="tpu_custom_call" | custom-call | flops 603979776 | bytes 9437184 | tf_op jit(solution)/shard_map/weight_in_grad/pallas_call | solution.py:162
  49.1 0.0 collective-permute-done.7.refs_1_
  49.1 0.0 collective-permute-done.8.refs_2_
  49.1 0.0 collective-permute-done.9.refs_3_
  49.2 0.0 copy-done
  49.2 1.4 %collective-permute-start.10 = (bf16[8,1536]{1,0:T(8,128)(2,1)S(1)}, bf16[8,1536]{1,0:T(8,128)(2,1)S(1)}, u32[]{:S(2)}, u32[]{:S(2)}) collective-permute-start(bf16[8,1536]{1,0:T(8,128)(2,1)S(1)} %get-tuple-element.34), channel_id=1, source_target_pairs={{0,8},{8,0},{1,9},{9,1},{2,10},{10,2},{3,11},{11,3},{4,12},{12,4},... | collective-permute-start | bytes 73736 | tf_op jit(solution)/shard_map/ppermute | solution.py:295
  50.6 5.8 %weight_out_grad.1 = bf16[3072,1536]{1,0:T(8,128)(2,1)} custom-call(bf16[64,3072]{1,0:T(8,128)(2,1)S(1)} %get-tuple-element.41.left_ref, bf16[64,1536]{1,0:T(8,128)(2,1)S(1)} %get-tuple-element.39.left_ref.right_ref), custom_call_target="tpu_custom_call" | custom-call | flops 603979776 | bytes 9437184 | tf_op jit(solution)/shard_map/weight_out_grad/pallas_call | solution.py:162
  56.4 0.6 %copy.12 = f32[3072]{0:T(1024)} copy(f32[3072]{0:T(1024)S(1)} %bitcast.4) | data formatting | bytes 24576
  57.0 0.0 collective-permute-done.11.got_sums_ref
  57.0 0.0 collective-permute-done.10.got_ref
  57.1 0.6 %final_rows.1 = (bf16[4,3072]{1,0:T(4,128)(2,1)}, bf16[4,3072]{1,0:T(4,128)(2,1)}, f32[1,3072]{1,0:T(1,128)}) custom-call(bf16[8,1536]{1,0:T(8,128)(2,1)S(1)} %get-tuple-element.33.own_ref, bf16[8,1536]{1,0:T(8,128)(2,1)S(1)} %collective-permute-done.10.got_ref, f32[1,1536]{1,0:T(1,128)S(1)} %get-tuple-element.35.own_sums_ref, ...), custom_call_target="tpu_custom_call" | custom-call | tf_op jit(solution)/shard_map/final_rows/pallas_call | solution.py:297
  (3 shorter events, 0.1 us)
Async XLA Ops:
  1.5 4.8 %collective-permute-start = (bf16[8,1536]{1,0:T(8,128)(2,1)S(1)}, bf16[8,1536]{1,0:T(8,128)(2,1)S(1)}, u32[]{:S(2)}, u32[]{:S(2)}) collective-permute-start(bf16[8,1536]{1,0:T(8,128)(2,1)S(1)} %get-tuple-element.44), channel_id=1, source_target_pairs={{0,8},{8,0},{1,9},{9,1},{2,10},{10,2},{3,11},{11,3},{4,12},{12,4},... | collective-permute-start | bytes 73736 | tf_op jit(solution)/shard_map/ppermute | solution.py:223
  6.3 11.2 %collective-permute-start.1 = (bf16[16,1536]{1,0:T(8,128)(2,1)S(1)}, bf16[16,1536]{1,0:T(8,128)(2,1)S(1)}, u32[]{:S(2)}, u32[]{:S(2)}) collective-permute-start(bf16[16,1536]{1,0:T(8,128)(2,1)S(1)} %pair_tiles.1.after_ref.refs_0_), channel_id=1, source_target_pairs={{0,1},{1,0},{2,3},{3,2},{4,5},{5,4},{6,7},{7,6},{8,9},{9,8},{10,11... | collective-permute-start | bytes 147464 | tf_op jit(solution)/shard_map/ppermute | solution.py:208
  8.5 9.0 %collective-permute-start.2 = (bf16[16,1536]{1,0:T(8,128)(2,1)S(1)}, bf16[16,1536]{1,0:T(8,128)(2,1)S(1)}, u32[]{:S(2)}, u32[]{:S(2)}) collective-permute-start(bf16[16,1536]{1,0:T(8,128)(2,1)S(1)} %pair_tiles.1.after_ref.refs_0_), channel_id=1, source_target_pairs={{0,2},{1,3},{2,0},{3,1},{4,6},{5,7},{6,4},{7,5},{8,10},{9,11},{10,... | collective-permute-start | bytes 147464 | tf_op jit(solution)/shard_map/ppermute | solution.py:208
  11.1 6.4 %collective-permute-start.3 = (bf16[16,1536]{1,0:T(8,128)(2,1)S(1)}, bf16[16,1536]{1,0:T(8,128)(2,1)S(1)}, u32[]{:S(2)}, u32[]{:S(2)}) collective-permute-start(bf16[16,1536]{1,0:T(8,128)(2,1)S(1)} %pair_tiles.1.after_ref.refs_0_), channel_id=1, source_target_pairs={{0,3},{1,2},{2,1},{3,0},{4,7},{5,6},{6,5},{7,4},{8,11},{9,10},{10,... | collective-permute-start | bytes 147464 | tf_op jit(solution)/shard_map/ppermute | solution.py:208
  17.5 13.9 %copy-start.1 = (f32[3072]{0:T(1024)S(1)}, f32[3072]{0:T(1024)}, u32[]{:S(2)}) copy-start(f32[3072]{0:T(1024)} %param.8) | copy-start | bytes 36868
  22.9 1.5 %collective-permute-start.4 = (bf16[32,3072]{1,0:T(8,128)(2,1)S(1)}, bf16[32,3072]{1,0:T(8,128)(2,1)S(1)}, u32[]{:S(2)}, u32[]{:S(2)}) collective-permute-start(bf16[32,3072]{1,0:T(8,128)(2,1)S(1)} %get-tuple-element.28), channel_id=1, source_target_pairs={{0,4},{4,0},{1,5},{5,1},{2,6},{6,2},{3,7},{7,3},{8,12},{12,8},{9,1... | collective-permute-start | bytes 589832 | tf_op jit(solution)/shard_map/ppermute | solution.py:255
  24.4 7.0 %collective-permute-start.5 = (bf16[32,3072]{1,0:T(8,128)(2,1)S(1)}, bf16[32,3072]{1,0:T(8,128)(2,1)S(1)}, u32[]{:S(2)}, u32[]{:S(2)}) collective-permute-start(bf16[32,3072]{1,0:T(8,128)(2,1)S(1)} %add_cores.1.refs_0_), channel_id=1, source_target_pairs={{0,8},{8,0},{1,9},{9,1},{2,10},{10,2},{3,11},{11,3},{4,12},{12,4},... | collective-permute-start | bytes 589832 | tf_op jit(solution)/shard_map/ppermute | solution.py:260
  31.8 1.9 %collective-permute-start.6 = (bf16[32,3072]{1,0:T(8,128)(2,1)S(1)}, bf16[32,3072]{1,0:T(8,128)(2,1)S(1)}, u32[]{:S(2)}, u32[]{:S(2)}) collective-permute-start(bf16[32,3072]{1,0:T(8,128)(2,1)S(1)} %gelu.1.own_ref), channel_id=1, source_target_pairs={{0,4},{4,0},{1,5},{5,1},{2,6},{6,2},{3,7},{7,3},{8,12},{12,8},{9,1... | collective-permute-start | bytes 589832 | tf_op jit(solution)/shard_map/ppermute | solution.py:270
  31.9 25.2 %collective-permute-start.11 = (f32[1,1536]{1,0:T(1,128)S(1)}, f32[1,1536]{1,0:T(1,128)S(1)}, u32[]{:S(2)}, u32[]{:S(2)}) collective-permute-start(f32[1,1536]{1,0:T(1,128)S(1)} %get-tuple-element.35.own_sums_ref), channel_id=1, source_target_pairs={{0,8},{8,0},{1,9},{9,1},{2,10},{10,2},{3,11},{11,3},{4,12},{12,4},... | collective-permute-start | bytes 18440 | tf_op jit(solution)/shard_map/ppermute | solution.py:296
  38.6 10.6 %copy-start = (f32[3072]{0:T(1024)S(1)}, f32[3072]{0:T(1024)}, u32[]{:S(2)}) copy-start(f32[3072]{0:T(1024)} %param.10) | copy-start | bytes 36868
  38.6 10.6 %collective-permute-start.7 = (bf16[16,1536]{1,0:T(8,128)(2,1)S(1)}, bf16[16,1536]{1,0:T(8,128)(2,1)S(1)}, u32[]{:S(2)}, u32[]{:S(2)}) collective-permute-start(bf16[16,1536]{1,0:T(8,128)(2,1)S(1)} %get-tuple-element.30), channel_id=1, source_target_pairs={{0,1},{1,0},{2,3},{3,2},{4,5},{5,4},{6,7},{7,6},{8,9},{9,8},{10,11... | collective-permute-start | bytes 147464 | tf_op jit(solution)/shard_map/ppermute | solution.py:208
  39.3 9.8 %collective-permute-start.8 = (bf16[16,1536]{1,0:T(8,128)(2,1)S(1)}, bf16[16,1536]{1,0:T(8,128)(2,1)S(1)}, u32[]{:S(2)}, u32[]{:S(2)}) collective-permute-start(bf16[16,1536]{1,0:T(8,128)(2,1)S(1)} %get-tuple-element.31), channel_id=1, source_target_pairs={{0,2},{1,3},{2,0},{3,1},{4,6},{5,7},{6,4},{7,5},{8,10},{9,11},{10,... | collective-permute-start | bytes 147464 | tf_op jit(solution)/shard_map/ppermute | solution.py:208
  42.8 6.4 %collective-permute-start.9 = (bf16[16,1536]{1,0:T(8,128)(2,1)S(1)}, bf16[16,1536]{1,0:T(8,128)(2,1)S(1)}, u32[]{:S(2)}, u32[]{:S(2)}) collective-permute-start(bf16[16,1536]{1,0:T(8,128)(2,1)S(1)} %get-tuple-element.32), channel_id=1, source_target_pairs={{0,3},{1,2},{2,1},{3,0},{4,7},{5,6},{6,5},{7,4},{8,11},{9,10},{10,... | collective-permute-start | bytes 147464 | tf_op jit(solution)/shard_map/ppermute | solution.py:208
  49.2 7.8 %collective-permute-start.10 = (bf16[8,1536]{1,0:T(8,128)(2,1)S(1)}, bf16[8,1536]{1,0:T(8,128)(2,1)S(1)}, u32[]{:S(2)}, u32[]{:S(2)}) collective-permute-start(bf16[8,1536]{1,0:T(8,128)(2,1)S(1)} %get-tuple-element.34), channel_id=1, source_target_pairs={{0,8},{8,0},{1,9},{9,1},{2,10},{10,2},{3,11},{11,3},{4,12},{12,4},... | collective-permute-start | bytes 73736 | tf_op jit(solution)/shard_map/ppermute | solution.py:295

commit v5 on v4

--- a/solution.py
+++ b/solution.py
@@ -64,40 +64,52 @@
     return jnp.concatenate([jnp.where(core == 0, own, far), jnp.where(core == 0, far, own)], axis=0)
 
 
-def load_body(in_hbm, out_hbm, after_ref, in_ref, out_ref, sems):
-    first = pltpu.make_async_copy(in_hbm, in_ref, sems.at[0])
-    second = pltpu.make_async_copy(out_hbm, out_ref, sems.at[1])
-    first.start()
-    second.start()
-    first.wait()
-    second.wait()
+def load_body(hbm_ref, after_ref, out_ref, sem):
+    copy = pltpu.make_async_copy(hbm_ref, out_ref, sem.at[0])
+    copy.start()
+    copy.wait()
 
 
 def pair_body(own_ref, got_ref, out_ref):
     out_ref[...] = ordered(lax.axis_index("tok"), own_ref[...], got_ref[...])
 
 
-def partial_body(rows, tile, *refs):
-    *piece_refs, w_in_ref, w_out_ref, own_ref, sent_ref, mixed_ref, sums_ref = refs
+def partial_body(rows, tile, count, *refs):
+    *piece_refs, w_in_ref, w_hbm = refs[: count + 2]
+    w_out_ref, own_ref, sent_ref, mixed_ref, sums_ref, sems = refs[count + 2 :]
+    hid = w_in_ref.shape[1]
+    tiles = [pl.ds(i * tile, tile) for i in range(hid // tile)]
+    copies = [
+        pltpu.make_async_copy(w_hbm.at[at, :], w_out_ref.at[at, :], sems.at[i])
+        for i, at in enumerate(tiles)
+    ]
+    for copy in copies:
+        copy.start()
     mixed = jnp.concatenate([ref[...] for ref in piece_refs], axis=0)
     mixed_ref[...] = mixed
     total = mixed.shape[0]
-    hid = w_in_ref.shape[1]
     core = lax.axis_index("kin")
-    is_fwd = forward_rows((total, tile), rows)
-
-    @pl.loop(0, hid // tile)
-    def _(step):
-        at = pl.ds(pl.multiple_of(step * tile, tile), tile)
+    is_fwd = forward_rows((total // 2, tile), rows)
+
+    for at in tiles:
         forward = dot(mixed, w_in_ref[:, at], 1, 0)
-        backward = dot(mixed, w_out_ref[at, :], 1, 1)
-        both = jnp.where(is_fwd, forward, backward)
-        low, high = both[: total // 2], both[total // 2 :]
+        low, high = forward[: total // 2], forward[total // 2 :]
         own_ref[:, at] = jnp.where(core == 0, low, high).astype(jnp.bfloat16)
         sent_ref[:, at] = jnp.where(core == 0, high, low).astype(jnp.bfloat16)
 
     cotangents = jnp.where(forward_rows(mixed.shape, rows), 0.0, mixed.astype(jnp.float32))
     sums_ref[...] = jnp.sum(cotangents, axis=0, keepdims=True)
+
+    for at, copy in zip(tiles, copies):
+        copy.wait()
+        backward = dot(mixed, w_out_ref[at, :], 1, 1)
+        low, high = backward[: total // 2], backward[total // 2 :]
+        for ref, part in (
+            (own_ref, jnp.where(core == 0, low, high)),
+            (sent_ref, jnp.where(core == 0, high, low)),
+        ):
+            forward = ref[:, at].astype(jnp.float32)
+            ref[:, at] = jnp.where(is_fwd, forward, part).astype(jnp.bfloat16)
 
 
 def add_body(left_ref, right_ref, out_ref):
@@ -106,7 +118,7 @@
     ).astype(jnp.bfloat16)
 
 
-def gelu_body(rows, tile, bias_ref, *refs):
+def gelu_body(rows, tile, bias_ref, after_ref, *refs):
     *part_refs, out_ref = refs
     is_fwd = forward_rows((out_ref.shape[0], tile), rows)
 
@@ -125,24 +137,21 @@
     is_fwd = forward_rows((both.shape[0], tile), rows)
     size = both.shape[0] // len(out_refs)
 
-    @pl.loop(0, wide // tile)
-    def _(step):
-        at = pl.ds(pl.multiple_of(step * tile, tile), tile)
+    for i in range(wide // tile):
+        at = pl.ds(i * tile, tile)
         forward = dot(both, w_out_ref[:, at], 1, 0)
         backward = dot(both, w_in_ref[at, :], 1, 1)
         terms = jnp.where(is_fwd, forward, backward).astype(jnp.bfloat16)
-        for i, out_ref in enumerate(out_refs):
-            out_ref[:, at] = terms[i * size : (i + 1) * size]
-
-
-def split_body(rows, own_ref, far_ref, mixed_ref, act_ref, grad_ref, turned_ref, bias_ref):
+        for j, out_ref in enumerate(out_refs):
+            out_ref[:, at] = terms[j * size : (j + 1) * size]
+
+
+def split_body(rows, own_ref, far_ref, mixed_ref, act_ref, grad_ref, turned_ref):
     both = ordered(lax.axis_index("kin"), own_ref[...], far_ref[...]).astype(jnp.float32)
     is_fwd = forward_rows(both.shape, rows)
     zero = jnp.zeros_like(both)
     act_ref[...] = jnp.where(is_fwd, both, zero).astype(jnp.bfloat16)
-    gradient = jnp.where(is_fwd, zero, both)
-    grad_ref[...] = gradient.astype(jnp.bfloat16)
-    bias_ref[...] = jnp.sum(gradient, axis=0, keepdims=True)
+    grad_ref[...] = jnp.where(is_fwd, zero, both).astype(jnp.bfloat16)
     mixed = mixed_ref[...].astype(jnp.float32)
     to_tokens = pltpu.roll(mixed, mixed.shape[0] - rows, 0)
     to_cotangents = pltpu.roll(mixed, rows, 0)
@@ -150,21 +159,31 @@
     turned_ref[...] = jnp.where(is_fwd, to_tokens, to_cotangents).astype(jnp.bfloat16)
 
 
-def product_body(size, left_ref, right_ref, out_ref):
+def product_body(size, tile, left_ref, right_ref, out_ref, *sums_refs):
     at = pl.ds(pl.multiple_of(pl.program_id(0) * size, size), size)
-    out_ref[...] = dot(left_ref[:, at], right_ref[...], 0, 0).astype(jnp.bfloat16)
-
-
-def product(left, right, name, most):
+    left = left_ref[:, at].T
+    for i in range(out_ref.shape[1] // tile):
+        part = pl.ds(i * tile, tile)
+        out_ref[:, part] = dot(left, right_ref[:, part], 1, 0).astype(jnp.bfloat16)
+    for sums_ref in sums_refs:
+
+        @pl.when(pl.program_id(0) == 0)
+        def _():
+            right = right_ref[...].astype(jnp.float32)
+            sums_ref[...] = jnp.sum(right, axis=0, keepdims=True)
+
+
+def product(left, right, name, most, sums=False):
     total, high = left.shape
     wide = right.shape[1]
     size = tile_of(high, most)
+    like = jax.ShapeDtypeStruct
     return pl.pallas_call(
-        functools.partial(product_body, size),
+        functools.partial(product_body, size, tile_of(wide, 512)),
         grid=(high // size,),
-        out_shape=jax.ShapeDtypeStruct((high, wide), jnp.bfloat16),
+        out_shape=[like((high, wide), jnp.bfloat16)] + [like((1, wide), jnp.float32)] * sums,
         in_specs=[whole] * 2,
-        out_specs=pl.BlockSpec((size, wide), lambda i: (i, 0)),
+        out_specs=[pl.BlockSpec((size, wide), lambda i: (i, 0))] + [whole] * sums,
         cost_estimate=cost(2 * total * wide * high, 2 * wide * high),
         compiler_params=pltpu.CompilerParams(vmem_limit_bytes=16 * MIB),
         name=name,
@@ -231,41 +250,45 @@
             tiles = tiles.reshape(nt * pair, wide)
             pieces = [lax.all_gather(tiles, "nout", axis=0, tiled=True)]
 
-        w_in, w_out = call(
+        hbm = pl.BlockSpec(memory_space=pltpu.HBM)
+        (w_in,) = call(
             load_body,
-            "load_weights",
-            [weight_in, weight_out],
+            "load_weight",
+            [weight_in],
             grant=MIB,
-            moved=8 * wide * hid,
-            scratch=[pltpu.SemaphoreType.DMA((2,))],
-        )(in_specs=[pl.BlockSpec(memory_space=pltpu.HBM)] * 2 + [pl.BlockSpec(memory_space=pl.ANY)])(
-            in_hbm(weight_in), in_hbm(weight_out), tiles
-        )
+            moved=4 * wide * hid,
+            scratch=[pltpu.SemaphoreType.DMA((1,))],
+        )(in_specs=[hbm, pl.BlockSpec(memory_space=pl.ANY)])(in_hbm(weight_in), tiles)
 
         tile = tile_of(hid, 512)
-        own, sent, mixed, sums = call(
-            functools.partial(partial_body, rows, tile),
+        w_out, own, sent, mixed, sums = call(
+            functools.partial(partial_body, rows, tile, len(pieces)),
             "partial_sums",
-            [like((half, hid), bf16)] * 2 + [like((total, wide), bf16), like((1, wide), f32)],
+            [weight_out]
+            + [like((half, hid), bf16)] * 2
+            + [like((total, wide), bf16), like((1, wide), f32)],
             grant=8 * MIB,
             flops=work,
-        )(in_specs=[whole] * (len(pieces) + 2))(
-            *[kept(piece) for piece in pieces], kept(w_in), kept(w_out)
+            moved=4 * wide * hid,
+            scratch=[pltpu.SemaphoreType.DMA((hid // tile,))],
+        )(in_specs=[whole] * (len(pieces) + 1) + [hbm])(
+            *[kept(piece) for piece in pieces], kept(w_in), in_hbm(weight_out)
         )
         got = lax.ppermute(sent, "kin", swap)
         (own,) = call(add_body, "add_cores", [like((half, hid), bf16)])(in_specs=[whole] * 2)(
             kept(own), kept(got)
         )
         if nt == 2:
-            others = [lax.ppermute(own, "tok", swap)]
-            own_others = [own] + others
+            got_sums = lax.ppermute(sums, "tok", swap)
+            own_others = [own, lax.ppermute(own, "tok", swap)]
         else:
+            got_sums = sums
             gathered = lax.all_gather(own, "tok", axis=0)
             own_others = [gathered[i] for i in range(nt)]
         (both,) = call(
             functools.partial(gelu_body, rows, tile), "gelu", [like((half, hid), bf16)]
-        )(in_specs=[whole] * (nt + 1))(
-            bias_in.reshape(1, hid), *[kept(part) for part in own_others]
+        )(in_specs=[whole] * (nt + 2))(
+            bias_in.reshape(1, hid), got_sums, *[kept(part) for part in own_others]
         )
         far = lax.ppermute(both, "kin", swap)
         blocks = call(
@@ -276,14 +299,14 @@
             flops=work,
         )(in_specs=[whole] * 4)(kept(both), kept(far), kept(w_in), kept(w_out))
 
-        act, grad, turned, bias_in_grad = call(
+        act, grad, turned = call(
             functools.partial(split_body, rows),
             "split_rows",
-            [like((total, hid), bf16)] * 2 + [like((total, wide), bf16), like((1, hid), f32)],
+            [like((total, hid), bf16)] * 2 + [like((total, wide), bf16)],
             grant=8 * MIB,
         )(in_specs=[whole] * 3)(kept(both), kept(far), kept(mixed))
-        weight_in_grad = product(turned, grad, "weight_in_grad", 256)
-        weight_out_grad = product(act, turned, "weight_out_grad", 512)
+        weight_in_grad, bias_in_grad = product(turned, grad, "weight_in_grad", 256, sums=True)
+        (weight_out_grad,) = product(act, turned, "weight_out_grad", 512)
 
         if small:
             terms = [blocks[0]] + [across(blocks[shift], shift) for shift in range(1, nn)]
@@ -293,7 +316,6 @@
                 bias_out.reshape(1, cols), *[kept(term) for term in terms]
             )
             got = lax.ppermute(sent, "tok", swap)
-            got_sums = lax.ppermute(sums, "tok", swap)
             output_rows, grad_tokens, bias_out_grad = call(
                 functools.partial(final_body, rows),
                 "final_rows",

time: 58 us -> 55 us (0.948)
  Pallas kernels: 29.6 us -> 26.7 us
  waiting for transfers between devices: 8.5 us -> 10.4 us
  starting transfers between devices: 17.3 us -> 16.1 us
  local copies, waits for them, and re-layouts: 0.61 us -> 0.01 us
    ppermute x1, waiting for transfers between devices: 5.24 us -> 0.01 us  [on_device(): own_others = [own, lax.ppermute(own, 'tok', swap)]]
    ppermute x1, waiting for transfers between devices: 0.01 us -> 5.05 us  [on_device(): got_sums = lax.ppermute(sums, 'tok', swap)]
    pallas_call x4, Pallas kernels: 23.4 us -> 20.8 us  [the longest x2 11.7 us: product(): pl.pallas_call(functools.partial(product_body, size, tile_of(wide, 512)),...]
    ppermute x1, waiting for transfers between devices: 0.01 us -> 1.43 us  [on_device(): far = lax.ppermute(both, 'kin', swap)]
    ppermute x1, starting transfers between devices: 1.77 us -> 0.54 us  [on_device(): got_sums = lax.ppermute(sums, 'tok', swap)]
    ppermute x6, waiting for transfers between devices: 0.02 us -> 0.64 us  [across(): return lax.ppermute(array, 'nout', [(i, i ^ shift) for i in range(nn)])]
    unnamed x5 -> x4, local copies, waits for them, and re-layouts: 0.61 us -> 0.01 us
  transfers between devices with their start and end apart: 12 -> 12, of which waited for: 3 -> 5; matrix products, arithmetic and copies ran while one was open for 1% -> 0% of each run, Pallas kernels for 40% -> 29%
where the time goes in v5:
time: 55 us; the launch traced here: 54.7 us
  Pallas kernels  26.7 us (49%)
  starting transfers between devices  16.1 us (29%)
  waiting for transfers between devices  10.4 us (19%)
  other arithmetic  0.86 us (2%)
  between operations  0.74 us (1%)
    pallas_call x2, Pallas kernels, product(): pl.pallas_call(functools.partial(product_body, size, tile_of(wide, 512)),...  11.7 us
    ppermute x6, starting transfers between devices, across(): return lax.ppermute(array, 'nout', [(i, i ^ shift) for i in range(nn)])  9.29 us
    pallas_call x1, Pallas kernels, on_device(): call(functools.partial(partial_body, rows, tile, len(pieces)), 'partial_s...  5.43 us
    ppermute x1, waiting for transfers between devices, on_device(): got_sums = lax.ppermute(sums, 'tok', swap)  5.05 us
    pallas_call x1, Pallas kernels, on_device(): call(functools.partial(block_body, rows, tile_of(wide, 512)), 'output_blo...  4.58 us
    ppermute x2, starting transfers between devices, on_device(): got = lax.ppermute(sent, 'tok', swap)  4.56 us
    pallas_call x1, Pallas kernels, on_device(): call(load_body, 'load_weight', [weight_in], grant=MIB, moved=4 * wide * h...  3.69 us
    ppermute x2, waiting for transfers between devices, on_device(): got = lax.ppermute(sent, 'tok', swap)  1.81 us
  transfers between devices with their start and end apart: 12, of which 5 were waited for; matrix products, arithmetic and copies ran while one was open for 0% of the time, Pallas kernels for 29%

profile of v5, /device:TPU:0, one launch (start us, length us, event | category | flops | bytes accessed | tf_op | source)
XLA Modules:
  0.0 54.7 jit_solution(18407548947278434674)
XLA Ops:
  0.6 0.9 %fusion = (bf16[8,1536]{1,0:T(8,128)(2,1)S(1)}, bf16[8,1536]{1,0:T(8,128)(2,1)S(1)}) fusion(s32[]{:T(128)S(6)} %select_n.7, bf16[4,3072]{1,0:T(4,128)(2,1)} %param.6, bf16[4,3072]{1,0:T(4,128)(2,1)} %param.11, s32[]{:T(128)S(6)} %select_n.6), kind=kLoop, calls=%fused_computation.4 | loop fusion | flops 98304 | bytes 98312 | tf_op jit(solution)/shard_map/concatenate | solution.py:237
  1.5 3.0 %collective-permute-start = (bf16[8,1536]{1,0:T(8,128)(2,1)S(1)}, bf16[8,1536]{1,0:T(8,128)(2,1)S(1)}, u32[]{:S(2)}, u32[]{:S(2)}) collective-permute-start(bf16[8,1536]{1,0:T(8,128)(2,1)S(1)} %get-tuple-element.44), channel_id=1, source_target_pairs={{0,8},{8,0},{1,9},{9,1},{2,10},{10,2},{3,11},{11,3},{4,12},{12,4},... | collective-permute-start | bytes 73736 | tf_op jit(solution)/shard_map/ppermute | solution.py:242
  4.5 1.8 %collective-permute-done.got_ref = bf16[8,1536]{1,0:T(8,128)(2,1)S(1)} collective-permute-done((bf16[8,1536]{1,0:T(8,128)(2,1)S(1)}, bf16[8,1536]{1,0:T(8,128)(2,1)S(1)}, u32[]{:S(2)}, u32[]{:S(2)}) %collective-permute-start) | collective-permute-done | bytes 24608 | tf_op jit(solution)/shard_map/ppermute | solution.py:242
  6.3 4.2 %collective-permute-start.3 = (bf16[16,1536]{1,0:T(8,128)(2,1)S(1)}, bf16[16,1536]{1,0:T(8,128)(2,1)S(1)}, u32[]{:S(2)}, u32[]{:S(2)}) collective-permute-start(bf16[16,1536]{1,0:T(8,128)(2,1)S(1)} %pair_tiles.1.after_ref.refs_0_), channel_id=1, source_target_pairs={{0,3},{1,2},{2,1},{3,0},{4,7},{5,6},{6,5},{7,4},{8,11},{9,10},{10,... | collective-permute-start | bytes 147464 | tf_op jit(solution)/shard_map/ppermute | solution.py:227
  10.5 0.0 collective-permute-start.2
  10.5 0.6 %collective-permute-start.1 = (bf16[16,1536]{1,0:T(8,128)(2,1)S(1)}, bf16[16,1536]{1,0:T(8,128)(2,1)S(1)}, u32[]{:S(2)}, u32[]{:S(2)}) collective-permute-start(bf16[16,1536]{1,0:T(8,128)(2,1)S(1)} %pair_tiles.1.after_ref.refs_0_), channel_id=1, source_target_pairs={{0,1},{1,0},{2,3},{3,2},{4,5},{5,4},{6,7},{7,6},{8,9},{9,8},{10,11... | collective-permute-start | bytes 147464 | tf_op jit(solution)/shard_map/ppermute | solution.py:227
  11.2 3.7 %load_weight.1.refs_4_.w_in_ref = bf16[1536,3072]{1,0:T(8,128)(2,1)S(1)} custom-call(bf16[1536,3072]{1,0:T(8,128)(2,1)} %hbm_ref.1, bf16[16,1536]{1,0:T(8,128)(2,1)S(1)} %pair_tiles.1.after_ref.refs_0_), custom_call_target="tpu_custom_call" | custom-call | bytes 18874368 | tf_op jit(solution)/shard_map/load_weight/pallas_call | solution.py:254
  14.9 0.0 copy-start.1
  14.9 0.0 collective-permute-done.3.refs_3_
  14.9 0.6 %collective-permute-done.2.refs_2_ = bf16[16,1536]{1,0:T(8,128)(2,1)S(1)} collective-permute-done((bf16[16,1536]{1,0:T(8,128)(2,1)S(1)}, bf16[16,1536]{1,0:T(8,128)(2,1)S(1)}, u32[]{:S(2)}, u32[]{:S(2)}) %collective-permute-start.2) | collective-permute-done | bytes 49184 | tf_op jit(solution)/shard_map/ppermute | solution.py:227
  15.5 0.0 collective-permute-done.1.refs_1_
  15.5 5.4 %partial_sums.1 = (bf16[3072,1536]{1,0:T(8,128)(2,1)S(1)}, bf16[32,3072]{1,0:T(8,128)(2,1)S(1)}, bf16[32,3072]{1,0:T(8,128)(2,1)S(1)}, bf16[64,1536]{1,0:T(8,128)(2,1)S(1)}, f32[1,1536]{1,0:T(1,128)S(1)}) custom-call(bf16[16,1536]{1,0:T(8,128)(2,1)S(1)} %pair_tiles.1.after_ref.refs_0_, bf16[16,1536]{1,0:T(8,128)(2,1)S(1)} %collective-permute-done.1.refs_1_, ...), custom_call_target="tpu_custom_call" | custom-call | flops 1207959552 | bytes 18874368 | tf_op jit(solution)/shard_map/partial_sums/pallas_call | solution.py:264
  21.0 0.1 collective-permute-start.5
  21.0 1.4 %collective-permute-done.5.right_ref = bf16[32,3072]{1,0:T(8,128)(2,1)S(1)} collective-permute-done((bf16[32,3072]{1,0:T(8,128)(2,1)S(1)}, bf16[32,3072]{1,0:T(8,128)(2,1)S(1)}, u32[]{:S(2)}, u32[]{:S(2)}) %collective-permute-start.5) | collective-permute-done | bytes 196640 | tf_op jit(solution)/shard_map/ppermute | solution.py:277
  22.5 1.6 %collective-permute-start.6 = (bf16[32,3072]{1,0:T(8,128)(2,1)S(1)}, bf16[32,3072]{1,0:T(8,128)(2,1)S(1)}, u32[]{:S(2)}, u32[]{:S(2)}) collective-permute-start(bf16[32,3072]{1,0:T(8,128)(2,1)S(1)} %add_cores.1.refs_0_), channel_id=1, source_target_pairs={{0,8},{8,0},{1,9},{9,1},{2,10},{10,2},{3,11},{11,3},{4,12},{12,4},... | collective-permute-start | bytes 589832 | tf_op jit(solution)/shard_map/ppermute | solution.py:283
  24.1 0.5 collective-permute-start.4
  24.6 5.0 %collective-permute-done.4.after_ref.got_sums_ref = f32[1,1536]{1,0:T(1,128)S(1)} collective-permute-done((f32[1,1536]{1,0:T(1,128)S(1)}, f32[1,1536]{1,0:T(1,128)S(1)}, u32[]{:S(2)}, u32[]{:S(2)}) %collective-permute-start.4) | collective-permute-done | bytes 6176 | tf_op jit(solution)/shard_map/ppermute | solution.py:282
  29.7 0.0 collective-permute-done.6.refs_1_
  29.7 0.0 copy-done.1
  29.7 0.3 gelu.1.own_ref
  30.0 0.1 collective-permute-start.7
  30.1 1.4 %collective-permute-done.7.far_ref = bf16[32,3072]{1,0:T(8,128)(2,1)S(1)} collective-permute-done((bf16[32,3072]{1,0:T(8,128)(2,1)S(1)}, bf16[32,3072]{1,0:T(8,128)(2,1)S(1)}, u32[]{:S(2)}, u32[]{:S(2)}) %collective-permute-start.7) | collective-permute-done | bytes 196640 | tf_op jit(solution)/shard_map/ppermute | solution.py:293
  31.5 0.0 copy-start
  31.5 4.6 %output_blocks.1 = (bf16[16,1536]{1,0:T(8,128)(2,1)S(1)}, bf16[16,1536]{1,0:T(8,128)(2,1)S(1)}, bf16[16,1536]{1,0:T(8,128)(2,1)S(1)}, bf16[16,1536]{1,0:T(8,128)(2,1)S(1)}) custom-call(bf16[32,3072]{1,0:T(8,128)(2,1)S(1)} %gelu.1.own_ref, bf16[32,3072]{1,0:T(8,128)(2,1)S(1)} %collective-permute-done.7.far_ref, ...), custom_call_target="tpu_custom_call" | custom-call | flops 1207959552 | tf_op jit(solution)/shard_map/output_blocks/pallas_call | solution.py:294
  36.1 0.8 %collective-permute-start.8 = (bf16[16,1536]{1,0:T(8,128)(2,1)S(1)}, bf16[16,1536]{1,0:T(8,128)(2,1)S(1)}, u32[]{:S(2)}, u32[]{:S(2)}) collective-permute-start(bf16[16,1536]{1,0:T(8,128)(2,1)S(1)} %get-tuple-element.30), channel_id=1, source_target_pairs={{0,1},{1,0},{2,3},{3,2},{4,5},{5,4},{6,7},{7,6},{8,9},{9,8},{10,11... | collective-permute-start | bytes 147464 | tf_op jit(solution)/shard_map/ppermute | solution.py:227
  36.9 2.9 %collective-permute-start.9 = (bf16[16,1536]{1,0:T(8,128)(2,1)S(1)}, bf16[16,1536]{1,0:T(8,128)(2,1)S(1)}, u32[]{:S(2)}, u32[]{:S(2)}) collective-permute-start(bf16[16,1536]{1,0:T(8,128)(2,1)S(1)} %get-tuple-element.31), channel_id=1, source_target_pairs={{0,2},{1,3},{2,0},{3,1},{4,6},{5,7},{6,4},{7,5},{8,10},{9,11},{10,... | collective-permute-start | bytes 147464 | tf_op jit(solution)/shard_map/ppermute | solution.py:227
  39.8 0.7 %collective-permute-start.10 = (bf16[16,1536]{1,0:T(8,128)(2,1)S(1)}, bf16[16,1536]{1,0:T(8,128)(2,1)S(1)}, u32[]{:S(2)}, u32[]{:S(2)}) collective-permute-start(bf16[16,1536]{1,0:T(8,128)(2,1)S(1)} %get-tuple-element.32), channel_id=1, source_target_pairs={{0,3},{1,2},{2,1},{3,0},{4,7},{5,6},{6,5},{7,4},{8,11},{9,10},{10,... | collective-permute-start | bytes 147464 | tf_op jit(solution)/shard_map/ppermute | solution.py:227
  40.5 0.2 split_rows.1
  40.7 5.9 %weight_in_grad.1 = (bf16[1536,3072]{1,0:T(8,128)(2,1)}, f32[1,3072]{1,0:T(1,128)}) custom-call(bf16[64,1536]{1,0:T(8,128)(2,1)S(1)} %get-tuple-element.38.left_ref.right_ref, bf16[64,3072]{1,0:T(8,128)(2,1)S(1)} %get-tuple-element.39.right_ref), custom_call_target="tpu_custom_call" | custom-call | flops 603979776 | bytes 9437184 | tf_op jit(solution)/shard_map/weight_in_grad/pallas_call | solution.py:181
  46.7 0.0 collective-permute-done.8.refs_1_
  46.7 0.0 collective-permute-done.9.refs_2_
  46.7 0.0 collective-permute-done.10.refs_3_
  46.7 0.0 copy-done
  46.7 1.6 %collective-permute-start.11 = (bf16[8,1536]{1,0:T(8,128)(2,1)S(1)}, bf16[8,1536]{1,0:T(8,128)(2,1)S(1)}, u32[]{:S(2)}, u32[]{:S(2)}) collective-permute-start(bf16[8,1536]{1,0:T(8,128)(2,1)S(1)} %get-tuple-element.34), channel_id=1, source_target_pairs={{0,8},{8,0},{1,9},{9,1},{2,10},{10,2},{3,11},{11,3},{4,12},{12,4},... | collective-permute-start | bytes 73736 | tf_op jit(solution)/shard_map/ppermute | solution.py:318
  48.3 5.8 %weight_out_grad.1 = bf16[3072,1536]{1,0:T(8,128)(2,1)} custom-call(bf16[64,3072]{1,0:T(8,128)(2,1)S(1)} %get-tuple-element.41.left_ref, bf16[64,1536]{1,0:T(8,128)(2,1)S(1)} %get-tuple-element.38.left_ref.right_ref), custom_call_target="tpu_custom_call" | custom-call | flops 603979776 | bytes 9437184 | tf_op jit(solution)/shard_map/weight_out_grad/pallas_call | solution.py:181
  54.1 0.0 collective-permute-done.11.got_ref
  54.1 0.6 %final_rows.1 = (bf16[4,3072]{1,0:T(4,128)(2,1)}, bf16[4,3072]{1,0:T(4,128)(2,1)}, f32[1,3072]{1,0:T(1,128)}) custom-call(bf16[8,1536]{1,0:T(8,128)(2,1)S(1)} %get-tuple-element.33.own_ref, bf16[8,1536]{1,0:T(8,128)(2,1)S(1)} %collective-permute-done.11.got_ref, f32[1,1536]{1,0:T(1,128)S(1)} %get-tuple-element.25.own_sums_ref, ...), custom_call_target="tpu_custom_call" | custom-call | tf_op jit(solution)/shard_map/final_rows/pallas_call | solution.py:319
  (3 shorter events, 0.1 us)
Async XLA Ops:
  1.5 4.8 %collective-permute-start = (bf16[8,1536]{1,0:T(8,128)(2,1)S(1)}, bf16[8,1536]{1,0:T(8,128)(2,1)S(1)}, u32[]{:S(2)}, u32[]{:S(2)}) collective-permute-start(bf16[8,1536]{1,0:T(8,128)(2,1)S(1)} %get-tuple-element.44), channel_id=1, source_target_pairs={{0,8},{8,0},{1,9},{9,1},{2,10},{10,2},{3,11},{11,3},{4,12},{12,4},... | collective-permute-start | bytes 73736 | tf_op jit(solution)/shard_map/ppermute | solution.py:242
  6.3 8.5 %collective-permute-start.3 = (bf16[16,1536]{1,0:T(8,128)(2,1)S(1)}, bf16[16,1536]{1,0:T(8,128)(2,1)S(1)}, u32[]{:S(2)}, u32[]{:S(2)}) collective-permute-start(bf16[16,1536]{1,0:T(8,128)(2,1)S(1)} %pair_tiles.1.after_ref.refs_0_), channel_id=1, source_target_pairs={{0,3},{1,2},{2,1},{3,0},{4,7},{5,6},{6,5},{7,4},{8,11},{9,10},{10,... | collective-permute-start | bytes 147464 | tf_op jit(solution)/shard_map/ppermute | solution.py:227
  10.5 5.0 %collective-permute-start.2 = (bf16[16,1536]{1,0:T(8,128)(2,1)S(1)}, bf16[16,1536]{1,0:T(8,128)(2,1)S(1)}, u32[]{:S(2)}, u32[]{:S(2)}) collective-permute-start(bf16[16,1536]{1,0:T(8,128)(2,1)S(1)} %pair_tiles.1.after_ref.refs_0_), channel_id=1, source_target_pairs={{0,2},{1,3},{2,0},{3,1},{4,6},{5,7},{6,4},{7,5},{8,10},{9,11},{10,... | collective-permute-start | bytes 147464 | tf_op jit(solution)/shard_map/ppermute | solution.py:227
  10.5 5.0 %collective-permute-start.1 = (bf16[16,1536]{1,0:T(8,128)(2,1)S(1)}, bf16[16,1536]{1,0:T(8,128)(2,1)S(1)}, u32[]{:S(2)}, u32[]{:S(2)}) collective-permute-start(bf16[16,1536]{1,0:T(8,128)(2,1)S(1)} %pair_tiles.1.after_ref.refs_0_), channel_id=1, source_target_pairs={{0,1},{1,0},{2,3},{3,2},{4,5},{5,4},{6,7},{7,6},{8,9},{9,8},{10,11... | collective-permute-start | bytes 147464 | tf_op jit(solution)/shard_map/ppermute | solution.py:227
  14.9 14.8 %copy-start.1 = (f32[3072]{0:T(1024)S(1)}, f32[3072]{0:T(1024)}, u32[]{:S(2)}) copy-start(f32[3072]{0:T(1024)} %param.8) | copy-start | bytes 36868
  21.0 1.5 %collective-permute-start.5 = (bf16[32,3072]{1,0:T(8,128)(2,1)S(1)}, bf16[32,3072]{1,0:T(8,128)(2,1)S(1)}, u32[]{:S(2)}, u32[]{:S(2)}) collective-permute-start(bf16[32,3072]{1,0:T(8,128)(2,1)S(1)} %get-tuple-element.27), channel_id=1, source_target_pairs={{0,4},{4,0},{1,5},{5,1},{2,6},{6,2},{3,7},{7,3},{8,12},{12,8},{9,1... | collective-permute-start | bytes 589832 | tf_op jit(solution)/shard_map/ppermute | solution.py:277
  22.5 7.1 %collective-permute-start.6 = (bf16[32,3072]{1,0:T(8,128)(2,1)S(1)}, bf16[32,3072]{1,0:T(8,128)(2,1)S(1)}, u32[]{:S(2)}, u32[]{:S(2)}) collective-permute-start(bf16[32,3072]{1,0:T(8,128)(2,1)S(1)} %add_cores.1.refs_0_), channel_id=1, source_target_pairs={{0,8},{8,0},{1,9},{9,1},{2,10},{10,2},{3,11},{11,3},{4,12},{12,4},... | collective-permute-start | bytes 589832 | tf_op jit(solution)/shard_map/ppermute | solution.py:283
  24.1 5.6 %collective-permute-start.4 = (f32[1,1536]{1,0:T(1,128)S(1)}, f32[1,1536]{1,0:T(1,128)S(1)}, u32[]{:S(2)}, u32[]{:S(2)}) collective-permute-start(f32[1,1536]{1,0:T(1,128)S(1)} %get-tuple-element.25.own_sums_ref), channel_id=1, source_target_pairs={{0,8},{8,0},{1,9},{9,1},{2,10},{10,2},{3,11},{11,3},{4,12},{12,4},... | collective-permute-start | bytes 18440 | tf_op jit(solution)/shard_map/ppermute | solution.py:282
  30.0 1.5 %collective-permute-start.7 = (bf16[32,3072]{1,0:T(8,128)(2,1)S(1)}, bf16[32,3072]{1,0:T(8,128)(2,1)S(1)}, u32[]{:S(2)}, u32[]{:S(2)}) collective-permute-start(bf16[32,3072]{1,0:T(8,128)(2,1)S(1)} %gelu.1.own_ref), channel_id=1, source_target_pairs={{0,4},{4,0},{1,5},{5,1},{2,6},{6,2},{3,7},{7,3},{8,12},{12,8},{9,1... | collective-permute-start | bytes 589832 | tf_op jit(solution)/shard_map/ppermute | solution.py:293
  31.5 15.2 %copy-start = (f32[3072]{0:T(1024)S(1)}, f32[3072]{0:T(1024)}, u32[]{:S(2)}) copy-start(f32[3072]{0:T(1024)} %param.10) | copy-start | bytes 36868
  36.1 10.6 %collective-permute-start.8 = (bf16[16,1536]{1,0:T(8,128)(2,1)S(1)}, bf16[16,1536]{1,0:T(8,128)(2,1)S(1)}, u32[]{:S(2)}, u32[]{:S(2)}) collective-permute-start(bf16[16,1536]{1,0:T(8,128)(2,1)S(1)} %get-tuple-element.30), channel_id=1, source_target_pairs={{0,1},{1,0},{2,3},{3,2},{4,5},{5,4},{6,7},{7,6},{8,9},{9,8},{10,11... | collective-permute-start | bytes 147464 | tf_op jit(solution)/shard_map/ppermute | solution.py:227
  36.9 9.8 %collective-permute-start.9 = (bf16[16,1536]{1,0:T(8,128)(2,1)S(1)}, bf16[16,1536]{1,0:T(8,128)(2,1)S(1)}, u32[]{:S(2)}, u32[]{:S(2)}) collective-permute-start(bf16[16,1536]{1,0:T(8,128)(2,1)S(1)} %get-tuple-element.31), channel_id=1, source_target_pairs={{0,2},{1,3},{2,0},{3,1},{4,6},{5,7},{6,4},{7,5},{8,10},{9,11},{10,... | collective-permute-start | bytes 147464 | tf_op jit(solution)/shard_map/ppermute | solution.py:227
  39.8 6.9 %collective-permute-start.10 = (bf16[16,1536]{1,0:T(8,128)(2,1)S(1)}, bf16[16,1536]{1,0:T(8,128)(2,1)S(1)}, u32[]{:S(2)}, u32[]{:S(2)}) collective-permute-start(bf16[16,1536]{1,0:T(8,128)(2,1)S(1)} %get-tuple-element.32), channel_id=1, source_target_pairs={{0,3},{1,2},{2,1},{3,0},{4,7},{5,6},{6,5},{7,4},{8,11},{9,10},{10,... | collective-permute-start | bytes 147464 | tf_op jit(solution)/shard_map/ppermute | solution.py:227
  46.7 7.4 %collective-permute-start.11 = (bf16[8,1536]{1,0:T(8,128)(2,1)S(1)}, bf16[8,1536]{1,0:T(8,128)(2,1)S(1)}, u32[]{:S(2)}, u32[]{:S(2)}) collective-permute-start(bf16[8,1536]{1,0:T(8,128)(2,1)S(1)} %get-tuple-element.34), channel_id=1, source_target_pairs={{0,8},{8,0},{1,9},{9,1},{2,10},{10,2},{3,11},{11,3},{4,12},{12,4},... | collective-permute-start | bytes 73736 | tf_op jit(solution)/shard_map/ppermute | solution.py:318

commit v6 on v5

--- a/solution.py
+++ b/solution.py
@@ -56,8 +56,24 @@
     return pltpu.with_memory_space_constraint(array, pltpu.HBM)
 
 
-def forward_rows(shape, rows):
-    return lax.rem(lax.broadcasted_iota(jnp.int32, shape, 0), 2 * rows) < rows
+def apart(mixed, rows):
+    total, wide = mixed.shape
+    tiles = mixed.reshape(total // (4 * rows), 2, 2 * rows, wide)
+    even, odd = tiles[:, 0], tiles[:, 1]
+    is_low = lax.broadcasted_iota(jnp.int32, even.shape, 1) < rows
+    first = jnp.where(is_low, even, pltpu.roll(odd, rows, 1))
+    second = jnp.where(is_low, pltpu.roll(even, rows, 1), odd)
+    return first.reshape(total // 2, wide), second.reshape(total // 2, wide)
+
+
+def together(first, second, rows):
+    total, wide = first.shape
+    first = first.reshape(total // (2 * rows), 2 * rows, wide)
+    second = second.reshape(total // (2 * rows), 2 * rows, wide)
+    is_low = lax.broadcasted_iota(jnp.int32, first.shape, 1) < rows
+    even = jnp.where(is_low, first, pltpu.roll(second, rows, 1))
+    odd = jnp.where(is_low, pltpu.roll(first, rows, 1), second)
+    return jnp.stack([even, odd], axis=1).reshape(2 * total, wide)
 
 
 def ordered(core, own, far):
@@ -76,7 +92,7 @@
 
 def partial_body(rows, tile, count, *refs):
     *piece_refs, w_in_ref, w_hbm = refs[: count + 2]
-    w_out_ref, own_ref, sent_ref, mixed_ref, sums_ref, sems = refs[count + 2 :]
+    w_out_ref, own_ref, sent_ref, x_ref, dy_ref, sums_ref, sems = refs[count + 2 :]
     hid = w_in_ref.shape[1]
     tiles = [pl.ds(i * tile, tile) for i in range(hid // tile)]
     copies = [
@@ -86,30 +102,24 @@
     for copy in copies:
         copy.start()
     mixed = jnp.concatenate([ref[...] for ref in piece_refs], axis=0)
-    mixed_ref[...] = mixed
-    total = mixed.shape[0]
+    x_cols, dy_cols = apart(mixed.astype(jnp.float32), rows)
+    sums_ref[...] = jnp.sum(dy_cols, axis=0, keepdims=True)
+    x_cols, dy_cols = x_cols.astype(jnp.bfloat16), dy_cols.astype(jnp.bfloat16)
+    x_ref[...], dy_ref[...] = x_cols, dy_cols
+    half = x_cols.shape[0] // 2
     core = lax.axis_index("kin")
-    is_fwd = forward_rows((total // 2, tile), rows)
+
+    def store(terms, first, at):
+        low, high = terms[:half], terms[half:]
+        put = pl.ds(first, half)
+        own_ref[put, at] = jnp.where(core == 0, low, high).astype(jnp.bfloat16)
+        sent_ref[put, at] = jnp.where(core == 0, high, low).astype(jnp.bfloat16)
 
     for at in tiles:
-        forward = dot(mixed, w_in_ref[:, at], 1, 0)
-        low, high = forward[: total // 2], forward[total // 2 :]
-        own_ref[:, at] = jnp.where(core == 0, low, high).astype(jnp.bfloat16)
-        sent_ref[:, at] = jnp.where(core == 0, high, low).astype(jnp.bfloat16)
-
-    cotangents = jnp.where(forward_rows(mixed.shape, rows), 0.0, mixed.astype(jnp.float32))
-    sums_ref[...] = jnp.sum(cotangents, axis=0, keepdims=True)
-
+        store(dot(x_cols, w_in_ref[:, at], 1, 0), 0, at)
     for at, copy in zip(tiles, copies):
         copy.wait()
-        backward = dot(mixed, w_out_ref[at, :], 1, 1)
-        low, high = backward[: total // 2], backward[total // 2 :]
-        for ref, part in (
-            (own_ref, jnp.where(core == 0, low, high)),
-            (sent_ref, jnp.where(core == 0, high, low)),
-        ):
-            forward = ref[:, at].astype(jnp.float32)
-            ref[:, at] = jnp.where(is_fwd, forward, part).astype(jnp.bfloat16)
+        store(dot(dy_cols, w_out_ref[at, :], 1, 1), half, at)
 
 
 def add_body(left_ref, right_ref, out_ref):
@@ -118,76 +128,34 @@
     ).astype(jnp.bfloat16)
 
 
-def gelu_body(rows, tile, bias_ref, after_ref, *refs):
+def gelu_body(tile, bias_ref, after_ref, *refs):
     *part_refs, out_ref = refs
-    is_fwd = forward_rows((out_ref.shape[0], tile), rows)
+    half = out_ref.shape[0] // 2
 
     @pl.loop(0, out_ref.shape[1] // tile)
     def _(step):
         at = pl.ds(pl.multiple_of(step * tile, tile), tile)
         summed = sum(ref[:, at].astype(jnp.float32) for ref in part_refs)
-        activated, slopes = gelu_parts(summed + bias_ref[:, at])
-        grad_pre = summed * pltpu.roll(slopes, rows, 0)
-        out_ref[:, at] = jnp.where(is_fwd, activated, grad_pre).astype(jnp.bfloat16)
-
-
-def block_body(rows, tile, own_ref, far_ref, w_in_ref, w_out_ref, *out_refs):
+        activated, slopes = gelu_parts(summed[:half] + bias_ref[:, at])
+        out_ref[:half, at] = activated.astype(jnp.bfloat16)
+        out_ref[half:, at] = (summed[half:] * slopes).astype(jnp.bfloat16)
+
+
+def block_body(rows, tile, own_ref, far_ref, w_in_ref, w_out_ref, act_ref, grad_ref, *out_refs):
     wide = w_in_ref.shape[0]
-    both = ordered(lax.axis_index("kin"), own_ref[...], far_ref[...])
-    is_fwd = forward_rows((both.shape[0], tile), rows)
-    size = both.shape[0] // len(out_refs)
-
+    half = own_ref.shape[0] // 2
+    core = lax.axis_index("kin")
+    act = ordered(core, own_ref[:half], far_ref[:half])
+    grad = ordered(core, own_ref[half:], far_ref[half:])
+    act_ref[...], grad_ref[...] = act, grad
+    size = out_refs[0].shape[0]
     for i in range(wide // tile):
         at = pl.ds(i * tile, tile)
-        forward = dot(both, w_out_ref[:, at], 1, 0)
-        backward = dot(both, w_in_ref[at, :], 1, 1)
-        terms = jnp.where(is_fwd, forward, backward).astype(jnp.bfloat16)
+        forward = dot(act, w_out_ref[:, at], 1, 0)
+        backward = dot(grad, w_in_ref[at, :], 1, 1)
+        terms = together(forward, backward, rows).astype(jnp.bfloat16)
         for j, out_ref in enumerate(out_refs):
             out_ref[:, at] = terms[j * size : (j + 1) * size]
-
-
-def split_body(rows, own_ref, far_ref, mixed_ref, act_ref, grad_ref, turned_ref):
-    both = ordered(lax.axis_index("kin"), own_ref[...], far_ref[...]).astype(jnp.float32)
-    is_fwd = forward_rows(both.shape, rows)
-    zero = jnp.zeros_like(both)
-    act_ref[...] = jnp.where(is_fwd, both, zero).astype(jnp.bfloat16)
-    grad_ref[...] = jnp.where(is_fwd, zero, both).astype(jnp.bfloat16)
-    mixed = mixed_ref[...].astype(jnp.float32)
-    to_tokens = pltpu.roll(mixed, mixed.shape[0] - rows, 0)
-    to_cotangents = pltpu.roll(mixed, rows, 0)
-    is_fwd = forward_rows(mixed.shape, rows)
-    turned_ref[...] = jnp.where(is_fwd, to_tokens, to_cotangents).astype(jnp.bfloat16)
-
-
-def product_body(size, tile, left_ref, right_ref, out_ref, *sums_refs):
-    at = pl.ds(pl.multiple_of(pl.program_id(0) * size, size), size)
-    left = left_ref[:, at].T
-    for i in range(out_ref.shape[1] // tile):
-        part = pl.ds(i * tile, tile)
-        out_ref[:, part] = dot(left, right_ref[:, part], 1, 0).astype(jnp.bfloat16)
-    for sums_ref in sums_refs:
-
-        @pl.when(pl.program_id(0) == 0)
-        def _():
-            right = right_ref[...].astype(jnp.float32)
-            sums_ref[...] = jnp.sum(right, axis=0, keepdims=True)
-
-
-def product(left, right, name, most, sums=False):
-    total, high = left.shape
-    wide = right.shape[1]
-    size = tile_of(high, most)
-    like = jax.ShapeDtypeStruct
-    return pl.pallas_call(
-        functools.partial(product_body, size, tile_of(wide, 512)),
-        grid=(high // size,),
-        out_shape=[like((high, wide), jnp.bfloat16)] + [like((1, wide), jnp.float32)] * sums,
-        in_specs=[whole] * 2,
-        out_specs=[pl.BlockSpec((size, wide), lambda i: (i, 0))] + [whole] * sums,
-        cost_estimate=cost(2 * total * wide * high, 2 * wide * high),
-        compiler_params=pltpu.CompilerParams(vmem_limit_bytes=16 * MIB),
-        name=name,
-    )(kept(left), kept(right))
 
 
 def sum_body(rows, bias_ref, *refs):
@@ -196,13 +164,16 @@
     me = lax.axis_index("tok")
     summed = sum(ref[...].astype(jnp.float32) for ref in term_refs)
     bias = jnp.where(me == 0, bias_ref[:, :wide], bias_ref[:, wide:])
-    summed = summed + jnp.where(forward_rows(summed.shape, rows), bias, 0.0)
+    is_fwd = lax.rem(lax.broadcasted_iota(jnp.int32, summed.shape, 0), 2 * rows) < rows
+    summed = summed + jnp.where(is_fwd, bias, 0.0)
     low, high = summed[: 2 * rows], summed[2 * rows :]
     own_ref[...] = jnp.where(me == 0, low, high).astype(jnp.bfloat16)
     sent_ref[...] = jnp.where(me == 0, high, low).astype(jnp.bfloat16)
 
 
-def final_body(rows, own_ref, got_ref, own_sums_ref, got_sums_ref, rows_ref, grad_ref, sums_ref):
+def final_body(
+    rows, own_ref, got_ref, own_sums_ref, got_sums_ref, hidden_ref, rows_ref, grad_ref, sums_ref, bias_ref
+):
     wide = own_ref.shape[1]
     me = lax.axis_index("tok")
     own, got = own_ref[...].astype(jnp.float32), got_ref[...].astype(jnp.float32)
@@ -213,6 +184,7 @@
         rows_ref[:, at] = part[:rows].astype(jnp.bfloat16)
         grad_ref[:, at] = part[rows:].astype(jnp.bfloat16)
         sums_ref[:, at] = jnp.where(me == i, own_sums, got_sums)
+    bias_ref[...] = jnp.sum(hidden_ref[...].astype(jnp.float32), axis=0, keepdims=True)
 
 
 def make(mesh):
@@ -261,12 +233,13 @@
         )(in_specs=[hbm, pl.BlockSpec(memory_space=pl.ANY)])(in_hbm(weight_in), tiles)
 
         tile = tile_of(hid, 512)
-        w_out, own, sent, mixed, sums = call(
+        w_out, own, sent, x_cols, dy_cols, sums = call(
             functools.partial(partial_body, rows, tile, len(pieces)),
             "partial_sums",
             [weight_out]
             + [like((half, hid), bf16)] * 2
-            + [like((total, wide), bf16), like((1, wide), f32)],
+            + [like((total // 2, wide), bf16)] * 2
+            + [like((1, wide), f32)],
             grant=8 * MIB,
             flops=work,
             moved=4 * wide * hid,
@@ -286,27 +259,22 @@
             gathered = lax.all_gather(own, "tok", axis=0)
             own_others = [gathered[i] for i in range(nt)]
         (both,) = call(
-            functools.partial(gelu_body, rows, tile), "gelu", [like((half, hid), bf16)]
+            functools.partial(gelu_body, tile), "gelu", [like((half, hid), bf16)]
         )(in_specs=[whole] * (nt + 2))(
             bias_in.reshape(1, hid), got_sums, *[kept(part) for part in own_others]
         )
         far = lax.ppermute(both, "kin", swap)
-        blocks = call(
+        act, grad, *blocks = call(
             functools.partial(block_body, rows, tile_of(wide, 512)),
             "output_blocks",
-            [like((total // len(pieces), wide), bf16)] * len(pieces),
+            [like((total // 2, hid), bf16)] * 2
+            + [like((total // len(pieces), wide), bf16)] * len(pieces),
             grant=8 * MIB,
             flops=work,
         )(in_specs=[whole] * 4)(kept(both), kept(far), kept(w_in), kept(w_out))
 
-        act, grad, turned = call(
-            functools.partial(split_body, rows),
-            "split_rows",
-            [like((total, hid), bf16)] * 2 + [like((total, wide), bf16)],
-            grant=8 * MIB,
-        )(in_specs=[whole] * 3)(kept(both), kept(far), kept(mixed))
-        weight_in_grad, bias_in_grad = product(turned, grad, "weight_in_grad", 256, sums=True)
-        (weight_out_grad,) = product(act, turned, "weight_out_grad", 512)
+        weight_in_grad = dot(x_cols, grad, 0, 0).astype(bf16)
+        weight_out_grad = dot(act, dy_cols, 0, 0).astype(bf16)
 
         if small:
             terms = [blocks[0]] + [across(blocks[shift], shift) for shift in range(1, nn)]
@@ -316,12 +284,12 @@
                 bias_out.reshape(1, cols), *[kept(term) for term in terms]
             )
             got = lax.ppermute(sent, "tok", swap)
-            output_rows, grad_tokens, bias_out_grad = call(
+            output_rows, grad_tokens, bias_out_grad, bias_in_grad = call(
                 functools.partial(final_body, rows),
                 "final_rows",
-                [like((rows, cols), bf16)] * 2 + [like((1, cols), f32)],
+                [like((rows, cols), bf16)] * 2 + [like((1, cols), f32), like((1, hid), f32)],
                 resident=False,
-            )(in_specs=[whole] * 4)(kept(own), kept(got), kept(sums), kept(got_sums))
+            )(in_specs=[whole] * 5)(kept(own), kept(got), kept(sums), kept(got_sums), kept(grad))
             bias_out_grad = bias_out_grad.reshape(cols)
         else:
             chunks = blocks[0].reshape(nn, nt * pair, wide)
@@ -335,6 +303,7 @@
             ends = ends.transpose(1, 0, 2).reshape(pair, cols)
             output_rows, grad_tokens = ends[:rows], ends[rows:]
             bias_out_grad = lax.all_gather(sums.reshape(wide), "tok", axis=0, tiled=True)
+            bias_in_grad = jnp.sum(grad.astype(f32), axis=0)
         return (
             output_rows,
             grad_tokens,

time: 55 us -> 53 us (0.964)
  Pallas kernels: 26.7 us -> 14.3 us
  matrix products: 0 us -> 10.3 us
    pallas_call x4 -> x1, Pallas kernels: 12.3 us -> 0.19 us  [on_device(): call(functools.partial(gelu_body, tile), 'gelu', [like((half, hid), bf16)])]
    dot_general x0 -> x2, matrix products: none -> 10.3 us  [dot(): lax.dot_general(left, right, (((left_dim,), (right_dim,)), ((), ())), pre...]
  transfers between devices with their start and end apart: 12 -> 12, of which waited for: 5 -> 5; matrix products, arithmetic and copies ran while one was open for 0% -> 20% of each run, Pallas kernels for 29% -> 7%
where the time goes in v6:
time: 53 us; the launch traced here: 52.7 us
  starting transfers between devices  16.1 us (30%)
  Pallas kernels  14.3 us (27%)
  waiting for transfers between devices  10.4 us (20%)
  matrix products  10.3 us (19%)
  other arithmetic  0.86 us (2%)
  between operations  0.73 us (1%)
    dot_general x2, matrix products, dot(): lax.dot_general(left, right, (((left_dim,), (right_dim,)), ((), ())), pre...  10.3 us
    ppermute x6, starting transfers between devices, across(): return lax.ppermute(array, 'nout', [(i, i ^ shift) for i in range(nn)])  9.29 us
    pallas_call x1, Pallas kernels, on_device(): call(functools.partial(partial_body, rows, tile, len(pieces)), 'partial_s...  5.2 us
    ppermute x1, waiting for transfers between devices, on_device(): got_sums = lax.ppermute(sums, 'tok', swap)  5.05 us
    ppermute x2, starting transfers between devices, on_device(): got = lax.ppermute(sent, 'tok', swap)  4.56 us
    pallas_call x1, Pallas kernels, on_device(): call(functools.partial(block_body, rows, tile_of(wide, 512)), 'output_blo...  4.44 us
    pallas_call x1, Pallas kernels, on_device(): call(load_body, 'load_weight', [weight_in], grant=MIB, moved=4 * wide * h...  3.69 us
    ppermute x2, waiting for transfers between devices, on_device(): got = lax.ppermute(sent, 'tok', swap)  1.81 us
  transfers between devices with their start and end apart: 12, of which 5 were waited for; matrix products, arithmetic and copies ran while one was open for 20% of the time, Pallas kernels for 7%

profile of v6, /device:TPU:0, one launch (start us, length us, event | category | flops | bytes accessed | tf_op | source)
XLA Modules:
  0.0 52.7 jit_solution(17800467160719900928)
XLA Ops:
  0.6 0.9 %fusion = (bf16[8,1536]{1,0:T(8,128)(2,1)S(1)}, bf16[8,1536]{1,0:T(8,128)(2,1)S(1)}) fusion(s32[]{:T(128)S(6)} %select_n.7, bf16[4,3072]{1,0:T(4,128)(2,1)} %param.6, bf16[4,3072]{1,0:T(4,128)(2,1)} %param.11, s32[]{:T(128)S(6)} %select_n.6), kind=kLoop, calls=%fused_computation.6 | loop fusion | flops 98304 | bytes 98312 | tf_op jit(solution)/shard_map/concatenate | solution.py:209
  1.5 3.0 %collective-permute-start = (bf16[8,1536]{1,0:T(8,128)(2,1)S(1)}, bf16[8,1536]{1,0:T(8,128)(2,1)S(1)}, u32[]{:S(2)}, u32[]{:S(2)}) collective-permute-start(bf16[8,1536]{1,0:T(8,128)(2,1)S(1)} %get-tuple-element.42), channel_id=1, source_target_pairs={{0,8},{8,0},{1,9},{9,1},{2,10},{10,2},{3,11},{11,3},{4,12},{12,4},... | collective-permute-start | bytes 73736 | tf_op jit(solution)/shard_map/ppermute | solution.py:214
  4.5 1.8 %collective-permute-done.got_ref = bf16[8,1536]{1,0:T(8,128)(2,1)S(1)} collective-permute-done((bf16[8,1536]{1,0:T(8,128)(2,1)S(1)}, bf16[8,1536]{1,0:T(8,128)(2,1)S(1)}, u32[]{:S(2)}, u32[]{:S(2)}) %collective-permute-start) | collective-permute-done | bytes 24608 | tf_op jit(solution)/shard_map/ppermute | solution.py:214
  6.3 4.2 %collective-permute-start.3 = (bf16[16,1536]{1,0:T(8,128)(2,1)S(1)}, bf16[16,1536]{1,0:T(8,128)(2,1)S(1)}, u32[]{:S(2)}, u32[]{:S(2)}) collective-permute-start(bf16[16,1536]{1,0:T(8,128)(2,1)S(1)} %pair_tiles.1.after_ref.refs_0_), channel_id=1, source_target_pairs={{0,3},{1,2},{2,1},{3,0},{4,7},{5,6},{6,5},{7,4},{8,11},{9,10},{10,... | collective-permute-start | bytes 147464 | tf_op jit(solution)/shard_map/ppermute | solution.py:199
  10.5 0.0 collective-permute-start.2
  10.5 0.6 %collective-permute-start.1 = (bf16[16,1536]{1,0:T(8,128)(2,1)S(1)}, bf16[16,1536]{1,0:T(8,128)(2,1)S(1)}, u32[]{:S(2)}, u32[]{:S(2)}) collective-permute-start(bf16[16,1536]{1,0:T(8,128)(2,1)S(1)} %pair_tiles.1.after_ref.refs_0_), channel_id=1, source_target_pairs={{0,1},{1,0},{2,3},{3,2},{4,5},{5,4},{6,7},{7,6},{8,9},{9,8},{10,11... | collective-permute-start | bytes 147464 | tf_op jit(solution)/shard_map/ppermute | solution.py:199
  11.2 3.7 %load_weight.1.refs_4_.w_in_ref = bf16[1536,3072]{1,0:T(8,128)(2,1)S(1)} custom-call(bf16[1536,3072]{1,0:T(8,128)(2,1)} %hbm_ref.1, bf16[16,1536]{1,0:T(8,128)(2,1)S(1)} %pair_tiles.1.after_ref.refs_0_), custom_call_target="tpu_custom_call" | custom-call | bytes 18874368 | tf_op jit(solution)/shard_map/load_weight/pallas_call | solution.py:226
  14.9 0.0 copy-start.1
  14.9 0.0 collective-permute-done.3.refs_3_
  14.9 0.6 %collective-permute-done.2.refs_2_ = bf16[16,1536]{1,0:T(8,128)(2,1)S(1)} collective-permute-done((bf16[16,1536]{1,0:T(8,128)(2,1)S(1)}, bf16[16,1536]{1,0:T(8,128)(2,1)S(1)}, u32[]{:S(2)}, u32[]{:S(2)}) %collective-permute-start.2) | collective-permute-done | bytes 49184 | tf_op jit(solution)/shard_map/ppermute | solution.py:199
  15.5 0.0 collective-permute-done.1.refs_1_
  15.5 5.2 %partial_sums.1 = (bf16[3072,1536]{1,0:T(8,128)(2,1)S(1)}, bf16[32,3072]{1,0:T(8,128)(2,1)S(1)}, bf16[32,3072]{1,0:T(8,128)(2,1)S(1)}, bf16[32,1536]{1,0:T(8,128...) custom-call(bf16[16,1536]{1,0:T(8,128)(2,1)S(1)} %pair_tiles.1.after_ref.refs_0_, ...), custom_call_target="tpu_custom_call" | custom-call | flops 1207959552 | bytes 18874368 | tf_op jit(solution)/shard_map/partial_sums/pallas_call | solution.py:236
  20.7 0.1 collective-permute-start.5
  20.8 1.4 %collective-permute-done.5.right_ref = bf16[32,3072]{1,0:T(8,128)(2,1)S(1)} collective-permute-done((bf16[32,3072]{1,0:T(8,128)(2,1)S(1)}, bf16[32,3072]{1,0:T(8,128)(2,1)S(1)}, u32[]{:S(2)}, u32[]{:S(2)}) %collective-permute-start.5) | collective-permute-done | bytes 196640 | tf_op jit(solution)/shard_map/ppermute | solution.py:250
  22.3 1.6 %collective-permute-start.6 = (bf16[32,3072]{1,0:T(8,128)(2,1)S(1)}, bf16[32,3072]{1,0:T(8,128)(2,1)S(1)}, u32[]{:S(2)}, u32[]{:S(2)}) collective-permute-start(bf16[32,3072]{1,0:T(8,128)(2,1)S(1)} %add_cores.1.refs_0_), channel_id=1, source_target_pairs={{0,8},{8,0},{1,9},{9,1},{2,10},{10,2},{3,11},{11,3},{4,12},{12,4},... | collective-permute-start | bytes 589832 | tf_op jit(solution)/shard_map/ppermute | solution.py:256
  23.8 0.5 %collective-permute-start.4 = (f32[1,1536]{1,0:T(1,128)S(1)}, f32[1,1536]{1,0:T(1,128)S(1)}, u32[]{:S(2)}, u32[]{:S(2)}) collective-permute-start(f32[1,1536]{1,0:T(1,128)S(1)} %get-tuple-element.24.own_sums_ref), channel_id=1, source_target_pairs={{0,8},{8,0},{1,9},{9,1},{2,10},{10,2},{3,11},{11,3},{4,12},{12,4},... | collective-permute-start | bytes 18440 | tf_op jit(solution)/shard_map/ppermute | solution.py:255
  24.4 5.0 %collective-permute-done.4.after_ref.got_sums_ref = f32[1,1536]{1,0:T(1,128)S(1)} collective-permute-done((f32[1,1536]{1,0:T(1,128)S(1)}, f32[1,1536]{1,0:T(1,128)S(1)}, u32[]{:S(2)}, u32[]{:S(2)}) %collective-permute-start.4) | collective-permute-done | bytes 6176 | tf_op jit(solution)/shard_map/ppermute | solution.py:255
  29.4 0.0 collective-permute-done.6.refs_1_
  29.4 0.0 copy-done.1
  29.4 0.2 gelu.1.own_ref
  29.6 0.1 collective-permute-start.7
  29.7 1.4 %collective-permute-done.7.far_ref = bf16[32,3072]{1,0:T(8,128)(2,1)S(1)} collective-permute-done((bf16[32,3072]{1,0:T(8,128)(2,1)S(1)}, bf16[32,3072]{1,0:T(8,128)(2,1)S(1)}, u32[]{:S(2)}, u32[]{:S(2)}) %collective-permute-start.7) | collective-permute-done | bytes 196640 | tf_op jit(solution)/shard_map/ppermute | solution.py:266
  31.1 4.4 %output_blocks.1 = (bf16[32,3072]{1,0:T(8,128)(2,1)S(1)}, bf16[32,3072]{1,0:T(8,128)(2,1)S(1)}, bf16[16,1536]{1,0:T(8,128)(2,1)S(1)}, bf16[16,1536]{1,0:T(8,128)...) custom-call(bf16[32,3072]{1,0:T(8,128)(2,1)S(1)} %gelu.1.own_ref, ...), custom_call_target="tpu_custom_call" | custom-call | flops 1207959552 | tf_op jit(solution)/shard_map/output_blocks/pallas_call | solution.py:267
  35.6 0.0 copy-start
  35.6 0.8 %collective-permute-start.8 = (bf16[16,1536]{1,0:T(8,128)(2,1)S(1)}, bf16[16,1536]{1,0:T(8,128)(2,1)S(1)}, u32[]{:S(2)}, u32[]{:S(2)}) collective-permute-start(bf16[16,1536]{1,0:T(8,128)(2,1)S(1)} %get-tuple-element.29), channel_id=1, source_target_pairs={{0,1},{1,0},{2,3},{3,2},{4,5},{5,4},{6,7},{7,6},{8,9},{9,8},{10,11... | collective-permute-start | bytes 147464 | tf_op jit(solution)/shard_map/ppermute | solution.py:199
  36.4 2.9 %collective-permute-start.9 = (bf16[16,1536]{1,0:T(8,128)(2,1)S(1)}, bf16[16,1536]{1,0:T(8,128)(2,1)S(1)}, u32[]{:S(2)}, u32[]{:S(2)}) collective-permute-start(bf16[16,1536]{1,0:T(8,128)(2,1)S(1)} %get-tuple-element.30), channel_id=1, source_target_pairs={{0,2},{1,3},{2,0},{3,1},{4,6},{5,7},{6,4},{7,5},{8,10},{9,11},{10,... | collective-permute-start | bytes 147464 | tf_op jit(solution)/shard_map/ppermute | solution.py:199
  39.4 0.7 %collective-permute-start.10 = (bf16[16,1536]{1,0:T(8,128)(2,1)S(1)}, bf16[16,1536]{1,0:T(8,128)(2,1)S(1)}, u32[]{:S(2)}, u32[]{:S(2)}) collective-permute-start(bf16[16,1536]{1,0:T(8,128)(2,1)S(1)} %get-tuple-element.31), channel_id=1, source_target_pairs={{0,3},{1,2},{2,1},{3,0},{4,7},{5,6},{6,5},{7,4},{8,11},{9,10},{10,... | collective-permute-start | bytes 147464 | tf_op jit(solution)/shard_map/ppermute | solution.py:199
  40.0 5.1 %convolution_convert_fusion.1 = bf16[1536,3072]{1,0:T(8,128)(2,1)} fusion(bf16[32,1536]{1,0:T(8,128)(2,1)S(1)} %get-tuple-element.37, bf16[32,3072]{1,0:T(8,128)(2,1)S(1)} %get-tuple-element.34.hidden_ref), kind=kOutput, calls=%fused_computation.1 | convolution fusion | flops 306708480 | bytes 9732096 | tf_op jit(solution)/shard_map/dot_general | solution.py:24
  45.2 0.0 collective-permute-done.8.refs_1_
  45.2 0.0 collective-permute-done.9.refs_2_
  45.2 0.0 collective-permute-done.10.refs_3_
  45.2 0.0 copy-done
  45.3 1.6 %collective-permute-start.11 = (bf16[8,1536]{1,0:T(8,128)(2,1)S(1)}, bf16[8,1536]{1,0:T(8,128)(2,1)S(1)}, u32[]{:S(2)}, u32[]{:S(2)}) collective-permute-start(bf16[8,1536]{1,0:T(8,128)(2,1)S(1)} %get-tuple-element.33), channel_id=1, source_target_pairs={{0,8},{8,0},{1,9},{9,1},{2,10},{10,2},{3,11},{11,3},{4,12},{12,4},... | collective-permute-start | bytes 73736 | tf_op jit(solution)/shard_map/ppermute | solution.py:286
  46.8 5.2 %convolution_convert_fusion = bf16[3072,1536]{1,0:T(8,128)(2,1)} fusion(bf16[32,3072]{1,0:T(8,128)(2,1)S(1)} %get-tuple-element.38, bf16[32,1536]{1,0:T(8,128)(2,1)S(1)} %get-tuple-element.39), kind=kOutput, calls=%fused_computation | convolution fusion | flops 306708480 | bytes 9732096 | tf_op jit(solution)/shard_map/dot_general | solution.py:24
  52.0 0.0 collective-permute-done.11.got_ref
  52.0 0.7 %final_rows.1 = (bf16[4,3072]{1,0:T(4,128)(2,1)}, bf16[4,3072]{1,0:T(4,128)(2,1)}, f32[1,3072]{1,0:T(1,128)}, f32[1,3072]{1,0:T(1,128)}) custom-call(bf16[8,1536]{1,0:T(8,128)(2,1)S(1)} %get-tuple-element.32.own_ref, bf16[8,1536]{1,0:T(8,128)(2,1)S(1)} %collective-permute-done.11.got_ref, f32[1,1536]{1,0:T(1,128)S(1)} %get-tuple-element.24.own_sums_ref, ...), custom_call_target="tpu_custom_call" | custom-call | tf_op jit(solution)/shard_map/final_rows/pallas_call | solution.py:287
  (3 shorter events, 0.1 us)
Async XLA Ops:
  1.5 4.8 %collective-permute-start = (bf16[8,1536]{1,0:T(8,128)(2,1)S(1)}, bf16[8,1536]{1,0:T(8,128)(2,1)S(1)}, u32[]{:S(2)}, u32[]{:S(2)}) collective-permute-start(bf16[8,1536]{1,0:T(8,128)(2,1)S(1)} %get-tuple-element.42), channel_id=1, source_target_pairs={{0,8},{8,0},{1,9},{9,1},{2,10},{10,2},{3,11},{11,3},{4,12},{12,4},... | collective-permute-start | bytes 73736 | tf_op jit(solution)/shard_map/ppermute | solution.py:214
  6.3 8.5 %collective-permute-start.3 = (bf16[16,1536]{1,0:T(8,128)(2,1)S(1)}, bf16[16,1536]{1,0:T(8,128)(2,1)S(1)}, u32[]{:S(2)}, u32[]{:S(2)}) collective-permute-start(bf16[16,1536]{1,0:T(8,128)(2,1)S(1)} %pair_tiles.1.after_ref.refs_0_), channel_id=1, source_target_pairs={{0,3},{1,2},{2,1},{3,0},{4,7},{5,6},{6,5},{7,4},{8,11},{9,10},{10,... | collective-permute-start | bytes 147464 | tf_op jit(solution)/shard_map/ppermute | solution.py:199
  10.5 5.0 %collective-permute-start.2 = (bf16[16,1536]{1,0:T(8,128)(2,1)S(1)}, bf16[16,1536]{1,0:T(8,128)(2,1)S(1)}, u32[]{:S(2)}, u32[]{:S(2)}) collective-permute-start(bf16[16,1536]{1,0:T(8,128)(2,1)S(1)} %pair_tiles.1.after_ref.refs_0_), channel_id=1, source_target_pairs={{0,2},{1,3},{2,0},{3,1},{4,6},{5,7},{6,4},{7,5},{8,10},{9,11},{10,... | collective-permute-start | bytes 147464 | tf_op jit(solution)/shard_map/ppermute | solution.py:199
  10.5 5.0 %collective-permute-start.1 = (bf16[16,1536]{1,0:T(8,128)(2,1)S(1)}, bf16[16,1536]{1,0:T(8,128)(2,1)S(1)}, u32[]{:S(2)}, u32[]{:S(2)}) collective-permute-start(bf16[16,1536]{1,0:T(8,128)(2,1)S(1)} %pair_tiles.1.after_ref.refs_0_), channel_id=1, source_target_pairs={{0,1},{1,0},{2,3},{3,2},{4,5},{5,4},{6,7},{7,6},{8,9},{9,8},{10,11... | collective-permute-start | bytes 147464 | tf_op jit(solution)/shard_map/ppermute | solution.py:199
  14.9 14.6 %copy-start.1 = (f32[3072]{0:T(1024)S(1)}, f32[3072]{0:T(1024)}, u32[]{:S(2)}) copy-start(f32[3072]{0:T(1024)} %param.8) | copy-start | bytes 36868
  20.7 1.5 %collective-permute-start.5 = (bf16[32,3072]{1,0:T(8,128)(2,1)S(1)}, bf16[32,3072]{1,0:T(8,128)(2,1)S(1)}, u32[]{:S(2)}, u32[]{:S(2)}) collective-permute-start(bf16[32,3072]{1,0:T(8,128)(2,1)S(1)} %get-tuple-element.26), channel_id=1, source_target_pairs={{0,4},{4,0},{1,5},{5,1},{2,6},{6,2},{3,7},{7,3},{8,12},{12,8},{9,1... | collective-permute-start | bytes 589832 | tf_op jit(solution)/shard_map/ppermute | solution.py:250
  22.3 7.1 %collective-permute-start.6 = (bf16[32,3072]{1,0:T(8,128)(2,1)S(1)}, bf16[32,3072]{1,0:T(8,128)(2,1)S(1)}, u32[]{:S(2)}, u32[]{:S(2)}) collective-permute-start(bf16[32,3072]{1,0:T(8,128)(2,1)S(1)} %add_cores.1.refs_0_), channel_id=1, source_target_pairs={{0,8},{8,0},{1,9},{9,1},{2,10},{10,2},{3,11},{11,3},{4,12},{12,4},... | collective-permute-start | bytes 589832 | tf_op jit(solution)/shard_map/ppermute | solution.py:256
  23.8 5.6 %collective-permute-start.4 = (f32[1,1536]{1,0:T(1,128)S(1)}, f32[1,1536]{1,0:T(1,128)S(1)}, u32[]{:S(2)}, u32[]{:S(2)}) collective-permute-start(f32[1,1536]{1,0:T(1,128)S(1)} %get-tuple-element.24.own_sums_ref), channel_id=1, source_target_pairs={{0,8},{8,0},{1,9},{9,1},{2,10},{10,2},{3,11},{11,3},{4,12},{12,4},... | collective-permute-start | bytes 18440 | tf_op jit(solution)/shard_map/ppermute | solution.py:255
  29.6 1.5 %collective-permute-start.7 = (bf16[32,3072]{1,0:T(8,128)(2,1)S(1)}, bf16[32,3072]{1,0:T(8,128)(2,1)S(1)}, u32[]{:S(2)}, u32[]{:S(2)}) collective-permute-start(bf16[32,3072]{1,0:T(8,128)(2,1)S(1)} %gelu.1.own_ref), channel_id=1, source_target_pairs={{0,4},{4,0},{1,5},{5,1},{2,6},{6,2},{3,7},{7,3},{8,12},{12,8},{9,1... | collective-permute-start | bytes 589832 | tf_op jit(solution)/shard_map/ppermute | solution.py:266
  35.6 9.7 %copy-start = (f32[3072]{0:T(1024)S(1)}, f32[3072]{0:T(1024)}, u32[]{:S(2)}) copy-start(f32[3072]{0:T(1024)} %param.10) | copy-start | bytes 36868
  35.6 9.6 %collective-permute-start.8 = (bf16[16,1536]{1,0:T(8,128)(2,1)S(1)}, bf16[16,1536]{1,0:T(8,128)(2,1)S(1)}, u32[]{:S(2)}, u32[]{:S(2)}) collective-permute-start(bf16[16,1536]{1,0:T(8,128)(2,1)S(1)} %get-tuple-element.29), channel_id=1, source_target_pairs={{0,1},{1,0},{2,3},{3,2},{4,5},{5,4},{6,7},{7,6},{8,9},{9,8},{10,11... | collective-permute-start | bytes 147464 | tf_op jit(solution)/shard_map/ppermute | solution.py:199
  36.4 8.8 %collective-permute-start.9 = (bf16[16,1536]{1,0:T(8,128)(2,1)S(1)}, bf16[16,1536]{1,0:T(8,128)(2,1)S(1)}, u32[]{:S(2)}, u32[]{:S(2)}) collective-permute-start(bf16[16,1536]{1,0:T(8,128)(2,1)S(1)} %get-tuple-element.30), channel_id=1, source_target_pairs={{0,2},{1,3},{2,0},{3,1},{4,6},{5,7},{6,4},{7,5},{8,10},{9,11},{10,... | collective-permute-start | bytes 147464 | tf_op jit(solution)/shard_map/ppermute | solution.py:199
  39.4 5.9 %collective-permute-start.10 = (bf16[16,1536]{1,0:T(8,128)(2,1)S(1)}, bf16[16,1536]{1,0:T(8,128)(2,1)S(1)}, u32[]{:S(2)}, u32[]{:S(2)}) collective-permute-start(bf16[16,1536]{1,0:T(8,128)(2,1)S(1)} %get-tuple-element.31), channel_id=1, source_target_pairs={{0,3},{1,2},{2,1},{3,0},{4,7},{5,6},{6,5},{7,4},{8,11},{9,10},{10,... | collective-permute-start | bytes 147464 | tf_op jit(solution)/shard_map/ppermute | solution.py:199
  45.3 6.7 %collective-permute-start.11 = (bf16[8,1536]{1,0:T(8,128)(2,1)S(1)}, bf16[8,1536]{1,0:T(8,128)(2,1)S(1)}, u32[]{:S(2)}, u32[]{:S(2)}) collective-permute-start(bf16[8,1536]{1,0:T(8,128)(2,1)S(1)} %get-tuple-element.33), channel_id=1, source_target_pairs={{0,8},{8,0},{1,9},{9,1},{2,10},{10,2},{3,11},{11,3},{4,12},{12,4},... | collective-permute-start | bytes 73736 | tf_op jit(solution)/shard_map/ppermute | solution.py:286

commit v7 on v1

--- a/solution.py
+++ b/solution.py
@@ -1,10 +1,21 @@
+import functools
+
 import jax
 import jax.numpy as jnp
 from jax import lax
+from jax.experimental import pallas as pl
+from jax.experimental.pallas import tpu as pltpu
 from jax.sharding import PartitionSpec as P
 
 inv_root_two = 0.7071067811865476
 inv_root_two_pi = 0.3989422804014327
+
+MIB = 1 << 20
+bf16, f32 = jnp.bfloat16, jnp.float32
+like = jax.ShapeDtypeStruct
+whole = pl.BlockSpec(memory_space=pltpu.VMEM)
+hbm = pl.BlockSpec(memory_space=pltpu.HBM)
+swap = [(0, 1), (1, 0)]
 
 
 def gelu_parts(hidden):
@@ -23,8 +34,304 @@
     return lax.all_to_all(chunks, axes, split_axis=0, concat_axis=0, tiled=True)
 
 
-def make(mesh):
-    nt, nk, nn = mesh.shape["tok"], mesh.shape["kin"], mesh.shape["nout"]
+def tile_of(size, most):
+    return max(t for t in range(128, most + 1, 128) if size % t == 0)
+
+
+def tiles_of(size, most=512):
+    tile = tile_of(size, most)
+    return [pl.ds(i * tile, tile) for i in range(size // tile)]
+
+
+def call(body, name, outs, grant=4 * MIB, flops=0, moved=0, scratch=(), resident=True, specs=None):
+    shapes = [pltpu.VMEM(o.shape, o.dtype) if resident else o for o in outs]
+
+    def run(*args):
+        cost = pl.CostEstimate(flops=flops, bytes_accessed=moved, transcendentals=0)
+        return pl.pallas_call(
+            body,
+            out_shape=shapes,
+            in_specs=specs or [whole] * len(args),
+            out_specs=[whole] * len(outs),
+            scratch_shapes=list(scratch),
+            cost_estimate=cost,
+            compiler_params=pltpu.CompilerParams(vmem_limit_bytes=grant),
+            name=name,
+        )(*args)
+
+    return run
+
+
+def kept(array):
+    return pltpu.with_memory_space_constraint(array, pltpu.VMEM)
+
+
+def in_hbm(array):
+    return pltpu.with_memory_space_constraint(array, pltpu.HBM)
+
+
+def apart(mixed, rows):
+    total, wide = mixed.shape
+    tiles = mixed.reshape(total // (4 * rows), 2, 2 * rows, wide)
+    even, odd = tiles[:, 0], tiles[:, 1]
+    is_low = lax.broadcasted_iota(jnp.int32, even.shape, 1) < rows
+    first = jnp.where(is_low, even, pltpu.roll(odd, rows, 1))
+    second = jnp.where(is_low, pltpu.roll(even, rows, 1), odd)
+    return first.reshape(total // 2, wide), second.reshape(total // 2, wide)
+
+
+def together(first, second, rows):
+    total, wide = first.shape
+    first = first.reshape(total // (2 * rows), 2 * rows, wide)
+    second = second.reshape(total // (2 * rows), 2 * rows, wide)
+    is_low = lax.broadcasted_iota(jnp.int32, first.shape, 1) < rows
+    even = jnp.where(is_low, first, pltpu.roll(second, rows, 1))
+    odd = jnp.where(is_low, pltpu.roll(first, rows, 1), second)
+    return jnp.stack([even, odd], axis=1).reshape(2 * total, wide)
+
+
+def ordered(me, own, far, axis=0):
+    low, high = jnp.where(me == 0, own, far), jnp.where(me == 0, far, own)
+    return jnp.concatenate([low, high], axis=axis)
+
+
+def half_of(size, mine):
+    core = lax.axis_index("kin")
+    at = core if mine else 1 - core
+    return pl.ds(pl.multiple_of(at * size, size), size)
+
+
+def load_out_body(hbm_ref, after_ref, out_ref, sem):
+    copy = pltpu.make_async_copy(hbm_ref.at[half_of(out_ref.shape[0], False), :], out_ref, sem.at[0])
+    copy.start()
+    copy.wait()
+
+
+def load_in_body(hbm_ref, after_ref, own_ref, far_ref, sems):
+    half = own_ref.shape[1]
+    copies = [
+        pltpu.make_async_copy(hbm_ref.at[:, half_of(half, mine)], ref, sems.at[i])
+        for i, (ref, mine) in enumerate(((far_ref, False), (own_ref, True)))
+    ]
+    for copy in copies:
+        copy.start()
+    for copy in copies:
+        copy.wait()
+
+
+def pair_body(own_ref, got_ref, after_ref, out_ref):
+    out_ref[...] = ordered(lax.axis_index("tok"), own_ref[...], got_ref[...])
+
+
+def partial_sums(x_cols, dy_cols, w_in_ref, w_out_ref, out_ref):
+    count = x_cols.shape[0]
+    for at in tiles_of(out_ref.shape[1]):
+        out_ref[:count, at] = dot(x_cols, w_in_ref[:, at], 1, 0).astype(bf16)
+        out_ref[count:, at] = dot(dy_cols, w_out_ref[at, :], 1, 1).astype(bf16)
+
+
+def far_half_body(rows, count, *refs):
+    *piece_refs, w_in_ref, w_out_ref, w_hbm = refs[: count + 3]
+    own_weight_ref, sent_ref, x_ref, dy_ref, sums_ref, sem = refs[count + 3 :]
+    copy = pltpu.make_async_copy(
+        w_hbm.at[half_of(own_weight_ref.shape[0], True), :], own_weight_ref, sem.at[0]
+    )
+    copy.start()
+    mixed = jnp.concatenate([ref[...] for ref in piece_refs], axis=0)
+    x_cols, dy_cols = apart(mixed.astype(f32), rows)
+    sums_ref[...] = jnp.sum(dy_cols, axis=0, keepdims=True)
+    x_cols, dy_cols = x_cols.astype(bf16), dy_cols.astype(bf16)
+    x_ref[...], dy_ref[...] = x_cols, dy_cols
+    partial_sums(x_cols, dy_cols, w_in_ref, w_out_ref, sent_ref)
+    copy.wait()
+
+
+def own_half_body(x_ref, dy_ref, w_in_ref, w_out_ref, own_ref):
+    partial_sums(x_ref[...], dy_ref[...], w_in_ref, w_out_ref, own_ref)
+
+
+def add_body(left_ref, right_ref, out_ref):
+    out_ref[...] = (left_ref[...].astype(f32) + right_ref[...].astype(f32)).astype(bf16)
+
+
+def gelu_body(bias_ref, after_ref, own_ref, other_ref, out_ref):
+    count, half = out_ref.shape[0] // 2, out_ref.shape[1]
+    bias = bias_ref[:, half_of(half, True)]
+    tile = tile_of(half, 512)
+    for i in range(half // tile):
+        at = pl.ds(i * tile, tile)
+        summed = own_ref[:, at].astype(f32) + other_ref[:, at].astype(f32)
+        activated, slopes = gelu_parts(summed[:count] + bias[:, i * tile : (i + 1) * tile])
+        out_ref[:count, at] = activated.astype(bf16)
+        out_ref[count:, at] = (summed[count:] * slopes).astype(bf16)
+
+
+def own_terms_body(both_ref, w_in_ref, w_out_ref, out_ref):
+    count = both_ref.shape[0] // 2
+    act, grad = both_ref[:count], both_ref[count:]
+    for at in tiles_of(out_ref.shape[1]):
+        out_ref[:count, at] = dot(act, w_out_ref[:, at], 1, 0)
+        out_ref[count:, at] = dot(grad, w_in_ref[at, :], 1, 1)
+
+
+def blocks_body(rows, own_ref, far_ref, terms_ref, w_in_ref, w_out_ref, act_ref, grad_ref, *out_refs):
+    count = far_ref.shape[0] // 2
+    core = lax.axis_index("kin")
+    act, grad = far_ref[:count], far_ref[count:]
+    act_ref[...] = ordered(core, own_ref[:count], act, 1)
+    grad_ref[...] = ordered(core, own_ref[count:], grad, 1)
+    size = out_refs[0].shape[0]
+    for at in tiles_of(terms_ref.shape[1]):
+        forward = terms_ref[:count, at] + dot(act, w_out_ref[:, at], 1, 0)
+        backward = terms_ref[count:, at] + dot(grad, w_in_ref[at, :], 1, 1)
+        terms = together(forward, backward, rows).astype(bf16)
+        for i, out_ref in enumerate(out_refs):
+            out_ref[:, at] = terms[i * size : (i + 1) * size]
+
+
+def sum_body(rows, bias_ref, *refs):
+    *term_refs, own_ref, sent_ref = refs
+    wide = own_ref.shape[1]
+    me = lax.axis_index("tok")
+    summed = sum(ref[...].astype(f32) for ref in term_refs)
+    bias = jnp.where(me == 0, bias_ref[:, :wide], bias_ref[:, wide:])
+    is_fwd = lax.rem(lax.broadcasted_iota(jnp.int32, summed.shape, 0), 2 * rows) < rows
+    summed = summed + jnp.where(is_fwd, bias, 0.0)
+    low, high = summed[: 2 * rows], summed[2 * rows :]
+    own_ref[...] = jnp.where(me == 0, low, high).astype(bf16)
+    sent_ref[...] = jnp.where(me == 0, high, low).astype(bf16)
+
+
+def final_body(
+    rows, own_ref, got_ref, own_sums_ref, got_sums_ref, hidden_ref, rows_ref, grad_ref, sums_ref, bias_ref
+):
+    wide = own_ref.shape[1]
+    me = lax.axis_index("tok")
+    own, got = own_ref[...].astype(f32), got_ref[...].astype(f32)
+    own_sums, got_sums = own_sums_ref[...], got_sums_ref[...]
+    for i in range(2):
+        at = pl.ds(i * wide, wide)
+        part = jnp.where(me == i, own, got)
+        rows_ref[:, at] = part[:rows].astype(bf16)
+        grad_ref[:, at] = part[rows:].astype(bf16)
+        sums_ref[:, at] = jnp.where(me == i, own_sums, got_sums)
+    bias_ref[...] = jnp.sum(hidden_ref[...].astype(f32), axis=0, keepdims=True)
+
+
+def make_small(nn):
+    def across(array, shift):
+        return lax.ppermute(array, "nout", [(i, i ^ shift) for i in range(nn)])
+
+    def on_device(tokens, weight_in, bias_in, weight_out, bias_out, grad_out):
+        rows, cols = tokens.shape
+        wide, hid = weight_in.shape
+        half = hid // 2
+        pair = 2 * rows
+        count = 2 * nn * rows
+        work = 4 * count * wide * half
+        piece = 2 * wide * half
+        sem = pltpu.SemaphoreType.DMA
+
+        mine = jnp.concatenate([tokens, grad_out], axis=0)
+        me = lax.axis_index("tok")
+        own = lax.dynamic_slice_in_dim(mine, me * wide, wide, 1)
+        sent = lax.dynamic_slice_in_dim(mine, (1 - me) * wide, wide, 1)
+        got = lax.ppermute(sent, "tok", swap)
+        (out_far,) = call(
+            load_out_body,
+            "load_out",
+            [like((half, wide), bf16)],
+            grant=MIB,
+            moved=piece,
+            scratch=[sem((1,))],
+            specs=[hbm, pl.BlockSpec(memory_space=pl.ANY)],
+        )(in_hbm(weight_out), sent)
+        (tiles,) = call(pair_body, "pair_tiles", [like((2 * pair, wide), bf16)])(
+            kept(own), kept(got), kept(out_far)
+        )
+        pieces = [tiles] + [across(tiles, shift) for shift in range(1, nn)]
+        in_own, in_far = call(
+            load_in_body,
+            "load_in",
+            [like((wide, half), bf16)] * 2,
+            grant=MIB,
+            moved=2 * piece,
+            scratch=[sem((2,))],
+            specs=[hbm, pl.BlockSpec(memory_space=pl.ANY)],
+        )(in_hbm(weight_in), tiles)
+
+        out_own, sent, x_cols, dy_cols, sums = call(
+            functools.partial(far_half_body, rows, nn),
+            "far_half",
+            [like((half, wide), bf16), like((2 * count, half), bf16)]
+            + [like((count, wide), bf16)] * 2
+            + [like((1, wide), f32)],
+            grant=8 * MIB,
+            flops=work,
+            moved=piece,
+            scratch=[sem((1,))],
+            specs=[whole] * (nn + 2) + [hbm],
+        )(*[kept(piece) for piece in pieces], kept(in_far), kept(out_far), in_hbm(weight_out))
+        got = lax.ppermute(sent, "kin", swap)
+        (own,) = call(
+            own_half_body,
+            "own_half",
+            [like((2 * count, half), bf16)],
+            grant=8 * MIB,
+            flops=work,
+            moved=2 * piece,
+        )(kept(x_cols), kept(dy_cols), kept(in_own), kept(out_own))
+        (own,) = call(add_body, "add_cores", [like((2 * count, half), bf16)])(kept(own), kept(got))
+        other = lax.ppermute(own, "tok", swap)
+        got_sums = lax.ppermute(sums, "tok", swap)
+        (both,) = call(gelu_body, "gelu", [like((2 * count, half), bf16)])(
+            bias_in.reshape(1, hid), got_sums, kept(own), kept(other)
+        )
+        far = lax.ppermute(both, "kin", swap)
+        (terms,) = call(
+            own_terms_body,
+            "own_terms",
+            [like((2 * count, wide), f32)],
+            grant=8 * MIB,
+            flops=work,
+            moved=2 * piece,
+        )(kept(both), kept(in_own), kept(out_own))
+        act, grad, *blocks = call(
+            functools.partial(blocks_body, rows),
+            "output_blocks",
+            [like((count, hid), bf16)] * 2 + [like((2 * pair, wide), bf16)] * nn,
+            grant=8 * MIB,
+            flops=work,
+            moved=2 * piece,
+        )(kept(both), kept(far), kept(terms), kept(in_far), kept(out_far))
+
+        weight_in_grad = dot(x_cols, grad, 0, 0).astype(bf16)
+        weight_out_grad = dot(act, dy_cols, 0, 0).astype(bf16)
+
+        terms = [blocks[0]] + [across(blocks[shift], shift) for shift in range(1, nn)]
+        own, sent = call(
+            functools.partial(sum_body, rows), "sum_blocks", [like((pair, wide), bf16)] * 2
+        )(bias_out.reshape(1, cols), *[kept(term) for term in terms])
+        got = lax.ppermute(sent, "tok", swap)
+        output_rows, grad_tokens, bias_out_grad, bias_in_grad = call(
+            functools.partial(final_body, rows),
+            "final_rows",
+            [like((rows, cols), bf16)] * 2 + [like((1, cols), f32), like((1, hid), f32)],
+            resident=False,
+        )(kept(own), kept(got), kept(sums), kept(got_sums), kept(grad))
+        return (
+            output_rows,
+            grad_tokens,
+            weight_in_grad,
+            weight_out_grad,
+            bias_in_grad.reshape(hid),
+            bias_out_grad.reshape(cols),
+        )
+
+    return on_device
+
+
+def make_plain(nt, nk, nn):
     spread, square = nt * nn, nk * nt
 
     def on_device(tokens, weight_in, bias_in, weight_out, bias_out, grad_out):
@@ -83,8 +390,9 @@
 
 
 def solution(mesh):
+    nt, nk, nn = mesh.shape["tok"], mesh.shape["kin"], mesh.shape["nout"]
     return jax.shard_map(
-        make(mesh),
+        make_small(nn) if (nt, nk) == (2, 2) and nn in (2, 4) else make_plain(nt, nk, nn),
         mesh=mesh,
         in_specs=(
             P(("groups", "tok", "nout"), "kin"),

time: 81.4 us -> 53.5 us (0.66)
  matrix products: 30.7 us -> 10.3 us
  Pallas kernels: 0 us -> 18.3 us
  waiting for transfers between devices: 15.3 us -> 7.28 us
  blocking collectives: 7.44 us -> 0 us
  local copies, waits for them, and re-layouts: 6.56 us -> 0.01 us
  starting transfers between devices: 17.6 us -> 15.7 us
  other arithmetic: 2.41 us -> 0.86 us
    dot_general x6 -> x2, matrix products: 30.7 us -> 10.3 us  [dot(): lax.dot_general(left, right, (((left_dim,), (right_dim,)), ((), ())), pre...]
    pallas_call x0 -> x11, Pallas kernels: none -> 18.3 us  [run(): pl.pallas_call(body, out_shape=shapes, in_specs=specs or [whole] * len(ar...]
    all_to_all x4 -> x0, starting transfers between devices: 17.6 us -> none  [exchange(): return lax.all_to_all(chunks, axes, split_axis=0, concat_axis=0, tiled=True)]
    ppermute x0 -> x12, starting transfers between devices: none -> 15.7 us  [the longest x6 8.9 us: across(): return lax.ppermute(array, 'nout', [(i, i ^ shift) for i in range(nn)])]
    all_to_all x4 -> x0, waiting for transfers between devices: 15.3 us -> none  [exchange(): return lax.all_to_all(chunks, axes, split_axis=0, concat_axis=0, tiled=True)]
    all_gather x1 -> x0, blocking collectives: 7.44 us -> none  [on_device(): bias_out_grad = lax.all_gather(col_sums, 'tok', axis=0, tiled=True)]
    ppermute x0 -> x12, waiting for transfers between devices: none -> 7.28 us  [the longest x1 5.41 us: on_device(): got_sums = lax.ppermute(sums, 'tok', swap)]
    broadcast_in_dim x2 -> x0, local copies, waits for them, and re-layouts: 1.46 us -> none  [the longest x1 0.77 us: on_device(): jnp.broadcast_to(both[None], (square, total, part))]
  transfers between devices with their start and end apart: 4 -> 12, of which waited for: 2 -> 2; matrix products, arithmetic and copies ran while one was open for 15% -> 19% of each run, Pallas kernels for 0% -> 20%
where the time goes in v7:
time: 53.5 us; the launch traced here: 53.2 us
  Pallas kernels  18.3 us (34%)
  starting transfers between devices  15.7 us (29%)
  matrix products  10.3 us (19%)
  waiting for transfers between devices  7.28 us (14%)
  other arithmetic  0.86 us (2%)
  between operations  0.81 us (2%)
    pallas_call x11, Pallas kernels, run(): pl.pallas_call(body, out_shape=shapes, in_specs=specs or [whole] * len(ar...  18.3 us
    dot_general x2, matrix products, dot(): lax.dot_general(left, right, (((left_dim,), (right_dim,)), ((), ())), pre...  10.3 us
    ppermute x6, starting transfers between devices, across(): return lax.ppermute(array, 'nout', [(i, i ^ shift) for i in range(nn)])  8.9 us
    ppermute x1, waiting for transfers between devices, on_device(): got_sums = lax.ppermute(sums, 'tok', swap)  5.41 us
    ppermute x2, starting transfers between devices, on_device(): got = lax.ppermute(sent, 'tok', swap)  4.52 us
    ppermute x6, waiting for transfers between devices, across(): return lax.ppermute(array, 'nout', [(i, i ^ shift) for i in range(nn)])  1.86 us
    ppermute x1, starting transfers between devices, on_device(): other = lax.ppermute(own, 'tok', swap)  1.52 us
  transfers between devices with their start and end apart: 12, of which 2 were waited for; matrix products, arithmetic and copies ran while one was open for 19% of the time, Pallas kernels for 20%

profile of v7, /device:TPU:0, one launch (start us, length us, event | category | flops | bytes accessed | tf_op | source)
XLA Modules:
  0.0 53.2 jit_solution(4417348313955385246)
XLA Ops:
  0.6 0.9 %fusion = (bf16[8,1536]{1,0:T(8,128)(2,1)S(1)}, bf16[8,1536]{1,0:T(8,128)(2,1)S(1)}) fusion(s32[]{:T(128)S(6)} %select_n.7, bf16[4,3072]{1,0:T(4,128)(2,1)} %param.6, bf16[4,3072]{1,0:T(4,128)(2,1)} %param.11, s32[]{:T(128)S(6)} %select_n.6), kind=kLoop, calls=%fused_computation.6 | loop fusion | flops 98304 | bytes 98312 | tf_op jit(solution)/shard_map/concatenate | solution.py:235
  1.5 3.0 %collective-permute-start = (bf16[8,1536]{1,0:T(8,128)(2,1)S(1)}, bf16[8,1536]{1,0:T(8,128)(2,1)S(1)}, u32[]{:S(2)}, u32[]{:S(2)}) collective-permute-start(bf16[8,1536]{1,0:T(8,128)(2,1)S(1)} %get-tuple-element.44.after_ref), channel_id=1, source_target_pairs={{0,8},{8,0},{1,9},{9,1},{2,10},{10,2},{3,11},{11,3},{4,12},{12,4},... | collective-permute-start | bytes 73736 | tf_op jit(solution)/shard_map/ppermute | solution.py:239
  4.5 2.3 %load_out.1.after_ref.refs_5_.w_out_ref = bf16[1536,1536]{1,0:T(8,128)(2,1)S(1)} custom-call(bf16[3072,1536]{1,0:T(8,128)(2,1)} %refs_6_.1, bf16[8,1536]{1,0:T(8,128)(2,1)S(1)} %get-tuple-element.44.after_ref), custom_call_target="tpu_custom_call" | custom-call | bytes 4718592 | tf_op jit(solution)/shard_map/load_out/pallas_call | solution.py:51
  6.9 0.0 collective-permute-done.got_ref
  6.9 1.6 %collective-permute-start.1 = (bf16[16,1536]{1,0:T(8,128)(2,1)S(1)}, bf16[16,1536]{1,0:T(8,128)(2,1)S(1)}, u32[]{:S(2)}, u32[]{:S(2)}) collective-permute-start(bf16[16,1536]{1,0:T(8,128)(2,1)S(1)} %pair_tiles.1.after_ref.refs_0_), channel_id=1, source_target_pairs={{0,1},{1,0},{2,3},{3,2},{4,5},{5,4},{6,7},{7,6},{8,9},{9,8},{10,11... | collective-permute-start | bytes 147464 | tf_op jit(solution)/shard_map/ppermute | solution.py:223
  8.5 2.6 %collective-permute-start.2 = (bf16[16,1536]{1,0:T(8,128)(2,1)S(1)}, bf16[16,1536]{1,0:T(8,128)(2,1)S(1)}, u32[]{:S(2)}, u32[]{:S(2)}) collective-permute-start(bf16[16,1536]{1,0:T(8,128)(2,1)S(1)} %pair_tiles.1.after_ref.refs_0_), channel_id=1, source_target_pairs={{0,2},{1,3},{2,0},{3,1},{4,6},{5,7},{6,4},{7,5},{8,10},{9,11},{10,... | collective-permute-start | bytes 147464 | tf_op jit(solution)/shard_map/ppermute | solution.py:223
  11.1 0.2 collective-permute-start.3
  11.3 3.8 %load_in.1 = (bf16[1536,1536]{1,0:T(8,128)(2,1)S(1)}, bf16[1536,1536]{1,0:T(8,128)(2,1)S(1)}) custom-call(bf16[1536,3072]{1,0:T(8,128)(2,1)} %hbm_ref.3, bf16[16,1536]{1,0:T(8,128)(2,1)S(1)} %pair_tiles.1.after_ref.refs_0_), custom_call_target="tpu_custom_call" | custom-call | bytes 9437184 | tf_op jit(solution)/shard_map/load_in/pallas_call | solution.py:51
  15.1 0.0 collective-permute-done.1.refs_1_
  15.2 0.0 collective-permute-done.2.refs_2_
  15.2 1.8 %collective-permute-done.3.refs_3_ = bf16[16,1536]{1,0:T(8,128)(2,1)S(1)} collective-permute-done((bf16[16,1536]{1,0:T(8,128)(2,1)S(1)}, bf16[16,1536]{1,0:T(8,128)(2,1)S(1)}, u32[]{:S(2)}, u32[]{:S(2)}) %collective-permute-start.3) | collective-permute-done | bytes 49184 | tf_op jit(solution)/shard_map/ppermute | solution.py:223
  17.0 4.4 %far_half.1 = (bf16[1536,1536]{1,0:T(8,128)(2,1)S(1)}, bf16[64,1536]{1,0:T(8,128)(2,1)S(1)}, bf16[32,1536]{1,0:T(8,128)(2,1)S(1)}, bf16[32,1536]{1,0:T(8,128)(2,1)S(1)}, f32[1,1536]{1,0:T(1,128)S(1)}) custom-call(bf16[16,1536]{1,0:T(8,128)(2,1)S(1)} %pair_tiles.1.after_ref.refs_0_, bf16[16,1536]{1,0:T(8,128)(2,1)S(1)} %collective-permute-done.1.refs_1_, ...), custom_call_target="tpu_custom_call" | custom-call | flops 301989888 | bytes 4718592 | tf_op jit(solution)/shard_map/far_half/pallas_call | solution.py:51
  21.5 0.0 copy-start.1
  21.5 0.1 collective-permute-start.5
  21.6 2.2 %own_half.1.left_ref = bf16[64,1536]{1,0:T(8,128)(2,1)S(1)} custom-call(bf16[32,1536]{1,0:T(8,128)(2,1)S(1)} %get-tuple-element.27.x_ref, bf16[32,1536]{1,0:T(8,128)(2,1)S(1)} %get-tuple-element.28.dy_ref, bf16[1536,1536]{1,0:T(8,128)(2,1)S(1)} %get-tuple-element.29.w_in_ref, bf16[1536,1536]{1,0:T(8,128)(2,1)S(1)} %get-tuple-element.30.w_out_ref), custom_call_target="tpu_custom_call" | custom-call | flops 301989888 | bytes 9437184 | tf_op jit(solution)/shard_map/own_half/pallas_call | solution.py:51
  23.8 0.0 collective-permute-done.5.right_ref
  23.8 0.1 add_cores.1.own_ref
  23.9 1.5 %collective-permute-start.6 = (bf16[64,1536]{1,0:T(8,128)(2,1)S(1)}, bf16[64,1536]{1,0:T(8,128)(2,1)S(1)}, u32[]{:S(2)}, u32[]{:S(2)}) collective-permute-start(bf16[64,1536]{1,0:T(8,128)(2,1)S(1)} %add_cores.1.own_ref), channel_id=1, source_target_pairs={{0,8},{8,0},{1,9},{9,1},{2,10},{10,2},{3,11},{11,3},{4,12},{12,4},... | collective-permute-start | bytes 589832 | tf_op jit(solution)/shard_map/ppermute | solution.py:285
  25.4 0.6 %collective-permute-start.4 = (f32[1,1536]{1,0:T(1,128)S(1)}, f32[1,1536]{1,0:T(1,128)S(1)}, u32[]{:S(2)}, u32[]{:S(2)}) collective-permute-start(f32[1,1536]{1,0:T(1,128)S(1)} %get-tuple-element.26.own_sums_ref), channel_id=1, source_target_pairs={{0,8},{8,0},{1,9},{9,1},{2,10},{10,2},{3,11},{11,3},{4,12},{12,4},... | collective-permute-start | bytes 18440 | tf_op jit(solution)/shard_map/ppermute | solution.py:286
  26.0 5.4 %collective-permute-done.4.after_ref.got_sums_ref = f32[1,1536]{1,0:T(1,128)S(1)} collective-permute-done((f32[1,1536]{1,0:T(1,128)S(1)}, f32[1,1536]{1,0:T(1,128)S(1)}, u32[]{:S(2)}, u32[]{:S(2)}) %collective-permute-start.4) | collective-permute-done | bytes 6176 | tf_op jit(solution)/shard_map/ppermute | solution.py:286
  31.4 0.0 collective-permute-done.6.other_ref
  31.4 0.0 copy-done.1
  31.4 0.1 gelu.1.both_ref.own_ref
  31.5 0.1 collective-permute-start.7
  31.6 2.2 %own_terms.1.terms_ref = f32[64,1536]{1,0:T(8,128)S(1)} custom-call(bf16[64,1536]{1,0:T(8,128)(2,1)S(1)} %gelu.1.both_ref.own_ref, bf16[1536,1536]{1,0:T(8,128)(2,1)S(1)} %get-tuple-element.29.w_in_ref, bf16[1536,1536]{1,0:T(8,128)(2,1)S(1)} %get-tuple-element.30.w_out_ref), custom_call_target="tpu_custom_call" | custom-call | flops 301989888 | bytes 9437184 | tf_op jit(solution)/shard_map/own_terms/pallas_call | solution.py:51
  33.8 0.0 collective-permute-done.7.far_ref
  33.8 2.3 %output_blocks.1 = (bf16[32,3072]{1,0:T(8,128)(2,1)S(1)}, bf16[32,3072]{1,0:T(8,128)(2,1)S(1)}, bf16[16,1536]{1,0:T(8,128)(2,1)S(1)}, bf16[16,1536]{1,0:T(8,128)...) custom-call(bf16[64,1536]{1,0:T(8,128)(2,1)S(1)} %gelu.1.both_ref.own_ref, ...), custom_call_target="tpu_custom_call" | custom-call | flops 301989888 | bytes 9437184 | tf_op jit(solution)/shard_map/output_blocks/pallas_call | solution.py:51
  36.2 0.0 copy-start
  36.2 1.8 %collective-permute-start.10 = (bf16[16,1536]{1,0:T(8,128)(2,1)S(1)}, bf16[16,1536]{1,0:T(8,128)(2,1)S(1)}, u32[]{:S(2)}, u32[]{:S(2)}) collective-permute-start(bf16[16,1536]{1,0:T(8,128)(2,1)S(1)} %get-tuple-element.35), channel_id=1, source_target_pairs={{0,3},{1,2},{2,1},{3,0},{4,7},{5,6},{6,5},{7,4},{8,11},{9,10},{10,... | collective-permute-start | bytes 147464 | tf_op jit(solution)/shard_map/ppermute | solution.py:223
  38.0 0.0 collective-permute-start.8
  38.0 2.6 %collective-permute-start.9 = (bf16[16,1536]{1,0:T(8,128)(2,1)S(1)}, bf16[16,1536]{1,0:T(8,128)(2,1)S(1)}, u32[]{:S(2)}, u32[]{:S(2)}) collective-permute-start(bf16[16,1536]{1,0:T(8,128)(2,1)S(1)} %get-tuple-element.34), channel_id=1, source_target_pairs={{0,2},{1,3},{2,0},{3,1},{4,6},{5,7},{6,4},{7,5},{8,10},{9,11},{10,... | collective-permute-start | bytes 147464 | tf_op jit(solution)/shard_map/ppermute | solution.py:223
  40.6 5.2 %convolution_convert_fusion = bf16[3072,1536]{1,0:T(8,128)(2,1)} fusion(bf16[32,3072]{1,0:T(8,128)(2,1)S(1)} %get-tuple-element.41, bf16[32,1536]{1,0:T(8,128)(2,1)S(1)} %get-tuple-element.28.dy_ref), kind=kOutput, calls=%fused_computation | convolution fusion | flops 306708480 | bytes 9732096 | tf_op jit(solution)/shard_map/dot_general | solution.py:28
  45.8 0.0 collective-permute-done.10.refs_3_
  45.8 0.0 collective-permute-done.8.refs_1_
  45.8 0.0 collective-permute-done.9.refs_2_
  45.8 0.0 copy-done
  45.9 1.5 %collective-permute-start.11 = (bf16[8,1536]{1,0:T(8,128)(2,1)S(1)}, bf16[8,1536]{1,0:T(8,128)(2,1)S(1)}, u32[]{:S(2)}, u32[]{:S(2)}) collective-permute-start(bf16[8,1536]{1,0:T(8,128)(2,1)S(1)} %get-tuple-element.37), channel_id=1, source_target_pairs={{0,8},{8,0},{1,9},{9,1},{2,10},{10,2},{3,11},{11,3},{4,12},{12,4},... | collective-permute-start | bytes 73736 | tf_op jit(solution)/shard_map/ppermute | solution.py:315
  47.4 5.2 %convolution_convert_fusion.1 = bf16[1536,3072]{1,0:T(8,128)(2,1)} fusion(bf16[32,1536]{1,0:T(8,128)(2,1)S(1)} %get-tuple-element.27.x_ref, bf16[32,3072]{1,0:T(8,128)(2,1)S(1)} %get-tuple-element.38.hidden_ref), kind=kOutput, calls=%fused_computation.1 | convolution fusion | flops 306708480 | bytes 9732096 | tf_op jit(solution)/shard_map/dot_general | solution.py:28
  52.5 0.0 collective-permute-done.11.got_ref
  52.5 0.7 %final_rows.1 = (bf16[4,3072]{1,0:T(4,128)(2,1)}, bf16[4,3072]{1,0:T(4,128)(2,1)}, f32[1,3072]{1,0:T(1,128)}, f32[1,3072]{1,0:T(1,128)}) custom-call(bf16[8,1536]{1,0:T(8,128)(2,1)S(1)} %get-tuple-element.36.own_ref, bf16[8,1536]{1,0:T(8,128)(2,1)S(1)} %collective-permute-done.11.got_ref, f32[1,1536]{1,0:T(1,128)S(1)} %get-tuple-element.26.own_sums_ref, ...), custom_call_target="tpu_custom_call" | custom-call | tf_op jit(solution)/shard_map/final_rows/pallas_call | solution.py:51
  (2 shorter events, 0.1 us)
Async XLA Ops:
  1.5 5.4 %collective-permute-start = (bf16[8,1536]{1,0:T(8,128)(2,1)S(1)}, bf16[8,1536]{1,0:T(8,128)(2,1)S(1)}, u32[]{:S(2)}, u32[]{:S(2)}) collective-permute-start(bf16[8,1536]{1,0:T(8,128)(2,1)S(1)} %get-tuple-element.44.after_ref), channel_id=1, source_target_pairs={{0,8},{8,0},{1,9},{9,1},{2,10},{10,2},{3,11},{11,3},{4,12},{12,4},... | collective-permute-start | bytes 73736 | tf_op jit(solution)/shard_map/ppermute | solution.py:239
  6.9 8.3 %collective-permute-start.1 = (bf16[16,1536]{1,0:T(8,128)(2,1)S(1)}, bf16[16,1536]{1,0:T(8,128)(2,1)S(1)}, u32[]{:S(2)}, u32[]{:S(2)}) collective-permute-start(bf16[16,1536]{1,0:T(8,128)(2,1)S(1)} %pair_tiles.1.after_ref.refs_0_), channel_id=1, source_target_pairs={{0,1},{1,0},{2,3},{3,2},{4,5},{5,4},{6,7},{7,6},{8,9},{9,8},{10,11... | collective-permute-start | bytes 147464 | tf_op jit(solution)/shard_map/ppermute | solution.py:223
  8.5 6.6 %collective-permute-start.2 = (bf16[16,1536]{1,0:T(8,128)(2,1)S(1)}, bf16[16,1536]{1,0:T(8,128)(2,1)S(1)}, u32[]{:S(2)}, u32[]{:S(2)}) collective-permute-start(bf16[16,1536]{1,0:T(8,128)(2,1)S(1)} %pair_tiles.1.after_ref.refs_0_), channel_id=1, source_target_pairs={{0,2},{1,3},{2,0},{3,1},{4,6},{5,7},{6,4},{7,5},{8,10},{9,11},{10,... | collective-permute-start | bytes 147464 | tf_op jit(solution)/shard_map/ppermute | solution.py:223
  11.1 5.9 %collective-permute-start.3 = (bf16[16,1536]{1,0:T(8,128)(2,1)S(1)}, bf16[16,1536]{1,0:T(8,128)(2,1)S(1)}, u32[]{:S(2)}, u32[]{:S(2)}) collective-permute-start(bf16[16,1536]{1,0:T(8,128)(2,1)S(1)} %pair_tiles.1.after_ref.refs_0_), channel_id=1, source_target_pairs={{0,3},{1,2},{2,1},{3,0},{4,7},{5,6},{6,5},{7,4},{8,11},{9,10},{10,... | collective-permute-start | bytes 147464 | tf_op jit(solution)/shard_map/ppermute | solution.py:223
  21.5 9.9 %copy-start.1 = (f32[3072]{0:T(1024)S(1)}, f32[3072]{0:T(1024)}, u32[]{:S(2)}) copy-start(f32[3072]{0:T(1024)} %param.8) | copy-start | bytes 36868
  21.5 2.3 %collective-permute-start.5 = (bf16[64,1536]{1,0:T(8,128)(2,1)S(1)}, bf16[64,1536]{1,0:T(8,128)(2,1)S(1)}, u32[]{:S(2)}, u32[]{:S(2)}) collective-permute-start(bf16[64,1536]{1,0:T(8,128)(2,1)S(1)} %get-tuple-element.31), channel_id=1, source_target_pairs={{0,4},{4,0},{1,5},{5,1},{2,6},{6,2},{3,7},{7,3},{8,12},{12,8},{9,1... | collective-permute-start | bytes 589832 | tf_op jit(solution)/shard_map/ppermute | solution.py:275
  23.9 7.5 %collective-permute-start.6 = (bf16[64,1536]{1,0:T(8,128)(2,1)S(1)}, bf16[64,1536]{1,0:T(8,128)(2,1)S(1)}, u32[]{:S(2)}, u32[]{:S(2)}) collective-permute-start(bf16[64,1536]{1,0:T(8,128)(2,1)S(1)} %add_cores.1.own_ref), channel_id=1, source_target_pairs={{0,8},{8,0},{1,9},{9,1},{2,10},{10,2},{3,11},{11,3},{4,12},{12,4},... | collective-permute-start | bytes 589832 | tf_op jit(solution)/shard_map/ppermute | solution.py:285
  25.4 6.0 %collective-permute-start.4 = (f32[1,1536]{1,0:T(1,128)S(1)}, f32[1,1536]{1,0:T(1,128)S(1)}, u32[]{:S(2)}, u32[]{:S(2)}) collective-permute-start(f32[1,1536]{1,0:T(1,128)S(1)} %get-tuple-element.26.own_sums_ref), channel_id=1, source_target_pairs={{0,8},{8,0},{1,9},{9,1},{2,10},{10,2},{3,11},{11,3},{4,12},{12,4},... | collective-permute-start | bytes 18440 | tf_op jit(solution)/shard_map/ppermute | solution.py:286
  31.5 2.3 %collective-permute-start.7 = (bf16[64,1536]{1,0:T(8,128)(2,1)S(1)}, bf16[64,1536]{1,0:T(8,128)(2,1)S(1)}, u32[]{:S(2)}, u32[]{:S(2)}) collective-permute-start(bf16[64,1536]{1,0:T(8,128)(2,1)S(1)} %gelu.1.both_ref.own_ref), channel_id=1, source_target_pairs={{0,4},{4,0},{1,5},{5,1},{2,6},{6,2},{3,7},{7,3},{8,12},{12,8},{9,1... | collective-permute-start | bytes 589832 | tf_op jit(solution)/shard_map/ppermute | solution.py:290
  36.2 9.6 %copy-start = (f32[3072]{0:T(1024)S(1)}, f32[3072]{0:T(1024)}, u32[]{:S(2)}) copy-start(f32[3072]{0:T(1024)} %param.10) | copy-start | bytes 36868
  36.2 9.6 %collective-permute-start.10 = (bf16[16,1536]{1,0:T(8,128)(2,1)S(1)}, bf16[16,1536]{1,0:T(8,128)(2,1)S(1)}, u32[]{:S(2)}, u32[]{:S(2)}) collective-permute-start(bf16[16,1536]{1,0:T(8,128)(2,1)S(1)} %get-tuple-element.35), channel_id=1, source_target_pairs={{0,3},{1,2},{2,1},{3,0},{4,7},{5,6},{6,5},{7,4},{8,11},{9,10},{10,... | collective-permute-start | bytes 147464 | tf_op jit(solution)/shard_map/ppermute | solution.py:223
  38.0 7.8 %collective-permute-start.8 = (bf16[16,1536]{1,0:T(8,128)(2,1)S(1)}, bf16[16,1536]{1,0:T(8,128)(2,1)S(1)}, u32[]{:S(2)}, u32[]{:S(2)}) collective-permute-start(bf16[16,1536]{1,0:T(8,128)(2,1)S(1)} %get-tuple-element.33), channel_id=1, source_target_pairs={{0,1},{1,0},{2,3},{3,2},{4,5},{5,4},{6,7},{7,6},{8,9},{9,8},{10,11... | collective-permute-start | bytes 147464 | tf_op jit(solution)/shard_map/ppermute | solution.py:223
  38.0 7.8 %collective-permute-start.9 = (bf16[16,1536]{1,0:T(8,128)(2,1)S(1)}, bf16[16,1536]{1,0:T(8,128)(2,1)S(1)}, u32[]{:S(2)}, u32[]{:S(2)}) collective-permute-start(bf16[16,1536]{1,0:T(8,128)(2,1)S(1)} %get-tuple-element.34), channel_id=1, source_target_pairs={{0,2},{1,3},{2,0},{3,1},{4,6},{5,7},{6,4},{7,5},{8,10},{9,11},{10,... | collective-permute-start | bytes 147464 | tf_op jit(solution)/shard_map/ppermute | solution.py:223
  45.9 6.7 %collective-permute-start.11 = (bf16[8,1536]{1,0:T(8,128)(2,1)S(1)}, bf16[8,1536]{1,0:T(8,128)(2,1)S(1)}, u32[]{:S(2)}, u32[]{:S(2)}) collective-permute-start(bf16[8,1536]{1,0:T(8,128)(2,1)S(1)} %get-tuple-element.37), channel_id=1, source_target_pairs={{0,8},{8,0},{1,9},{9,1},{2,10},{10,2},{3,11},{11,3},{4,12},{12,4},... | collective-permute-start | bytes 73736 | tf_op jit(solution)/shard_map/ppermute | solution.py:315

commit v8 on v7

--- a/solution.py
+++ b/solution.py
@@ -101,18 +101,27 @@
     return pl.ds(pl.multiple_of(at * size, size), size)
 
 
-def load_out_body(hbm_ref, after_ref, out_ref, sem):
-    copy = pltpu.make_async_copy(hbm_ref.at[half_of(out_ref.shape[0], False), :], out_ref, sem.at[0])
-    copy.start()
-    copy.wait()
-
-
-def load_in_body(hbm_ref, after_ref, own_ref, far_ref, sems):
+def quarters(source, target, sems):
+    size = target.shape[0] // 4
+    return [
+        pltpu.make_async_copy(source.at[part, :], target.at[part, :], sems.at[i])
+        for i, part in enumerate(pl.ds(j * size, size) for j in range(4))
+    ]
+
+
+def load_far_body(hbm_ref, after_ref, out_ref, sems):
+    copies = quarters(hbm_ref.at[half_of(out_ref.shape[0], False), :], out_ref, sems)
+    for copy in copies:
+        copy.start()
+    for copy in copies:
+        copy.wait()
+
+
+def load_body(in_hbm_ref, out_hbm_ref, after_ref, far_ref, own_ref, out_ref, sems):
     half = own_ref.shape[1]
-    copies = [
-        pltpu.make_async_copy(hbm_ref.at[:, half_of(half, mine)], ref, sems.at[i])
-        for i, (ref, mine) in enumerate(((far_ref, False), (own_ref, True)))
-    ]
+    copies = quarters(in_hbm_ref.at[:, half_of(half, False)], far_ref, sems.at[0])
+    copies += quarters(in_hbm_ref.at[:, half_of(half, True)], own_ref, sems.at[1])
+    copies += quarters(out_hbm_ref.at[half_of(half, True), :], out_ref, sems.at[2])
     for copy in copies:
         copy.start()
     for copy in copies:
@@ -131,19 +140,14 @@
 
 
 def far_half_body(rows, count, *refs):
-    *piece_refs, w_in_ref, w_out_ref, w_hbm = refs[: count + 3]
-    own_weight_ref, sent_ref, x_ref, dy_ref, sums_ref, sem = refs[count + 3 :]
-    copy = pltpu.make_async_copy(
-        w_hbm.at[half_of(own_weight_ref.shape[0], True), :], own_weight_ref, sem.at[0]
-    )
-    copy.start()
+    *piece_refs, w_in_ref, w_out_ref = refs[: count + 2]
+    sent_ref, x_ref, dy_ref, sums_ref = refs[count + 2 :]
     mixed = jnp.concatenate([ref[...] for ref in piece_refs], axis=0)
     x_cols, dy_cols = apart(mixed.astype(f32), rows)
     sums_ref[...] = jnp.sum(dy_cols, axis=0, keepdims=True)
     x_cols, dy_cols = x_cols.astype(bf16), dy_cols.astype(bf16)
     x_ref[...], dy_ref[...] = x_cols, dy_cols
     partial_sums(x_cols, dy_cols, w_in_ref, w_out_ref, sent_ref)
-    copy.wait()
 
 
 def own_half_body(x_ref, dy_ref, w_in_ref, w_out_ref, own_ref):
@@ -187,6 +191,40 @@
         terms = together(forward, backward, rows).astype(bf16)
         for i, out_ref in enumerate(out_refs):
             out_ref[:, at] = terms[i * size : (i + 1) * size]
+
+
+def outer_body(most, left_ref, right_ref, out_hbm, block_ref, sems):
+    copies = []
+    for i, at in enumerate(tiles_of(out_hbm.shape[0], 256)):
+        left = left_ref[:, at].T
+        for part in tiles_of(out_hbm.shape[1], most):
+            block_ref[at, part] = dot(left, right_ref[:, part], 1, 0).astype(bf16)
+        copies.append(
+            pltpu.make_async_copy(block_ref.at[at, :], out_hbm.at[at, :], sems.at[i])
+        )
+        copies[-1].start()
+    for copy in copies:
+        copy.wait()
+
+
+def outer(left, right, name, most):
+    count, high = left.shape
+    wide = right.shape[1]
+    return pl.pallas_call(
+        functools.partial(outer_body, most),
+        out_shape=like((high, wide), bf16),
+        in_specs=[whole] * 2,
+        out_specs=pl.BlockSpec(memory_space=pl.ANY),
+        scratch_shapes=[
+            pltpu.VMEM((high, wide), bf16),
+            pltpu.SemaphoreType.DMA((len(tiles_of(high, 256)),)),
+        ],
+        cost_estimate=pl.CostEstimate(
+            flops=2 * count * wide * high, bytes_accessed=2 * wide * high, transcendentals=0
+        ),
+        compiler_params=pltpu.CompilerParams(vmem_limit_bytes=16 * MIB),
+        name=name,
+    )(kept(left), kept(right))
 
 
 def sum_body(rows, bias_ref, *refs):
@@ -238,40 +276,38 @@
         sent = lax.dynamic_slice_in_dim(mine, (1 - me) * wide, wide, 1)
         got = lax.ppermute(sent, "tok", swap)
         (out_far,) = call(
-            load_out_body,
-            "load_out",
+            load_far_body,
+            "load_far",
             [like((half, wide), bf16)],
             grant=MIB,
             moved=piece,
-            scratch=[sem((1,))],
+            scratch=[sem((4,))],
             specs=[hbm, pl.BlockSpec(memory_space=pl.ANY)],
         )(in_hbm(weight_out), sent)
         (tiles,) = call(pair_body, "pair_tiles", [like((2 * pair, wide), bf16)])(
             kept(own), kept(got), kept(out_far)
         )
-        pieces = [tiles] + [across(tiles, shift) for shift in range(1, nn)]
-        in_own, in_far = call(
-            load_in_body,
-            "load_in",
-            [like((wide, half), bf16)] * 2,
+        pieces = [across(tiles, shift) for shift in reversed(range(1, nn))] + [tiles]
+        in_far, in_own, out_own = call(
+            load_body,
+            "load_rest",
+            [like((wide, half), bf16)] * 2 + [like((half, wide), bf16)],
             grant=MIB,
-            moved=2 * piece,
-            scratch=[sem((2,))],
-            specs=[hbm, pl.BlockSpec(memory_space=pl.ANY)],
-        )(in_hbm(weight_in), tiles)
-
-        out_own, sent, x_cols, dy_cols, sums = call(
+            moved=3 * piece,
+            scratch=[sem((3, 4))],
+            specs=[hbm] * 2 + [pl.BlockSpec(memory_space=pl.ANY)],
+        )(in_hbm(weight_in), in_hbm(weight_out), tiles)
+
+        sent, x_cols, dy_cols, sums = call(
             functools.partial(far_half_body, rows, nn),
             "far_half",
-            [like((half, wide), bf16), like((2 * count, half), bf16)]
+            [like((2 * count, half), bf16)]
             + [like((count, wide), bf16)] * 2
             + [like((1, wide), f32)],
             grant=8 * MIB,
             flops=work,
-            moved=piece,
-            scratch=[sem((1,))],
-            specs=[whole] * (nn + 2) + [hbm],
-        )(*[kept(piece) for piece in pieces], kept(in_far), kept(out_far), in_hbm(weight_out))
+            moved=2 * piece,
+        )(*[kept(piece) for piece in pieces], kept(in_far), kept(out_far))
         got = lax.ppermute(sent, "kin", swap)
         (own,) = call(
             own_half_body,
@@ -305,10 +341,10 @@
             moved=2 * piece,
         )(kept(both), kept(far), kept(terms), kept(in_far), kept(out_far))
 
-        weight_in_grad = dot(x_cols, grad, 0, 0).astype(bf16)
-        weight_out_grad = dot(act, dy_cols, 0, 0).astype(bf16)
-
-        terms = [blocks[0]] + [across(blocks[shift], shift) for shift in range(1, nn)]
+        weight_in_grad = outer(x_cols, grad, "weight_in_grad", 256)
+        weight_out_grad = outer(act, dy_cols, "weight_out_grad", 1536)
+
+        terms = [across(blocks[i], nn - 1 - i) for i in range(nn - 1)] + [blocks[-1]]
         own, sent = call(
             functools.partial(sum_body, rows), "sum_blocks", [like((pair, wide), bf16)] * 2
         )(bias_out.reshape(1, cols), *[kept(term) for term in terms])

time: 53.5 us -> 49.9 us (0.933)
  matrix products: 10.3 us -> 0 us
  Pallas kernels: 18.3 us -> 25.8 us
  waiting for transfers between devices: 7.28 us -> 6.66 us
    dot_general x2 -> x0, matrix products: 10.3 us -> none  [dot(): lax.dot_general(left, right, (((left_dim,), (right_dim,)), ((), ())), pre...]
    pallas_call x0 -> x2, Pallas kernels: none -> 8.39 us  [outer(): pl.pallas_call(functools.partial(outer_body, most), out_shape=like((high,...]
    pallas_call x11, Pallas kernels: 18.3 us -> 17.4 us  [run(): pl.pallas_call(body, out_shape=shapes, in_specs=specs or [whole] * len(ar...]
    ppermute x6, waiting for transfers between devices: 1.86 us -> 1.2 us  [across(): return lax.ppermute(array, 'nout', [(i, i ^ shift) for i in range(nn)])]
  transfers between devices with their start and end apart: 12 -> 12, of which waited for: 2 -> 2; matrix products, arithmetic and copies ran while one was open for 19% -> 0% of each run, Pallas kernels for 20% -> 41%
where the time goes in v8:
time: 49.9 us; the launch traced here: 49.6 us
  Pallas kernels  25.8 us (52%)
  starting transfers between devices  15.3 us (31%)
  waiting for transfers between devices  6.66 us (13%)
  other arithmetic  0.86 us (2%)
  between operations  0.85 us (2%)
    pallas_call x11, Pallas kernels, run(): pl.pallas_call(body, out_shape=shapes, in_specs=specs or [whole] * len(ar...  17.4 us
    ppermute x6, starting transfers between devices, across(): return lax.ppermute(array, 'nout', [(i, i ^ shift) for i in range(nn)])  8.69 us
    pallas_call x2, Pallas kernels, outer(): pl.pallas_call(functools.partial(outer_body, most), out_shape=like((high,...  8.39 us
    ppermute x1, waiting for transfers between devices, on_device(): got_sums = lax.ppermute(sums, 'tok', swap)  5.42 us
    ppermute x2, starting transfers between devices, on_device(): got = lax.ppermute(sent, 'tok', swap)  4.49 us
    ppermute x1, starting transfers between devices, on_device(): other = lax.ppermute(own, 'tok', swap)  1.49 us
    ppermute x6, waiting for transfers between devices, across(): return lax.ppermute(array, 'nout', [(i, i ^ shift) for i in range(nn)])  1.2 us
  transfers between devices with their start and end apart: 12, of which 2 were waited for; matrix products, arithmetic and copies ran while one was open for 0% of the time, Pallas kernels for 41%

profile of v8, /device:TPU:0, one launch (start us, length us, event | category | flops | bytes accessed | tf_op | source)
XLA Modules:
  0.0 49.6 jit_solution(4389114302174932536)
XLA Ops:
  0.6 0.9 %fusion = (bf16[8,1536]{1,0:T(8,128)(2,1)S(1)}, bf16[8,1536]{1,0:T(8,128)(2,1)S(1)}) fusion(s32[]{:T(128)S(6)} %select_n.7, bf16[4,3072]{1,0:T(4,128)(2,1)} %param.6, bf16[4,3072]{1,0:T(4,128)(2,1)} %param.11, s32[]{:T(128)S(6)} %select_n.6), kind=kLoop, calls=%fused_computation.4 | loop fusion | flops 98304 | bytes 98312 | tf_op jit(solution)/shard_map/concatenate | solution.py:273
  1.5 3.0 %collective-permute-start = (bf16[8,1536]{1,0:T(8,128)(2,1)S(1)}, bf16[8,1536]{1,0:T(8,128)(2,1)S(1)}, u32[]{:S(2)}, u32[]{:S(2)}) collective-permute-start(bf16[8,1536]{1,0:T(8,128)(2,1)S(1)} %get-tuple-element.44.after_ref), channel_id=1, source_target_pairs={{0,8},{8,0},{1,9},{9,1},{2,10},{10,2},{3,11},{11,3},{4,12},{12,4},... | collective-permute-start | bytes 73736 | tf_op jit(solution)/shard_map/ppermute | solution.py:277
  4.5 2.4 %load_far.1.after_ref.refs_5_.w_out_ref = bf16[1536,1536]{1,0:T(8,128)(2,1)S(1)} custom-call(bf16[3072,1536]{1,0:T(8,128)(2,1)} %out_hbm_ref.1, bf16[8,1536]{1,0:T(8,128)(2,1)S(1)} %get-tuple-element.44.after_ref), custom_call_target="tpu_custom_call" | custom-call | bytes 4718592 | tf_op jit(solution)/shard_map/load_far/pallas_call | solution.py:51
  6.9 0.0 collective-permute-done.got_ref
  6.9 3.7 %collective-permute-start.1 = (bf16[16,1536]{1,0:T(8,128)(2,1)S(1)}, bf16[16,1536]{1,0:T(8,128)(2,1)S(1)}, u32[]{:S(2)}, u32[]{:S(2)}) collective-permute-start(bf16[16,1536]{1,0:T(8,128)(2,1)S(1)} %pair_tiles.1.after_ref.refs_3_), channel_id=1, source_target_pairs={{0,3},{1,2},{2,1},{3,0},{4,7},{5,6},{6,5},{7,4},{8,11},{9,10},{10,... | collective-permute-start | bytes 147464 | tf_op jit(solution)/shard_map/ppermute | solution.py:261
  10.6 0.0 collective-permute-start.2
  10.6 0.8 %collective-permute-start.3 = (bf16[16,1536]{1,0:T(8,128)(2,1)S(1)}, bf16[16,1536]{1,0:T(8,128)(2,1)S(1)}, u32[]{:S(2)}, u32[]{:S(2)}) collective-permute-start(bf16[16,1536]{1,0:T(8,128)(2,1)S(1)} %pair_tiles.1.after_ref.refs_3_), channel_id=1, source_target_pairs={{0,1},{1,0},{2,3},{3,2},{4,5},{5,4},{6,7},{7,6},{8,9},{9,8},{10,11... | collective-permute-start | bytes 147464 | tf_op jit(solution)/shard_map/ppermute | solution.py:261
  11.4 5.2 %load_rest.1 = (bf16[1536,1536]{1,0:T(8,128)(2,1)S(1)}, bf16[1536,1536]{1,0:T(8,128)(2,1)S(1)}, bf16[1536,1536]{1,0:T(8,128)(2,1)S(1)}) custom-call(bf16[1536,3072]{1,0:T(8,128)(2,1)} %in_hbm_ref.1, bf16[3072,1536]{1,0:T(8,128)(2,1)} %out_hbm_ref.1, bf16[16,1536]{1,0:T(8,128)(2,1)S(1)} %pair_tiles.1.after_ref.refs_3_), custom_call_target="tpu_custom_call" | custom-call | bytes 14155776 | tf_op jit(solution)/shard_map/load_rest/pallas_call | solution.py:51
  16.5 0.0 collective-permute-done.1.refs_0_
  16.5 0.0 collective-permute-done.2.refs_1_
  16.6 0.0 collective-permute-done.3.refs_2_
  16.6 0.0 copy-start.1
  16.6 2.2 %far_half.1 = (bf16[64,1536]{1,0:T(8,128)(2,1)S(1)}, bf16[32,1536]{1,0:T(8,128)(2,1)S(1)}, bf16[32,1536]{1,0:T(8,128)(2,1)S(1)}, f32[1,1536]{1,0:T(1,128)S(1)}) custom-call(bf16[16,1536]{1,0:T(8,128)(2,1)S(1)} %collective-permute-done.1.refs_0_, bf16[16,1536]{1,0:T(8,128)(2,1)S(1)} %collective-permute-done.2.refs_1_, ...), custom_call_target="tpu_custom_call" | custom-call | flops 301989888 | bytes 9437184 | tf_op jit(solution)/shard_map/far_half/pallas_call | solution.py:51
  18.8 0.0 collective-permute-start.5
  18.8 2.2 %own_half.1.left_ref = bf16[64,1536]{1,0:T(8,128)(2,1)S(1)} custom-call(bf16[32,1536]{1,0:T(8,128)(2,1)S(1)} %get-tuple-element.27.x_ref.left_ref, bf16[32,1536]{1,0:T(8,128)(2,1)S(1)} %get-tuple-element.28.dy_ref.right_ref, bf16[1536,1536]{1,0:T(8,128)(2,1)S(1)} %get-tuple-element.29.w_in_ref, bf16[1536,1536]{1,0:T(8,128)(2,1)S(1)} %get-tuple-element.30.w_out_ref), custom_call_target="tpu_custom_call" | custom-call | flops 301989888 | bytes 9437184 | tf_op jit(solution)/shard_map/own_half/pallas_call | solution.py:51
  21.1 0.0 collective-permute-done.5.right_ref
  21.1 0.1 add_cores.1.own_ref
  21.2 1.5 %collective-permute-start.6 = (bf16[64,1536]{1,0:T(8,128)(2,1)S(1)}, bf16[64,1536]{1,0:T(8,128)(2,1)S(1)}, u32[]{:S(2)}, u32[]{:S(2)}) collective-permute-start(bf16[64,1536]{1,0:T(8,128)(2,1)S(1)} %add_cores.1.own_ref), channel_id=1, source_target_pairs={{0,8},{8,0},{1,9},{9,1},{2,10},{10,2},{3,11},{11,3},{4,12},{12,4},... | collective-permute-start | bytes 589832 | tf_op jit(solution)/shard_map/ppermute | solution.py:321
  22.7 0.6 %collective-permute-start.4 = (f32[1,1536]{1,0:T(1,128)S(1)}, f32[1,1536]{1,0:T(1,128)S(1)}, u32[]{:S(2)}, u32[]{:S(2)}) collective-permute-start(f32[1,1536]{1,0:T(1,128)S(1)} %get-tuple-element.26.own_sums_ref), channel_id=1, source_target_pairs={{0,8},{8,0},{1,9},{9,1},{2,10},{10,2},{3,11},{11,3},{4,12},{12,4},... | collective-permute-start | bytes 18440 | tf_op jit(solution)/shard_map/ppermute | solution.py:322
  23.3 5.4 %collective-permute-done.4.after_ref.got_sums_ref = f32[1,1536]{1,0:T(1,128)S(1)} collective-permute-done((f32[1,1536]{1,0:T(1,128)S(1)}, f32[1,1536]{1,0:T(1,128)S(1)}, u32[]{:S(2)}, u32[]{:S(2)}) %collective-permute-start.4) | collective-permute-done | bytes 6176 | tf_op jit(solution)/shard_map/ppermute | solution.py:322
  28.7 0.0 collective-permute-done.6.other_ref
  28.7 0.0 copy-done.1
  28.7 0.1 gelu.1.both_ref.own_ref
  28.8 0.1 collective-permute-start.7
  28.9 2.2 %own_terms.1.terms_ref = f32[64,1536]{1,0:T(8,128)S(1)} custom-call(bf16[64,1536]{1,0:T(8,128)(2,1)S(1)} %gelu.1.both_ref.own_ref, bf16[1536,1536]{1,0:T(8,128)(2,1)S(1)} %get-tuple-element.29.w_in_ref, bf16[1536,1536]{1,0:T(8,128)(2,1)S(1)} %get-tuple-element.30.w_out_ref), custom_call_target="tpu_custom_call" | custom-call | flops 301989888 | bytes 9437184 | tf_op jit(solution)/shard_map/own_terms/pallas_call | solution.py:51
  31.2 0.0 copy-start
  31.2 0.0 collective-permute-done.7.far_ref
  31.2 2.3 %output_blocks.1 = (bf16[32,3072]{1,0:T(8,128)(2,1)S(1)}, bf16[32,3072]{1,0:T(8,128)(2,1)S(1)}, bf16[16,1536]{1,0:T(8,128)(2,1)S(1)}, bf16[16,1536]{1,0:T(8,128)...) custom-call(bf16[64,1536]{1,0:T(8,128)(2,1)S(1)} %gelu.1.both_ref.own_ref, ...), custom_call_target="tpu_custom_call" | custom-call | flops 301989888 | bytes 9437184 | tf_op jit(solution)/shard_map/output_blocks/pallas_call | solution.py:51
  33.5 1.3 %collective-permute-start.10 = (bf16[16,1536]{1,0:T(8,128)(2,1)S(1)}, bf16[16,1536]{1,0:T(8,128)(2,1)S(1)}, u32[]{:S(2)}, u32[]{:S(2)}) collective-permute-start(bf16[16,1536]{1,0:T(8,128)(2,1)S(1)} %get-tuple-element.34), channel_id=1, source_target_pairs={{0,1},{1,0},{2,3},{3,2},{4,5},{5,4},{6,7},{7,6},{8,9},{9,8},{10,11... | collective-permute-start | bytes 147464 | tf_op jit(solution)/shard_map/ppermute | solution.py:261
  34.8 2.4 %collective-permute-start.8 = (bf16[16,1536]{1,0:T(8,128)(2,1)S(1)}, bf16[16,1536]{1,0:T(8,128)(2,1)S(1)}, u32[]{:S(2)}, u32[]{:S(2)}) collective-permute-start(bf16[16,1536]{1,0:T(8,128)(2,1)S(1)} %get-tuple-element.32), channel_id=1, source_target_pairs={{0,3},{1,2},{2,1},{3,0},{4,7},{5,6},{6,5},{7,4},{8,11},{9,10},{10,... | collective-permute-start | bytes 147464 | tf_op jit(solution)/shard_map/ppermute | solution.py:261
  37.2 0.5 collective-permute-start.9
  37.7 4.1 %weight_out_grad.1 = bf16[3072,1536]{1,0:T(8,128)(2,1)} custom-call(bf16[32,3072]{1,0:T(8,128)(2,1)S(1)} %get-tuple-element.41.left_ref, bf16[32,1536]{1,0:T(8,128)(2,1)S(1)} %get-tuple-element.28.dy_ref.right_ref), custom_call_target="tpu_custom_call" | custom-call | flops 301989888 | bytes 9437184 | tf_op jit(solution)/shard_map/weight_out_grad/pallas_call | solution.py:213
  41.8 0.0 collective-permute-done.10.refs_2_
  41.8 0.0 collective-permute-done.8.refs_0_
  41.9 1.2 %collective-permute-done.9.refs_1_ = bf16[16,1536]{1,0:T(8,128)(2,1)S(1)} collective-permute-done((bf16[16,1536]{1,0:T(8,128)(2,1)S(1)}, bf16[16,1536]{1,0:T(8,128)(2,1)S(1)}, u32[]{:S(2)}, u32[]{:S(2)}) %collective-permute-start.9) | collective-permute-done | bytes 49184 | tf_op jit(solution)/shard_map/ppermute | solution.py:261
  43.0 0.0 copy-done
  43.1 1.5 %collective-permute-start.11 = (bf16[8,1536]{1,0:T(8,128)(2,1)S(1)}, bf16[8,1536]{1,0:T(8,128)(2,1)S(1)}, u32[]{:S(2)}, u32[]{:S(2)}) collective-permute-start(bf16[8,1536]{1,0:T(8,128)(2,1)S(1)} %get-tuple-element.37), channel_id=1, source_target_pairs={{0,8},{8,0},{1,9},{9,1},{2,10},{10,2},{3,11},{11,3},{4,12},{12,4},... | collective-permute-start | bytes 73736 | tf_op jit(solution)/shard_map/ppermute | solution.py:351
  44.6 4.3 %weight_in_grad.1 = bf16[1536,3072]{1,0:T(8,128)(2,1)} custom-call(bf16[32,1536]{1,0:T(8,128)(2,1)S(1)} %get-tuple-element.27.x_ref.left_ref, bf16[32,3072]{1,0:T(8,128)(2,1)S(1)} %get-tuple-element.38.hidden_ref.right_ref), custom_call_target="tpu_custom_call" | custom-call | flops 301989888 | bytes 9437184 | tf_op jit(solution)/shard_map/weight_in_grad/pallas_call | solution.py:213
  48.9 0.0 collective-permute-done.11.got_ref
  48.9 0.7 %final_rows.1 = (bf16[4,3072]{1,0:T(4,128)(2,1)}, bf16[4,3072]{1,0:T(4,128)(2,1)}, f32[1,3072]{1,0:T(1,128)}, f32[1,3072]{1,0:T(1,128)}) custom-call(bf16[8,1536]{1,0:T(8,128)(2,1)S(1)} %get-tuple-element.36.own_ref, bf16[8,1536]{1,0:T(8,128)(2,1)S(1)} %collective-permute-done.11.got_ref, f32[1,1536]{1,0:T(1,128)S(1)} %get-tuple-element.26.own_sums_ref, ...), custom_call_target="tpu_custom_call" | custom-call | tf_op jit(solution)/shard_map/final_rows/pallas_call | solution.py:51
  (2 shorter events, 0.1 us)
Async XLA Ops:
  1.5 5.4 %collective-permute-start = (bf16[8,1536]{1,0:T(8,128)(2,1)S(1)}, bf16[8,1536]{1,0:T(8,128)(2,1)S(1)}, u32[]{:S(2)}, u32[]{:S(2)}) collective-permute-start(bf16[8,1536]{1,0:T(8,128)(2,1)S(1)} %get-tuple-element.44.after_ref), channel_id=1, source_target_pairs={{0,8},{8,0},{1,9},{9,1},{2,10},{10,2},{3,11},{11,3},{4,12},{12,4},... | collective-permute-start | bytes 73736 | tf_op jit(solution)/shard_map/ppermute | solution.py:277
  6.9 9.6 %collective-permute-start.1 = (bf16[16,1536]{1,0:T(8,128)(2,1)S(1)}, bf16[16,1536]{1,0:T(8,128)(2,1)S(1)}, u32[]{:S(2)}, u32[]{:S(2)}) collective-permute-start(bf16[16,1536]{1,0:T(8,128)(2,1)S(1)} %pair_tiles.1.after_ref.refs_3_), channel_id=1, source_target_pairs={{0,3},{1,2},{2,1},{3,0},{4,7},{5,6},{6,5},{7,4},{8,11},{9,10},{10,... | collective-permute-start | bytes 147464 | tf_op jit(solution)/shard_map/ppermute | solution.py:261
  10.6 6.0 %collective-permute-start.2 = (bf16[16,1536]{1,0:T(8,128)(2,1)S(1)}, bf16[16,1536]{1,0:T(8,128)(2,1)S(1)}, u32[]{:S(2)}, u32[]{:S(2)}) collective-permute-start(bf16[16,1536]{1,0:T(8,128)(2,1)S(1)} %pair_tiles.1.after_ref.refs_3_), channel_id=1, source_target_pairs={{0,2},{1,3},{2,0},{3,1},{4,6},{5,7},{6,4},{7,5},{8,10},{9,11},{10,... | collective-permute-start | bytes 147464 | tf_op jit(solution)/shard_map/ppermute | solution.py:261
  10.6 6.0 %collective-permute-start.3 = (bf16[16,1536]{1,0:T(8,128)(2,1)S(1)}, bf16[16,1536]{1,0:T(8,128)(2,1)S(1)}, u32[]{:S(2)}, u32[]{:S(2)}) collective-permute-start(bf16[16,1536]{1,0:T(8,128)(2,1)S(1)} %pair_tiles.1.after_ref.refs_3_), channel_id=1, source_target_pairs={{0,1},{1,0},{2,3},{3,2},{4,5},{5,4},{6,7},{7,6},{8,9},{9,8},{10,11... | collective-permute-start | bytes 147464 | tf_op jit(solution)/shard_map/ppermute | solution.py:261
  16.6 12.1 %copy-start.1 = (f32[3072]{0:T(1024)S(1)}, f32[3072]{0:T(1024)}, u32[]{:S(2)}) copy-start(f32[3072]{0:T(1024)} %param.8) | copy-start | bytes 36868
  18.8 2.3 %collective-permute-start.5 = (bf16[64,1536]{1,0:T(8,128)(2,1)S(1)}, bf16[64,1536]{1,0:T(8,128)(2,1)S(1)}, u32[]{:S(2)}, u32[]{:S(2)}) collective-permute-start(bf16[64,1536]{1,0:T(8,128)(2,1)S(1)} %get-tuple-element.31), channel_id=1, source_target_pairs={{0,4},{4,0},{1,5},{5,1},{2,6},{6,2},{3,7},{7,3},{8,12},{12,8},{9,1... | collective-permute-start | bytes 589832 | tf_op jit(solution)/shard_map/ppermute | solution.py:311
  21.2 7.5 %collective-permute-start.6 = (bf16[64,1536]{1,0:T(8,128)(2,1)S(1)}, bf16[64,1536]{1,0:T(8,128)(2,1)S(1)}, u32[]{:S(2)}, u32[]{:S(2)}) collective-permute-start(bf16[64,1536]{1,0:T(8,128)(2,1)S(1)} %add_cores.1.own_ref), channel_id=1, source_target_pairs={{0,8},{8,0},{1,9},{9,1},{2,10},{10,2},{3,11},{11,3},{4,12},{12,4},... | collective-permute-start | bytes 589832 | tf_op jit(solution)/shard_map/ppermute | solution.py:321
  22.7 6.0 %collective-permute-start.4 = (f32[1,1536]{1,0:T(1,128)S(1)}, f32[1,1536]{1,0:T(1,128)S(1)}, u32[]{:S(2)}, u32[]{:S(2)}) collective-permute-start(f32[1,1536]{1,0:T(1,128)S(1)} %get-tuple-element.26.own_sums_ref), channel_id=1, source_target_pairs={{0,8},{8,0},{1,9},{9,1},{2,10},{10,2},{3,11},{11,3},{4,12},{12,4},... | collective-permute-start | bytes 18440 | tf_op jit(solution)/shard_map/ppermute | solution.py:322
  28.8 2.3 %collective-permute-start.7 = (bf16[64,1536]{1,0:T(8,128)(2,1)S(1)}, bf16[64,1536]{1,0:T(8,128)(2,1)S(1)}, u32[]{:S(2)}, u32[]{:S(2)}) collective-permute-start(bf16[64,1536]{1,0:T(8,128)(2,1)S(1)} %gelu.1.both_ref.own_ref), channel_id=1, source_target_pairs={{0,4},{4,0},{1,5},{5,1},{2,6},{6,2},{3,7},{7,3},{8,12},{12,8},{9,1... | collective-permute-start | bytes 589832 | tf_op jit(solution)/shard_map/ppermute | solution.py:326
  31.2 11.9 %copy-start = (f32[3072]{0:T(1024)S(1)}, f32[3072]{0:T(1024)}, u32[]{:S(2)}) copy-start(f32[3072]{0:T(1024)} %param.10) | copy-start | bytes 36868
  33.5 8.4 %collective-permute-start.10 = (bf16[16,1536]{1,0:T(8,128)(2,1)S(1)}, bf16[16,1536]{1,0:T(8,128)(2,1)S(1)}, u32[]{:S(2)}, u32[]{:S(2)}) collective-permute-start(bf16[16,1536]{1,0:T(8,128)(2,1)S(1)} %get-tuple-element.34), channel_id=1, source_target_pairs={{0,1},{1,0},{2,3},{3,2},{4,5},{5,4},{6,7},{7,6},{8,9},{9,8},{10,11... | collective-permute-start | bytes 147464 | tf_op jit(solution)/shard_map/ppermute | solution.py:261
  34.8 7.0 %collective-permute-start.8 = (bf16[16,1536]{1,0:T(8,128)(2,1)S(1)}, bf16[16,1536]{1,0:T(8,128)(2,1)S(1)}, u32[]{:S(2)}, u32[]{:S(2)}) collective-permute-start(bf16[16,1536]{1,0:T(8,128)(2,1)S(1)} %get-tuple-element.32), channel_id=1, source_target_pairs={{0,3},{1,2},{2,1},{3,0},{4,7},{5,6},{6,5},{7,4},{8,11},{9,10},{10,... | collective-permute-start | bytes 147464 | tf_op jit(solution)/shard_map/ppermute | solution.py:261
  37.2 5.8 %collective-permute-start.9 = (bf16[16,1536]{1,0:T(8,128)(2,1)S(1)}, bf16[16,1536]{1,0:T(8,128)(2,1)S(1)}, u32[]{:S(2)}, u32[]{:S(2)}) collective-permute-start(bf16[16,1536]{1,0:T(8,128)(2,1)S(1)} %get-tuple-element.33), channel_id=1, source_target_pairs={{0,2},{1,3},{2,0},{3,1},{4,6},{5,7},{6,4},{7,5},{8,10},{9,11},{10,... | collective-permute-start | bytes 147464 | tf_op jit(solution)/shard_map/ppermute | solution.py:261
  43.1 5.8 %collective-permute-start.11 = (bf16[8,1536]{1,0:T(8,128)(2,1)S(1)}, bf16[8,1536]{1,0:T(8,128)(2,1)S(1)}, u32[]{:S(2)}, u32[]{:S(2)}) collective-permute-start(bf16[8,1536]{1,0:T(8,128)(2,1)S(1)} %get-tuple-element.37), channel_id=1, source_target_pairs={{0,8},{8,0},{1,9},{9,1},{2,10},{10,2},{3,11},{11,3},{4,12},{12,4},... | collective-permute-start | bytes 73736 | tf_op jit(solution)/shard_map/ppermute | solution.py:351

commit v9 on v8

--- a/solution.py
+++ b/solution.py
@@ -132,63 +132,81 @@
     out_ref[...] = ordered(lax.axis_index("tok"), own_ref[...], got_ref[...])
 
 
-def partial_sums(x_cols, dy_cols, w_in_ref, w_out_ref, out_ref):
-    count = x_cols.shape[0]
-    for at in tiles_of(out_ref.shape[1]):
-        out_ref[:count, at] = dot(x_cols, w_in_ref[:, at], 1, 0).astype(bf16)
-        out_ref[count:, at] = dot(dy_cols, w_out_ref[at, :], 1, 1).astype(bf16)
-
-
-def far_half_body(rows, count, *refs):
-    *piece_refs, w_in_ref, w_out_ref = refs[: count + 2]
-    sent_ref, x_ref, dy_ref, sums_ref = refs[count + 2 :]
+def far_pre_body(rows, count, *refs):
+    *piece_refs, w_in_ref = refs[: count + 1]
+    sent_ref, x_ref, dy_ref, sums_ref = refs[count + 1 :]
     mixed = jnp.concatenate([ref[...] for ref in piece_refs], axis=0)
     x_cols, dy_cols = apart(mixed.astype(f32), rows)
     sums_ref[...] = jnp.sum(dy_cols, axis=0, keepdims=True)
     x_cols, dy_cols = x_cols.astype(bf16), dy_cols.astype(bf16)
     x_ref[...], dy_ref[...] = x_cols, dy_cols
-    partial_sums(x_cols, dy_cols, w_in_ref, w_out_ref, sent_ref)
-
-
-def own_half_body(x_ref, dy_ref, w_in_ref, w_out_ref, own_ref):
-    partial_sums(x_ref[...], dy_ref[...], w_in_ref, w_out_ref, own_ref)
-
-
-def add_body(left_ref, right_ref, out_ref):
-    out_ref[...] = (left_ref[...].astype(f32) + right_ref[...].astype(f32)).astype(bf16)
-
-
-def gelu_body(bias_ref, after_ref, own_ref, other_ref, out_ref):
-    count, half = out_ref.shape[0] // 2, out_ref.shape[1]
+    for at in tiles_of(sent_ref.shape[1]):
+        sent_ref[:, at] = dot(x_cols, w_in_ref[:, at], 1, 0).astype(bf16)
+
+
+def far_grad_body(dy_ref, w_out_ref, sent_ref):
+    dy_cols = dy_ref[...]
+    for at in tiles_of(sent_ref.shape[1]):
+        sent_ref[:, at] = dot(dy_cols, w_out_ref[at, :], 1, 1).astype(bf16)
+
+
+def own_pre_body(x_ref, w_in_ref, got_ref, after_ref, own_ref):
+    x_cols = x_ref[...]
+    for at in tiles_of(own_ref.shape[1]):
+        own = dot(x_cols, w_in_ref[:, at], 1, 0) + got_ref[:, at].astype(f32)
+        own_ref[:, at] = own.astype(bf16)
+
+
+def own_grad_body(dy_ref, w_out_ref, got_ref, after_ref, own_ref):
+    dy_cols = dy_ref[...]
+    for at in tiles_of(own_ref.shape[1]):
+        own = dot(dy_cols, w_out_ref[at, :], 1, 1) + got_ref[:, at].astype(f32)
+        own_ref[:, at] = own.astype(bf16)
+
+
+def gelu_body(bias_ref, own_ref, other_ref, after_ref, act_ref, slopes_ref):
+    half = act_ref.shape[1]
     bias = bias_ref[:, half_of(half, True)]
     tile = tile_of(half, 512)
     for i in range(half // tile):
         at = pl.ds(i * tile, tile)
-        summed = own_ref[:, at].astype(f32) + other_ref[:, at].astype(f32)
-        activated, slopes = gelu_parts(summed[:count] + bias[:, i * tile : (i + 1) * tile])
-        out_ref[:count, at] = activated.astype(bf16)
-        out_ref[count:, at] = (summed[count:] * slopes).astype(bf16)
-
-
-def own_terms_body(both_ref, w_in_ref, w_out_ref, out_ref):
-    count = both_ref.shape[0] // 2
-    act, grad = both_ref[:count], both_ref[count:]
+        pre_act = own_ref[:, at].astype(f32) + other_ref[:, at].astype(f32)
+        activated, slopes = gelu_parts(pre_act + bias[:, i * tile : (i + 1) * tile])
+        act_ref[:, at] = activated.astype(bf16)
+        slopes_ref[:, at] = slopes
+
+
+def grad_pre_body(slopes_ref, own_ref, other_ref, after_ref, sums_ref, grad_ref):
+    grad_act = own_ref[...].astype(f32) + other_ref[...].astype(f32)
+    grad_ref[...] = (grad_act * slopes_ref[...]).astype(bf16)
+
+
+def own_forward_body(act_ref, w_out_ref, out_ref):
+    act = act_ref[...]
     for at in tiles_of(out_ref.shape[1]):
-        out_ref[:count, at] = dot(act, w_out_ref[:, at], 1, 0)
-        out_ref[count:, at] = dot(grad, w_in_ref[at, :], 1, 1)
-
-
-def blocks_body(rows, own_ref, far_ref, terms_ref, w_in_ref, w_out_ref, act_ref, grad_ref, *out_refs):
-    count = far_ref.shape[0] // 2
-    core = lax.axis_index("kin")
-    act, grad = far_ref[:count], far_ref[count:]
-    act_ref[...] = ordered(core, own_ref[:count], act, 1)
-    grad_ref[...] = ordered(core, own_ref[count:], grad, 1)
+        out_ref[:, at] = dot(act, w_out_ref[:, at], 1, 0)
+
+
+def far_forward_body(own_ref, far_ref, w_out_ref, terms_ref, act_ref, out_ref):
+    act = far_ref[...]
+    act_ref[...] = ordered(lax.axis_index("kin"), own_ref[...], act, 1)
+    for at in tiles_of(out_ref.shape[1]):
+        out_ref[:, at] = terms_ref[:, at] + dot(act, w_out_ref[:, at], 1, 0)
+
+
+def own_backward_body(grad_ref, w_in_ref, out_ref):
+    grad = grad_ref[...]
+    for at in tiles_of(out_ref.shape[1]):
+        out_ref[:, at] = dot(grad, w_in_ref[at, :], 1, 1)
+
+
+def blocks_body(rows, own_ref, far_ref, forward_ref, backward_ref, w_in_ref, grad_ref, *out_refs):
+    grad = far_ref[...]
+    grad_ref[...] = ordered(lax.axis_index("kin"), own_ref[...], grad, 1)
     size = out_refs[0].shape[0]
-    for at in tiles_of(terms_ref.shape[1]):
-        forward = terms_ref[:count, at] + dot(act, w_out_ref[:, at], 1, 0)
-        backward = terms_ref[count:, at] + dot(grad, w_in_ref[at, :], 1, 1)
-        terms = together(forward, backward, rows).astype(bf16)
+    for at in tiles_of(forward_ref.shape[1]):
+        backward = backward_ref[:, at] + dot(grad, w_in_ref[at, :], 1, 1)
+        terms = together(forward_ref[:, at], backward, rows).astype(bf16)
         for i, out_ref in enumerate(out_refs):
             out_ref[:, at] = terms[i * size : (i + 1) * size]
 
@@ -266,7 +284,6 @@
         half = hid // 2
         pair = 2 * rows
         count = 2 * nn * rows
-        work = 4 * count * wide * half
         piece = 2 * wide * half
         sem = pltpu.SemaphoreType.DMA
 
@@ -298,48 +315,56 @@
             specs=[hbm] * 2 + [pl.BlockSpec(memory_space=pl.ANY)],
         )(in_hbm(weight_in), in_hbm(weight_out), tiles)
 
-        sent, x_cols, dy_cols, sums = call(
-            functools.partial(far_half_body, rows, nn),
-            "far_half",
-            [like((2 * count, half), bf16)]
-            + [like((count, wide), bf16)] * 2
-            + [like((1, wide), f32)],
-            grant=8 * MIB,
-            flops=work,
-            moved=2 * piece,
-        )(*[kept(piece) for piece in pieces], kept(in_far), kept(out_far))
-        got = lax.ppermute(sent, "kin", swap)
-        (own,) = call(
-            own_half_body,
-            "own_half",
-            [like((2 * count, half), bf16)],
-            grant=8 * MIB,
-            flops=work,
-            moved=2 * piece,
-        )(kept(x_cols), kept(dy_cols), kept(in_own), kept(out_own))
-        (own,) = call(add_body, "add_cores", [like((2 * count, half), bf16)])(kept(own), kept(got))
-        other = lax.ppermute(own, "tok", swap)
+        def product(body, name, outs, *args):
+            return call(body, name, outs, grant=8 * MIB)(*map(kept, args))
+
+        side, ends = like((count, half), bf16), like((count, wide), f32)
+        sent, x_cols, dy_cols, sums = product(
+            functools.partial(far_pre_body, rows, nn),
+            "far_pre",
+            [side] + [like((count, wide), bf16)] * 2 + [like((1, wide), f32)],
+            *pieces,
+            in_far,
+        )
+        got_pre = lax.ppermute(sent, "kin", swap)
+        (sent,) = product(far_grad_body, "far_grad", [side], dy_cols, out_far)
+        got_grad = lax.ppermute(sent, "kin", swap)
+        (own_pre,) = product(own_pre_body, "own_pre", [side], x_cols, in_own, got_pre, sent)
+        other_pre = lax.ppermute(own_pre, "tok", swap)
+        (own_grad,) = product(
+            own_grad_body, "own_grad", [side], dy_cols, out_own, got_grad, own_pre
+        )
+        other_grad = lax.ppermute(own_grad, "tok", swap)
         got_sums = lax.ppermute(sums, "tok", swap)
-        (both,) = call(gelu_body, "gelu", [like((2 * count, half), bf16)])(
-            bias_in.reshape(1, hid), got_sums, kept(own), kept(other)
-        )
-        far = lax.ppermute(both, "kin", swap)
-        (terms,) = call(
-            own_terms_body,
-            "own_terms",
-            [like((2 * count, wide), f32)],
-            grant=8 * MIB,
-            flops=work,
-            moved=2 * piece,
-        )(kept(both), kept(in_own), kept(out_own))
-        act, grad, *blocks = call(
+        act_own, slopes = call(gelu_body, "gelu", [side, like((count, half), f32)])(
+            bias_in.reshape(1, hid), kept(own_pre), kept(other_pre), kept(own_grad)
+        )
+        act_far = lax.ppermute(act_own, "kin", swap)
+        (forward,) = product(own_forward_body, "own_forward", [ends], act_own, out_own)
+        (grad_own,) = call(grad_pre_body, "grad_pre", [side])(
+            kept(slopes), kept(own_grad), kept(other_grad), kept(forward), kept(got_sums)
+        )
+        act, forward = product(
+            far_forward_body,
+            "far_forward",
+            [like((count, hid), bf16), ends],
+            act_own,
+            act_far,
+            out_far,
+            forward,
+        )
+        grad_far = lax.ppermute(grad_own, "kin", swap)
+        (backward,) = product(own_backward_body, "own_backward", [ends], grad_own, in_own)
+        grad, *blocks = product(
             functools.partial(blocks_body, rows),
             "output_blocks",
-            [like((count, hid), bf16)] * 2 + [like((2 * pair, wide), bf16)] * nn,
-            grant=8 * MIB,
-            flops=work,
-            moved=2 * piece,
-        )(kept(both), kept(far), kept(terms), kept(in_far), kept(out_far))
+            [like((count, hid), bf16)] + [like((2 * pair, wide), bf16)] * nn,
+            grad_own,
+            grad_far,
+            forward,
+            backward,
+            in_far,
+        )
 
         weight_in_grad = outer(x_cols, grad, "weight_in_grad", 256)
         weight_out_grad = outer(act, dy_cols, "weight_out_grad", 1536)

time: 49.9 us -> 47.1 us (0.944)
  waiting for transfers between devices: 6.66 us -> 1.75 us
  starting transfers between devices: 15.3 us -> 17.1 us
    ppermute x1, waiting for transfers between devices: 5.42 us -> 1.63 us  [on_device(): got_sums = lax.ppermute(sums, 'tok', swap)]
    ppermute x3 -> x6, starting transfers between devices: 1.57 us -> 2.72 us  [the longest x1 1.45 us: on_device(): other_pre = lax.ppermute(own_pre, 'tok', swap)]
    ppermute x6, waiting for transfers between devices: 1.2 us -> 0.07 us  [across(): return lax.ppermute(array, 'nout', [(i, i ^ shift) for i in range(nn)])]
    ppermute x1, starting transfers between devices: 0.6 us -> 1.43 us  [on_device(): got_sums = lax.ppermute(sums, 'tok', swap)]
    pallas_call x11 -> x15, Pallas kernels: 17.4 us -> 17.8 us  [run(): pl.pallas_call(body, out_shape=shapes, in_specs=specs or [whole] * len(ar...]
  transfers between devices with their start and end apart: 12 -> 15, of which waited for: 2 -> 2; matrix products, arithmetic and copies ran while one was open for 0% -> 0% of each run, Pallas kernels for 41% -> 49%
where the time goes in v9:
time: 47.1 us; the launch traced here: 46.8 us
  Pallas kernels  26.2 us (56%)
  starting transfers between devices  17.1 us (36%)
  waiting for transfers between devices  1.75 us (4%)
  other arithmetic  0.86 us (2%)
  between operations  0.83 us (2%)
    pallas_call x15, Pallas kernels, run(): pl.pallas_call(body, out_shape=shapes, in_specs=specs or [whole] * len(ar...  17.8 us
    ppermute x6, starting transfers between devices, across(): return lax.ppermute(array, 'nout', [(i, i ^ shift) for i in range(nn)])  8.91 us
    pallas_call x2, Pallas kernels, outer(): pl.pallas_call(functools.partial(outer_body, most), out_shape=like((high,...  8.38 us
    ppermute x2, starting transfers between devices, on_device(): got = lax.ppermute(sent, 'tok', swap)  4.04 us
    ppermute x1, waiting for transfers between devices, on_device(): got_sums = lax.ppermute(sums, 'tok', swap)  1.63 us
    ppermute x1, starting transfers between devices, on_device(): other_pre = lax.ppermute(own_pre, 'tok', swap)  1.45 us
    ppermute x1, starting transfers between devices, on_device(): got_sums = lax.ppermute(sums, 'tok', swap)  1.43 us
  transfers between devices with their start and end apart: 15, of which 2 were waited for; matrix products, arithmetic and copies ran while one was open for 0% of the time, Pallas kernels for 49%

profile of v9, /device:TPU:0, one launch (start us, length us, event | category | flops | bytes accessed | tf_op | source)
XLA Modules:
  0.0 46.8 jit_solution(10499882333673205954)
XLA Ops:
  0.6 0.9 %fusion = (bf16[8,1536]{1,0:T(8,128)(2,1)S(1)}, bf16[8,1536]{1,0:T(8,128)(2,1)S(1)}) fusion(s32[]{:T(128)S(6)} %select_n.7, bf16[4,3072]{1,0:T(4,128)(2,1)} %param.6, bf16[4,3072]{1,0:T(4,128)(2,1)} %param.11, s32[]{:T(128)S(6)} %select_n.6), kind=kLoop, calls=%fused_computation.4 | loop fusion | flops 98304 | bytes 98312 | tf_op jit(solution)/shard_map/concatenate | solution.py:290
  1.5 3.0 %collective-permute-start = (bf16[8,1536]{1,0:T(8,128)(2,1)S(1)}, bf16[8,1536]{1,0:T(8,128)(2,1)S(1)}, u32[]{:S(2)}, u32[]{:S(2)}) collective-permute-start(bf16[8,1536]{1,0:T(8,128)(2,1)S(1)} %get-tuple-element.50.after_ref), channel_id=1, source_target_pairs={{0,8},{8,0},{1,9},{9,1},{2,10},{10,2},{3,11},{11,3},{4,12},{12,4},... | collective-permute-start | bytes 73736 | tf_op jit(solution)/shard_map/ppermute | solution.py:294
  4.5 2.4 %load_far.1.after_ref.w_out_ref = bf16[1536,1536]{1,0:T(8,128)(2,1)S(1)} custom-call(bf16[3072,1536]{1,0:T(8,128)(2,1)} %out_hbm_ref.1, bf16[8,1536]{1,0:T(8,128)(2,1)S(1)} %get-tuple-element.50.after_ref), custom_call_target="tpu_custom_call" | custom-call | bytes 4718592 | tf_op jit(solution)/shard_map/load_far/pallas_call | solution.py:51
  6.9 0.0 collective-permute-done.got_ref
  6.9 3.7 %collective-permute-start.1 = (bf16[16,1536]{1,0:T(8,128)(2,1)S(1)}, bf16[16,1536]{1,0:T(8,128)(2,1)S(1)}, u32[]{:S(2)}, u32[]{:S(2)}) collective-permute-start(bf16[16,1536]{1,0:T(8,128)(2,1)S(1)} %pair_tiles.1.after_ref.refs_3_), channel_id=1, source_target_pairs={{0,3},{1,2},{2,1},{3,0},{4,7},{5,6},{6,5},{7,4},{8,11},{9,10},{10,... | collective-permute-start | bytes 147464 | tf_op jit(solution)/shard_map/ppermute | solution.py:279
  10.6 0.0 collective-permute-start.2
  10.6 0.8 %collective-permute-start.3 = (bf16[16,1536]{1,0:T(8,128)(2,1)S(1)}, bf16[16,1536]{1,0:T(8,128)(2,1)S(1)}, u32[]{:S(2)}, u32[]{:S(2)}) collective-permute-start(bf16[16,1536]{1,0:T(8,128)(2,1)S(1)} %pair_tiles.1.after_ref.refs_3_), channel_id=1, source_target_pairs={{0,1},{1,0},{2,3},{3,2},{4,5},{5,4},{6,7},{7,6},{8,9},{9,8},{10,11... | collective-permute-start | bytes 147464 | tf_op jit(solution)/shard_map/ppermute | solution.py:279
  11.4 5.2 %load_rest.1 = (bf16[1536,1536]{1,0:T(8,128)(2,1)S(1)}, bf16[1536,1536]{1,0:T(8,128)(2,1)S(1)}, bf16[1536,1536]{1,0:T(8,128)(2,1)S(1)}) custom-call(bf16[1536,3072]{1,0:T(8,128)(2,1)} %in_hbm_ref.1, bf16[3072,1536]{1,0:T(8,128)(2,1)} %out_hbm_ref.1, bf16[16,1536]{1,0:T(8,128)(2,1)S(1)} %pair_tiles.1.after_ref.refs_3_), custom_call_target="tpu_custom_call" | custom-call | bytes 14155776 | tf_op jit(solution)/shard_map/load_rest/pallas_call | solution.py:51
  16.5 0.0 collective-permute-done.1.refs_0_
  16.5 0.0 collective-permute-done.2.refs_1_
  16.6 0.0 collective-permute-done.3.refs_2_
  16.6 0.0 copy-start
  16.6 0.9 %far_pre.1 = (bf16[32,1536]{1,0:T(8,128)(2,1)S(1)}, bf16[32,1536]{1,0:T(8,128)(2,1)S(1)}, bf16[32,1536]{1,0:T(8,128)(2,1)S(1)}, f32[1,1536]{1,0:T(1,128)S(1)}) custom-call(bf16[16,1536]{1,0:T(8,128)(2,1)S(1)} %collective-permute-done.1.refs_0_, bf16[16,1536]{1,0:T(8,128)(2,1)S(1)} %collective-permute-done.2.refs_1_, ...), custom_call_target="tpu_custom_call" | custom-call | tf_op jit(solution)/shard_map/far_pre/pallas_call | solution.py:51
  17.5 0.0 collective-permute-start.4
  17.5 1.5 %far_grad.1.after_ref = bf16[32,1536]{1,0:T(8,128)(2,1)S(1)} custom-call(bf16[32,1536]{1,0:T(8,128)(2,1)S(1)} %get-tuple-element.32.dy_ref.right_ref, bf16[1536,1536]{1,0:T(8,128)(2,1)S(1)} %load_far.1.after_ref.w_out_ref), custom_call_target="tpu_custom_call" | custom-call | tf_op jit(solution)/shard_map/far_grad/pallas_call | solution.py:51
  19.0 0.5 %collective-permute-start.6 = (bf16[32,1536]{1,0:T(8,128)(2,1)S(1)}, bf16[32,1536]{1,0:T(8,128)(2,1)S(1)}, u32[]{:S(2)}, u32[]{:S(2)}) collective-permute-start(bf16[32,1536]{1,0:T(8,128)(2,1)S(1)} %far_grad.1.after_ref), channel_id=1, source_target_pairs={{0,4},{4,0},{1,5},{5,1},{2,6},{6,2},{3,7},{7,3},{8,12},{12,8},{9,1... | collective-permute-start | bytes 294920 | tf_op jit(solution)/shard_map/ppermute | solution.py:331
  19.5 0.0 collective-permute-done.4.got_ref
  19.5 0.9 %own_pre.1.after_ref.own_ref = bf16[32,1536]{1,0:T(8,128)(2,1)S(1)} custom-call(bf16[32,1536]{1,0:T(8,128)(2,1)S(1)} %get-tuple-element.29.x_ref.left_ref, bf16[1536,1536]{1,0:T(8,128)(2,1)S(1)} %get-tuple-element.30.w_in_ref, bf16[32,1536]{1,0:T(8,128)(2,1)S(1)} %collective-permute-done.4.got_ref, bf16[32,1536]{1,0:T(8,128)(2,1)S(1)} %far_grad.1.after_ref), custom_call_target="tpu_custom_call" | custom-call | tf_op jit(solution)/shard_map/own_pre/pallas_call | solution.py:51
  20.4 1.4 %collective-permute-start.5 = (bf16[32,1536]{1,0:T(8,128)(2,1)S(1)}, bf16[32,1536]{1,0:T(8,128)(2,1)S(1)}, u32[]{:S(2)}, u32[]{:S(2)}) collective-permute-start(bf16[32,1536]{1,0:T(8,128)(2,1)S(1)} %own_pre.1.after_ref.own_ref), channel_id=1, source_target_pairs={{0,8},{8,0},{1,9},{9,1},{2,10},{10,2},{3,11},{11,3},{4,12},{12,4},... | collective-permute-start | bytes 294920 | tf_op jit(solution)/shard_map/ppermute | solution.py:333
  21.8 0.0 collective-permute-done.6.got_ref
  21.8 1.5 %own_grad.1.after_ref.own_ref = bf16[32,1536]{1,0:T(8,128)(2,1)S(1)} custom-call(bf16[32,1536]{1,0:T(8,128)(2,1)S(1)} %get-tuple-element.32.dy_ref.right_ref, bf16[1536,1536]{1,0:T(8,128)(2,1)S(1)} %get-tuple-element.33.w_out_ref, bf16[32,1536]{1,0:T(8,128)(2,1)S(1)} %collective-permute-done.6.got_ref, bf16[32,1536]{1,0:T(8,128)(2,1)S(1)} %own_pre.1.after_ref.own_ref), custom_call_target="tpu_custom_call" | custom-call | tf_op jit(solution)/shard_map/own_grad/pallas_call | solution.py:51
  23.3 0.7 %collective-permute-start.7 = (bf16[32,1536]{1,0:T(8,128)(2,1)S(1)}, bf16[32,1536]{1,0:T(8,128)(2,1)S(1)}, u32[]{:S(2)}, u32[]{:S(2)}) collective-permute-start(bf16[32,1536]{1,0:T(8,128)(2,1)S(1)} %own_grad.1.after_ref.own_ref), channel_id=1, source_target_pairs={{0,8},{8,0},{1,9},{9,1},{2,10},{10,2},{3,11},{11,3},{4,12},{12,4},... | collective-permute-start | bytes 294920 | tf_op jit(solution)/shard_map/ppermute | solution.py:337
  24.0 1.4 %collective-permute-start.8 = (f32[1,1536]{1,0:T(1,128)S(1)}, f32[1,1536]{1,0:T(1,128)S(1)}, u32[]{:S(2)}, u32[]{:S(2)}) collective-permute-start(f32[1,1536]{1,0:T(1,128)S(1)} %get-tuple-element.36.own_sums_ref), channel_id=1, source_target_pairs={{0,8},{8,0},{1,9},{9,1},{2,10},{10,2},{3,11},{11,3},{4,12},{12,4},... | collective-permute-start | bytes 18440 | tf_op jit(solution)/shard_map/ppermute | solution.py:338
  25.4 0.0 collective-permute-done.5.other_ref
  25.4 0.0 copy-done
  25.4 0.1 gelu.1
  25.5 0.9 %own_forward.1.after_ref.terms_ref = f32[32,1536]{1,0:T(8,128)S(1)} custom-call(bf16[32,1536]{1,0:T(8,128)(2,1)S(1)} %get-tuple-element.35.act_ref.own_ref, bf16[1536,1536]{1,0:T(8,128)(2,1)S(1)} %get-tuple-element.33.w_out_ref), custom_call_target="tpu_custom_call" | custom-call | tf_op jit(solution)/shard_map/own_forward/pallas_call | solution.py:51
  26.4 0.0 collective-permute-start.10
  26.4 1.6 %collective-permute-done.8.sums_ref.got_sums_ref = f32[1,1536]{1,0:T(1,128)S(1)} collective-permute-done((f32[1,1536]{1,0:T(1,128)S(1)}, f32[1,1536]{1,0:T(1,128)S(1)}, u32[]{:S(2)}, u32[]{:S(2)}) %collective-permute-start.8) | collective-permute-done | bytes 6176 | tf_op jit(solution)/shard_map/ppermute | solution.py:338
  28.1 0.0 collective-permute-done.7.other_ref
  28.1 0.1 collective-permute-start.9
  28.2 1.5 %own_backward.1.backward_ref = f32[32,1536]{1,0:T(8,128)S(1)} custom-call(bf16[32,1536]{1,0:T(8,128)(2,1)S(1)} %grad_pre.1.grad_ref.own_ref, bf16[1536,1536]{1,0:T(8,128)(2,1)S(1)} %get-tuple-element.30.w_in_ref), custom_call_target="tpu_custom_call" | custom-call | tf_op jit(solution)/shard_map/own_backward/pallas_call | solution.py:51
  29.6 0.0 copy-start.1
  29.6 0.0 collective-permute-done.10.far_ref
  29.7 0.9 %far_forward.1 = (bf16[32,3072]{1,0:T(8,128)(2,1)S(1)}, f32[32,1536]{1,0:T(8,128)S(1)}) custom-call(bf16[32,1536]{1,0:T(8,128)(2,1)S(1)} %get-tuple-element.35.act_ref.own_ref, bf16[32,1536]{1,0:T(8,128)(2,1)S(1)} %collective-permute-done.10.far_ref, bf16[1536,1536]{1,0:T(8,128)(2,1)S(1)} %load_far.1.after_ref.w_out_ref, ...), custom_call_target="tpu_custom_call" | custom-call | tf_op jit(solution)/shard_map/far_forward/pallas_call | solution.py:51
  30.6 0.0 collective-permute-done.9.far_ref
  30.6 1.5 %output_blocks.1 = (bf16[32,3072]{1,0:T(8,128)(2,1)S(1)}, bf16[16,1536]{1,0:T(8,128)(2,1)S(1)}, bf16[16,1536]{1,0:T(8,128)(2,1)S(1)}, bf16[16,1536]{1,0:T(8,128)(2,1)S(1)}, bf16[16,1536]{1,0:T(8,128)(2,1)S(1)}) custom-call(bf16[32,1536]{1,0:T(8,128)(2,1)S(1)} %grad_pre.1.grad_ref.own_ref, bf16[32,1536]{1,0:T(8,128)(2,1)S(1)} %collective-permute-done.9.far_ref, ...), custom_call_target="tpu_custom_call" | custom-call | tf_op jit(solution)/shard_map/output_blocks/pallas_call | solution.py:51
  32.1 3.7 %collective-permute-start.11 = (bf16[16,1536]{1,0:T(8,128)(2,1)S(1)}, bf16[16,1536]{1,0:T(8,128)(2,1)S(1)}, u32[]{:S(2)}, u32[]{:S(2)}) collective-permute-start(bf16[16,1536]{1,0:T(8,128)(2,1)S(1)} %get-tuple-element.38), channel_id=1, source_target_pairs={{0,3},{1,2},{2,1},{3,0},{4,7},{5,6},{6,5},{7,4},{8,11},{9,10},{10,... | collective-permute-start | bytes 147464 | tf_op jit(solution)/shard_map/ppermute | solution.py:279
  35.7 0.0 collective-permute-start.12
  35.7 0.8 %collective-permute-start.13 = (bf16[16,1536]{1,0:T(8,128)(2,1)S(1)}, bf16[16,1536]{1,0:T(8,128)(2,1)S(1)}, u32[]{:S(2)}, u32[]{:S(2)}) collective-permute-start(bf16[16,1536]{1,0:T(8,128)(2,1)S(1)} %get-tuple-element.40), channel_id=1, source_target_pairs={{0,1},{1,0},{2,3},{3,2},{4,5},{5,4},{6,7},{7,6},{8,9},{9,8},{10,11... | collective-permute-start | bytes 147464 | tf_op jit(solution)/shard_map/ppermute | solution.py:279
  36.5 4.3 %weight_in_grad.1 = bf16[1536,3072]{1,0:T(8,128)(2,1)} custom-call(bf16[32,1536]{1,0:T(8,128)(2,1)S(1)} %get-tuple-element.29.x_ref.left_ref, bf16[32,3072]{1,0:T(8,128)(2,1)S(1)} %get-tuple-element.44.hidden_ref.right_ref), custom_call_target="tpu_custom_call" | custom-call | flops 301989888 | bytes 9437184 | tf_op jit(solution)/shard_map/weight_in_grad/pallas_call | solution.py:231
  40.8 0.0 collective-permute-done.11.refs_0_
  40.8 0.0 collective-permute-done.12.refs_1_
  40.8 0.1 collective-permute-done.13.refs_2_
  40.9 0.0 copy-done.1
  40.9 1.0 %collective-permute-start.14 = (bf16[8,1536]{1,0:T(8,128)(2,1)S(1)}, bf16[8,1536]{1,0:T(8,128)(2,1)S(1)}, u32[]{:S(2)}, u32[]{:S(2)}) collective-permute-start(bf16[8,1536]{1,0:T(8,128)(2,1)S(1)} %get-tuple-element.43), channel_id=1, source_target_pairs={{0,8},{8,0},{1,9},{9,1},{2,10},{10,2},{3,11},{11,3},{4,12},{12,4},... | collective-permute-start | bytes 73736 | tf_op jit(solution)/shard_map/ppermute | solution.py:376
  42.0 4.1 %weight_out_grad.1 = bf16[3072,1536]{1,0:T(8,128)(2,1)} custom-call(bf16[32,3072]{1,0:T(8,128)(2,1)S(1)} %get-tuple-element.47.left_ref, bf16[32,1536]{1,0:T(8,128)(2,1)S(1)} %get-tuple-element.32.dy_ref.right_ref), custom_call_target="tpu_custom_call" | custom-call | flops 301989888 | bytes 9437184 | tf_op jit(solution)/shard_map/weight_out_grad/pallas_call | solution.py:231
  46.1 0.0 collective-permute-done.14.got_ref
  46.1 0.7 %final_rows.1 = (bf16[4,3072]{1,0:T(4,128)(2,1)}, bf16[4,3072]{1,0:T(4,128)(2,1)}, f32[1,3072]{1,0:T(1,128)}, f32[1,3072]{1,0:T(1,128)}) custom-call(bf16[8,1536]{1,0:T(8,128)(2,1)S(1)} %get-tuple-element.42.own_ref, bf16[8,1536]{1,0:T(8,128)(2,1)S(1)} %collective-permute-done.14.got_ref, f32[1,1536]{1,0:T(1,128)S(1)} %get-tuple-element.36.own_sums_ref, ...), custom_call_target="tpu_custom_call" | custom-call | tf_op jit(solution)/shard_map/final_rows/pallas_call | solution.py:51
  (3 shorter events, 0.1 us)
Async XLA Ops:
  1.5 5.4 %collective-permute-start = (bf16[8,1536]{1,0:T(8,128)(2,1)S(1)}, bf16[8,1536]{1,0:T(8,128)(2,1)S(1)}, u32[]{:S(2)}, u32[]{:S(2)}) collective-permute-start(bf16[8,1536]{1,0:T(8,128)(2,1)S(1)} %get-tuple-element.50.after_ref), channel_id=1, source_target_pairs={{0,8},{8,0},{1,9},{9,1},{2,10},{10,2},{3,11},{11,3},{4,12},{12,4},... | collective-permute-start | bytes 73736 | tf_op jit(solution)/shard_map/ppermute | solution.py:294
  6.9 9.6 %collective-permute-start.1 = (bf16[16,1536]{1,0:T(8,128)(2,1)S(1)}, bf16[16,1536]{1,0:T(8,128)(2,1)S(1)}, u32[]{:S(2)}, u32[]{:S(2)}) collective-permute-start(bf16[16,1536]{1,0:T(8,128)(2,1)S(1)} %pair_tiles.1.after_ref.refs_3_), channel_id=1, source_target_pairs={{0,3},{1,2},{2,1},{3,0},{4,7},{5,6},{6,5},{7,4},{8,11},{9,10},{10,... | collective-permute-start | bytes 147464 | tf_op jit(solution)/shard_map/ppermute | solution.py:279
  10.6 6.0 %collective-permute-start.2 = (bf16[16,1536]{1,0:T(8,128)(2,1)S(1)}, bf16[16,1536]{1,0:T(8,128)(2,1)S(1)}, u32[]{:S(2)}, u32[]{:S(2)}) collective-permute-start(bf16[16,1536]{1,0:T(8,128)(2,1)S(1)} %pair_tiles.1.after_ref.refs_3_), channel_id=1, source_target_pairs={{0,2},{1,3},{2,0},{3,1},{4,6},{5,7},{6,4},{7,5},{8,10},{9,11},{10,... | collective-permute-start | bytes 147464 | tf_op jit(solution)/shard_map/ppermute | solution.py:279
  10.6 6.0 %collective-permute-start.3 = (bf16[16,1536]{1,0:T(8,128)(2,1)S(1)}, bf16[16,1536]{1,0:T(8,128)(2,1)S(1)}, u32[]{:S(2)}, u32[]{:S(2)}) collective-permute-start(bf16[16,1536]{1,0:T(8,128)(2,1)S(1)} %pair_tiles.1.after_ref.refs_3_), channel_id=1, source_target_pairs={{0,1},{1,0},{2,3},{3,2},{4,5},{5,4},{6,7},{7,6},{8,9},{9,8},{10,11... | collective-permute-start | bytes 147464 | tf_op jit(solution)/shard_map/ppermute | solution.py:279
  16.6 8.8 %copy-start = (f32[3072]{0:T(1024)S(1)}, f32[3072]{0:T(1024)}, u32[]{:S(2)}) copy-start(f32[3072]{0:T(1024)} %param.8) | copy-start | bytes 36868
  17.5 2.0 %collective-permute-start.4 = (bf16[32,1536]{1,0:T(8,128)(2,1)S(1)}, bf16[32,1536]{1,0:T(8,128)(2,1)S(1)}, u32[]{:S(2)}, u32[]{:S(2)}) collective-permute-start(bf16[32,1536]{1,0:T(8,128)(2,1)S(1)} %get-tuple-element.31), channel_id=1, source_target_pairs={{0,4},{4,0},{1,5},{5,1},{2,6},{6,2},{3,7},{7,3},{8,12},{12,8},{9,1... | collective-permute-start | bytes 294920 | tf_op jit(solution)/shard_map/ppermute | solution.py:329
  19.0 2.9 %collective-permute-start.6 = (bf16[32,1536]{1,0:T(8,128)(2,1)S(1)}, bf16[32,1536]{1,0:T(8,128)(2,1)S(1)}, u32[]{:S(2)}, u32[]{:S(2)}) collective-permute-start(bf16[32,1536]{1,0:T(8,128)(2,1)S(1)} %far_grad.1.after_ref), channel_id=1, source_target_pairs={{0,4},{4,0},{1,5},{5,1},{2,6},{6,2},{3,7},{7,3},{8,12},{12,8},{9,1... | collective-permute-start | bytes 294920 | tf_op jit(solution)/shard_map/ppermute | solution.py:331
  20.4 5.0 %collective-permute-start.5 = (bf16[32,1536]{1,0:T(8,128)(2,1)S(1)}, bf16[32,1536]{1,0:T(8,128)(2,1)S(1)}, u32[]{:S(2)}, u32[]{:S(2)}) collective-permute-start(bf16[32,1536]{1,0:T(8,128)(2,1)S(1)} %own_pre.1.after_ref.own_ref), channel_id=1, source_target_pairs={{0,8},{8,0},{1,9},{9,1},{2,10},{10,2},{3,11},{11,3},{4,12},{12,4},... | collective-permute-start | bytes 294920 | tf_op jit(solution)/shard_map/ppermute | solution.py:333
  23.3 4.8 %collective-permute-start.7 = (bf16[32,1536]{1,0:T(8,128)(2,1)S(1)}, bf16[32,1536]{1,0:T(8,128)(2,1)S(1)}, u32[]{:S(2)}, u32[]{:S(2)}) collective-permute-start(bf16[32,1536]{1,0:T(8,128)(2,1)S(1)} %own_grad.1.after_ref.own_ref), channel_id=1, source_target_pairs={{0,8},{8,0},{1,9},{9,1},{2,10},{10,2},{3,11},{11,3},{4,12},{12,4},... | collective-permute-start | bytes 294920 | tf_op jit(solution)/shard_map/ppermute | solution.py:337
  24.0 4.1 %collective-permute-start.8 = (f32[1,1536]{1,0:T(1,128)S(1)}, f32[1,1536]{1,0:T(1,128)S(1)}, u32[]{:S(2)}, u32[]{:S(2)}) collective-permute-start(f32[1,1536]{1,0:T(1,128)S(1)} %get-tuple-element.36.own_sums_ref), channel_id=1, source_target_pairs={{0,8},{8,0},{1,9},{9,1},{2,10},{10,2},{3,11},{11,3},{4,12},{12,4},... | collective-permute-start | bytes 18440 | tf_op jit(solution)/shard_map/ppermute | solution.py:338
  26.4 3.2 %collective-permute-start.10 = (bf16[32,1536]{1,0:T(8,128)(2,1)S(1)}, bf16[32,1536]{1,0:T(8,128)(2,1)S(1)}, u32[]{:S(2)}, u32[]{:S(2)}) collective-permute-start(bf16[32,1536]{1,0:T(8,128)(2,1)S(1)} %get-tuple-element.35.act_ref.own_ref), channel_id=1, source_target_pairs={{0,4},{4,0},{1,5},{5,1},{2,6},{6,2},{3,7},{7,3},{8,12},{12,8},{9,1... | collective-permute-start | bytes 294920 | tf_op jit(solution)/shard_map/ppermute | solution.py:342
  28.1 2.5 %collective-permute-start.9 = (bf16[32,1536]{1,0:T(8,128)(2,1)S(1)}, bf16[32,1536]{1,0:T(8,128)(2,1)S(1)}, u32[]{:S(2)}, u32[]{:S(2)}) collective-permute-start(bf16[32,1536]{1,0:T(8,128)(2,1)S(1)} %grad_pre.1.grad_ref.own_ref), channel_id=1, source_target_pairs={{0,4},{4,0},{1,5},{5,1},{2,6},{6,2},{3,7},{7,3},{8,12},{12,8},{9,1... | collective-permute-start | bytes 294920 | tf_op jit(solution)/shard_map/ppermute | solution.py:356
  29.6 11.3 %copy-start.1 = (f32[3072]{0:T(1024)S(1)}, f32[3072]{0:T(1024)}, u32[]{:S(2)}) copy-start(f32[3072]{0:T(1024)} %param.10) | copy-start | bytes 36868
  32.1 8.7 %collective-permute-start.11 = (bf16[16,1536]{1,0:T(8,128)(2,1)S(1)}, bf16[16,1536]{1,0:T(8,128)(2,1)S(1)}, u32[]{:S(2)}, u32[]{:S(2)}) collective-permute-start(bf16[16,1536]{1,0:T(8,128)(2,1)S(1)} %get-tuple-element.38), channel_id=1, source_target_pairs={{0,3},{1,2},{2,1},{3,0},{4,7},{5,6},{6,5},{7,4},{8,11},{9,10},{10,... | collective-permute-start | bytes 147464 | tf_op jit(solution)/shard_map/ppermute | solution.py:279
  35.7 5.1 %collective-permute-start.12 = (bf16[16,1536]{1,0:T(8,128)(2,1)S(1)}, bf16[16,1536]{1,0:T(8,128)(2,1)S(1)}, u32[]{:S(2)}, u32[]{:S(2)}) collective-permute-start(bf16[16,1536]{1,0:T(8,128)(2,1)S(1)} %get-tuple-element.39), channel_id=1, source_target_pairs={{0,2},{1,3},{2,0},{3,1},{4,6},{5,7},{6,4},{7,5},{8,10},{9,11},{10,... | collective-permute-start | bytes 147464 | tf_op jit(solution)/shard_map/ppermute | solution.py:279
  35.7 5.1 %collective-permute-start.13 = (bf16[16,1536]{1,0:T(8,128)(2,1)S(1)}, bf16[16,1536]{1,0:T(8,128)(2,1)S(1)}, u32[]{:S(2)}, u32[]{:S(2)}) collective-permute-start(bf16[16,1536]{1,0:T(8,128)(2,1)S(1)} %get-tuple-element.40), channel_id=1, source_target_pairs={{0,1},{1,0},{2,3},{3,2},{4,5},{5,4},{6,7},{7,6},{8,9},{9,8},{10,11... | collective-permute-start | bytes 147464 | tf_op jit(solution)/shard_map/ppermute | solution.py:279
  40.9 5.2 %collective-permute-start.14 = (bf16[8,1536]{1,0:T(8,128)(2,1)S(1)}, bf16[8,1536]{1,0:T(8,128)(2,1)S(1)}, u32[]{:S(2)}, u32[]{:S(2)}) collective-permute-start(bf16[8,1536]{1,0:T(8,128)(2,1)S(1)} %get-tuple-element.43), channel_id=1, source_target_pairs={{0,8},{8,0},{1,9},{9,1},{2,10},{10,2},{3,11},{11,3},{4,12},{12,4},... | collective-permute-start | bytes 73736 | tf_op jit(solution)/shard_map/ppermute | solution.py:376

commit v10 on v9

--- a/solution.py
+++ b/solution.py
@@ -32,6 +32,10 @@
 
 def exchange(chunks, axes):
     return lax.all_to_all(chunks, axes, split_axis=0, concat_axis=0, tiled=True)
+
+
+def dot_turned(rows, weight):
+    return dot(weight, rows, 1, 1).T
 
 
 def tile_of(size, most):
@@ -144,52 +148,62 @@
         sent_ref[:, at] = dot(x_cols, w_in_ref[:, at], 1, 0).astype(bf16)
 
 
-def far_grad_body(dy_ref, w_out_ref, sent_ref):
-    dy_cols = dy_ref[...]
-    for at in tiles_of(sent_ref.shape[1]):
-        sent_ref[:, at] = dot(dy_cols, w_out_ref[at, :], 1, 1).astype(bf16)
-
-
-def own_pre_body(x_ref, w_in_ref, got_ref, after_ref, own_ref):
+def own_pre_body(x_ref, w_in_ref, after_ref, own_ref):
     x_cols = x_ref[...]
     for at in tiles_of(own_ref.shape[1]):
-        own = dot(x_cols, w_in_ref[:, at], 1, 0) + got_ref[:, at].astype(f32)
-        own_ref[:, at] = own.astype(bf16)
-
-
-def own_grad_body(dy_ref, w_out_ref, got_ref, after_ref, own_ref):
+        own_ref[:, at] = dot(x_cols, w_in_ref[:, at], 1, 0)
+
+
+def far_grad_body(dy_ref, w_out_ref, after_ref, *sent_refs):
+    dy_cols = dy_ref[...]
+    size = sent_refs[0].shape[0]
+    for at in tiles_of(sent_refs[0].shape[1]):
+        terms = dot_turned(dy_cols, w_out_ref[at, :]).astype(bf16)
+        for i, sent_ref in enumerate(sent_refs):
+            sent_ref[:, at] = terms[i * size : (i + 1) * size]
+
+
+def own_grad_body(dy_ref, w_out_ref, own_ref):
     dy_cols = dy_ref[...]
     for at in tiles_of(own_ref.shape[1]):
-        own = dot(dy_cols, w_out_ref[at, :], 1, 1) + got_ref[:, at].astype(f32)
-        own_ref[:, at] = own.astype(bf16)
-
-
-def gelu_body(bias_ref, own_ref, other_ref, after_ref, act_ref, slopes_ref):
-    half = act_ref.shape[1]
+        own_ref[:, at] = dot_turned(dy_cols, w_out_ref[at, :])
+
+
+def add_body(own_ref, *refs):
+    *got_refs, out_ref = refs
+    got = jnp.concatenate([ref[...] for ref in got_refs], axis=0)
+    out_ref[...] = (own_ref[...] + got.astype(f32)).astype(bf16)
+
+
+def gelu_body(bias_ref, own_ref, other_ref, after_ref, slopes_ref, *act_refs):
+    size, half = act_refs[0].shape
     bias = bias_ref[:, half_of(half, True)]
     tile = tile_of(half, 512)
     for i in range(half // tile):
         at = pl.ds(i * tile, tile)
         pre_act = own_ref[:, at].astype(f32) + other_ref[:, at].astype(f32)
         activated, slopes = gelu_parts(pre_act + bias[:, i * tile : (i + 1) * tile])
-        act_ref[:, at] = activated.astype(bf16)
         slopes_ref[:, at] = slopes
-
-
-def grad_pre_body(slopes_ref, own_ref, other_ref, after_ref, sums_ref, grad_ref):
+        activated = activated.astype(bf16)
+        for j, act_ref in enumerate(act_refs):
+            act_ref[:, at] = activated[j * size : (j + 1) * size]
+
+
+def grad_pre_body(slopes_ref, own_ref, other_ref, after_ref, grad_ref):
     grad_act = own_ref[...].astype(f32) + other_ref[...].astype(f32)
     grad_ref[...] = (grad_act * slopes_ref[...]).astype(bf16)
 
 
-def own_forward_body(act_ref, w_out_ref, out_ref):
-    act = act_ref[...]
+def own_forward_body(low_ref, high_ref, w_out_ref, out_ref):
+    act = jnp.concatenate([low_ref[...], high_ref[...]], axis=0)
     for at in tiles_of(out_ref.shape[1]):
         out_ref[:, at] = dot(act, w_out_ref[:, at], 1, 0)
 
 
-def far_forward_body(own_ref, far_ref, w_out_ref, terms_ref, act_ref, out_ref):
-    act = far_ref[...]
-    act_ref[...] = ordered(lax.axis_index("kin"), own_ref[...], act, 1)
+def far_forward_body(own_low, own_high, low_ref, high_ref, w_out_ref, terms_ref, act_ref, out_ref):
+    own = jnp.concatenate([own_low[...], own_high[...]], axis=0)
+    act = jnp.concatenate([low_ref[...], high_ref[...]], axis=0)
+    act_ref[...] = ordered(lax.axis_index("kin"), own, act, 1)
     for at in tiles_of(out_ref.shape[1]):
         out_ref[:, at] = terms_ref[:, at] + dot(act, w_out_ref[:, at], 1, 0)
 
@@ -197,7 +211,7 @@
 def own_backward_body(grad_ref, w_in_ref, out_ref):
     grad = grad_ref[...]
     for at in tiles_of(out_ref.shape[1]):
-        out_ref[:, at] = dot(grad, w_in_ref[at, :], 1, 1)
+        out_ref[:, at] = dot_turned(grad, w_in_ref[at, :])
 
 
 def blocks_body(rows, own_ref, far_ref, forward_ref, backward_ref, w_in_ref, grad_ref, *out_refs):
@@ -205,7 +219,7 @@
     grad_ref[...] = ordered(lax.axis_index("kin"), own_ref[...], grad, 1)
     size = out_refs[0].shape[0]
     for at in tiles_of(forward_ref.shape[1]):
-        backward = backward_ref[:, at] + dot(grad, w_in_ref[at, :], 1, 1)
+        backward = backward_ref[:, at] + dot_turned(grad, w_in_ref[at, :])
         terms = together(forward_ref[:, at], backward, rows).astype(bf16)
         for i, out_ref in enumerate(out_refs):
             out_ref[:, at] = terms[i * size : (i + 1) * size]
@@ -245,32 +259,38 @@
     )(kept(left), kept(right))
 
 
-def sum_body(rows, bias_ref, *refs):
-    *term_refs, own_ref, sent_ref = refs
+def sum_body(rows, bias_ref, sums_ref, *refs):
+    *term_refs, after_ref, own_ref, sent_ref = refs
     wide = own_ref.shape[1]
     me = lax.axis_index("tok")
     summed = sum(ref[...].astype(f32) for ref in term_refs)
     bias = jnp.where(me == 0, bias_ref[:, :wide], bias_ref[:, wide:])
-    is_fwd = lax.rem(lax.broadcasted_iota(jnp.int32, summed.shape, 0), 2 * rows) < rows
-    summed = summed + jnp.where(is_fwd, bias, 0.0)
+    row = lax.broadcasted_iota(jnp.int32, summed.shape, 0)
+    summed = summed + jnp.where(lax.rem(row, 2 * rows) < rows, bias, 0.0)
     low, high = summed[: 2 * rows], summed[2 * rows :]
     own_ref[...] = jnp.where(me == 0, low, high).astype(bf16)
-    sent_ref[...] = jnp.where(me == 0, high, low).astype(bf16)
-
-
-def final_body(
-    rows, own_ref, got_ref, own_sums_ref, got_sums_ref, hidden_ref, rows_ref, grad_ref, sums_ref, bias_ref
-):
+    rest = sums_ref[...]
+    row = lax.broadcasted_iota(jnp.int32, low.shape, 0)
+    extra = jnp.zeros_like(low)
+    for i in range(3):
+        term = rest.astype(bf16).astype(f32)
+        extra = jnp.where(row == i, term, extra)
+        rest = rest - term
+    sent = jnp.concatenate([jnp.where(me == 0, high, low), extra], axis=0)
+    sent_ref[...] = sent.astype(bf16)
+
+
+def final_body(rows, own_ref, got_ref, sums_ref, hidden_ref, rows_ref, grad_ref, out_sums_ref, bias_ref):
     wide = own_ref.shape[1]
     me = lax.axis_index("tok")
     own, got = own_ref[...].astype(f32), got_ref[...].astype(f32)
-    own_sums, got_sums = own_sums_ref[...], got_sums_ref[...]
+    own_sums, got_sums = sums_ref[...], jnp.sum(got[2 * rows :], axis=0, keepdims=True)
     for i in range(2):
         at = pl.ds(i * wide, wide)
-        part = jnp.where(me == i, own, got)
+        part = jnp.where(me == i, own, got[: 2 * rows])
         rows_ref[:, at] = part[:rows].astype(bf16)
         grad_ref[:, at] = part[rows:].astype(bf16)
-        sums_ref[:, at] = jnp.where(me == i, own_sums, got_sums)
+        out_sums_ref[:, at] = jnp.where(me == i, own_sums, got_sums)
     bias_ref[...] = jnp.sum(hidden_ref[...].astype(f32), axis=0, keepdims=True)
 
 
@@ -326,32 +346,32 @@
             *pieces,
             in_far,
         )
-        got_pre = lax.ppermute(sent, "kin", swap)
-        (sent,) = product(far_grad_body, "far_grad", [side], dy_cols, out_far)
-        got_grad = lax.ppermute(sent, "kin", swap)
-        (own_pre,) = product(own_pre_body, "own_pre", [side], x_cols, in_own, got_pre, sent)
+        got = lax.ppermute(sent, "kin", swap)
+        (own,) = product(own_pre_body, "own_pre", [like((count, half), f32)], x_cols, in_own, sent)
+        (own_pre,) = product(add_body, "add_pre", [side], own, got)
         other_pre = lax.ppermute(own_pre, "tok", swap)
-        (own_grad,) = product(
-            own_grad_body, "own_grad", [side], dy_cols, out_own, got_grad, own_pre
-        )
+        sides = [like((count // 2, half), bf16)] * 2
+        sent = product(far_grad_body, "far_grad", sides, dy_cols, out_far, own_pre)
+        got = [lax.ppermute(part, "kin", swap) for part in sent]
+        (own,) = product(own_grad_body, "own_grad", [like((count, half), f32)], dy_cols, out_own)
+        (own_grad,) = product(add_body, "add_grad", [side], own, *got)
         other_grad = lax.ppermute(own_grad, "tok", swap)
-        got_sums = lax.ppermute(sums, "tok", swap)
-        act_own, slopes = call(gelu_body, "gelu", [side, like((count, half), f32)])(
+        slopes, *act_own = call(gelu_body, "gelu", [like((count, half), f32)] + sides)(
             bias_in.reshape(1, hid), kept(own_pre), kept(other_pre), kept(own_grad)
         )
-        act_far = lax.ppermute(act_own, "kin", swap)
-        (forward,) = product(own_forward_body, "own_forward", [ends], act_own, out_own)
-        (grad_own,) = call(grad_pre_body, "grad_pre", [side])(
-            kept(slopes), kept(own_grad), kept(other_grad), kept(forward), kept(got_sums)
-        )
+        act_far = [lax.ppermute(part, "kin", swap) for part in act_own]
+        (forward,) = product(own_forward_body, "own_forward", [ends], *act_own, out_own)
         act, forward = product(
             far_forward_body,
             "far_forward",
             [like((count, hid), bf16), ends],
-            act_own,
-            act_far,
+            *act_own,
+            *act_far,
             out_far,
             forward,
+        )
+        (grad_own,) = product(
+            grad_pre_body, "grad_pre", [side], slopes, own_grad, other_grad, forward
         )
         grad_far = lax.ppermute(grad_own, "kin", swap)
         (backward,) = product(own_backward_body, "own_backward", [ends], grad_own, in_own)
@@ -371,15 +391,23 @@
 
         terms = [across(blocks[i], nn - 1 - i) for i in range(nn - 1)] + [blocks[-1]]
         own, sent = call(
-            functools.partial(sum_body, rows), "sum_blocks", [like((pair, wide), bf16)] * 2
-        )(bias_out.reshape(1, cols), *[kept(term) for term in terms])
+            functools.partial(sum_body, rows),
+            "sum_blocks",
+            [like((pair, wide), bf16), like((2 * pair, wide), bf16)],
+            specs=[whole] * (nn + 2) + [hbm],
+        )(
+            bias_out.reshape(1, cols),
+            kept(sums),
+            *[kept(term) for term in terms],
+            in_hbm(weight_in_grad),
+        )
         got = lax.ppermute(sent, "tok", swap)
         output_rows, grad_tokens, bias_out_grad, bias_in_grad = call(
             functools.partial(final_body, rows),
             "final_rows",
             [like((rows, cols), bf16)] * 2 + [like((1, cols), f32), like((1, hid), f32)],
             resident=False,
-        )(kept(own), kept(got), kept(sums), kept(got_sums), kept(grad))
+        )(kept(own), kept(got), kept(sums), kept(grad))
         return (
             output_rows,
             grad_tokens,

time: 47.1 us -> 46.7 us (level)
  starting transfers between devices: 17.1 us -> 15.9 us
  waiting for transfers between devices: 1.75 us -> 2.61 us
    ppermute x1, waiting for transfers between devices: 0.01 us -> 1.67 us  [on_device(): other_grad = lax.ppermute(own_grad, 'tok', swap)]
    ppermute x4 -> x5, waiting for transfers between devices: 1.66 us -> 0.43 us  [the longest x1 0.4 us: on_device(): got = lax.ppermute(sent, 'kin', swap)]
    ppermute x4 -> x5, starting transfers between devices: 1.97 us -> 1.13 us  [the longest x2 0.57 us: on_device(): act_far = [lax.ppermute(part, 'kin', swap) for part in act_own]]
    pallas_call x15 -> x17, Pallas kernels: 17.8 us -> 17.8 us  [run(): pl.pallas_call(body, out_shape=shapes, in_specs=specs or [whole] * len(ar...]
  transfers between devices with their start and end apart: 15 -> 16, of which waited for: 2 -> 3; matrix products, arithmetic and copies ran while one was open for 0% -> 0% of each run, Pallas kernels for 49% -> 50%
where the time goes in v10:
time: 46.7 us; the launch traced here: 46.4 us
  Pallas kernels  26.2 us (56%)
  starting transfers between devices  15.9 us (34%)
  waiting for transfers between devices  2.61 us (6%)
  other arithmetic  0.86 us (2%)
  between operations  0.85 us (2%)
    pallas_call x17, Pallas kernels, run(): pl.pallas_call(body, out_shape=shapes, in_specs=specs or [whole] * len(ar...  17.8 us
    ppermute x6, starting transfers between devices, across(): return lax.ppermute(array, 'nout', [(i, i ^ shift) for i in range(nn)])  8.9 us
    pallas_call x2, Pallas kernels, outer(): pl.pallas_call(functools.partial(outer_body, most), out_shape=like((high,...  8.39 us
    ppermute x2, starting transfers between devices, on_device(): got = lax.ppermute(sent, 'tok', swap)  3.65 us
    ppermute x1, waiting for transfers between devices, on_device(): other_grad = lax.ppermute(own_grad, 'tok', swap)  1.67 us
    ppermute x1, starting transfers between devices, on_device(): other_pre = lax.ppermute(own_pre, 'tok', swap)  1.49 us
  transfers between devices with their start and end apart: 16, of which 3 were waited for; matrix products, arithmetic and copies ran while one was open for 0% of the time, Pallas kernels for 50%

profile of v10, /device:TPU:0, one launch (start us, length us, event | category | flops | bytes accessed | tf_op | source)
XLA Modules:
  0.0 46.4 jit_solution(997407456437980025)
XLA Ops:
  0.6 0.9 %fusion = (bf16[8,1536]{1,0:T(8,128)(2,1)S(1)}, bf16[8,1536]{1,0:T(8,128)(2,1)S(1)}) fusion(s32[]{:T(128)S(6)} %select_n.7, bf16[4,3072]{1,0:T(4,128)(2,1)} %param.6, bf16[4,3072]{1,0:T(4,128)(2,1)} %param.11, s32[]{:T(128)S(6)} %select_n.6), kind=kLoop, calls=%fused_computation.4 | loop fusion | flops 98304 | bytes 98312 | tf_op jit(solution)/shard_map/concatenate | solution.py:310
  1.5 3.0 %collective-permute-start = (bf16[8,1536]{1,0:T(8,128)(2,1)S(1)}, bf16[8,1536]{1,0:T(8,128)(2,1)S(1)}, u32[]{:S(2)}, u32[]{:S(2)}) collective-permute-start(bf16[8,1536]{1,0:T(8,128)(2,1)S(1)} %get-tuple-element.56.after_ref), channel_id=1, source_target_pairs={{0,8},{8,0},{1,9},{9,1},{2,10},{10,2},{3,11},{11,3},{4,12},{12,4},... | collective-permute-start | bytes 73736 | tf_op jit(solution)/shard_map/ppermute | solution.py:314
  4.5 2.4 %load_far.1.after_ref.w_out_ref = bf16[1536,1536]{1,0:T(8,128)(2,1)S(1)} custom-call(bf16[3072,1536]{1,0:T(8,128)(2,1)} %out_hbm_ref.1, bf16[8,1536]{1,0:T(8,128)(2,1)S(1)} %get-tuple-element.56.after_ref), custom_call_target="tpu_custom_call" | custom-call | bytes 4718592 | tf_op jit(solution)/shard_map/load_far/pallas_call | solution.py:55
  6.9 0.0 collective-permute-done.got_ref
  6.9 1.6 %collective-permute-start.3 = (bf16[16,1536]{1,0:T(8,128)(2,1)S(1)}, bf16[16,1536]{1,0:T(8,128)(2,1)S(1)}, u32[]{:S(2)}, u32[]{:S(2)}) collective-permute-start(bf16[16,1536]{1,0:T(8,128)(2,1)S(1)} %pair_tiles.1.after_ref.refs_3_), channel_id=1, source_target_pairs={{0,1},{1,0},{2,3},{3,2},{4,5},{5,4},{6,7},{7,6},{8,9},{9,8},{10,11... | collective-permute-start | bytes 147464 | tf_op jit(solution)/shard_map/ppermute | solution.py:299
  8.6 2.6 %collective-permute-start.2 = (bf16[16,1536]{1,0:T(8,128)(2,1)S(1)}, bf16[16,1536]{1,0:T(8,128)(2,1)S(1)}, u32[]{:S(2)}, u32[]{:S(2)}) collective-permute-start(bf16[16,1536]{1,0:T(8,128)(2,1)S(1)} %pair_tiles.1.after_ref.refs_3_), channel_id=1, source_target_pairs={{0,2},{1,3},{2,0},{3,1},{4,6},{5,7},{6,4},{7,5},{8,10},{9,11},{10,... | collective-permute-start | bytes 147464 | tf_op jit(solution)/shard_map/ppermute | solution.py:299
  11.2 0.2 collective-permute-start.1
  11.4 5.2 %load_rest.1 = (bf16[1536,1536]{1,0:T(8,128)(2,1)S(1)}, bf16[1536,1536]{1,0:T(8,128)(2,1)S(1)}, bf16[1536,1536]{1,0:T(8,128)(2,1)S(1)}) custom-call(bf16[1536,3072]{1,0:T(8,128)(2,1)} %in_hbm_ref.1, bf16[3072,1536]{1,0:T(8,128)(2,1)} %out_hbm_ref.1, bf16[16,1536]{1,0:T(8,128)(2,1)S(1)} %pair_tiles.1.after_ref.refs_3_), custom_call_target="tpu_custom_call" | custom-call | bytes 14155776 | tf_op jit(solution)/shard_map/load_rest/pallas_call | solution.py:55
  16.5 0.0 collective-permute-done.3.refs_2_
  16.5 0.0 collective-permute-done.2.refs_1_
  16.6 0.5 %collective-permute-done.1.refs_0_ = bf16[16,1536]{1,0:T(8,128)(2,1)S(1)} collective-permute-done((bf16[16,1536]{1,0:T(8,128)(2,1)S(1)}, bf16[16,1536]{1,0:T(8,128)(2,1)S(1)}, u32[]{:S(2)}, u32[]{:S(2)}) %collective-permute-start.1) | collective-permute-done | bytes 49184 | tf_op jit(solution)/shard_map/ppermute | solution.py:299
  17.0 0.0 copy-start
  17.0 0.9 %far_pre.1 = (bf16[32,1536]{1,0:T(8,128)(2,1)S(1)}, bf16[32,1536]{1,0:T(8,128)(2,1)S(1)}, bf16[32,1536]{1,0:T(8,128)(2,1)S(1)}, f32[1,1536]{1,0:T(1,128)S(1)}) custom-call(bf16[16,1536]{1,0:T(8,128)(2,1)S(1)} %collective-permute-done.1.refs_0_, bf16[16,1536]{1,0:T(8,128)(2,1)S(1)} %collective-permute-done.2.refs_1_, ...), custom_call_target="tpu_custom_call" | custom-call | tf_op jit(solution)/shard_map/far_pre/pallas_call | solution.py:55
  17.9 0.0 collective-permute-start.4
  17.9 0.9 %own_pre.1.own_ref = f32[32,1536]{1,0:T(8,128)S(1)} custom-call(bf16[32,1536]{1,0:T(8,128)(2,1)S(1)} %get-tuple-element.33.x_ref.left_ref, bf16[1536,1536]{1,0:T(8,128)(2,1)S(1)} %get-tuple-element.34.w_in_ref, bf16[32,1536]{1,0:T(8,128)(2,1)S(1)} %get-tuple-element.35.after_ref), custom_call_target="tpu_custom_call" | custom-call | tf_op jit(solution)/shard_map/own_pre/pallas_call | solution.py:55
  18.9 0.4 collective-permute-done.4.refs_0_
  19.3 1.5 %collective-permute-start.5 = (bf16[32,1536]{1,0:T(8,128)(2,1)S(1)}, bf16[32,1536]{1,0:T(8,128)(2,1)S(1)}, u32[]{:S(2)}, u32[]{:S(2)}) collective-permute-start(bf16[32,1536]{1,0:T(8,128)(2,1)S(1)} %add_pre.1.after_ref.own_ref), channel_id=1, source_target_pairs={{0,8},{8,0},{1,9},{9,1},{2,10},{10,2},{3,11},{11,3},{4,12},{12,4},... | collective-permute-start | bytes 294920 | tf_op jit(solution)/shard_map/ppermute | solution.py:352
  20.8 1.4 %far_grad.1 = (bf16[16,1536]{1,0:T(8,128)(2,1)S(1)}, bf16[16,1536]{1,0:T(8,128)(2,1)S(1)}) custom-call(bf16[32,1536]{1,0:T(8,128)(2,1)S(1)} %get-tuple-element.36.dy_ref.right_ref, bf16[1536,1536]{1,0:T(8,128)(2,1)S(1)} %load_far.1.after_ref.w_out_ref, bf16[32,1536]{1,0:T(8,128)(2,1)S(1)} %add_pre.1.after_ref.own_ref), custom_call_target="tpu_custom_call" | custom-call | tf_op jit(solution)/shard_map/far_grad/pallas_call | solution.py:55
  22.2 0.1 collective-permute-start.6
  22.3 0.5 %collective-permute-start.7 = (bf16[16,1536]{1,0:T(8,128)(2,1)S(1)}, bf16[16,1536]{1,0:T(8,128)(2,1)S(1)}, u32[]{:S(2)}, u32[]{:S(2)}) collective-permute-start(bf16[16,1536]{1,0:T(8,128)(2,1)S(1)} %get-tuple-element.39), channel_id=1, source_target_pairs={{0,4},{4,0},{1,5},{5,1},{2,6},{6,2},{3,7},{7,3},{8,12},{12,8},{9,1... | collective-permute-start | bytes 147464 | tf_op jit(solution)/shard_map/ppermute | solution.py:355
  22.8 1.4 %own_grad.1.own_ref = f32[32,1536]{1,0:T(8,128)S(1)} custom-call(bf16[32,1536]{1,0:T(8,128)(2,1)S(1)} %get-tuple-element.36.dy_ref.right_ref, bf16[1536,1536]{1,0:T(8,128)(2,1)S(1)} %get-tuple-element.37.w_out_ref), custom_call_target="tpu_custom_call" | custom-call | tf_op jit(solution)/shard_map/own_grad/pallas_call | solution.py:55
  24.2 0.0 collective-permute-done.6.refs_0_
  24.2 0.0 collective-permute-done.7.refs_1_
  24.2 0.7 %collective-permute-start.8 = (bf16[32,1536]{1,0:T(8,128)(2,1)S(1)}, bf16[32,1536]{1,0:T(8,128)(2,1)S(1)}, u32[]{:S(2)}, u32[]{:S(2)}) collective-permute-start(bf16[32,1536]{1,0:T(8,128)(2,1)S(1)} %add_grad.1.after_ref.own_ref), channel_id=1, source_target_pairs={{0,8},{8,0},{1,9},{9,1},{2,10},{10,2},{3,11},{11,3},{4,12},{12,4},... | collective-permute-start | bytes 294920 | tf_op jit(solution)/shard_map/ppermute | solution.py:358
  24.9 0.0 collective-permute-done.5.other_ref
  24.9 0.0 copy-done
  24.9 0.1 gelu.1
  25.0 0.1 collective-permute-start.9
  25.1 0.5 %collective-permute-start.10 = (bf16[16,1536]{1,0:T(8,128)(2,1)S(1)}, bf16[16,1536]{1,0:T(8,128)(2,1)S(1)}, u32[]{:S(2)}, u32[]{:S(2)}) collective-permute-start(bf16[16,1536]{1,0:T(8,128)(2,1)S(1)} %get-tuple-element.42.high_ref.own_high), channel_id=1, source_target_pairs={{0,4},{4,0},{1,5},{5,1},{2,6},{6,2},{3,7},{7,3},{8,12},{12,8},{9,1... | collective-permute-start | bytes 147464 | tf_op jit(solution)/shard_map/ppermute | solution.py:362
  25.6 0.9 %own_forward.1.terms_ref = f32[32,1536]{1,0:T(8,128)S(1)} custom-call(bf16[16,1536]{1,0:T(8,128)(2,1)S(1)} %get-tuple-element.41.low_ref.own_low, bf16[16,1536]{1,0:T(8,128)(2,1)S(1)} %get-tuple-element.42.high_ref.own_high, bf16[1536,1536]{1,0:T(8,128)(2,1)S(1)} %get-tuple-element.37.w_out_ref), custom_call_target="tpu_custom_call" | custom-call | tf_op jit(solution)/shard_map/own_forward/pallas_call | solution.py:55
  26.5 0.0 collective-permute-done.9.low_ref
  26.5 0.0 collective-permute-done.10.high_ref
  26.5 0.9 %far_forward.1 = (bf16[32,3072]{1,0:T(8,128)(2,1)S(1)}, f32[32,1536]{1,0:T(8,128)S(1)}) custom-call(bf16[16,1536]{1,0:T(8,128)(2,1)S(1)} %get-tuple-element.41.low_ref.own_low, bf16[16,1536]{1,0:T(8,128)(2,1)S(1)} %get-tuple-element.42.high_ref.own_high, bf16[16,1536]{1,0:T(8,128)(2,1)S(1)} %collective-permute-done.9.low_ref, ...), custom_call_target="tpu_custom_call" | custom-call | tf_op jit(solution)/shard_map/far_forward/pallas_call | solution.py:55
  27.4 1.7 %collective-permute-done.8.other_ref = bf16[32,1536]{1,0:T(8,128)(2,1)S(1)} collective-permute-done((bf16[32,1536]{1,0:T(8,128)(2,1)S(1)}, bf16[32,1536]{1,0:T(8,128)(2,1)S(1)}, u32[]{:S(2)}, u32[]{:S(2)}) %collective-permute-start.8) | collective-permute-done | bytes 98336 | tf_op jit(solution)/shard_map/ppermute | solution.py:358
  29.1 0.0 copy-start.1
  29.1 0.1 collective-permute-start.11
  29.2 1.4 %own_backward.1.backward_ref = f32[32,1536]{1,0:T(8,128)S(1)} custom-call(bf16[32,1536]{1,0:T(8,128)(2,1)S(1)} %grad_pre.1.grad_ref.own_ref, bf16[1536,1536]{1,0:T(8,128)(2,1)S(1)} %get-tuple-element.34.w_in_ref), custom_call_target="tpu_custom_call" | custom-call | tf_op jit(solution)/shard_map/own_backward/pallas_call | solution.py:55
  30.6 0.0 collective-permute-done.11.far_ref
  30.6 1.5 %output_blocks.1 = (bf16[32,3072]{1,0:T(8,128)(2,1)S(1)}, bf16[16,1536]{1,0:T(8,128)(2,1)S(1)}, bf16[16,1536]{1,0:T(8,128)(2,1)S(1)}, bf16[16,1536]{1,0:T(8,128)(2,1)S(1)}, bf16[16,1536]{1,0:T(8,128)(2,1)S(1)}) custom-call(bf16[32,1536]{1,0:T(8,128)(2,1)S(1)} %grad_pre.1.grad_ref.own_ref, bf16[32,1536]{1,0:T(8,128)(2,1)S(1)} %collective-permute-done.11.far_ref, ...), custom_call_target="tpu_custom_call" | custom-call | tf_op jit(solution)/shard_map/output_blocks/pallas_call | solution.py:55
  32.1 3.2 %collective-permute-start.12 = (bf16[16,1536]{1,0:T(8,128)(2,1)S(1)}, bf16[16,1536]{1,0:T(8,128)(2,1)S(1)}, u32[]{:S(2)}, u32[]{:S(2)}) collective-permute-start(bf16[16,1536]{1,0:T(8,128)(2,1)S(1)} %get-tuple-element.44), channel_id=1, source_target_pairs={{0,3},{1,2},{2,1},{3,0},{4,7},{5,6},{6,5},{7,4},{8,11},{9,10},{10,... | collective-permute-start | bytes 147464 | tf_op jit(solution)/shard_map/ppermute | solution.py:299
  35.3 0.0 collective-permute-start.13
  35.3 1.2 %collective-permute-start.14 = (bf16[16,1536]{1,0:T(8,128)(2,1)S(1)}, bf16[16,1536]{1,0:T(8,128)(2,1)S(1)}, u32[]{:S(2)}, u32[]{:S(2)}) collective-permute-start(bf16[16,1536]{1,0:T(8,128)(2,1)S(1)} %get-tuple-element.46), channel_id=1, source_target_pairs={{0,1},{1,0},{2,3},{3,2},{4,5},{5,4},{6,7},{7,6},{8,9},{9,8},{10,11... | collective-permute-start | bytes 147464 | tf_op jit(solution)/shard_map/ppermute | solution.py:299
  36.5 4.3 %weight_in_grad.1.refs_4_ = bf16[1536,3072]{1,0:T(8,128)(2,1)} custom-call(bf16[32,1536]{1,0:T(8,128)(2,1)S(1)} %get-tuple-element.33.x_ref.left_ref, bf16[32,3072]{1,0:T(8,128)(2,1)S(1)} %get-tuple-element.48.right_ref.hidden_ref), custom_call_target="tpu_custom_call" | custom-call | flops 301989888 | bytes 9437184 | tf_op jit(solution)/shard_map/weight_in_grad/pallas_call | solution.py:245
  40.8 0.0 collective-permute-done.12.refs_0_
  40.8 0.0 collective-permute-done.13.refs_1_
  40.8 0.0 collective-permute-done.14.refs_2_
  40.9 0.0 copy-done.1
  40.9 0.1 sum_blocks.1
  40.9 0.6 %collective-permute-start.15 = (bf16[16,1536]{1,0:T(8,128)(2,1)S(1)}, bf16[16,1536]{1,0:T(8,128)(2,1)S(1)}, u32[]{:S(2)}, u32[]{:S(2)}) collective-permute-start(bf16[16,1536]{1,0:T(8,128)(2,1)S(1)} %get-tuple-element.50), channel_id=1, source_target_pairs={{0,8},{8,0},{1,9},{9,1},{2,10},{10,2},{3,11},{11,3},{4,12},{12,4},... | collective-permute-start | bytes 147464 | tf_op jit(solution)/shard_map/ppermute | solution.py:404
  41.6 4.1 %weight_out_grad.1 = bf16[3072,1536]{1,0:T(8,128)(2,1)} custom-call(bf16[32,3072]{1,0:T(8,128)(2,1)S(1)} %get-tuple-element.53.left_ref, bf16[32,1536]{1,0:T(8,128)(2,1)S(1)} %get-tuple-element.36.dy_ref.right_ref), custom_call_target="tpu_custom_call" | custom-call | flops 301989888 | bytes 9437184 | tf_op jit(solution)/shard_map/weight_out_grad/pallas_call | solution.py:245
  45.7 0.0 collective-permute-done.15.got_ref
  45.7 0.7 %final_rows.1 = (bf16[4,3072]{1,0:T(4,128)(2,1)}, bf16[4,3072]{1,0:T(4,128)(2,1)}, f32[1,3072]{1,0:T(1,128)}, f32[1,3072]{1,0:T(1,128)}) custom-call(bf16[8,1536]{1,0:T(8,128)(2,1)S(1)} %get-tuple-element.49.own_ref, bf16[16,1536]{1,0:T(8,128)(2,1)S(1)} %collective-permute-done.15.got_ref, f32[1,1536]{1,0:T(1,128)S(1)} %get-tuple-element.32.sums_ref, ...), custom_call_target="tpu_custom_call" | custom-call | tf_op jit(solution)/shard_map/final_rows/pallas_call | solution.py:55
  (4 shorter events, 0.1 us)
Async XLA Ops:
  1.5 5.4 %collective-permute-start = (bf16[8,1536]{1,0:T(8,128)(2,1)S(1)}, bf16[8,1536]{1,0:T(8,128)(2,1)S(1)}, u32[]{:S(2)}, u32[]{:S(2)}) collective-permute-start(bf16[8,1536]{1,0:T(8,128)(2,1)S(1)} %get-tuple-element.56.after_ref), channel_id=1, source_target_pairs={{0,8},{8,0},{1,9},{9,1},{2,10},{10,2},{3,11},{11,3},{4,12},{12,4},... | collective-permute-start | bytes 73736 | tf_op jit(solution)/shard_map/ppermute | solution.py:314
  6.9 9.6 %collective-permute-start.3 = (bf16[16,1536]{1,0:T(8,128)(2,1)S(1)}, bf16[16,1536]{1,0:T(8,128)(2,1)S(1)}, u32[]{:S(2)}, u32[]{:S(2)}) collective-permute-start(bf16[16,1536]{1,0:T(8,128)(2,1)S(1)} %pair_tiles.1.after_ref.refs_3_), channel_id=1, source_target_pairs={{0,1},{1,0},{2,3},{3,2},{4,5},{5,4},{6,7},{7,6},{8,9},{9,8},{10,11... | collective-permute-start | bytes 147464 | tf_op jit(solution)/shard_map/ppermute | solution.py:299
  8.6 8.0 %collective-permute-start.2 = (bf16[16,1536]{1,0:T(8,128)(2,1)S(1)}, bf16[16,1536]{1,0:T(8,128)(2,1)S(1)}, u32[]{:S(2)}, u32[]{:S(2)}) collective-permute-start(bf16[16,1536]{1,0:T(8,128)(2,1)S(1)} %pair_tiles.1.after_ref.refs_3_), channel_id=1, source_target_pairs={{0,2},{1,3},{2,0},{3,1},{4,6},{5,7},{6,4},{7,5},{8,10},{9,11},{10,... | collective-permute-start | bytes 147464 | tf_op jit(solution)/shard_map/ppermute | solution.py:299
  11.2 5.9 %collective-permute-start.1 = (bf16[16,1536]{1,0:T(8,128)(2,1)S(1)}, bf16[16,1536]{1,0:T(8,128)(2,1)S(1)}, u32[]{:S(2)}, u32[]{:S(2)}) collective-permute-start(bf16[16,1536]{1,0:T(8,128)(2,1)S(1)} %pair_tiles.1.after_ref.refs_3_), channel_id=1, source_target_pairs={{0,3},{1,2},{2,1},{3,0},{4,7},{5,6},{6,5},{7,4},{8,11},{9,10},{10,... | collective-permute-start | bytes 147464 | tf_op jit(solution)/shard_map/ppermute | solution.py:299
  17.0 7.8 %copy-start = (f32[3072]{0:T(1024)S(1)}, f32[3072]{0:T(1024)}, u32[]{:S(2)}) copy-start(f32[3072]{0:T(1024)} %param.8) | copy-start | bytes 36868
  17.9 1.3 %collective-permute-start.4 = (bf16[32,1536]{1,0:T(8,128)(2,1)S(1)}, bf16[32,1536]{1,0:T(8,128)(2,1)S(1)}, u32[]{:S(2)}, u32[]{:S(2)}) collective-permute-start(bf16[32,1536]{1,0:T(8,128)(2,1)S(1)} %get-tuple-element.35.after_ref), channel_id=1, source_target_pairs={{0,4},{4,0},{1,5},{5,1},{2,6},{6,2},{3,7},{7,3},{8,12},{12,8},{9,1... | collective-permute-start | bytes 294920 | tf_op jit(solution)/shard_map/ppermute | solution.py:349
  19.3 5.6 %collective-permute-start.5 = (bf16[32,1536]{1,0:T(8,128)(2,1)S(1)}, bf16[32,1536]{1,0:T(8,128)(2,1)S(1)}, u32[]{:S(2)}, u32[]{:S(2)}) collective-permute-start(bf16[32,1536]{1,0:T(8,128)(2,1)S(1)} %add_pre.1.after_ref.own_ref), channel_id=1, source_target_pairs={{0,8},{8,0},{1,9},{9,1},{2,10},{10,2},{3,11},{11,3},{4,12},{12,4},... | collective-permute-start | bytes 294920 | tf_op jit(solution)/shard_map/ppermute | solution.py:352
  22.2 2.0 %collective-permute-start.6 = (bf16[16,1536]{1,0:T(8,128)(2,1)S(1)}, bf16[16,1536]{1,0:T(8,128)(2,1)S(1)}, u32[]{:S(2)}, u32[]{:S(2)}) collective-permute-start(bf16[16,1536]{1,0:T(8,128)(2,1)S(1)} %get-tuple-element.38), channel_id=1, source_target_pairs={{0,4},{4,0},{1,5},{5,1},{2,6},{6,2},{3,7},{7,3},{8,12},{12,8},{9,1... | collective-permute-start | bytes 147464 | tf_op jit(solution)/shard_map/ppermute | solution.py:355
  22.3 1.9 %collective-permute-start.7 = (bf16[16,1536]{1,0:T(8,128)(2,1)S(1)}, bf16[16,1536]{1,0:T(8,128)(2,1)S(1)}, u32[]{:S(2)}, u32[]{:S(2)}) collective-permute-start(bf16[16,1536]{1,0:T(8,128)(2,1)S(1)} %get-tuple-element.39), channel_id=1, source_target_pairs={{0,4},{4,0},{1,5},{5,1},{2,6},{6,2},{3,7},{7,3},{8,12},{12,8},{9,1... | collective-permute-start | bytes 147464 | tf_op jit(solution)/shard_map/ppermute | solution.py:355
  24.2 4.8 %collective-permute-start.8 = (bf16[32,1536]{1,0:T(8,128)(2,1)S(1)}, bf16[32,1536]{1,0:T(8,128)(2,1)S(1)}, u32[]{:S(2)}, u32[]{:S(2)}) collective-permute-start(bf16[32,1536]{1,0:T(8,128)(2,1)S(1)} %add_grad.1.after_ref.own_ref), channel_id=1, source_target_pairs={{0,8},{8,0},{1,9},{9,1},{2,10},{10,2},{3,11},{11,3},{4,12},{12,4},... | collective-permute-start | bytes 294920 | tf_op jit(solution)/shard_map/ppermute | solution.py:358
  25.0 1.5 %collective-permute-start.9 = (bf16[16,1536]{1,0:T(8,128)(2,1)S(1)}, bf16[16,1536]{1,0:T(8,128)(2,1)S(1)}, u32[]{:S(2)}, u32[]{:S(2)}) collective-permute-start(bf16[16,1536]{1,0:T(8,128)(2,1)S(1)} %get-tuple-element.41.low_ref.own_low), channel_id=1, source_target_pairs={{0,4},{4,0},{1,5},{5,1},{2,6},{6,2},{3,7},{7,3},{8,12},{12,8},{9,1... | collective-permute-start | bytes 147464 | tf_op jit(solution)/shard_map/ppermute | solution.py:362
  25.1 1.4 %collective-permute-start.10 = (bf16[16,1536]{1,0:T(8,128)(2,1)S(1)}, bf16[16,1536]{1,0:T(8,128)(2,1)S(1)}, u32[]{:S(2)}, u32[]{:S(2)}) collective-permute-start(bf16[16,1536]{1,0:T(8,128)(2,1)S(1)} %get-tuple-element.42.high_ref.own_high), channel_id=1, source_target_pairs={{0,4},{4,0},{1,5},{5,1},{2,6},{6,2},{3,7},{7,3},{8,12},{12,8},{9,1... | collective-permute-start | bytes 147464 | tf_op jit(solution)/shard_map/ppermute | solution.py:362
  29.1 11.7 %copy-start.1 = (f32[3072]{0:T(1024)S(1)}, f32[3072]{0:T(1024)}, u32[]{:S(2)}) copy-start(f32[3072]{0:T(1024)} %param.10) | copy-start | bytes 36868
  29.1 1.5 %collective-permute-start.11 = (bf16[32,1536]{1,0:T(8,128)(2,1)S(1)}, bf16[32,1536]{1,0:T(8,128)(2,1)S(1)}, u32[]{:S(2)}, u32[]{:S(2)}) collective-permute-start(bf16[32,1536]{1,0:T(8,128)(2,1)S(1)} %grad_pre.1.grad_ref.own_ref), channel_id=1, source_target_pairs={{0,4},{4,0},{1,5},{5,1},{2,6},{6,2},{3,7},{7,3},{8,12},{12,8},{9,1... | collective-permute-start | bytes 294920 | tf_op jit(solution)/shard_map/ppermute | solution.py:376
  32.1 8.7 %collective-permute-start.12 = (bf16[16,1536]{1,0:T(8,128)(2,1)S(1)}, bf16[16,1536]{1,0:T(8,128)(2,1)S(1)}, u32[]{:S(2)}, u32[]{:S(2)}) collective-permute-start(bf16[16,1536]{1,0:T(8,128)(2,1)S(1)} %get-tuple-element.44), channel_id=1, source_target_pairs={{0,3},{1,2},{2,1},{3,0},{4,7},{5,6},{6,5},{7,4},{8,11},{9,10},{10,... | collective-permute-start | bytes 147464 | tf_op jit(solution)/shard_map/ppermute | solution.py:299
  35.3 5.6 %collective-permute-start.13 = (bf16[16,1536]{1,0:T(8,128)(2,1)S(1)}, bf16[16,1536]{1,0:T(8,128)(2,1)S(1)}, u32[]{:S(2)}, u32[]{:S(2)}) collective-permute-start(bf16[16,1536]{1,0:T(8,128)(2,1)S(1)} %get-tuple-element.45), channel_id=1, source_target_pairs={{0,2},{1,3},{2,0},{3,1},{4,6},{5,7},{6,4},{7,5},{8,10},{9,11},{10,... | collective-permute-start | bytes 147464 | tf_op jit(solution)/shard_map/ppermute | solution.py:299
  35.3 5.6 %collective-permute-start.14 = (bf16[16,1536]{1,0:T(8,128)(2,1)S(1)}, bf16[16,1536]{1,0:T(8,128)(2,1)S(1)}, u32[]{:S(2)}, u32[]{:S(2)}) collective-permute-start(bf16[16,1536]{1,0:T(8,128)(2,1)S(1)} %get-tuple-element.46), channel_id=1, source_target_pairs={{0,1},{1,0},{2,3},{3,2},{4,5},{5,4},{6,7},{7,6},{8,9},{9,8},{10,11... | collective-permute-start | bytes 147464 | tf_op jit(solution)/shard_map/ppermute | solution.py:299
  40.9 4.8 %collective-permute-start.15 = (bf16[16,1536]{1,0:T(8,128)(2,1)S(1)}, bf16[16,1536]{1,0:T(8,128)(2,1)S(1)}, u32[]{:S(2)}, u32[]{:S(2)}) collective-permute-start(bf16[16,1536]{1,0:T(8,128)(2,1)S(1)} %get-tuple-element.50), channel_id=1, source_target_pairs={{0,8},{8,0},{1,9},{9,1},{2,10},{10,2},{3,11},{11,3},{4,12},{12,4},... | collective-permute-start | bytes 147464 | tf_op jit(solution)/shard_map/ppermute | solution.py:404

commit v11 on v10

--- a/solution.py
+++ b/solution.py
@@ -132,14 +132,20 @@
         copy.wait()
 
 
-def pair_body(own_ref, got_ref, after_ref, out_ref):
-    out_ref[...] = ordered(lax.axis_index("tok"), own_ref[...], got_ref[...])
+def pair_body(own_ref, got_ref, after_ref, *out_refs):
+    tiles = ordered(lax.axis_index("tok"), own_ref[...], got_ref[...])
+    count, wide = tiles.shape
+    for out_ref in out_refs:
+        out_ref[:, :wide] = tiles
+        if out_ref.shape[1] > wide:
+            out_ref[:, wide:] = jnp.zeros((count, out_ref.shape[1] - wide), bf16)
 
 
 def far_pre_body(rows, count, *refs):
     *piece_refs, w_in_ref = refs[: count + 1]
     sent_ref, x_ref, dy_ref, sums_ref = refs[count + 1 :]
-    mixed = jnp.concatenate([ref[...] for ref in piece_refs], axis=0)
+    wide = x_ref.shape[1]
+    mixed = jnp.concatenate([ref[:, :wide] for ref in piece_refs], axis=0)
     x_cols, dy_cols = apart(mixed.astype(f32), rows)
     sums_ref[...] = jnp.sum(dy_cols, axis=0, keepdims=True)
     x_cols, dy_cols = x_cols.astype(bf16), dy_cols.astype(bf16)
@@ -169,10 +175,10 @@
         own_ref[:, at] = dot_turned(dy_cols, w_out_ref[at, :])
 
 
-def add_body(own_ref, *refs):
-    *got_refs, out_ref = refs
-    got = jnp.concatenate([ref[...] for ref in got_refs], axis=0)
-    out_ref[...] = (own_ref[...] + got.astype(f32)).astype(bf16)
+def add_body(own_ref, got_ref, out_ref):
+    half = own_ref.shape[1]
+    out_ref[:, :half] = (own_ref[...] + got_ref[...].astype(f32)).astype(bf16)
+    out_ref[:, half:] = jnp.zeros((own_ref.shape[0], out_ref.shape[1] - half), bf16)
 
 
 def gelu_body(bias_ref, own_ref, other_ref, after_ref, slopes_ref, *act_refs):
@@ -190,20 +196,20 @@
 
 
 def grad_pre_body(slopes_ref, own_ref, other_ref, after_ref, grad_ref):
-    grad_act = own_ref[...].astype(f32) + other_ref[...].astype(f32)
+    half = pl.ds(0, grad_ref.shape[1])
+    grad_act = own_ref[:, half].astype(f32) + other_ref[:, half].astype(f32)
     grad_ref[...] = (grad_act * slopes_ref[...]).astype(bf16)
 
 
-def own_forward_body(low_ref, high_ref, w_out_ref, out_ref):
-    act = jnp.concatenate([low_ref[...], high_ref[...]], axis=0)
+def own_forward_body(act_ref, w_out_ref, out_ref):
+    act = act_ref[...]
     for at in tiles_of(out_ref.shape[1]):
         out_ref[:, at] = dot(act, w_out_ref[:, at], 1, 0)
 
 
-def far_forward_body(own_low, own_high, low_ref, high_ref, w_out_ref, terms_ref, act_ref, out_ref):
-    own = jnp.concatenate([own_low[...], own_high[...]], axis=0)
-    act = jnp.concatenate([low_ref[...], high_ref[...]], axis=0)
-    act_ref[...] = ordered(lax.axis_index("kin"), own, act, 1)
+def far_forward_body(own_ref, far_ref, w_out_ref, terms_ref, act_ref, out_ref):
+    act = far_ref[...]
+    act_ref[...] = ordered(lax.axis_index("kin"), own_ref[...], act, 1)
     for at in tiles_of(out_ref.shape[1]):
         out_ref[:, at] = terms_ref[:, at] + dot(act, w_out_ref[:, at], 1, 0)
 
@@ -321,10 +327,13 @@
             scratch=[sem((4,))],
             specs=[hbm, pl.BlockSpec(memory_space=pl.ANY)],
         )(in_hbm(weight_out), sent)
-        (tiles,) = call(pair_body, "pair_tiles", [like((2 * pair, wide), bf16)])(
+        tiles, farthest = call(
+            pair_body, "pair_tiles", [like((2 * pair, wide + more), bf16) for more in (0, 128)]
+        )(
             kept(own), kept(got), kept(out_far)
         )
-        pieces = [across(tiles, shift) for shift in reversed(range(1, nn))] + [tiles]
+        pieces = [across(tiles, shift) for shift in range(1, nn - 1)]
+        pieces = [across(farthest, nn - 1)] + pieces[::-1] + [tiles]
         in_far, in_own, out_own = call(
             load_body,
             "load_rest",
@@ -338,6 +347,7 @@
         def product(body, name, outs, *args):
             return call(body, name, outs, grant=8 * MIB)(*map(kept, args))
 
+        crossing = like((count, half + 128), bf16)
         side, ends = like((count, half), bf16), like((count, wide), f32)
         sent, x_cols, dy_cols, sums = product(
             functools.partial(far_pre_body, rows, nn),
@@ -348,13 +358,13 @@
         )
         got = lax.ppermute(sent, "kin", swap)
         (own,) = product(own_pre_body, "own_pre", [like((count, half), f32)], x_cols, in_own, sent)
-        (own_pre,) = product(add_body, "add_pre", [side], own, got)
+        (own_pre,) = product(add_body, "add_pre", [crossing], own, got)
         other_pre = lax.ppermute(own_pre, "tok", swap)
-        sides = [like((count // 2, half), bf16)] * 2
+        sides = [side]
         sent = product(far_grad_body, "far_grad", sides, dy_cols, out_far, own_pre)
         got = [lax.ppermute(part, "kin", swap) for part in sent]
         (own,) = product(own_grad_body, "own_grad", [like((count, half), f32)], dy_cols, out_own)
-        (own_grad,) = product(add_body, "add_grad", [side], own, *got)
+        (own_grad,) = product(add_body, "add_grad", [crossing], own, *got)
         other_grad = lax.ppermute(own_grad, "tok", swap)
         slopes, *act_own = call(gelu_body, "gelu", [like((count, half), f32)] + sides)(
             bias_in.reshape(1, hid), kept(own_pre), kept(other_pre), kept(own_grad)

time: 46.7 us -> 46.4 us (level)
  starting transfers between devices: 15.9 us -> 15.2 us
    ppermute x1, waiting for transfers between devices: 1.67 us -> 2.38 us  [on_device(): other_grad = lax.ppermute(own_grad, 'tok', swap)]
    ppermute x2 -> x1, starting transfers between devices: 0.56 us -> 0.06 us  [on_device(): got = [lax.ppermute(part, 'kin', swap) for part in sent]]
  transfers between devices with their start and end apart: 16 -> 14, of which waited for: 3 -> 3; matrix products, arithmetic and copies ran while one was open for 0% -> 0% of each run, Pallas kernels for 50% -> 50%
where the time goes in v11:
time: 46.4 us; the launch traced here: 46.1 us
  Pallas kernels  26.2 us (56%)
  starting transfers between devices  15.2 us (33%)
  waiting for transfers between devices  3.04 us (7%)
  other arithmetic  0.86 us (2%)
  between operations  0.82 us (2%)
    pallas_call x17, Pallas kernels, run(): pl.pallas_call(body, out_shape=shapes, in_specs=specs or [whole] * len(ar...  17.8 us
    ppermute x6, starting transfers between devices, across(): return lax.ppermute(array, 'nout', [(i, i ^ shift) for i in range(nn)])  8.92 us
    pallas_call x2, Pallas kernels, outer(): pl.pallas_call(functools.partial(outer_body, most), out_shape=like((high,...  8.38 us
    ppermute x2, starting transfers between devices, on_device(): got = lax.ppermute(sent, 'tok', swap)  3.67 us
    ppermute x1, waiting for transfers between devices, on_device(): other_grad = lax.ppermute(own_grad, 'tok', swap)  2.38 us
    ppermute x1, starting transfers between devices, on_device(): other_pre = lax.ppermute(own_pre, 'tok', swap)  1.49 us
  transfers between devices with their start and end apart: 14, of which 3 were waited for; matrix products, arithmetic and copies ran while one was open for 0% of the time, Pallas kernels for 50%

profile of v11, /device:TPU:0, one launch (start us, length us, event | category | flops | bytes accessed | tf_op | source)
XLA Modules:
  0.0 46.1 jit_solution(3027985312096794870)
XLA Ops:
  0.6 0.9 %fusion = (bf16[8,1536]{1,0:T(8,128)(2,1)S(1)}, bf16[8,1536]{1,0:T(8,128)(2,1)S(1)}) fusion(s32[]{:T(128)S(6)} %select_n.7, bf16[4,3072]{1,0:T(4,128)(2,1)} %param.6, bf16[4,3072]{1,0:T(4,128)(2,1)} %param.11, s32[]{:T(128)S(6)} %select_n.6), kind=kLoop, calls=%fused_computation.4 | loop fusion | flops 98304 | bytes 98312 | tf_op jit(solution)/shard_map/concatenate | solution.py:316
  1.5 3.0 %collective-permute-start = (bf16[8,1536]{1,0:T(8,128)(2,1)S(1)}, bf16[8,1536]{1,0:T(8,128)(2,1)S(1)}, u32[]{:S(2)}, u32[]{:S(2)}) collective-permute-start(bf16[8,1536]{1,0:T(8,128)(2,1)S(1)} %get-tuple-element.54.after_ref), channel_id=1, source_target_pairs={{0,8},{8,0},{1,9},{9,1},{2,10},{10,2},{3,11},{11,3},{4,12},{12,4},... | collective-permute-start | bytes 73736 | tf_op jit(solution)/shard_map/ppermute | solution.py:320
  4.5 2.4 %load_far.1.after_ref.w_out_ref = bf16[1536,1536]{1,0:T(8,128)(2,1)S(1)} custom-call(bf16[3072,1536]{1,0:T(8,128)(2,1)} %out_hbm_ref.1, bf16[8,1536]{1,0:T(8,128)(2,1)S(1)} %get-tuple-element.54.after_ref), custom_call_target="tpu_custom_call" | custom-call | bytes 4718592 | tf_op jit(solution)/shard_map/load_far/pallas_call | solution.py:55
  6.9 0.0 collective-permute-done.got_ref
  6.9 3.7 %collective-permute-start.1 = (bf16[16,1664]{1,0:T(8,128)(2,1)S(1)}, bf16[16,1664]{1,0:T(8,128)(2,1)S(1)}, u32[]{:S(2)}, u32[]{:S(2)}) collective-permute-start(bf16[16,1664]{1,0:T(8,128)(2,1)S(1)} %get-tuple-element.30), channel_id=1, source_target_pairs={{0,3},{1,2},{2,1},{3,0},{4,7},{5,6},{6,5},{7,4},{8,11},{9,10},{10,... | collective-permute-start | bytes 159752 | tf_op jit(solution)/shard_map/ppermute | solution.py:305
  10.6 0.0 collective-permute-start.3
  10.6 0.8 %collective-permute-start.2 = (bf16[16,1536]{1,0:T(8,128)(2,1)S(1)}, bf16[16,1536]{1,0:T(8,128)(2,1)S(1)}, u32[]{:S(2)}, u32[]{:S(2)}) collective-permute-start(bf16[16,1536]{1,0:T(8,128)(2,1)S(1)} %get-tuple-element.31.after_ref.refs_3_), channel_id=1, source_target_pairs={{0,2},{1,3},{2,0},{3,1},{4,6},{5,7},{6,4},{7,5},{8,10},{9,11},{10,... | collective-permute-start | bytes 147464 | tf_op jit(solution)/shard_map/ppermute | solution.py:305
  11.4 5.2 %load_rest.1 = (bf16[1536,1536]{1,0:T(8,128)(2,1)S(1)}, bf16[1536,1536]{1,0:T(8,128)(2,1)S(1)}, bf16[1536,1536]{1,0:T(8,128)(2,1)S(1)}) custom-call(bf16[1536,3072]{1,0:T(8,128)(2,1)} %in_hbm_ref.1, bf16[3072,1536]{1,0:T(8,128)(2,1)} %out_hbm_ref.1, bf16[16,1536]{1,0:T(8,128)(2,1)S(1)} %get-tuple-element.31.after_ref.refs_3_), custom_call_target="tpu_custom_call" | custom-call | bytes 14155776 | tf_op jit(solution)/shard_map/load_rest/pallas_call | solution.py:55
  16.5 0.0 collective-permute-done.3.refs_2_
  16.6 0.0 collective-permute-done.2.refs_1_
  16.6 0.0 collective-permute-done.1.refs_0_
  16.6 0.0 copy-start
  16.6 0.9 %far_pre.1 = (bf16[32,1536]{1,0:T(8,128)(2,1)S(1)}, bf16[32,1536]{1,0:T(8,128)(2,1)S(1)}, bf16[32,1536]{1,0:T(8,128)(2,1)S(1)}, f32[1,1536]{1,0:T(1,128)S(1)}) custom-call(bf16[16,1664]{1,0:T(8,128)(2,1)S(1)} %collective-permute-done.1.refs_0_, bf16[16,1536]{1,0:T(8,128)(2,1)S(1)} %collective-permute-done.2.refs_1_, ...), custom_call_target="tpu_custom_call" | custom-call | tf_op jit(solution)/shard_map/far_pre/pallas_call | solution.py:55
  17.5 0.0 collective-permute-start.4
  17.5 0.9 %own_pre.1.own_ref = f32[32,1536]{1,0:T(8,128)S(1)} custom-call(bf16[32,1536]{1,0:T(8,128)(2,1)S(1)} %get-tuple-element.34.x_ref.left_ref, bf16[1536,1536]{1,0:T(8,128)(2,1)S(1)} %get-tuple-element.35.w_in_ref, bf16[32,1536]{1,0:T(8,128)(2,1)S(1)} %get-tuple-element.36.after_ref), custom_call_target="tpu_custom_call" | custom-call | tf_op jit(solution)/shard_map/own_pre/pallas_call | solution.py:55
  18.4 0.4 collective-permute-done.4.got_ref
  18.8 1.5 %collective-permute-start.5 = (bf16[32,1664]{1,0:T(8,128)(2,1)S(1)}, bf16[32,1664]{1,0:T(8,128)(2,1)S(1)}, u32[]{:S(2)}, u32[]{:S(2)}) collective-permute-start(bf16[32,1664]{1,0:T(8,128)(2,1)S(1)} %add_pre.1.after_ref.own_ref), channel_id=1, source_target_pairs={{0,8},{8,0},{1,9},{9,1},{2,10},{10,2},{3,11},{11,3},{4,12},{12,4},... | collective-permute-start | bytes 319496 | tf_op jit(solution)/shard_map/ppermute | solution.py:362
  20.3 1.4 %far_grad.1 = bf16[32,1536]{1,0:T(8,128)(2,1)S(1)} custom-call(bf16[32,1536]{1,0:T(8,128)(2,1)S(1)} %get-tuple-element.37.dy_ref.right_ref, bf16[1536,1536]{1,0:T(8,128)(2,1)S(1)} %load_far.1.after_ref.w_out_ref, bf16[32,1664]{1,0:T(8,128)(2,1)S(1)} %add_pre.1.after_ref.own_ref), custom_call_target="tpu_custom_call" | custom-call | tf_op jit(solution)/shard_map/far_grad/pallas_call | solution.py:55
  21.7 0.1 collective-permute-start.6
  21.8 1.4 %own_grad.1.own_ref = f32[32,1536]{1,0:T(8,128)S(1)} custom-call(bf16[32,1536]{1,0:T(8,128)(2,1)S(1)} %get-tuple-element.37.dy_ref.right_ref, bf16[1536,1536]{1,0:T(8,128)(2,1)S(1)} %get-tuple-element.38.w_out_ref), custom_call_target="tpu_custom_call" | custom-call | tf_op jit(solution)/shard_map/own_grad/pallas_call | solution.py:55
  23.2 0.0 collective-permute-done.6.got_ref
  23.3 0.7 %collective-permute-start.7 = (bf16[32,1664]{1,0:T(8,128)(2,1)S(1)}, bf16[32,1664]{1,0:T(8,128)(2,1)S(1)}, u32[]{:S(2)}, u32[]{:S(2)}) collective-permute-start(bf16[32,1664]{1,0:T(8,128)(2,1)S(1)} %add_grad.1.after_ref.own_ref), channel_id=1, source_target_pairs={{0,8},{8,0},{1,9},{9,1},{2,10},{10,2},{3,11},{11,3},{4,12},{12,4},... | collective-permute-start | bytes 319496 | tf_op jit(solution)/shard_map/ppermute | solution.py:368
  23.9 0.0 collective-permute-done.5.other_ref
  23.9 0.0 copy-done
  23.9 0.1 gelu.1
  24.0 0.3 collective-permute-start.8
  24.3 0.9 %own_forward.1.terms_ref = f32[32,1536]{1,0:T(8,128)S(1)} custom-call(bf16[32,1536]{1,0:T(8,128)(2,1)S(1)} %get-tuple-element.40.act_ref.own_ref, bf16[1536,1536]{1,0:T(8,128)(2,1)S(1)} %get-tuple-element.38.w_out_ref), custom_call_target="tpu_custom_call" | custom-call | tf_op jit(solution)/shard_map/own_forward/pallas_call | solution.py:55
  25.2 0.2 collective-permute-done.8.far_ref
  25.4 0.9 %far_forward.1 = (bf16[32,3072]{1,0:T(8,128)(2,1)S(1)}, f32[32,1536]{1,0:T(8,128)S(1)}) custom-call(bf16[32,1536]{1,0:T(8,128)(2,1)S(1)} %get-tuple-element.40.act_ref.own_ref, bf16[32,1536]{1,0:T(8,128)(2,1)S(1)} %collective-permute-done.8.far_ref, bf16[1536,1536]{1,0:T(8,128)(2,1)S(1)} %load_far.1.after_ref.w_out_ref, f32[32,1536]{1,0:T(8,128)S(1)} %own_forward.1.terms_ref), custom_call_target="tpu_custom_call" | custom-call | tf_op jit(solution)/shard_map/far_forward/pallas_call | solution.py:55
  26.3 2.4 %collective-permute-done.7.other_ref = bf16[32,1664]{1,0:T(8,128)(2,1)S(1)} collective-permute-done((bf16[32,1664]{1,0:T(8,128)(2,1)S(1)}, bf16[32,1664]{1,0:T(8,128)(2,1)S(1)}, u32[]{:S(2)}, u32[]{:S(2)}) %collective-permute-start.7) | collective-permute-done | bytes 106528 | tf_op jit(solution)/shard_map/ppermute | solution.py:368
  28.7 0.0 copy-start.1
  28.7 0.1 collective-permute-start.9
  28.8 1.4 %own_backward.1.backward_ref = f32[32,1536]{1,0:T(8,128)S(1)} custom-call(bf16[32,1536]{1,0:T(8,128)(2,1)S(1)} %grad_pre.1.grad_ref.own_ref, bf16[1536,1536]{1,0:T(8,128)(2,1)S(1)} %get-tuple-element.35.w_in_ref), custom_call_target="tpu_custom_call" | custom-call | tf_op jit(solution)/shard_map/own_backward/pallas_call | solution.py:55
  30.2 0.0 collective-permute-done.9.far_ref
  30.2 1.5 %output_blocks.1 = (bf16[32,3072]{1,0:T(8,128)(2,1)S(1)}, bf16[16,1536]{1,0:T(8,128)(2,1)S(1)}, bf16[16,1536]{1,0:T(8,128)(2,1)S(1)}, bf16[16,1536]{1,0:T(8,128)(2,1)S(1)}, bf16[16,1536]{1,0:T(8,128)(2,1)S(1)}) custom-call(bf16[32,1536]{1,0:T(8,128)(2,1)S(1)} %grad_pre.1.grad_ref.own_ref, bf16[32,1536]{1,0:T(8,128)(2,1)S(1)} %collective-permute-done.9.far_ref, ...), custom_call_target="tpu_custom_call" | custom-call | tf_op jit(solution)/shard_map/output_blocks/pallas_call | solution.py:55
  31.7 3.7 %collective-permute-start.10 = (bf16[16,1536]{1,0:T(8,128)(2,1)S(1)}, bf16[16,1536]{1,0:T(8,128)(2,1)S(1)}, u32[]{:S(2)}, u32[]{:S(2)}) collective-permute-start(bf16[16,1536]{1,0:T(8,128)(2,1)S(1)} %get-tuple-element.42), channel_id=1, source_target_pairs={{0,3},{1,2},{2,1},{3,0},{4,7},{5,6},{6,5},{7,4},{8,11},{9,10},{10,... | collective-permute-start | bytes 147464 | tf_op jit(solution)/shard_map/ppermute | solution.py:305
  35.4 0.0 collective-permute-start.11
  35.4 0.8 %collective-permute-start.12 = (bf16[16,1536]{1,0:T(8,128)(2,1)S(1)}, bf16[16,1536]{1,0:T(8,128)(2,1)S(1)}, u32[]{:S(2)}, u32[]{:S(2)}) collective-permute-start(bf16[16,1536]{1,0:T(8,128)(2,1)S(1)} %get-tuple-element.44), channel_id=1, source_target_pairs={{0,1},{1,0},{2,3},{3,2},{4,5},{5,4},{6,7},{7,6},{8,9},{9,8},{10,11... | collective-permute-start | bytes 147464 | tf_op jit(solution)/shard_map/ppermute | solution.py:305
  36.2 4.3 %weight_in_grad.1.refs_4_ = bf16[1536,3072]{1,0:T(8,128)(2,1)} custom-call(bf16[32,1536]{1,0:T(8,128)(2,1)S(1)} %get-tuple-element.34.x_ref.left_ref, bf16[32,3072]{1,0:T(8,128)(2,1)S(1)} %get-tuple-element.46.right_ref.hidden_ref), custom_call_target="tpu_custom_call" | custom-call | flops 301989888 | bytes 9437184 | tf_op jit(solution)/shard_map/weight_in_grad/pallas_call | solution.py:251
  40.5 0.0 collective-permute-done.10.refs_0_
  40.5 0.0 collective-permute-done.11.refs_1_
  40.5 0.0 collective-permute-done.12.refs_2_
  40.5 0.0 copy-done.1
  40.5 0.1 sum_blocks.1
  40.6 0.7 %collective-permute-start.13 = (bf16[16,1536]{1,0:T(8,128)(2,1)S(1)}, bf16[16,1536]{1,0:T(8,128)(2,1)S(1)}, u32[]{:S(2)}, u32[]{:S(2)}) collective-permute-start(bf16[16,1536]{1,0:T(8,128)(2,1)S(1)} %get-tuple-element.48), channel_id=1, source_target_pairs={{0,8},{8,0},{1,9},{9,1},{2,10},{10,2},{3,11},{11,3},{4,12},{12,4},... | collective-permute-start | bytes 147464 | tf_op jit(solution)/shard_map/ppermute | solution.py:414
  41.3 4.1 %weight_out_grad.1 = bf16[3072,1536]{1,0:T(8,128)(2,1)} custom-call(bf16[32,3072]{1,0:T(8,128)(2,1)S(1)} %get-tuple-element.51.left_ref, bf16[32,1536]{1,0:T(8,128)(2,1)S(1)} %get-tuple-element.37.dy_ref.right_ref), custom_call_target="tpu_custom_call" | custom-call | flops 301989888 | bytes 9437184 | tf_op jit(solution)/shard_map/weight_out_grad/pallas_call | solution.py:251
  45.4 0.0 collective-permute-done.13.got_ref
  45.4 0.7 %final_rows.1 = (bf16[4,3072]{1,0:T(4,128)(2,1)}, bf16[4,3072]{1,0:T(4,128)(2,1)}, f32[1,3072]{1,0:T(1,128)}, f32[1,3072]{1,0:T(1,128)}) custom-call(bf16[8,1536]{1,0:T(8,128)(2,1)S(1)} %get-tuple-element.47.own_ref, bf16[16,1536]{1,0:T(8,128)(2,1)S(1)} %collective-permute-done.13.got_ref, f32[1,1536]{1,0:T(1,128)S(1)} %get-tuple-element.33.sums_ref, ...), custom_call_target="tpu_custom_call" | custom-call | tf_op jit(solution)/shard_map/final_rows/pallas_call | solution.py:55
  (4 shorter events, 0.1 us)
Async XLA Ops:
  1.5 5.4 %collective-permute-start = (bf16[8,1536]{1,0:T(8,128)(2,1)S(1)}, bf16[8,1536]{1,0:T(8,128)(2,1)S(1)}, u32[]{:S(2)}, u32[]{:S(2)}) collective-permute-start(bf16[8,1536]{1,0:T(8,128)(2,1)S(1)} %get-tuple-element.54.after_ref), channel_id=1, source_target_pairs={{0,8},{8,0},{1,9},{9,1},{2,10},{10,2},{3,11},{11,3},{4,12},{12,4},... | collective-permute-start | bytes 73736 | tf_op jit(solution)/shard_map/ppermute | solution.py:320
  6.9 9.6 %collective-permute-start.1 = (bf16[16,1664]{1,0:T(8,128)(2,1)S(1)}, bf16[16,1664]{1,0:T(8,128)(2,1)S(1)}, u32[]{:S(2)}, u32[]{:S(2)}) collective-permute-start(bf16[16,1664]{1,0:T(8,128)(2,1)S(1)} %get-tuple-element.30), channel_id=1, source_target_pairs={{0,3},{1,2},{2,1},{3,0},{4,7},{5,6},{6,5},{7,4},{8,11},{9,10},{10,... | collective-permute-start | bytes 159752 | tf_op jit(solution)/shard_map/ppermute | solution.py:305
  10.6 6.0 %collective-permute-start.3 = (bf16[16,1536]{1,0:T(8,128)(2,1)S(1)}, bf16[16,1536]{1,0:T(8,128)(2,1)S(1)}, u32[]{:S(2)}, u32[]{:S(2)}) collective-permute-start(bf16[16,1536]{1,0:T(8,128)(2,1)S(1)} %get-tuple-element.31.after_ref.refs_3_), channel_id=1, source_target_pairs={{0,1},{1,0},{2,3},{3,2},{4,5},{5,4},{6,7},{7,6},{8,9},{9,8},{10,11... | collective-permute-start | bytes 147464 | tf_op jit(solution)/shard_map/ppermute | solution.py:305
  10.6 6.0 %collective-permute-start.2 = (bf16[16,1536]{1,0:T(8,128)(2,1)S(1)}, bf16[16,1536]{1,0:T(8,128)(2,1)S(1)}, u32[]{:S(2)}, u32[]{:S(2)}) collective-permute-start(bf16[16,1536]{1,0:T(8,128)(2,1)S(1)} %get-tuple-element.31.after_ref.refs_3_), channel_id=1, source_target_pairs={{0,2},{1,3},{2,0},{3,1},{4,6},{5,7},{6,4},{7,5},{8,10},{9,11},{10,... | collective-permute-start | bytes 147464 | tf_op jit(solution)/shard_map/ppermute | solution.py:305
  16.6 7.4 %copy-start = (f32[3072]{0:T(1024)S(1)}, f32[3072]{0:T(1024)}, u32[]{:S(2)}) copy-start(f32[3072]{0:T(1024)} %param.8) | copy-start | bytes 36868
  17.5 1.3 %collective-permute-start.4 = (bf16[32,1536]{1,0:T(8,128)(2,1)S(1)}, bf16[32,1536]{1,0:T(8,128)(2,1)S(1)}, u32[]{:S(2)}, u32[]{:S(2)}) collective-permute-start(bf16[32,1536]{1,0:T(8,128)(2,1)S(1)} %get-tuple-element.36.after_ref), channel_id=1, source_target_pairs={{0,4},{4,0},{1,5},{5,1},{2,6},{6,2},{3,7},{7,3},{8,12},{12,8},{9,1... | collective-permute-start | bytes 294920 | tf_op jit(solution)/shard_map/ppermute | solution.py:359
  18.8 5.1 %collective-permute-start.5 = (bf16[32,1664]{1,0:T(8,128)(2,1)S(1)}, bf16[32,1664]{1,0:T(8,128)(2,1)S(1)}, u32[]{:S(2)}, u32[]{:S(2)}) collective-permute-start(bf16[32,1664]{1,0:T(8,128)(2,1)S(1)} %add_pre.1.after_ref.own_ref), channel_id=1, source_target_pairs={{0,8},{8,0},{1,9},{9,1},{2,10},{10,2},{3,11},{11,3},{4,12},{12,4},... | collective-permute-start | bytes 319496 | tf_op jit(solution)/shard_map/ppermute | solution.py:362
  21.7 1.5 %collective-permute-start.6 = (bf16[32,1536]{1,0:T(8,128)(2,1)S(1)}, bf16[32,1536]{1,0:T(8,128)(2,1)S(1)}, u32[]{:S(2)}, u32[]{:S(2)}) collective-permute-start(bf16[32,1536]{1,0:T(8,128)(2,1)S(1)} %far_grad.1), channel_id=1, source_target_pairs={{0,4},{4,0},{1,5},{5,1},{2,6},{6,2},{3,7},{7,3},{8,12},{12,8},{9,1... | collective-permute-start | bytes 294920 | tf_op jit(solution)/shard_map/ppermute | solution.py:365
  23.3 5.4 %collective-permute-start.7 = (bf16[32,1664]{1,0:T(8,128)(2,1)S(1)}, bf16[32,1664]{1,0:T(8,128)(2,1)S(1)}, u32[]{:S(2)}, u32[]{:S(2)}) collective-permute-start(bf16[32,1664]{1,0:T(8,128)(2,1)S(1)} %add_grad.1.after_ref.own_ref), channel_id=1, source_target_pairs={{0,8},{8,0},{1,9},{9,1},{2,10},{10,2},{3,11},{11,3},{4,12},{12,4},... | collective-permute-start | bytes 319496 | tf_op jit(solution)/shard_map/ppermute | solution.py:368
  24.0 1.4 %collective-permute-start.8 = (bf16[32,1536]{1,0:T(8,128)(2,1)S(1)}, bf16[32,1536]{1,0:T(8,128)(2,1)S(1)}, u32[]{:S(2)}, u32[]{:S(2)}) collective-permute-start(bf16[32,1536]{1,0:T(8,128)(2,1)S(1)} %get-tuple-element.40.act_ref.own_ref), channel_id=1, source_target_pairs={{0,4},{4,0},{1,5},{5,1},{2,6},{6,2},{3,7},{7,3},{8,12},{12,8},{9,1... | collective-permute-start | bytes 294920 | tf_op jit(solution)/shard_map/ppermute | solution.py:372
  28.7 11.8 %copy-start.1 = (f32[3072]{0:T(1024)S(1)}, f32[3072]{0:T(1024)}, u32[]{:S(2)}) copy-start(f32[3072]{0:T(1024)} %param.10) | copy-start | bytes 36868
  28.7 1.5 %collective-permute-start.9 = (bf16[32,1536]{1,0:T(8,128)(2,1)S(1)}, bf16[32,1536]{1,0:T(8,128)(2,1)S(1)}, u32[]{:S(2)}, u32[]{:S(2)}) collective-permute-start(bf16[32,1536]{1,0:T(8,128)(2,1)S(1)} %grad_pre.1.grad_ref.own_ref), channel_id=1, source_target_pairs={{0,4},{4,0},{1,5},{5,1},{2,6},{6,2},{3,7},{7,3},{8,12},{12,8},{9,1... | collective-permute-start | bytes 294920 | tf_op jit(solution)/shard_map/ppermute | solution.py:386
  31.7 8.8 %collective-permute-start.10 = (bf16[16,1536]{1,0:T(8,128)(2,1)S(1)}, bf16[16,1536]{1,0:T(8,128)(2,1)S(1)}, u32[]{:S(2)}, u32[]{:S(2)}) collective-permute-start(bf16[16,1536]{1,0:T(8,128)(2,1)S(1)} %get-tuple-element.42), channel_id=1, source_target_pairs={{0,3},{1,2},{2,1},{3,0},{4,7},{5,6},{6,5},{7,4},{8,11},{9,10},{10,... | collective-permute-start | bytes 147464 | tf_op jit(solution)/shard_map/ppermute | solution.py:305
  35.4 5.1 %collective-permute-start.11 = (bf16[16,1536]{1,0:T(8,128)(2,1)S(1)}, bf16[16,1536]{1,0:T(8,128)(2,1)S(1)}, u32[]{:S(2)}, u32[]{:S(2)}) collective-permute-start(bf16[16,1536]{1,0:T(8,128)(2,1)S(1)} %get-tuple-element.43), channel_id=1, source_target_pairs={{0,2},{1,3},{2,0},{3,1},{4,6},{5,7},{6,4},{7,5},{8,10},{9,11},{10,... | collective-permute-start | bytes 147464 | tf_op jit(solution)/shard_map/ppermute | solution.py:305
  35.4 5.1 %collective-permute-start.12 = (bf16[16,1536]{1,0:T(8,128)(2,1)S(1)}, bf16[16,1536]{1,0:T(8,128)(2,1)S(1)}, u32[]{:S(2)}, u32[]{:S(2)}) collective-permute-start(bf16[16,1536]{1,0:T(8,128)(2,1)S(1)} %get-tuple-element.44), channel_id=1, source_target_pairs={{0,1},{1,0},{2,3},{3,2},{4,5},{5,4},{6,7},{7,6},{8,9},{9,8},{10,11... | collective-permute-start | bytes 147464 | tf_op jit(solution)/shard_map/ppermute | solution.py:305
  40.6 4.8 %collective-permute-start.13 = (bf16[16,1536]{1,0:T(8,128)(2,1)S(1)}, bf16[16,1536]{1,0:T(8,128)(2,1)S(1)}, u32[]{:S(2)}, u32[]{:S(2)}) collective-permute-start(bf16[16,1536]{1,0:T(8,128)(2,1)S(1)} %get-tuple-element.48), channel_id=1, source_target_pairs={{0,8},{8,0},{1,9},{9,1},{2,10},{10,2},{3,11},{11,3},{4,12},{12,4},... | collective-permute-start | bytes 147464 | tf_op jit(solution)/shard_map/ppermute | solution.py:414

commit v12 on v11

--- a/solution.py
+++ b/solution.py
@@ -105,27 +105,23 @@
     return pl.ds(pl.multiple_of(at * size, size), size)
 
 
-def quarters(source, target, sems):
-    size = target.shape[0] // 4
+def half_tiles(half, mine):
+    core = lax.axis_index("kin")
+    first = (core if mine else 1 - core) * half
+    tile = tile_of(half, 512)
     return [
-        pltpu.make_async_copy(source.at[part, :], target.at[part, :], sems.at[i])
+        (pl.ds(i * tile, tile), pl.ds(pl.multiple_of(first + i * tile, tile), tile))
+        for i in range(half // tile)
+    ]
+
+
+def load_body(mine, hbm_ref, after_ref, out_ref, sems):
+    size = out_ref.shape[0] // 4
+    source = hbm_ref.at[:, half_of(out_ref.shape[1], mine)]
+    copies = [
+        pltpu.make_async_copy(source.at[part, :], out_ref.at[part, :], sems.at[i])
         for i, part in enumerate(pl.ds(j * size, size) for j in range(4))
     ]
-
-
-def load_far_body(hbm_ref, after_ref, out_ref, sems):
-    copies = quarters(hbm_ref.at[half_of(out_ref.shape[0], False), :], out_ref, sems)
-    for copy in copies:
-        copy.start()
-    for copy in copies:
-        copy.wait()
-
-
-def load_body(in_hbm_ref, out_hbm_ref, after_ref, far_ref, own_ref, out_ref, sems):
-    half = own_ref.shape[1]
-    copies = quarters(in_hbm_ref.at[:, half_of(half, False)], far_ref, sems.at[0])
-    copies += quarters(in_hbm_ref.at[:, half_of(half, True)], own_ref, sems.at[1])
-    copies += quarters(out_hbm_ref.at[half_of(half, True), :], out_ref, sems.at[2])
     for copy in copies:
         copy.start()
     for copy in copies:
@@ -142,8 +138,8 @@
 
 
 def far_pre_body(rows, count, *refs):
-    *piece_refs, w_in_ref = refs[: count + 1]
-    sent_ref, x_ref, dy_ref, sums_ref = refs[count + 1 :]
+    *piece_refs, w_in_ref, after_ref = refs[: count + 2]
+    sent_ref, x_ref, dy_ref, sums_ref = refs[count + 2 :]
     wide = x_ref.shape[1]
     mixed = jnp.concatenate([ref[:, :wide] for ref in piece_refs], axis=0)
     x_cols, dy_cols = apart(mixed.astype(f32), rows)
@@ -163,16 +159,16 @@
 def far_grad_body(dy_ref, w_out_ref, after_ref, *sent_refs):
     dy_cols = dy_ref[...]
     size = sent_refs[0].shape[0]
-    for at in tiles_of(sent_refs[0].shape[1]):
-        terms = dot_turned(dy_cols, w_out_ref[at, :]).astype(bf16)
+    for at, there in half_tiles(sent_refs[0].shape[1], False):
+        terms = dot_turned(dy_cols, w_out_ref[there, :]).astype(bf16)
         for i, sent_ref in enumerate(sent_refs):
             sent_ref[:, at] = terms[i * size : (i + 1) * size]
 
 
 def own_grad_body(dy_ref, w_out_ref, own_ref):
     dy_cols = dy_ref[...]
-    for at in tiles_of(own_ref.shape[1]):
-        own_ref[:, at] = dot_turned(dy_cols, w_out_ref[at, :])
+    for at, there in half_tiles(own_ref.shape[1], True):
+        own_ref[:, at] = dot_turned(dy_cols, w_out_ref[there, :])
 
 
 def add_body(own_ref, got_ref, out_ref):
@@ -203,15 +199,17 @@
 
 def own_forward_body(act_ref, w_out_ref, out_ref):
     act = act_ref[...]
+    part = half_of(act.shape[1], True)
     for at in tiles_of(out_ref.shape[1]):
-        out_ref[:, at] = dot(act, w_out_ref[:, at], 1, 0)
+        out_ref[:, at] = dot(act, w_out_ref[part, at], 1, 0)
 
 
 def far_forward_body(own_ref, far_ref, w_out_ref, terms_ref, act_ref, out_ref):
     act = far_ref[...]
     act_ref[...] = ordered(lax.axis_index("kin"), own_ref[...], act, 1)
+    part = half_of(act.shape[1], False)
     for at in tiles_of(out_ref.shape[1]):
-        out_ref[:, at] = terms_ref[:, at] + dot(act, w_out_ref[:, at], 1, 0)
+        out_ref[:, at] = terms_ref[:, at] + dot(act, w_out_ref[part, at], 1, 0)
 
 
 def own_backward_body(grad_ref, w_in_ref, out_ref):
@@ -310,7 +308,6 @@
         half = hid // 2
         pair = 2 * rows
         count = 2 * nn * rows
-        piece = 2 * wide * half
         sem = pltpu.SemaphoreType.DMA
 
         mine = jnp.concatenate([tokens, grad_out], axis=0)
@@ -318,31 +315,26 @@
         own = lax.dynamic_slice_in_dim(mine, me * wide, wide, 1)
         sent = lax.dynamic_slice_in_dim(mine, (1 - me) * wide, wide, 1)
         got = lax.ppermute(sent, "tok", swap)
-        (out_far,) = call(
-            load_far_body,
-            "load_far",
-            [like((half, wide), bf16)],
-            grant=MIB,
-            moved=piece,
-            scratch=[sem((4,))],
-            specs=[hbm, pl.BlockSpec(memory_space=pl.ANY)],
-        )(in_hbm(weight_out), sent)
+
+        def load_in(mine, name, after):
+            return call(
+                functools.partial(load_body, mine),
+                name,
+                [like((wide, half), bf16)],
+                grant=MIB,
+                scratch=[sem((4,))],
+                specs=[hbm, pl.BlockSpec(memory_space=pl.ANY)],
+            )(in_hbm(weight_in), after)
+
+        (in_far,) = load_in(False, "load_far", sent)
         tiles, farthest = call(
             pair_body, "pair_tiles", [like((2 * pair, wide + more), bf16) for more in (0, 128)]
         )(
-            kept(own), kept(got), kept(out_far)
+            kept(own), kept(got), kept(in_far)
         )
         pieces = [across(tiles, shift) for shift in range(1, nn - 1)]
         pieces = [across(farthest, nn - 1)] + pieces[::-1] + [tiles]
-        in_far, in_own, out_own = call(
-            load_body,
-            "load_rest",
-            [like((wide, half), bf16)] * 2 + [like((half, wide), bf16)],
-            grant=MIB,
-            moved=3 * piece,
-            scratch=[sem((3, 4))],
-            specs=[hbm] * 2 + [pl.BlockSpec(memory_space=pl.ANY)],
-        )(in_hbm(weight_in), in_hbm(weight_out), tiles)
+        (in_own,) = load_in(True, "load_own", tiles)
 
         def product(body, name, outs, *args):
             return call(body, name, outs, grant=8 * MIB)(*map(kept, args))
@@ -355,29 +347,30 @@
             [side] + [like((count, wide), bf16)] * 2 + [like((1, wide), f32)],
             *pieces,
             in_far,
+            in_own,
         )
         got = lax.ppermute(sent, "kin", swap)
         (own,) = product(own_pre_body, "own_pre", [like((count, half), f32)], x_cols, in_own, sent)
         (own_pre,) = product(add_body, "add_pre", [crossing], own, got)
         other_pre = lax.ppermute(own_pre, "tok", swap)
         sides = [side]
-        sent = product(far_grad_body, "far_grad", sides, dy_cols, out_far, own_pre)
+        sent = product(far_grad_body, "far_grad", sides, dy_cols, weight_out, own_pre)
         got = [lax.ppermute(part, "kin", swap) for part in sent]
-        (own,) = product(own_grad_body, "own_grad", [like((count, half), f32)], dy_cols, out_own)
+        (own,) = product(own_grad_body, "own_grad", [like((count, half), f32)], dy_cols, weight_out)
         (own_grad,) = product(add_body, "add_grad", [crossing], own, *got)
         other_grad = lax.ppermute(own_grad, "tok", swap)
         slopes, *act_own = call(gelu_body, "gelu", [like((count, half), f32)] + sides)(
             bias_in.reshape(1, hid), kept(own_pre), kept(other_pre), kept(own_grad)
         )
         act_far = [lax.ppermute(part, "kin", swap) for part in act_own]
-        (forward,) = product(own_forward_body, "own_forward", [ends], *act_own, out_own)
+        (forward,) = product(own_forward_body, "own_forward", [ends], *act_own, weight_out)
         act, forward = product(
             far_forward_body,
             "far_forward",
             [like((count, hid), bf16), ends],
             *act_own,
             *act_far,
-            out_far,
+            weight_out,
             forward,
         )
         (grad_own,) = product(

time: 46.4 us -> 45.4 us (0.978)
  Pallas kernels: 26.2 us -> 23.6 us
  waiting for transfers between devices: 3.04 us -> 4.65 us
    pallas_call x17, Pallas kernels: 17.8 us -> 15.2 us  [run(): pl.pallas_call(body, out_shape=shapes, in_specs=specs or [whole] * len(ar...]
    ppermute x6, waiting for transfers between devices: 0.06 us -> 1.67 us  [across(): return lax.ppermute(array, 'nout', [(i, i ^ shift) for i in range(nn)])]
  transfers between devices with their start and end apart: 14 -> 14, of which waited for: 3 -> 4; matrix products, arithmetic and copies ran while one was open for 0% -> 0% of each run, Pallas kernels for 50% -> 45%
where the time goes in v12:
time: 45.4 us; the launch traced here: 45.1 us
  Pallas kernels  23.6 us (52%)
  starting transfers between devices  15.1 us (33%)
  waiting for transfers between devices  4.65 us (10%)
  other arithmetic  0.86 us (2%)
  between operations  0.83 us (2%)
    pallas_call x17, Pallas kernels, run(): pl.pallas_call(body, out_shape=shapes, in_specs=specs or [whole] * len(ar...  15.2 us
    ppermute x6, starting transfers between devices, across(): return lax.ppermute(array, 'nout', [(i, i ^ shift) for i in range(nn)])  8.91 us
    pallas_call x2, Pallas kernels, outer(): pl.pallas_call(functools.partial(outer_body, most), out_shape=like((high,...  8.39 us
    ppermute x2, starting transfers between devices, on_device(): got = lax.ppermute(sent, 'tok', swap)  3.67 us
    ppermute x1, waiting for transfers between devices, on_device(): other_grad = lax.ppermute(own_grad, 'tok', swap)  2.37 us
    ppermute x6, waiting for transfers between devices, across(): return lax.ppermute(array, 'nout', [(i, i ^ shift) for i in range(nn)])  1.67 us
    ppermute x1, starting transfers between devices, on_device(): other_pre = lax.ppermute(own_pre, 'tok', swap)  1.49 us
  transfers between devices with their start and end apart: 14, of which 4 were waited for; matrix products, arithmetic and copies ran while one was open for 0% of the time, Pallas kernels for 45%

profile of v12, /device:TPU:0, one launch (start us, length us, event | category | flops | bytes accessed | tf_op | source)
XLA Modules:
  0.0 45.1 jit_solution(11525688379123514148)
XLA Ops:
  0.6 0.9 %fusion = (bf16[8,1536]{1,0:T(8,128)(2,1)S(1)}, bf16[8,1536]{1,0:T(8,128)(2,1)S(1)}) fusion(s32[]{:T(128)S(6)} %select_n.7, bf16[4,3072]{1,0:T(4,128)(2,1)} %param.6, bf16[4,3072]{1,0:T(4,128)(2,1)} %param.11, s32[]{:T(128)S(6)} %select_n.6), kind=kLoop, calls=%fused_computation.4 | loop fusion | flops 98304 | bytes 98312 | tf_op jit(solution)/shard_map/concatenate | solution.py:313
  1.5 3.0 %collective-permute-start = (bf16[8,1536]{1,0:T(8,128)(2,1)S(1)}, bf16[8,1536]{1,0:T(8,128)(2,1)S(1)}, u32[]{:S(2)}, u32[]{:S(2)}) collective-permute-start(bf16[8,1536]{1,0:T(8,128)(2,1)S(1)} %get-tuple-element.48.after_ref), channel_id=1, source_target_pairs={{0,8},{8,0},{1,9},{9,1},{2,10},{10,2},{3,11},{11,3},{4,12},{12,4},... | collective-permute-start | bytes 73736 | tf_op jit(solution)/shard_map/ppermute | solution.py:317
  4.5 2.4 %load_far.1.after_ref.refs_4_.w_in_ref = bf16[1536,1536]{1,0:T(8,128)(2,1)S(1)} custom-call(bf16[1536,3072]{1,0:T(8,128)(2,1)} %hbm_ref.3, bf16[8,1536]{1,0:T(8,128)(2,1)S(1)} %get-tuple-element.48.after_ref), custom_call_target="tpu_custom_call" | custom-call | tf_op jit(solution)/shard_map/load_far/pallas_call | solution.py:55
  6.9 0.0 collective-permute-done.got_ref
  6.9 3.7 %collective-permute-start.1 = (bf16[16,1664]{1,0:T(8,128)(2,1)S(1)}, bf16[16,1664]{1,0:T(8,128)(2,1)S(1)}, u32[]{:S(2)}, u32[]{:S(2)}) collective-permute-start(bf16[16,1664]{1,0:T(8,128)(2,1)S(1)} %get-tuple-element.27), channel_id=1, source_target_pairs={{0,3},{1,2},{2,1},{3,0},{4,7},{5,6},{6,5},{7,4},{8,11},{9,10},{10,... | collective-permute-start | bytes 159752 | tf_op jit(solution)/shard_map/ppermute | solution.py:303
  10.6 0.0 collective-permute-start.2
  10.6 0.8 %collective-permute-start.3 = (bf16[16,1536]{1,0:T(8,128)(2,1)S(1)}, bf16[16,1536]{1,0:T(8,128)(2,1)S(1)}, u32[]{:S(2)}, u32[]{:S(2)}) collective-permute-start(bf16[16,1536]{1,0:T(8,128)(2,1)S(1)} %get-tuple-element.28.after_ref.refs_3_), channel_id=1, source_target_pairs={{0,1},{1,0},{2,3},{3,2},{4,5},{5,4},{6,7},{7,6},{8,9},{9,8},{10,11... | collective-permute-start | bytes 147464 | tf_op jit(solution)/shard_map/ppermute | solution.py:303
  11.4 0.0 slice-start
  11.4 0.0 slice-start.1
  11.4 2.5 %load_own.1.refs_5_.w_in_ref = bf16[1536,1536]{1,0:T(8,128)(2,1)S(1)} custom-call(bf16[1536,3072]{1,0:T(8,128)(2,1)} %hbm_ref.3, bf16[16,1536]{1,0:T(8,128)(2,1)S(1)} %get-tuple-element.28.after_ref.refs_3_), custom_call_target="tpu_custom_call" | custom-call | tf_op jit(solution)/shard_map/load_own/pallas_call | solution.py:55
  13.9 0.0 slice-start.2
  13.9 1.7 %collective-permute-done.2.refs_1_ = bf16[16,1536]{1,0:T(8,128)(2,1)S(1)} collective-permute-done((bf16[16,1536]{1,0:T(8,128)(2,1)S(1)}, bf16[16,1536]{1,0:T(8,128)(2,1)S(1)}, u32[]{:S(2)}, u32[]{:S(2)}) %collective-permute-start.2) | collective-permute-done | bytes 49184 | tf_op jit(solution)/shard_map/ppermute | solution.py:303
  15.6 0.0 collective-permute-done.3.refs_2_
  15.6 0.0 collective-permute-done.1.refs_0_
  15.6 0.9 %far_pre.1 = (bf16[32,1536]{1,0:T(8,128)(2,1)S(1)}, bf16[32,1536]{1,0:T(8,128)(2,1)S(1)}, bf16[32,1536]{1,0:T(8,128)(2,1)S(1)}, f32[1,1536]{1,0:T(1,128)S(1)}) custom-call(bf16[16,1664]{1,0:T(8,128)(2,1)S(1)} %collective-permute-done.1.refs_0_, bf16[16,1536]{1,0:T(8,128)(2,1)S(1)} %collective-permute-done.2.refs_1_, ...), custom_call_target="tpu_custom_call" | custom-call | tf_op jit(solution)/shard_map/far_pre/pallas_call | solution.py:55
  16.5 0.0 collective-permute-start.4
  16.5 0.9 %own_pre.1.own_ref = f32[32,1536]{1,0:T(8,128)S(1)} custom-call(bf16[32,1536]{1,0:T(8,128)(2,1)S(1)} %get-tuple-element.30.x_ref.left_ref, bf16[1536,1536]{1,0:T(8,128)(2,1)S(1)} %load_own.1.refs_5_.w_in_ref, bf16[32,1536]{1,0:T(8,128)(2,1)S(1)} %get-tuple-element.31.after_ref), custom_call_target="tpu_custom_call" | custom-call | tf_op jit(solution)/shard_map/own_pre/pallas_call | solution.py:55
  17.4 0.4 collective-permute-done.4.got_ref
  17.8 1.5 %collective-permute-start.5 = (bf16[32,1664]{1,0:T(8,128)(2,1)S(1)}, bf16[32,1664]{1,0:T(8,128)(2,1)S(1)}, u32[]{:S(2)}, u32[]{:S(2)}) collective-permute-start(bf16[32,1664]{1,0:T(8,128)(2,1)S(1)} %add_pre.1.after_ref.own_ref), channel_id=1, source_target_pairs={{0,8},{8,0},{1,9},{9,1},{2,10},{10,2},{3,11},{11,3},{4,12},{12,4},... | collective-permute-start | bytes 319496 | tf_op jit(solution)/shard_map/ppermute | solution.py:355
  19.3 0.0 slice-done
  19.3 0.0 slice-done.1
  19.3 0.0 slice-done.2
  19.3 0.0 copy-start
  19.3 1.4 %far_grad.1 = bf16[32,1536]{1,0:T(8,128)(2,1)S(1)} custom-call(bf16[32,1536]{1,0:T(8,128)(2,1)S(1)} %get-tuple-element.32.dy_ref.right_ref, bf16[3072,1536]{1,0:T(8,128)(2,1)S(1)} %bitcast.5, bf16[32,1664]{1,0:T(8,128)(2,1)S(1)} %add_pre.1.after_ref.own_ref), custom_call_target="tpu_custom_call" | custom-call | tf_op jit(solution)/shard_map/far_grad/pallas_call | solution.py:55
  20.8 0.1 collective-permute-start.6
  20.8 1.4 %own_grad.1.own_ref = f32[32,1536]{1,0:T(8,128)S(1)} custom-call(bf16[32,1536]{1,0:T(8,128)(2,1)S(1)} %get-tuple-element.32.dy_ref.right_ref, bf16[3072,1536]{1,0:T(8,128)(2,1)S(1)} %bitcast.5), custom_call_target="tpu_custom_call" | custom-call | tf_op jit(solution)/shard_map/own_grad/pallas_call | solution.py:55
  22.3 0.0 collective-permute-done.6.got_ref
  22.3 0.7 %collective-permute-start.7 = (bf16[32,1664]{1,0:T(8,128)(2,1)S(1)}, bf16[32,1664]{1,0:T(8,128)(2,1)S(1)}, u32[]{:S(2)}, u32[]{:S(2)}) collective-permute-start(bf16[32,1664]{1,0:T(8,128)(2,1)S(1)} %add_grad.1.after_ref.own_ref), channel_id=1, source_target_pairs={{0,8},{8,0},{1,9},{9,1},{2,10},{10,2},{3,11},{11,3},{4,12},{12,4},... | collective-permute-start | bytes 319496 | tf_op jit(solution)/shard_map/ppermute | solution.py:361
  23.0 0.0 collective-permute-done.5.other_ref
  23.0 0.0 copy-done
  23.0 0.1 gelu.1
  23.1 0.3 collective-permute-start.8
  23.4 0.9 %own_forward.1.terms_ref = f32[32,1536]{1,0:T(8,128)S(1)} custom-call(bf16[32,1536]{1,0:T(8,128)(2,1)S(1)} %get-tuple-element.34.act_ref.own_ref, bf16[3072,1536]{1,0:T(8,128)(2,1)S(1)} %bitcast.5), custom_call_target="tpu_custom_call" | custom-call | tf_op jit(solution)/shard_map/own_forward/pallas_call | solution.py:55
  24.3 0.2 collective-permute-done.8.far_ref
  24.5 0.9 %far_forward.1 = (bf16[32,3072]{1,0:T(8,128)(2,1)S(1)}, f32[32,1536]{1,0:T(8,128)S(1)}) custom-call(bf16[32,1536]{1,0:T(8,128)(2,1)S(1)} %get-tuple-element.34.act_ref.own_ref, bf16[32,1536]{1,0:T(8,128)(2,1)S(1)} %collective-permute-done.8.far_ref, bf16[3072,1536]{1,0:T(8,128)(2,1)S(1)} %bitcast.5, f32[32,1536]{1,0:T(8,128)S(1)} %own_forward.1.terms_ref), custom_call_target="tpu_custom_call" | custom-call | tf_op jit(solution)/shard_map/far_forward/pallas_call | solution.py:55
  25.4 2.4 %collective-permute-done.7.other_ref = bf16[32,1664]{1,0:T(8,128)(2,1)S(1)} collective-permute-done((bf16[32,1664]{1,0:T(8,128)(2,1)S(1)}, bf16[32,1664]{1,0:T(8,128)(2,1)S(1)}, u32[]{:S(2)}, u32[]{:S(2)}) %collective-permute-start.7) | collective-permute-done | bytes 106528 | tf_op jit(solution)/shard_map/ppermute | solution.py:361
  27.8 0.0 copy-start.1
  27.8 0.1 collective-permute-start.9
  27.9 1.4 %own_backward.1.backward_ref = f32[32,1536]{1,0:T(8,128)S(1)} custom-call(bf16[32,1536]{1,0:T(8,128)(2,1)S(1)} %grad_pre.1.grad_ref.own_ref, bf16[1536,1536]{1,0:T(8,128)(2,1)S(1)} %load_own.1.refs_5_.w_in_ref), custom_call_target="tpu_custom_call" | custom-call | tf_op jit(solution)/shard_map/own_backward/pallas_call | solution.py:55
  29.3 0.0 collective-permute-done.9.far_ref
  29.3 1.5 %output_blocks.1 = (bf16[32,3072]{1,0:T(8,128)(2,1)S(1)}, bf16[16,1536]{1,0:T(8,128)(2,1)S(1)}, bf16[16,1536]{1,0:T(8,128)(2,1)S(1)}, bf16[16,1536]{1,0:T(8,128)(2,1)S(1)}, bf16[16,1536]{1,0:T(8,128)(2,1)S(1)}) custom-call(bf16[32,1536]{1,0:T(8,128)(2,1)S(1)} %grad_pre.1.grad_ref.own_ref, bf16[32,1536]{1,0:T(8,128)(2,1)S(1)} %collective-permute-done.9.far_ref, ...), custom_call_target="tpu_custom_call" | custom-call | tf_op jit(solution)/shard_map/output_blocks/pallas_call | solution.py:55
  30.7 2.0 %collective-permute-start.10 = (bf16[16,1536]{1,0:T(8,128)(2,1)S(1)}, bf16[16,1536]{1,0:T(8,128)(2,1)S(1)}, u32[]{:S(2)}, u32[]{:S(2)}) collective-permute-start(bf16[16,1536]{1,0:T(8,128)(2,1)S(1)} %get-tuple-element.36), channel_id=1, source_target_pairs={{0,3},{1,2},{2,1},{3,0},{4,7},{5,6},{6,5},{7,4},{8,11},{9,10},{10,... | collective-permute-start | bytes 147464 | tf_op jit(solution)/shard_map/ppermute | solution.py:303
  32.8 0.1 collective-permute-start.11
  32.9 2.3 %collective-permute-start.12 = (bf16[16,1536]{1,0:T(8,128)(2,1)S(1)}, bf16[16,1536]{1,0:T(8,128)(2,1)S(1)}, u32[]{:S(2)}, u32[]{:S(2)}) collective-permute-start(bf16[16,1536]{1,0:T(8,128)(2,1)S(1)} %get-tuple-element.38), channel_id=1, source_target_pairs={{0,1},{1,0},{2,3},{3,2},{4,5},{5,4},{6,7},{7,6},{8,9},{9,8},{10,11... | collective-permute-start | bytes 147464 | tf_op jit(solution)/shard_map/ppermute | solution.py:303
  35.2 4.3 %weight_in_grad.1.refs_4_ = bf16[1536,3072]{1,0:T(8,128)(2,1)} custom-call(bf16[32,1536]{1,0:T(8,128)(2,1)S(1)} %get-tuple-element.30.x_ref.left_ref, bf16[32,3072]{1,0:T(8,128)(2,1)S(1)} %get-tuple-element.40.right_ref.hidden_ref), custom_call_target="tpu_custom_call" | custom-call | flops 301989888 | bytes 9437184 | tf_op jit(solution)/shard_map/weight_in_grad/pallas_call | solution.py:249
  39.5 0.0 collective-permute-done.10.refs_0_
  39.5 0.0 collective-permute-done.11.refs_1_
  39.5 0.0 collective-permute-done.12.refs_2_
  39.5 0.0 copy-done.1
  39.5 0.1 sum_blocks.1
  39.6 0.7 %collective-permute-start.13 = (bf16[16,1536]{1,0:T(8,128)(2,1)S(1)}, bf16[16,1536]{1,0:T(8,128)(2,1)S(1)}, u32[]{:S(2)}, u32[]{:S(2)}) collective-permute-start(bf16[16,1536]{1,0:T(8,128)(2,1)S(1)} %get-tuple-element.42), channel_id=1, source_target_pairs={{0,8},{8,0},{1,9},{9,1},{2,10},{10,2},{3,11},{11,3},{4,12},{12,4},... | collective-permute-start | bytes 147464 | tf_op jit(solution)/shard_map/ppermute | solution.py:407
  40.3 4.1 %weight_out_grad.1 = bf16[3072,1536]{1,0:T(8,128)(2,1)} custom-call(bf16[32,3072]{1,0:T(8,128)(2,1)S(1)} %get-tuple-element.45.left_ref, bf16[32,1536]{1,0:T(8,128)(2,1)S(1)} %get-tuple-element.32.dy_ref.right_ref), custom_call_target="tpu_custom_call" | custom-call | flops 301989888 | bytes 9437184 | tf_op jit(solution)/shard_map/weight_out_grad/pallas_call | solution.py:249
  44.4 0.0 collective-permute-done.13.got_ref
  44.4 0.7 %final_rows.1 = (bf16[4,3072]{1,0:T(4,128)(2,1)}, bf16[4,3072]{1,0:T(4,128)(2,1)}, f32[1,3072]{1,0:T(1,128)}, f32[1,3072]{1,0:T(1,128)}) custom-call(bf16[8,1536]{1,0:T(8,128)(2,1)S(1)} %get-tuple-element.41.own_ref, bf16[16,1536]{1,0:T(8,128)(2,1)S(1)} %collective-permute-done.13.got_ref, f32[1,1536]{1,0:T(1,128)S(1)} %get-tuple-element.29.sums_ref, ...), custom_call_target="tpu_custom_call" | custom-call | tf_op jit(solution)/shard_map/final_rows/pallas_call | solution.py:55
  (5 shorter events, 0.1 us)
Async XLA Ops:
  1.5 5.4 %collective-permute-start = (bf16[8,1536]{1,0:T(8,128)(2,1)S(1)}, bf16[8,1536]{1,0:T(8,128)(2,1)S(1)}, u32[]{:S(2)}, u32[]{:S(2)}) collective-permute-start(bf16[8,1536]{1,0:T(8,128)(2,1)S(1)} %get-tuple-element.48.after_ref), channel_id=1, source_target_pairs={{0,8},{8,0},{1,9},{9,1},{2,10},{10,2},{3,11},{11,3},{4,12},{12,4},... | collective-permute-start | bytes 73736 | tf_op jit(solution)/shard_map/ppermute | solution.py:317
  6.9 8.7 %collective-permute-start.1 = (bf16[16,1664]{1,0:T(8,128)(2,1)S(1)}, bf16[16,1664]{1,0:T(8,128)(2,1)S(1)}, u32[]{:S(2)}, u32[]{:S(2)}) collective-permute-start(bf16[16,1664]{1,0:T(8,128)(2,1)S(1)} %get-tuple-element.27), channel_id=1, source_target_pairs={{0,3},{1,2},{2,1},{3,0},{4,7},{5,6},{6,5},{7,4},{8,11},{9,10},{10,... | collective-permute-start | bytes 159752 | tf_op jit(solution)/shard_map/ppermute | solution.py:303
  10.6 5.0 %collective-permute-start.2 = (bf16[16,1536]{1,0:T(8,128)(2,1)S(1)}, bf16[16,1536]{1,0:T(8,128)(2,1)S(1)}, u32[]{:S(2)}, u32[]{:S(2)}) collective-permute-start(bf16[16,1536]{1,0:T(8,128)(2,1)S(1)} %get-tuple-element.28.after_ref.refs_3_), channel_id=1, source_target_pairs={{0,2},{1,3},{2,0},{3,1},{4,6},{5,7},{6,4},{7,5},{8,10},{9,11},{10,... | collective-permute-start | bytes 147464 | tf_op jit(solution)/shard_map/ppermute | solution.py:303
  10.6 5.0 %collective-permute-start.3 = (bf16[16,1536]{1,0:T(8,128)(2,1)S(1)}, bf16[16,1536]{1,0:T(8,128)(2,1)S(1)}, u32[]{:S(2)}, u32[]{:S(2)}) collective-permute-start(bf16[16,1536]{1,0:T(8,128)(2,1)S(1)} %get-tuple-element.28.after_ref.refs_3_), channel_id=1, source_target_pairs={{0,1},{1,0},{2,3},{3,2},{4,5},{5,4},{6,7},{7,6},{8,9},{9,8},{10,11... | collective-permute-start | bytes 147464 | tf_op jit(solution)/shard_map/ppermute | solution.py:303
  11.4 7.9 %slice-start = ((s8[9437184]{0:T(1024)(128)(4,1)}), s8[4194304]{0:T(1024)(128)(4,1)S(1)}, s32[]{:S(2)}) async-start(s8[9437184]{0:T(1024)(128)(4,1)} %bitcast.4), calls=%async_computation | async-start | bytes 8388608
  11.4 7.9 %slice-start.1 = ((s8[9437184]{0:T(1024)(128)(4,1)}), s8[4194304]{0:T(1024)(128)(4,1)S(1)}, s32[]{:S(2)}) async-start(s8[9437184]{0:T(1024)(128)(4,1)} %bitcast.4), calls=%async_computation.1 | async-start | bytes 8388608
  13.9 5.4 %slice-start.2 = ((s8[9437184]{0:T(1024)(128)(4,1)}), s8[1048576]{0:T(1024)(128)(4,1)S(1)}, s32[]{:S(2)}) async-start(s8[9437184]{0:T(1024)(128)(4,1)} %bitcast.4), calls=%async_computation.2 | async-start | bytes 2097152
  16.5 1.3 %collective-permute-start.4 = (bf16[32,1536]{1,0:T(8,128)(2,1)S(1)}, bf16[32,1536]{1,0:T(8,128)(2,1)S(1)}, u32[]{:S(2)}, u32[]{:S(2)}) collective-permute-start(bf16[32,1536]{1,0:T(8,128)(2,1)S(1)} %get-tuple-element.31.after_ref), channel_id=1, source_target_pairs={{0,4},{4,0},{1,5},{5,1},{2,6},{6,2},{3,7},{7,3},{8,12},{12,8},{9,1... | collective-permute-start | bytes 294920 | tf_op jit(solution)/shard_map/ppermute | solution.py:352
  17.8 5.1 %collective-permute-start.5 = (bf16[32,1664]{1,0:T(8,128)(2,1)S(1)}, bf16[32,1664]{1,0:T(8,128)(2,1)S(1)}, u32[]{:S(2)}, u32[]{:S(2)}) collective-permute-start(bf16[32,1664]{1,0:T(8,128)(2,1)S(1)} %add_pre.1.after_ref.own_ref), channel_id=1, source_target_pairs={{0,8},{8,0},{1,9},{9,1},{2,10},{10,2},{3,11},{11,3},{4,12},{12,4},... | collective-permute-start | bytes 319496 | tf_op jit(solution)/shard_map/ppermute | solution.py:355
  19.3 3.6 %copy-start = (f32[3072]{0:T(1024)S(1)}, f32[3072]{0:T(1024)}, u32[]{:S(2)}) copy-start(f32[3072]{0:T(1024)} %param.8) | copy-start | bytes 36868
  20.8 1.5 %collective-permute-start.6 = (bf16[32,1536]{1,0:T(8,128)(2,1)S(1)}, bf16[32,1536]{1,0:T(8,128)(2,1)S(1)}, u32[]{:S(2)}, u32[]{:S(2)}) collective-permute-start(bf16[32,1536]{1,0:T(8,128)(2,1)S(1)} %far_grad.1), channel_id=1, source_target_pairs={{0,4},{4,0},{1,5},{5,1},{2,6},{6,2},{3,7},{7,3},{8,12},{12,8},{9,1... | collective-permute-start | bytes 294920 | tf_op jit(solution)/shard_map/ppermute | solution.py:358
  22.3 5.4 %collective-permute-start.7 = (bf16[32,1664]{1,0:T(8,128)(2,1)S(1)}, bf16[32,1664]{1,0:T(8,128)(2,1)S(1)}, u32[]{:S(2)}, u32[]{:S(2)}) collective-permute-start(bf16[32,1664]{1,0:T(8,128)(2,1)S(1)} %add_grad.1.after_ref.own_ref), channel_id=1, source_target_pairs={{0,8},{8,0},{1,9},{9,1},{2,10},{10,2},{3,11},{11,3},{4,12},{12,4},... | collective-permute-start | bytes 319496 | tf_op jit(solution)/shard_map/ppermute | solution.py:361
  23.1 1.4 %collective-permute-start.8 = (bf16[32,1536]{1,0:T(8,128)(2,1)S(1)}, bf16[32,1536]{1,0:T(8,128)(2,1)S(1)}, u32[]{:S(2)}, u32[]{:S(2)}) collective-permute-start(bf16[32,1536]{1,0:T(8,128)(2,1)S(1)} %get-tuple-element.34.act_ref.own_ref), channel_id=1, source_target_pairs={{0,4},{4,0},{1,5},{5,1},{2,6},{6,2},{3,7},{7,3},{8,12},{12,8},{9,1... | collective-permute-start | bytes 294920 | tf_op jit(solution)/shard_map/ppermute | solution.py:365
  27.8 11.7 %copy-start.1 = (f32[3072]{0:T(1024)S(1)}, f32[3072]{0:T(1024)}, u32[]{:S(2)}) copy-start(f32[3072]{0:T(1024)} %param.10) | copy-start | bytes 36868
  27.8 1.5 %collective-permute-start.9 = (bf16[32,1536]{1,0:T(8,128)(2,1)S(1)}, bf16[32,1536]{1,0:T(8,128)(2,1)S(1)}, u32[]{:S(2)}, u32[]{:S(2)}) collective-permute-start(bf16[32,1536]{1,0:T(8,128)(2,1)S(1)} %grad_pre.1.grad_ref.own_ref), channel_id=1, source_target_pairs={{0,4},{4,0},{1,5},{5,1},{2,6},{6,2},{3,7},{7,3},{8,12},{12,8},{9,1... | collective-permute-start | bytes 294920 | tf_op jit(solution)/shard_map/ppermute | solution.py:379
  30.7 8.8 %collective-permute-start.10 = (bf16[16,1536]{1,0:T(8,128)(2,1)S(1)}, bf16[16,1536]{1,0:T(8,128)(2,1)S(1)}, u32[]{:S(2)}, u32[]{:S(2)}) collective-permute-start(bf16[16,1536]{1,0:T(8,128)(2,1)S(1)} %get-tuple-element.36), channel_id=1, source_target_pairs={{0,3},{1,2},{2,1},{3,0},{4,7},{5,6},{6,5},{7,4},{8,11},{9,10},{10,... | collective-permute-start | bytes 147464 | tf_op jit(solution)/shard_map/ppermute | solution.py:303
  32.8 6.7 %collective-permute-start.11 = (bf16[16,1536]{1,0:T(8,128)(2,1)S(1)}, bf16[16,1536]{1,0:T(8,128)(2,1)S(1)}, u32[]{:S(2)}, u32[]{:S(2)}) collective-permute-start(bf16[16,1536]{1,0:T(8,128)(2,1)S(1)} %get-tuple-element.37), channel_id=1, source_target_pairs={{0,2},{1,3},{2,0},{3,1},{4,6},{5,7},{6,4},{7,5},{8,10},{9,11},{10,... | collective-permute-start | bytes 147464 | tf_op jit(solution)/shard_map/ppermute | solution.py:303
  32.9 6.6 %collective-permute-start.12 = (bf16[16,1536]{1,0:T(8,128)(2,1)S(1)}, bf16[16,1536]{1,0:T(8,128)(2,1)S(1)}, u32[]{:S(2)}, u32[]{:S(2)}) collective-permute-start(bf16[16,1536]{1,0:T(8,128)(2,1)S(1)} %get-tuple-element.38), channel_id=1, source_target_pairs={{0,1},{1,0},{2,3},{3,2},{4,5},{5,4},{6,7},{7,6},{8,9},{9,8},{10,11... | collective-permute-start | bytes 147464 | tf_op jit(solution)/shard_map/ppermute | solution.py:303
  39.6 4.8 %collective-permute-start.13 = (bf16[16,1536]{1,0:T(8,128)(2,1)S(1)}, bf16[16,1536]{1,0:T(8,128)(2,1)S(1)}, u32[]{:S(2)}, u32[]{:S(2)}) collective-permute-start(bf16[16,1536]{1,0:T(8,128)(2,1)S(1)} %get-tuple-element.42), channel_id=1, source_target_pairs={{0,8},{8,0},{1,9},{9,1},{2,10},{10,2},{3,11},{11,3},{4,12},{12,4},... | collective-permute-start | bytes 147464 | tf_op jit(solution)/shard_map/ppermute | solution.py:407

commit v13 on v12

--- a/solution.py
+++ b/solution.py
@@ -105,9 +105,16 @@
     return pl.ds(pl.multiple_of(at * size, size), size)
 
 
+def own_rows(half):
+    return lax.axis_index("kin") * half
+
+
+def far_rows(half):
+    return (1 - lax.axis_index("kin")) * half
+
+
 def half_tiles(half, mine):
-    core = lax.axis_index("kin")
-    first = (core if mine else 1 - core) * half
+    first = own_rows(half) if mine else far_rows(half)
     tile = tile_of(half, 512)
     return [
         (pl.ds(i * tile, tile), pl.ds(pl.multiple_of(first + i * tile, tile), tile))
@@ -115,13 +122,17 @@
     ]
 
 
-def load_body(mine, hbm_ref, after_ref, out_ref, sems):
-    size = out_ref.shape[0] // 4
-    source = hbm_ref.at[:, half_of(out_ref.shape[1], mine)]
-    copies = [
-        pltpu.make_async_copy(source.at[part, :], out_ref.at[part, :], sems.at[i])
-        for i, part in enumerate(pl.ds(j * size, size) for j in range(4))
-    ]
+def load_body(firsts_of, hbm_ref, after_ref, *refs):
+    *out_refs, sems = refs
+    copies = []
+    for i, (first_of, out_ref) in enumerate(zip(firsts_of, out_refs)):
+        size, wide = out_ref.shape
+        source = hbm_ref.at[:, pl.ds(pl.multiple_of(first_of(), 128), wide)]
+        for j in range(4):
+            part = pl.ds(j * (size // 4), size // 4)
+            copies.append(
+                pltpu.make_async_copy(source.at[part, :], out_ref.at[part, :], sems.at[i, j])
+            )
     for copy in copies:
         copy.start()
     for copy in copies:
@@ -138,16 +149,18 @@
 
 
 def far_pre_body(rows, count, *refs):
-    *piece_refs, w_in_ref, after_ref = refs[: count + 2]
-    sent_ref, x_ref, dy_ref, sums_ref = refs[count + 2 :]
+    *piece_refs, w_in_ref, w_last_ref, after_ref = refs[: count + 3]
+    sent_ref, x_ref, dy_ref, sums_ref = refs[count + 3 :]
     wide = x_ref.shape[1]
     mixed = jnp.concatenate([ref[:, :wide] for ref in piece_refs], axis=0)
     x_cols, dy_cols = apart(mixed.astype(f32), rows)
     sums_ref[...] = jnp.sum(dy_cols, axis=0, keepdims=True)
     x_cols, dy_cols = x_cols.astype(bf16), dy_cols.astype(bf16)
     x_ref[...], dy_ref[...] = x_cols, dy_cols
-    for at in tiles_of(sent_ref.shape[1]):
+    first = w_in_ref.shape[1]
+    for at in tiles_of(first):
         sent_ref[:, at] = dot(x_cols, w_in_ref[:, at], 1, 0).astype(bf16)
+    sent_ref[:, first:] = dot(x_cols, w_last_ref[...], 1, 0).astype(bf16)
 
 
 def own_pre_body(x_ref, w_in_ref, after_ref, own_ref):
@@ -156,13 +169,10 @@
         own_ref[:, at] = dot(x_cols, w_in_ref[:, at], 1, 0)
 
 
-def far_grad_body(dy_ref, w_out_ref, after_ref, *sent_refs):
+def far_grad_body(dy_ref, w_out_ref, after_ref, sent_ref):
     dy_cols = dy_ref[...]
-    size = sent_refs[0].shape[0]
-    for at, there in half_tiles(sent_refs[0].shape[1], False):
-        terms = dot_turned(dy_cols, w_out_ref[there, :]).astype(bf16)
-        for i, sent_ref in enumerate(sent_refs):
-            sent_ref[:, at] = terms[i * size : (i + 1) * size]
+    for at, there in half_tiles(sent_ref.shape[1], False):
+        sent_ref[:, at] = dot_turned(dy_cols, w_out_ref[there, :]).astype(bf16)
 
 
 def own_grad_body(dy_ref, w_out_ref, own_ref):
@@ -177,8 +187,8 @@
     out_ref[:, half:] = jnp.zeros((own_ref.shape[0], out_ref.shape[1] - half), bf16)
 
 
-def gelu_body(bias_ref, own_ref, other_ref, after_ref, slopes_ref, *act_refs):
-    size, half = act_refs[0].shape
+def gelu_body(bias_ref, own_ref, other_ref, after_ref, slopes_ref, act_ref):
+    half = act_ref.shape[1]
     bias = bias_ref[:, half_of(half, True)]
     tile = tile_of(half, 512)
     for i in range(half // tile):
@@ -186,12 +196,10 @@
         pre_act = own_ref[:, at].astype(f32) + other_ref[:, at].astype(f32)
         activated, slopes = gelu_parts(pre_act + bias[:, i * tile : (i + 1) * tile])
         slopes_ref[:, at] = slopes
-        activated = activated.astype(bf16)
-        for j, act_ref in enumerate(act_refs):
-            act_ref[:, at] = activated[j * size : (j + 1) * size]
-
-
-def grad_pre_body(slopes_ref, own_ref, other_ref, after_ref, grad_ref):
+        act_ref[:, at] = activated.astype(bf16)
+
+
+def grad_pre_body(slopes_ref, own_ref, other_ref, after_ref, later_ref, grad_ref):
     half = pl.ds(0, grad_ref.shape[1])
     grad_act = own_ref[:, half].astype(f32) + other_ref[:, half].astype(f32)
     grad_ref[...] = (grad_act * slopes_ref[...]).astype(bf16)
@@ -204,9 +212,8 @@
         out_ref[:, at] = dot(act, w_out_ref[part, at], 1, 0)
 
 
-def far_forward_body(own_ref, far_ref, w_out_ref, terms_ref, act_ref, out_ref):
+def far_forward_body(far_ref, w_out_ref, terms_ref, out_ref):
     act = far_ref[...]
-    act_ref[...] = ordered(lax.axis_index("kin"), own_ref[...], act, 1)
     part = half_of(act.shape[1], False)
     for at in tiles_of(out_ref.shape[1]):
         out_ref[:, at] = terms_ref[:, at] + dot(act, w_out_ref[part, at], 1, 0)
@@ -218,49 +225,55 @@
         out_ref[:, at] = dot_turned(grad, w_in_ref[at, :])
 
 
-def blocks_body(rows, own_ref, far_ref, forward_ref, backward_ref, w_in_ref, grad_ref, *out_refs):
+def blocks_body(
+    rows, own_ref, far_ref, forward_ref, backward_ref, w_in_ref, w_last_ref, grad_ref, *out_refs
+):
     grad = far_ref[...]
     grad_ref[...] = ordered(lax.axis_index("kin"), own_ref[...], grad, 1)
     size = out_refs[0].shape[0]
+    first = w_in_ref.shape[1]
     for at in tiles_of(forward_ref.shape[1]):
-        backward = backward_ref[:, at] + dot_turned(grad, w_in_ref[at, :])
+        backward = backward_ref[:, at] + dot_turned(grad[:, :first], w_in_ref[at, :])
+        backward = backward + dot_turned(grad[:, first:], w_last_ref[at, :])
         terms = together(forward_ref[:, at], backward, rows).astype(bf16)
         for i, out_ref in enumerate(out_refs):
             out_ref[:, at] = terms[i * size : (i + 1) * size]
 
 
-def outer_body(most, left_ref, right_ref, out_hbm, block_ref, sems):
+def outer_body(most, first_of, left_ref, right_ref, *refs):
+    out_hbm, block_ref, sems = refs[-3:]
+    first = first_of(left_ref.shape[1])
     copies = []
-    for i, at in enumerate(tiles_of(out_hbm.shape[0], 256)):
+    for i, at in enumerate(tiles_of(left_ref.shape[1], most)):
         left = left_ref[:, at].T
-        for part in tiles_of(out_hbm.shape[1], most):
+        for part in tiles_of(out_hbm.shape[1], 512):
             block_ref[at, part] = dot(left, right_ref[:, part], 1, 0).astype(bf16)
+        there = pl.ds(pl.multiple_of(first + at.start, at.size), at.size)
         copies.append(
-            pltpu.make_async_copy(block_ref.at[at, :], out_hbm.at[at, :], sems.at[i])
+            pltpu.make_async_copy(block_ref.at[at, :], out_hbm.at[there, :], sems.at[i])
         )
         copies[-1].start()
     for copy in copies:
         copy.wait()
 
 
-def outer(left, right, name, most):
-    count, high = left.shape
+def outer(left, right, high, name, first_of, into=None, most=128):
+    count, size = left.shape
     wide = right.shape[1]
+    anywhere = pl.BlockSpec(memory_space=pl.ANY)
     return pl.pallas_call(
-        functools.partial(outer_body, most),
+        functools.partial(outer_body, most, first_of),
         out_shape=like((high, wide), bf16),
-        in_specs=[whole] * 2,
-        out_specs=pl.BlockSpec(memory_space=pl.ANY),
+        in_specs=[whole] * 2 + ([] if into is None else [anywhere]),
+        out_specs=anywhere,
         scratch_shapes=[
-            pltpu.VMEM((high, wide), bf16),
-            pltpu.SemaphoreType.DMA((len(tiles_of(high, 256)),)),
+            pltpu.VMEM((size, wide), bf16),
+            pltpu.SemaphoreType.DMA((len(tiles_of(size, most)),)),
         ],
-        cost_estimate=pl.CostEstimate(
-            flops=2 * count * wide * high, bytes_accessed=2 * wide * high, transcendentals=0
-        ),
+        input_output_aliases={} if into is None else {2: 0},
         compiler_params=pltpu.CompilerParams(vmem_limit_bytes=16 * MIB),
         name=name,
-    )(kept(left), kept(right))
+    )(kept(left), kept(right), *([] if into is None else [into]))
 
 
 def sum_body(rows, bias_ref, sums_ref, *refs):
@@ -316,17 +329,19 @@
         sent = lax.dynamic_slice_in_dim(mine, (1 - me) * wide, wide, 1)
         got = lax.ppermute(sent, "tok", swap)
 
-        def load_in(mine, name, after):
+        last = tile_of(half, 512)
+
+        def load_in(name, after, *parts):
             return call(
-                functools.partial(load_body, mine),
+                functools.partial(load_body, [first_of for first_of, _ in parts]),
                 name,
-                [like((wide, half), bf16)],
+                [like((wide, width), bf16) for _, width in parts],
                 grant=MIB,
-                scratch=[sem((4,))],
+                scratch=[sem((len(parts), 4))],
                 specs=[hbm, pl.BlockSpec(memory_space=pl.ANY)],
             )(in_hbm(weight_in), after)
 
-        (in_far,) = load_in(False, "load_far", sent)
+        (in_far,) = load_in("load_far", sent, (lambda: far_rows(half), half - last))
         tiles, farthest = call(
             pair_body, "pair_tiles", [like((2 * pair, wide + more), bf16) for more in (0, 128)]
         )(
@@ -334,7 +349,12 @@
         )
         pieces = [across(tiles, shift) for shift in range(1, nn - 1)]
         pieces = [across(farthest, nn - 1)] + pieces[::-1] + [tiles]
-        (in_own,) = load_in(True, "load_own", tiles)
+        in_own, in_last = load_in(
+            "load_own",
+            tiles,
+            (lambda: own_rows(half), half),
+            (lambda: far_rows(half) + half - last, last),
+        )
 
         def product(body, name, outs, *args):
             return call(body, name, outs, grant=8 * MIB)(*map(kept, args))
@@ -347,34 +367,35 @@
             [side] + [like((count, wide), bf16)] * 2 + [like((1, wide), f32)],
             *pieces,
             in_far,
+            in_last,
             in_own,
         )
         got = lax.ppermute(sent, "kin", swap)
         (own,) = product(own_pre_body, "own_pre", [like((count, half), f32)], x_cols, in_own, sent)
         (own_pre,) = product(add_body, "add_pre", [crossing], own, got)
         other_pre = lax.ppermute(own_pre, "tok", swap)
-        sides = [side]
-        sent = product(far_grad_body, "far_grad", sides, dy_cols, weight_out, own_pre)
-        got = [lax.ppermute(part, "kin", swap) for part in sent]
+        (sent,) = product(far_grad_body, "far_grad", [side], dy_cols, weight_out, own_pre)
+        got = lax.ppermute(sent, "kin", swap)
         (own,) = product(own_grad_body, "own_grad", [like((count, half), f32)], dy_cols, weight_out)
-        (own_grad,) = product(add_body, "add_grad", [crossing], own, *got)
+        (own_grad,) = product(add_body, "add_grad", [crossing], own, got)
         other_grad = lax.ppermute(own_grad, "tok", swap)
-        slopes, *act_own = call(gelu_body, "gelu", [like((count, half), f32)] + sides)(
+        slopes, act_own = call(gelu_body, "gelu", [like((count, half), f32), side])(
             bias_in.reshape(1, hid), kept(own_pre), kept(other_pre), kept(own_grad)
         )
-        act_far = [lax.ppermute(part, "kin", swap) for part in act_own]
-        (forward,) = product(own_forward_body, "own_forward", [ends], *act_own, weight_out)
-        act, forward = product(
-            far_forward_body,
-            "far_forward",
-            [like((count, hid), bf16), ends],
-            *act_own,
-            *act_far,
-            weight_out,
-            forward,
-        )
-        (grad_own,) = product(
-            grad_pre_body, "grad_pre", [side], slopes, own_grad, other_grad, forward
+        act_far = lax.ppermute(act_own, "kin", swap)
+        (forward,) = product(own_forward_body, "own_forward", [ends], act_own, weight_out)
+        (forward,) = product(
+            far_forward_body, "far_forward", [ends], act_far, weight_out, forward
+        )
+        weight_out_grad = outer(act_own, dy_cols, hid, "weight_out_grad_own", own_rows)
+        (grad_own,) = call(
+            grad_pre_body, "grad_pre", [side], specs=[whole] * 4 + [hbm]
+        )(
+            kept(slopes),
+            kept(own_grad),
+            kept(other_grad),
+            kept(forward),
+            in_hbm(weight_out_grad),
         )
         grad_far = lax.ppermute(grad_own, "kin", swap)
         (backward,) = product(own_backward_body, "own_backward", [ends], grad_own, in_own)
@@ -387,10 +408,13 @@
             forward,
             backward,
             in_far,
-        )
-
-        weight_in_grad = outer(x_cols, grad, "weight_in_grad", 256)
-        weight_out_grad = outer(act, dy_cols, "weight_out_grad", 1536)
+            in_last,
+        )
+
+        weight_in_grad = outer(x_cols, grad, wide, "weight_in_grad", lambda size: 0)
+        weight_out_grad = outer(
+            act_far, dy_cols, hid, "weight_out_grad_far", far_rows, into=weight_out_grad
+        )
 
         terms = [across(blocks[i], nn - 1 - i) for i in range(nn - 1)] + [blocks[-1]]
         own, sent = call(

time: 45.4 us -> 45 us (level)
  waiting for transfers between devices: 4.65 us -> 1.94 us
  starting transfers between devices: 15.1 us -> 16.6 us
  Pallas kernels: 23.6 us -> 24.4 us
    ppermute x1, waiting for transfers between devices: 2.37 us -> 0.03 us  [on_device(): other_grad = lax.ppermute(own_grad, 'tok', swap)]
    ppermute x2, starting transfers between devices: 3.67 us -> 4.56 us  [on_device(): got = lax.ppermute(sent, 'tok', swap)]
    pallas_call x2 -> x3, Pallas kernels: 8.39 us -> 9.22 us  [outer(): pl.pallas_call(functools.partial(outer_body, most, first_of), out_shape=l...]
  transfers between devices with their start and end apart: 14 -> 14, of which waited for: 4 -> 4; matrix products, arithmetic and copies ran while one was open for 0% -> 0% of each run, Pallas kernels for 45% -> 47%
where the time goes in v13:
time: 45 us; the launch traced here: 44.7 us
  Pallas kernels  24.4 us (54%)
  starting transfers between devices  16.6 us (37%)
  waiting for transfers between devices  1.94 us (4%)
  other arithmetic  0.86 us (2%)
  between operations  0.8 us (2%)
    pallas_call x17, Pallas kernels, run(): pl.pallas_call(body, out_shape=shapes, in_specs=specs or [whole] * len(ar...  15.2 us
    pallas_call x3, Pallas kernels, outer(): pl.pallas_call(functools.partial(outer_body, most, first_of), out_shape=l...  9.22 us
    ppermute x6, starting transfers between devices, across(): return lax.ppermute(array, 'nout', [(i, i ^ shift) for i in range(nn)])  9.18 us
    ppermute x2, starting transfers between devices, on_device(): got = lax.ppermute(sent, 'tok', swap)  4.56 us
    ppermute x1, starting transfers between devices, on_device(): other_pre = lax.ppermute(own_pre, 'tok', swap)  1.56 us
    ppermute x6, waiting for transfers between devices, across(): return lax.ppermute(array, 'nout', [(i, i ^ shift) for i in range(nn)])  1.47 us
  transfers between devices with their start and end apart: 14, of which 4 were waited for; matrix products, arithmetic and copies ran while one was open for 0% of the time, Pallas kernels for 47%

profile of v13, /device:TPU:0, one launch (start us, length us, event | category | flops | bytes accessed | tf_op | source)
XLA Modules:
  0.0 44.7 jit_solution(7596507193456408497)
XLA Ops:
  0.6 0.9 %fusion = (bf16[8,1536]{1,0:T(8,128)(2,1)S(1)}, bf16[8,1536]{1,0:T(8,128)(2,1)S(1)}) fusion(s32[]{:T(128)S(6)} %select_n.7, bf16[4,3072]{1,0:T(4,128)(2,1)} %param.6, bf16[4,3072]{1,0:T(4,128)(2,1)} %param.11, s32[]{:T(128)S(6)} %select_n.6), kind=kLoop, calls=%fused_computation.4 | loop fusion | flops 98304 | bytes 98312 | tf_op jit(solution)/shard_map/concatenate | solution.py:326
  1.5 3.0 %collective-permute-start = (bf16[8,1536]{1,0:T(8,128)(2,1)S(1)}, bf16[8,1536]{1,0:T(8,128)(2,1)S(1)}, u32[]{:S(2)}, u32[]{:S(2)}) collective-permute-start(bf16[8,1536]{1,0:T(8,128)(2,1)S(1)} %get-tuple-element.48.after_ref), channel_id=1, source_target_pairs={{0,8},{8,0},{1,9},{9,1},{2,10},{10,2},{3,11},{11,3},{4,12},{12,4},... | collective-permute-start | bytes 73736 | tf_op jit(solution)/shard_map/ppermute | solution.py:330
  4.5 1.9 %load_far.1.after_ref.refs_4_.w_in_ref = bf16[1536,1024]{1,0:T(8,128)(2,1)S(1)} custom-call(bf16[1536,3072]{1,0:T(8,128)(2,1)} %hbm_ref.3, bf16[8,1536]{1,0:T(8,128)(2,1)S(1)} %get-tuple-element.48.after_ref), custom_call_target="tpu_custom_call" | custom-call | tf_op jit(solution)/shard_map/load_far/pallas_call | solution.py:55
  6.4 0.0 collective-permute-done.got_ref
  6.4 4.1 %collective-permute-start.1 = (bf16[16,1664]{1,0:T(8,128)(2,1)S(1)}, bf16[16,1664]{1,0:T(8,128)(2,1)S(1)}, u32[]{:S(2)}, u32[]{:S(2)}) collective-permute-start(bf16[16,1664]{1,0:T(8,128)(2,1)S(1)} %get-tuple-element.27), channel_id=1, source_target_pairs={{0,3},{1,2},{2,1},{3,0},{4,7},{5,6},{6,5},{7,4},{8,11},{9,10},{10,... | collective-permute-start | bytes 159752 | tf_op jit(solution)/shard_map/ppermute | solution.py:316
  10.5 0.0 collective-permute-start.3
  10.5 0.6 %collective-permute-start.2 = (bf16[16,1536]{1,0:T(8,128)(2,1)S(1)}, bf16[16,1536]{1,0:T(8,128)(2,1)S(1)}, u32[]{:S(2)}, u32[]{:S(2)}) collective-permute-start(bf16[16,1536]{1,0:T(8,128)(2,1)S(1)} %get-tuple-element.28.after_ref.refs_3_), channel_id=1, source_target_pairs={{0,2},{1,3},{2,0},{3,1},{4,6},{5,7},{6,4},{7,5},{8,10},{9,11},{10,... | collective-permute-start | bytes 147464 | tf_op jit(solution)/shard_map/ppermute | solution.py:316
  11.2 0.0 slice-start
  11.2 0.0 slice-start.1
  11.2 3.0 %load_own.1 = (bf16[1536,1536]{1,0:T(8,128)(2,1)S(1)}, bf16[1536,512]{1,0:T(8,128)(2,1)S(1)}) custom-call(bf16[1536,3072]{1,0:T(8,128)(2,1)} %hbm_ref.3, bf16[16,1536]{1,0:T(8,128)(2,1)S(1)} %get-tuple-element.28.after_ref.refs_3_), custom_call_target="tpu_custom_call" | custom-call | tf_op jit(solution)/shard_map/load_own/pallas_call | solution.py:55
  14.2 0.4 collective-permute-done.3.refs_2_
  14.6 0.9 %collective-permute-done.2.refs_1_ = bf16[16,1536]{1,0:T(8,128)(2,1)S(1)} collective-permute-done((bf16[16,1536]{1,0:T(8,128)(2,1)S(1)}, bf16[16,1536]{1,0:T(8,128)(2,1)S(1)}, u32[]{:S(2)}, u32[]{:S(2)}) %collective-permute-start.2) | collective-permute-done | bytes 49184 | tf_op jit(solution)/shard_map/ppermute | solution.py:316
  15.5 0.0 collective-permute-done.1.refs_0_
  15.5 0.0 slice-start.2
  15.5 0.9 %far_pre.1 = (bf16[32,1536]{1,0:T(8,128)(2,1)S(1)}, bf16[32,1536]{1,0:T(8,128)(2,1)S(1)}, bf16[32,1536]{1,0:T(8,128)(2,1)S(1)}, f32[1,1536]{1,0:T(1,128)S(1)}) custom-call(bf16[16,1664]{1,0:T(8,128)(2,1)S(1)} %collective-permute-done.1.refs_0_, bf16[16,1536]{1,0:T(8,128)(2,1)S(1)} %collective-permute-done.2.refs_1_, ...), custom_call_target="tpu_custom_call" | custom-call | tf_op jit(solution)/shard_map/far_pre/pallas_call | solution.py:55
  16.4 0.0 collective-permute-start.4
  16.5 0.9 %own_pre.1.own_ref = f32[32,1536]{1,0:T(8,128)S(1)} custom-call(bf16[32,1536]{1,0:T(8,128)(2,1)S(1)} %get-tuple-element.32.x_ref.left_ref, bf16[1536,1536]{1,0:T(8,128)(2,1)S(1)} %get-tuple-element.30.refs_6_.w_in_ref, bf16[32,1536]{1,0:T(8,128)(2,1)S(1)} %get-tuple-element.33.after_ref), custom_call_target="tpu_custom_call" | custom-call | tf_op jit(solution)/shard_map/own_pre/pallas_call | solution.py:55
  17.4 0.4 collective-permute-done.4.got_ref
  17.8 1.6 %collective-permute-start.5 = (bf16[32,1664]{1,0:T(8,128)(2,1)S(1)}, bf16[32,1664]{1,0:T(8,128)(2,1)S(1)}, u32[]{:S(2)}, u32[]{:S(2)}) collective-permute-start(bf16[32,1664]{1,0:T(8,128)(2,1)S(1)} %add_pre.1.after_ref.own_ref), channel_id=1, source_target_pairs={{0,8},{8,0},{1,9},{9,1},{2,10},{10,2},{3,11},{11,3},{4,12},{12,4},... | collective-permute-start | bytes 319496 | tf_op jit(solution)/shard_map/ppermute | solution.py:376
  19.3 0.0 slice-done
  19.3 0.0 slice-done.1
  19.3 0.0 slice-done.2
  19.4 0.0 copy-start
  19.4 1.4 %far_grad.1 = bf16[32,1536]{1,0:T(8,128)(2,1)S(1)} custom-call(bf16[32,1536]{1,0:T(8,128)(2,1)S(1)} %get-tuple-element.34.dy_ref.right_ref, bf16[3072,1536]{1,0:T(8,128)(2,1)S(1)} %bitcast.5, bf16[32,1664]{1,0:T(8,128)(2,1)S(1)} %add_pre.1.after_ref.own_ref), custom_call_target="tpu_custom_call" | custom-call | tf_op jit(solution)/shard_map/far_grad/pallas_call | solution.py:55
  20.8 0.1 collective-permute-start.6
  20.9 1.4 %own_grad.1.own_ref = f32[32,1536]{1,0:T(8,128)S(1)} custom-call(bf16[32,1536]{1,0:T(8,128)(2,1)S(1)} %get-tuple-element.34.dy_ref.right_ref, bf16[3072,1536]{1,0:T(8,128)(2,1)S(1)} %bitcast.5), custom_call_target="tpu_custom_call" | custom-call | tf_op jit(solution)/shard_map/own_grad/pallas_call | solution.py:55
  22.3 0.0 collective-permute-done.6.got_ref
  22.3 0.6 %collective-permute-start.7 = (bf16[32,1664]{1,0:T(8,128)(2,1)S(1)}, bf16[32,1664]{1,0:T(8,128)(2,1)S(1)}, u32[]{:S(2)}, u32[]{:S(2)}) collective-permute-start(bf16[32,1664]{1,0:T(8,128)(2,1)S(1)} %add_grad.1.after_ref.own_ref), channel_id=1, source_target_pairs={{0,8},{8,0},{1,9},{9,1},{2,10},{10,2},{3,11},{11,3},{4,12},{12,4},... | collective-permute-start | bytes 319496 | tf_op jit(solution)/shard_map/ppermute | solution.py:381
  22.9 0.0 collective-permute-done.5.other_ref
  22.9 0.0 copy-done
  22.9 0.1 gelu.1
  23.1 0.3 collective-permute-start.8
  23.3 0.9 %own_forward.1.terms_ref = f32[32,1536]{1,0:T(8,128)S(1)} custom-call(bf16[32,1536]{1,0:T(8,128)(2,1)S(1)} %get-tuple-element.36.act_ref.left_ref, bf16[3072,1536]{1,0:T(8,128)(2,1)S(1)} %bitcast.5), custom_call_target="tpu_custom_call" | custom-call | tf_op jit(solution)/shard_map/own_forward/pallas_call | solution.py:55
  24.2 2.6 %weight_out_grad_own.1.later_ref.refs_0_ = bf16[3072,1536]{1,0:T(8,128)(2,1)} custom-call(bf16[32,1536]{1,0:T(8,128)(2,1)S(1)} %get-tuple-element.36.act_ref.left_ref, bf16[32,1536]{1,0:T(8,128)(2,1)S(1)} %get-tuple-element.34.dy_ref.right_ref), custom_call_target="tpu_custom_call" | custom-call | tf_op jit(solution)/shard_map/weight_out_grad_own/pallas_call | solution.py:264
  26.8 0.0 collective-permute-done.8.far_ref.left_ref
  26.8 0.9 %far_forward.1.after_ref.forward_ref = f32[32,1536]{1,0:T(8,128)S(1)} custom-call(bf16[32,1536]{1,0:T(8,128)(2,1)S(1)} %collective-permute-done.8.far_ref.left_ref, bf16[3072,1536]{1,0:T(8,128)(2,1)S(1)} %bitcast.5, f32[32,1536]{1,0:T(8,128)S(1)} %own_forward.1.terms_ref), custom_call_target="tpu_custom_call" | custom-call | tf_op jit(solution)/shard_map/far_forward/pallas_call | solution.py:55
  27.7 0.0 collective-permute-done.7.other_ref
  27.8 0.0 copy-start.1
  27.8 0.4 collective-permute-start.9
  28.2 1.4 %own_backward.1.backward_ref = f32[32,1536]{1,0:T(8,128)S(1)} custom-call(bf16[32,1536]{1,0:T(8,128)(2,1)S(1)} %grad_pre.1.grad_ref.own_ref, bf16[1536,1536]{1,0:T(8,128)(2,1)S(1)} %get-tuple-element.30.refs_6_.w_in_ref), custom_call_target="tpu_custom_call" | custom-call | tf_op jit(solution)/shard_map/own_backward/pallas_call | solution.py:55
  29.6 0.0 collective-permute-done.9.far_ref
  29.6 1.5 %output_blocks.1 = (bf16[32,3072]{1,0:T(8,128)(2,1)S(1)}, bf16[16,1536]{1,0:T(8,128)(2,1)S(1)}, bf16[16,1536]{1,0:T(8,128)(2,1)S(1)}, bf16[16,1536]{1,0:T(8,128)(2,1)S(1)}, bf16[16,1536]{1,0:T(8,128)(2,1)S(1)}) custom-call(bf16[32,1536]{1,0:T(8,128)(2,1)S(1)} %grad_pre.1.grad_ref.own_ref, bf16[32,1536]{1,0:T(8,128)(2,1)S(1)} %collective-permute-done.9.far_ref, ...), custom_call_target="tpu_custom_call" | custom-call | tf_op jit(solution)/shard_map/output_blocks/pallas_call | solution.py:55
  31.1 2.5 %collective-permute-start.10 = (bf16[16,1536]{1,0:T(8,128)(2,1)S(1)}, bf16[16,1536]{1,0:T(8,128)(2,1)S(1)}, u32[]{:S(2)}, u32[]{:S(2)}) collective-permute-start(bf16[16,1536]{1,0:T(8,128)(2,1)S(1)} %get-tuple-element.37), channel_id=1, source_target_pairs={{0,3},{1,2},{2,1},{3,0},{4,7},{5,6},{6,5},{7,4},{8,11},{9,10},{10,... | collective-permute-start | bytes 147464 | tf_op jit(solution)/shard_map/ppermute | solution.py:316
  33.6 1.1 %collective-permute-start.11 = (bf16[16,1536]{1,0:T(8,128)(2,1)S(1)}, bf16[16,1536]{1,0:T(8,128)(2,1)S(1)}, u32[]{:S(2)}, u32[]{:S(2)}) collective-permute-start(bf16[16,1536]{1,0:T(8,128)(2,1)S(1)} %get-tuple-element.38), channel_id=1, source_target_pairs={{0,2},{1,3},{2,0},{3,1},{4,6},{5,7},{6,4},{7,5},{8,10},{9,11},{10,... | collective-permute-start | bytes 147464 | tf_op jit(solution)/shard_map/ppermute | solution.py:316
  34.6 0.9 %collective-permute-start.12 = (bf16[16,1536]{1,0:T(8,128)(2,1)S(1)}, bf16[16,1536]{1,0:T(8,128)(2,1)S(1)}, u32[]{:S(2)}, u32[]{:S(2)}) collective-permute-start(bf16[16,1536]{1,0:T(8,128)(2,1)S(1)} %get-tuple-element.39), channel_id=1, source_target_pairs={{0,1},{1,0},{2,3},{3,2},{4,5},{5,4},{6,7},{7,6},{8,9},{9,8},{10,11... | collective-permute-start | bytes 147464 | tf_op jit(solution)/shard_map/ppermute | solution.py:316
  35.5 4.1 %weight_in_grad.1.refs_4_ = bf16[1536,3072]{1,0:T(8,128)(2,1)} custom-call(bf16[32,1536]{1,0:T(8,128)(2,1)S(1)} %get-tuple-element.32.x_ref.left_ref, bf16[32,3072]{1,0:T(8,128)(2,1)S(1)} %get-tuple-element.41.right_ref.hidden_ref), custom_call_target="tpu_custom_call" | custom-call | tf_op jit(solution)/shard_map/weight_in_grad/pallas_call | solution.py:264
  39.6 0.0 collective-permute-done.10.refs_0_
  39.6 0.1 collective-permute-done.11.refs_1_
  39.7 0.0 collective-permute-done.12.refs_2_
  39.8 0.0 copy-done.1
  39.8 0.1 sum_blocks.1
  39.8 1.6 %collective-permute-start.13 = (bf16[16,1536]{1,0:T(8,128)(2,1)S(1)}, bf16[16,1536]{1,0:T(8,128)(2,1)S(1)}, u32[]{:S(2)}, u32[]{:S(2)}) collective-permute-start(bf16[16,1536]{1,0:T(8,128)(2,1)S(1)} %get-tuple-element.43), channel_id=1, source_target_pairs={{0,8},{8,0},{1,9},{9,1},{2,10},{10,2},{3,11},{11,3},{4,12},{12,4},... | collective-permute-start | bytes 147464 | tf_op jit(solution)/shard_map/ppermute | solution.py:431
  41.4 2.6 %weight_out_grad_far.1 = bf16[3072,1536]{1,0:T(8,128)(2,1)} custom-call(bf16[32,1536]{1,0:T(8,128)(2,1)S(1)} %collective-permute-done.8.far_ref.left_ref, bf16[32,1536]{1,0:T(8,128)(2,1)S(1)} %get-tuple-element.34.dy_ref.right_ref, bf16[3072,1536]{1,0:T(8,128)(2,1)} %weight_out_grad_own.1.later_ref.refs_0_), custom_call_target="tpu_custom_call", output_to_operand_aliasing={{}: (2, {})} | custom-call | tf_op jit(solution)/shard_map/weight_out_grad_far/pallas_call | solution.py:264
  44.0 0.0 collective-permute-done.13.got_ref
  44.0 0.7 %final_rows.1 = (bf16[4,3072]{1,0:T(4,128)(2,1)}, bf16[4,3072]{1,0:T(4,128)(2,1)}, f32[1,3072]{1,0:T(1,128)}, f32[1,3072]{1,0:T(1,128)}) custom-call(bf16[8,1536]{1,0:T(8,128)(2,1)S(1)} %get-tuple-element.42.own_ref, bf16[16,1536]{1,0:T(8,128)(2,1)S(1)} %collective-permute-done.13.got_ref, f32[1,1536]{1,0:T(1,128)S(1)} %get-tuple-element.31.sums_ref, ...), custom_call_target="tpu_custom_call" | custom-call | tf_op jit(solution)/shard_map/final_rows/pallas_call | solution.py:55
  (5 shorter events, 0.1 us)
Async XLA Ops:
  1.5 4.9 %collective-permute-start = (bf16[8,1536]{1,0:T(8,128)(2,1)S(1)}, bf16[8,1536]{1,0:T(8,128)(2,1)S(1)}, u32[]{:S(2)}, u32[]{:S(2)}) collective-permute-start(bf16[8,1536]{1,0:T(8,128)(2,1)S(1)} %get-tuple-element.48.after_ref), channel_id=1, source_target_pairs={{0,8},{8,0},{1,9},{9,1},{2,10},{10,2},{3,11},{11,3},{4,12},{12,4},... | collective-permute-start | bytes 73736 | tf_op jit(solution)/shard_map/ppermute | solution.py:330
  6.4 9.1 %collective-permute-start.1 = (bf16[16,1664]{1,0:T(8,128)(2,1)S(1)}, bf16[16,1664]{1,0:T(8,128)(2,1)S(1)}, u32[]{:S(2)}, u32[]{:S(2)}) collective-permute-start(bf16[16,1664]{1,0:T(8,128)(2,1)S(1)} %get-tuple-element.27), channel_id=1, source_target_pairs={{0,3},{1,2},{2,1},{3,0},{4,7},{5,6},{6,5},{7,4},{8,11},{9,10},{10,... | collective-permute-start | bytes 159752 | tf_op jit(solution)/shard_map/ppermute | solution.py:316
  10.5 4.1 %collective-permute-start.3 = (bf16[16,1536]{1,0:T(8,128)(2,1)S(1)}, bf16[16,1536]{1,0:T(8,128)(2,1)S(1)}, u32[]{:S(2)}, u32[]{:S(2)}) collective-permute-start(bf16[16,1536]{1,0:T(8,128)(2,1)S(1)} %get-tuple-element.28.after_ref.refs_3_), channel_id=1, source_target_pairs={{0,1},{1,0},{2,3},{3,2},{4,5},{5,4},{6,7},{7,6},{8,9},{9,8},{10,11... | collective-permute-start | bytes 147464 | tf_op jit(solution)/shard_map/ppermute | solution.py:316
  10.5 5.0 %collective-permute-start.2 = (bf16[16,1536]{1,0:T(8,128)(2,1)S(1)}, bf16[16,1536]{1,0:T(8,128)(2,1)S(1)}, u32[]{:S(2)}, u32[]{:S(2)}) collective-permute-start(bf16[16,1536]{1,0:T(8,128)(2,1)S(1)} %get-tuple-element.28.after_ref.refs_3_), channel_id=1, source_target_pairs={{0,2},{1,3},{2,0},{3,1},{4,6},{5,7},{6,4},{7,5},{8,10},{9,11},{10,... | collective-permute-start | bytes 147464 | tf_op jit(solution)/shard_map/ppermute | solution.py:316
  11.2 8.2 %slice-start = ((s8[9437184]{0:T(1024)(128)(4,1)}), s8[4194304]{0:T(1024)(128)(4,1)S(1)}, s32[]{:S(2)}) async-start(s8[9437184]{0:T(1024)(128)(4,1)} %bitcast.4), calls=%async_computation | async-start | bytes 8388608
  11.2 8.2 %slice-start.1 = ((s8[9437184]{0:T(1024)(128)(4,1)}), s8[4194304]{0:T(1024)(128)(4,1)S(1)}, s32[]{:S(2)}) async-start(s8[9437184]{0:T(1024)(128)(4,1)} %bitcast.4), calls=%async_computation.1 | async-start | bytes 8388608
  15.5 3.8 %slice-start.2 = ((s8[9437184]{0:T(1024)(128)(4,1)}), s8[1048576]{0:T(1024)(128)(4,1)S(1)}, s32[]{:S(2)}) async-start(s8[9437184]{0:T(1024)(128)(4,1)} %bitcast.4), calls=%async_computation.2 | async-start | bytes 2097152
  16.4 1.3 %collective-permute-start.4 = (bf16[32,1536]{1,0:T(8,128)(2,1)S(1)}, bf16[32,1536]{1,0:T(8,128)(2,1)S(1)}, u32[]{:S(2)}, u32[]{:S(2)}) collective-permute-start(bf16[32,1536]{1,0:T(8,128)(2,1)S(1)} %get-tuple-element.33.after_ref), channel_id=1, source_target_pairs={{0,4},{4,0},{1,5},{5,1},{2,6},{6,2},{3,7},{7,3},{8,12},{12,8},{9,1... | collective-permute-start | bytes 294920 | tf_op jit(solution)/shard_map/ppermute | solution.py:373
  17.8 5.2 %collective-permute-start.5 = (bf16[32,1664]{1,0:T(8,128)(2,1)S(1)}, bf16[32,1664]{1,0:T(8,128)(2,1)S(1)}, u32[]{:S(2)}, u32[]{:S(2)}) collective-permute-start(bf16[32,1664]{1,0:T(8,128)(2,1)S(1)} %add_pre.1.after_ref.own_ref), channel_id=1, source_target_pairs={{0,8},{8,0},{1,9},{9,1},{2,10},{10,2},{3,11},{11,3},{4,12},{12,4},... | collective-permute-start | bytes 319496 | tf_op jit(solution)/shard_map/ppermute | solution.py:376
  19.4 3.6 %copy-start = (f32[3072]{0:T(1024)S(1)}, f32[3072]{0:T(1024)}, u32[]{:S(2)}) copy-start(f32[3072]{0:T(1024)} %param.8) | copy-start | bytes 36868
  20.8 1.5 %collective-permute-start.6 = (bf16[32,1536]{1,0:T(8,128)(2,1)S(1)}, bf16[32,1536]{1,0:T(8,128)(2,1)S(1)}, u32[]{:S(2)}, u32[]{:S(2)}) collective-permute-start(bf16[32,1536]{1,0:T(8,128)(2,1)S(1)} %far_grad.1), channel_id=1, source_target_pairs={{0,4},{4,0},{1,5},{5,1},{2,6},{6,2},{3,7},{7,3},{8,12},{12,8},{9,1... | collective-permute-start | bytes 294920 | tf_op jit(solution)/shard_map/ppermute | solution.py:378
  22.3 5.4 %collective-permute-start.7 = (bf16[32,1664]{1,0:T(8,128)(2,1)S(1)}, bf16[32,1664]{1,0:T(8,128)(2,1)S(1)}, u32[]{:S(2)}, u32[]{:S(2)}) collective-permute-start(bf16[32,1664]{1,0:T(8,128)(2,1)S(1)} %add_grad.1.after_ref.own_ref), channel_id=1, source_target_pairs={{0,8},{8,0},{1,9},{9,1},{2,10},{10,2},{3,11},{11,3},{4,12},{12,4},... | collective-permute-start | bytes 319496 | tf_op jit(solution)/shard_map/ppermute | solution.py:381
  23.1 3.8 %collective-permute-start.8 = (bf16[32,1536]{1,0:T(8,128)(2,1)S(1)}, bf16[32,1536]{1,0:T(8,128)(2,1)S(1)}, u32[]{:S(2)}, u32[]{:S(2)}) collective-permute-start(bf16[32,1536]{1,0:T(8,128)(2,1)S(1)} %get-tuple-element.36.act_ref.left_ref), channel_id=1, source_target_pairs={{0,4},{4,0},{1,5},{5,1},{2,6},{6,2},{3,7},{7,3},{8,12},{12,8},{9,1... | collective-permute-start | bytes 294920 | tf_op jit(solution)/shard_map/ppermute | solution.py:385
  27.8 12.0 %copy-start.1 = (f32[3072]{0:T(1024)S(1)}, f32[3072]{0:T(1024)}, u32[]{:S(2)}) copy-start(f32[3072]{0:T(1024)} %param.10) | copy-start | bytes 36868
  27.8 1.8 %collective-permute-start.9 = (bf16[32,1536]{1,0:T(8,128)(2,1)S(1)}, bf16[32,1536]{1,0:T(8,128)(2,1)S(1)}, u32[]{:S(2)}, u32[]{:S(2)}) collective-permute-start(bf16[32,1536]{1,0:T(8,128)(2,1)S(1)} %grad_pre.1.grad_ref.own_ref), channel_id=1, source_target_pairs={{0,4},{4,0},{1,5},{5,1},{2,6},{6,2},{3,7},{7,3},{8,12},{12,8},{9,1... | collective-permute-start | bytes 294920 | tf_op jit(solution)/shard_map/ppermute | solution.py:400
  31.1 8.6 %collective-permute-start.10 = (bf16[16,1536]{1,0:T(8,128)(2,1)S(1)}, bf16[16,1536]{1,0:T(8,128)(2,1)S(1)}, u32[]{:S(2)}, u32[]{:S(2)}) collective-permute-start(bf16[16,1536]{1,0:T(8,128)(2,1)S(1)} %get-tuple-element.37), channel_id=1, source_target_pairs={{0,3},{1,2},{2,1},{3,0},{4,7},{5,6},{6,5},{7,4},{8,11},{9,10},{10,... | collective-permute-start | bytes 147464 | tf_op jit(solution)/shard_map/ppermute | solution.py:316
  33.6 6.2 %collective-permute-start.11 = (bf16[16,1536]{1,0:T(8,128)(2,1)S(1)}, bf16[16,1536]{1,0:T(8,128)(2,1)S(1)}, u32[]{:S(2)}, u32[]{:S(2)}) collective-permute-start(bf16[16,1536]{1,0:T(8,128)(2,1)S(1)} %get-tuple-element.38), channel_id=1, source_target_pairs={{0,2},{1,3},{2,0},{3,1},{4,6},{5,7},{6,4},{7,5},{8,10},{9,11},{10,... | collective-permute-start | bytes 147464 | tf_op jit(solution)/shard_map/ppermute | solution.py:316
  34.6 5.1 %collective-permute-start.12 = (bf16[16,1536]{1,0:T(8,128)(2,1)S(1)}, bf16[16,1536]{1,0:T(8,128)(2,1)S(1)}, u32[]{:S(2)}, u32[]{:S(2)}) collective-permute-start(bf16[16,1536]{1,0:T(8,128)(2,1)S(1)} %get-tuple-element.39), channel_id=1, source_target_pairs={{0,1},{1,0},{2,3},{3,2},{4,5},{5,4},{6,7},{7,6},{8,9},{9,8},{10,11... | collective-permute-start | bytes 147464 | tf_op jit(solution)/shard_map/ppermute | solution.py:316
  39.8 4.2 %collective-permute-start.13 = (bf16[16,1536]{1,0:T(8,128)(2,1)S(1)}, bf16[16,1536]{1,0:T(8,128)(2,1)S(1)}, u32[]{:S(2)}, u32[]{:S(2)}) collective-permute-start(bf16[16,1536]{1,0:T(8,128)(2,1)S(1)} %get-tuple-element.43), channel_id=1, source_target_pairs={{0,8},{8,0},{1,9},{9,1},{2,10},{10,2},{3,11},{11,3},{4,12},{12,4},... | collective-permute-start | bytes 147464 | tf_op jit(solution)/shard_map/ppermute | solution.py:431

commit v14 on v13

--- a/solution.py
+++ b/solution.py
@@ -113,30 +113,55 @@
     return (1 - lax.axis_index("kin")) * half
 
 
-def half_tiles(half, mine):
+def half_tiles(half, mine, most):
     first = own_rows(half) if mine else far_rows(half)
-    tile = tile_of(half, 512)
+    tile = tile_of(half, most)
     return [
         (pl.ds(i * tile, tile), pl.ds(pl.multiple_of(first + i * tile, tile), tile))
         for i in range(half // tile)
     ]
 
 
-def load_body(firsts_of, hbm_ref, after_ref, *refs):
-    *out_refs, sems = refs
+def load_body(hbm_ref, after_ref, out_ref, sems):
+    size, wide = out_ref.shape
+    half = hbm_ref.shape[1] // 2
+    source = pl.ds(pl.multiple_of(far_rows(half), 128), wide)
     copies = []
-    for i, (first_of, out_ref) in enumerate(zip(firsts_of, out_refs)):
-        size, wide = out_ref.shape
-        source = hbm_ref.at[:, pl.ds(pl.multiple_of(first_of(), 128), wide)]
-        for j in range(4):
-            part = pl.ds(j * (size // 4), size // 4)
-            copies.append(
-                pltpu.make_async_copy(source.at[part, :], out_ref.at[part, :], sems.at[i, j])
-            )
+    for j in range(4):
+        part = pl.ds(j * (size // 4), size // 4)
+        copies.append(
+            pltpu.make_async_copy(hbm_ref.at[part, source], out_ref.at[part, :], sems.at[j])
+        )
     for copy in copies:
         copy.start()
     for copy in copies:
         copy.wait()
+
+
+def load_and_turn_body(hbm_ref, after_ref, far_ref, own_ref, last_ref, own_turned, far_turned, sems):
+    wide, half = own_ref.shape
+    first, last = far_ref.shape[1], last_ref.shape[1]
+    size = wide // 4
+    parts = [pl.ds(j * size, size) for j in range(4)]
+    from_own = pl.ds(pl.multiple_of(own_rows(half), 128), half)
+    from_last = pl.ds(pl.multiple_of(far_rows(half) + first, 128), last)
+    copies = [
+        [
+            pltpu.make_async_copy(hbm_ref.at[part, source], ref.at[part, :], sems.at[i, j])
+            for j, part in enumerate(parts)
+        ]
+        for i, (source, ref) in enumerate(((from_own, own_ref), (from_last, last_ref)))
+    ]
+    for copy in copies[0] + copies[1]:
+        copy.start()
+    for part in parts:
+        far_turned[:first, part] = far_ref[part, :].T
+    for part, copy in zip(parts, copies[0]):
+        copy.wait()
+        own_turned[:, part] = own_ref[part, :].T
+    for part, copy in zip(parts, copies[1]):
+        copy.wait()
+        far_turned[first:, part] = last_ref[part, :].T
 
 
 def pair_body(own_ref, got_ref, after_ref, *out_refs):
@@ -171,20 +196,30 @@
 
 def far_grad_body(dy_ref, w_out_ref, after_ref, sent_ref):
     dy_cols = dy_ref[...]
-    for at, there in half_tiles(sent_ref.shape[1], False):
+    for at, there in half_tiles(sent_ref.shape[1], False, 1536):
         sent_ref[:, at] = dot_turned(dy_cols, w_out_ref[there, :]).astype(bf16)
 
 
 def own_grad_body(dy_ref, w_out_ref, own_ref):
     dy_cols = dy_ref[...]
-    for at, there in half_tiles(own_ref.shape[1], True):
-        own_ref[:, at] = dot_turned(dy_cols, w_out_ref[there, :])
+    for at, there in half_tiles(own_ref.shape[1], True, 1536):
+        own_ref[:, at] = dot(dy_cols, w_out_ref[there, :], 1, 1)
 
 
 def add_body(own_ref, got_ref, out_ref):
-    half = own_ref.shape[1]
+    count, half = own_ref.shape
     out_ref[:, :half] = (own_ref[...] + got_ref[...].astype(f32)).astype(bf16)
-    out_ref[:, half:] = jnp.zeros((own_ref.shape[0], out_ref.shape[1] - half), bf16)
+    out_ref[:, half:] = jnp.zeros((count, out_ref.shape[1] - half), bf16)
+
+
+def add_pre_body(own_ref, got_ref, sums_ref, out_ref):
+    count, half = own_ref.shape
+    out_ref[:, :half] = (own_ref[...] + got_ref[...].astype(f32)).astype(bf16)
+    sums = [sums_ref[:, at] for at in tiles_of(sums_ref.shape[1], 128)]
+    sums = jnp.concatenate(sums, axis=0)
+    high = sums.astype(bf16).astype(f32)
+    rest = jnp.zeros((count - 2 * sums.shape[0], 128), f32)
+    out_ref[:, half:] = jnp.concatenate([high, sums - high, rest], axis=0).astype(bf16)
 
 
 def gelu_body(bias_ref, own_ref, other_ref, after_ref, slopes_ref, act_ref):
@@ -215,26 +250,22 @@
 def far_forward_body(far_ref, w_out_ref, terms_ref, out_ref):
     act = far_ref[...]
     part = half_of(act.shape[1], False)
-    for at in tiles_of(out_ref.shape[1]):
+    for at in tiles_of(out_ref.shape[1], 1536):
         out_ref[:, at] = terms_ref[:, at] + dot(act, w_out_ref[part, at], 1, 0)
 
 
-def own_backward_body(grad_ref, w_in_ref, out_ref):
+def own_backward_body(grad_ref, turned_ref, out_ref):
     grad = grad_ref[...]
     for at in tiles_of(out_ref.shape[1]):
-        out_ref[:, at] = dot_turned(grad, w_in_ref[at, :])
-
-
-def blocks_body(
-    rows, own_ref, far_ref, forward_ref, backward_ref, w_in_ref, w_last_ref, grad_ref, *out_refs
-):
+        out_ref[:, at] = dot(grad, turned_ref[:, at], 1, 0)
+
+
+def blocks_body(rows, own_ref, far_ref, forward_ref, backward_ref, turned_ref, grad_ref, *out_refs):
     grad = far_ref[...]
     grad_ref[...] = ordered(lax.axis_index("kin"), own_ref[...], grad, 1)
     size = out_refs[0].shape[0]
-    first = w_in_ref.shape[1]
     for at in tiles_of(forward_ref.shape[1]):
-        backward = backward_ref[:, at] + dot_turned(grad[:, :first], w_in_ref[at, :])
-        backward = backward + dot_turned(grad[:, first:], w_last_ref[at, :])
+        backward = backward_ref[:, at] + dot(grad, turned_ref[:, at], 1, 0)
         terms = together(forward_ref[:, at], backward, rows).astype(bf16)
         for i, out_ref in enumerate(out_refs):
             out_ref[:, at] = terms[i * size : (i + 1) * size]
@@ -276,7 +307,7 @@
     )(kept(left), kept(right), *([] if into is None else [into]))
 
 
-def sum_body(rows, bias_ref, sums_ref, *refs):
+def sum_body(rows, bias_ref, *refs):
     *term_refs, after_ref, own_ref, sent_ref = refs
     wide = own_ref.shape[1]
     me = lax.axis_index("tok")
@@ -286,28 +317,25 @@
     summed = summed + jnp.where(lax.rem(row, 2 * rows) < rows, bias, 0.0)
     low, high = summed[: 2 * rows], summed[2 * rows :]
     own_ref[...] = jnp.where(me == 0, low, high).astype(bf16)
-    rest = sums_ref[...]
-    row = lax.broadcasted_iota(jnp.int32, low.shape, 0)
-    extra = jnp.zeros_like(low)
-    for i in range(3):
-        term = rest.astype(bf16).astype(f32)
-        extra = jnp.where(row == i, term, extra)
-        rest = rest - term
-    sent = jnp.concatenate([jnp.where(me == 0, high, low), extra], axis=0)
-    sent_ref[...] = sent.astype(bf16)
-
-
-def final_body(rows, own_ref, got_ref, sums_ref, hidden_ref, rows_ref, grad_ref, out_sums_ref, bias_ref):
+    sent_ref[...] = jnp.where(me == 0, high, low).astype(bf16)
+
+
+def final_body(
+    rows, own_ref, got_ref, sums_ref, other_ref, hidden_ref, rows_ref, grad_ref, out_sums_ref, bias_ref
+):
     wide = own_ref.shape[1]
     me = lax.axis_index("tok")
     own, got = own_ref[...].astype(f32), got_ref[...].astype(f32)
-    own_sums, got_sums = sums_ref[...], jnp.sum(got[2 * rows :], axis=0, keepdims=True)
+    extra = other_ref[:, other_ref.shape[1] - 128 :].astype(f32)
+    steps = wide // 128
+    got_sums = extra[:steps] + extra[steps : 2 * steps]
+    got_sums = jnp.concatenate([got_sums[i : i + 1] for i in range(steps)], axis=1)
     for i in range(2):
         at = pl.ds(i * wide, wide)
-        part = jnp.where(me == i, own, got[: 2 * rows])
+        part = jnp.where(me == i, own, got)
         rows_ref[:, at] = part[:rows].astype(bf16)
         grad_ref[:, at] = part[rows:].astype(bf16)
-        out_sums_ref[:, at] = jnp.where(me == i, own_sums, got_sums)
+        out_sums_ref[:, at] = jnp.where(me == i, sums_ref[...], got_sums)
     bias_ref[...] = jnp.sum(hidden_ref[...].astype(f32), axis=0, keepdims=True)
 
 
@@ -330,18 +358,14 @@
         got = lax.ppermute(sent, "tok", swap)
 
         last = tile_of(half, 512)
-
-        def load_in(name, after, *parts):
-            return call(
-                functools.partial(load_body, [first_of for first_of, _ in parts]),
-                name,
-                [like((wide, width), bf16) for _, width in parts],
-                grant=MIB,
-                scratch=[sem((len(parts), 4))],
-                specs=[hbm, pl.BlockSpec(memory_space=pl.ANY)],
-            )(in_hbm(weight_in), after)
-
-        (in_far,) = load_in("load_far", sent, (lambda: far_rows(half), half - last))
+        (in_far,) = call(
+            load_body,
+            "load_far",
+            [like((wide, half - last), bf16)],
+            grant=MIB,
+            scratch=[sem((4,))],
+            specs=[hbm, pl.BlockSpec(memory_space=pl.ANY)],
+        )(in_hbm(weight_in), sent)
         tiles, farthest = call(
             pair_body, "pair_tiles", [like((2 * pair, wide + more), bf16) for more in (0, 128)]
         )(
@@ -349,12 +373,14 @@
         )
         pieces = [across(tiles, shift) for shift in range(1, nn - 1)]
         pieces = [across(farthest, nn - 1)] + pieces[::-1] + [tiles]
-        in_own, in_last = load_in(
+        in_own, in_last, own_turned, far_turned = call(
+            load_and_turn_body,
             "load_own",
-            tiles,
-            (lambda: own_rows(half), half),
-            (lambda: far_rows(half) + half - last, last),
-        )
+            [like((wide, half), bf16), like((wide, last), bf16)] + [like((half, wide), bf16)] * 2,
+            grant=8 * MIB,
+            scratch=[sem((2, 4))],
+            specs=[hbm, pl.BlockSpec(memory_space=pl.ANY), whole],
+        )(in_hbm(weight_in), tiles, kept(in_far))
 
         def product(body, name, outs, *args):
             return call(body, name, outs, grant=8 * MIB)(*map(kept, args))
@@ -372,7 +398,7 @@
         )
         got = lax.ppermute(sent, "kin", swap)
         (own,) = product(own_pre_body, "own_pre", [like((count, half), f32)], x_cols, in_own, sent)
-        (own_pre,) = product(add_body, "add_pre", [crossing], own, got)
+        (own_pre,) = product(add_pre_body, "add_pre", [crossing], own, got, sums)
         other_pre = lax.ppermute(own_pre, "tok", swap)
         (sent,) = product(far_grad_body, "far_grad", [side], dy_cols, weight_out, own_pre)
         got = lax.ppermute(sent, "kin", swap)
@@ -398,7 +424,7 @@
             in_hbm(weight_out_grad),
         )
         grad_far = lax.ppermute(grad_own, "kin", swap)
-        (backward,) = product(own_backward_body, "own_backward", [ends], grad_own, in_own)
+        (backward,) = product(own_backward_body, "own_backward", [ends], grad_own, own_turned)
         grad, *blocks = product(
             functools.partial(blocks_body, rows),
             "output_blocks",
@@ -407,8 +433,7 @@
             grad_far,
             forward,
             backward,
-            in_far,
-            in_last,
+            far_turned,
         )
 
         weight_in_grad = outer(x_cols, grad, wide, "weight_in_grad", lambda size: 0)
@@ -420,11 +445,10 @@
         own, sent = call(
             functools.partial(sum_body, rows),
             "sum_blocks",
-            [like((pair, wide), bf16), like((2 * pair, wide), bf16)],
-            specs=[whole] * (nn + 2) + [hbm],
+            [like((pair, wide), bf16)] * 2,
+            specs=[whole] * (nn + 1) + [hbm],
         )(
             bias_out.reshape(1, cols),
-            kept(sums),
             *[kept(term) for term in terms],
             in_hbm(weight_in_grad),
         )
@@ -434,7 +458,7 @@
             "final_rows",
             [like((rows, cols), bf16)] * 2 + [like((1, cols), f32), like((1, hid), f32)],
             resident=False,
-        )(kept(own), kept(got), kept(sums), kept(grad))
+        )(kept(own), kept(got), kept(sums), kept(other_pre), kept(grad))
         return (
             output_rows,
             grad_tokens,

time: 45 us -> 44 us (0.978)
  waiting for transfers between devices: 1.94 us -> 1.42 us
    ppermute x6, waiting for transfers between devices: 1.47 us -> 0.88 us  [across(): return lax.ppermute(array, 'nout', [(i, i ^ shift) for i in range(nn)])]
    pallas_call x17, Pallas kernels: 15.2 us -> 14.7 us  [run(): pl.pallas_call(body, out_shape=shapes, in_specs=specs or [whole] * len(ar...]
  transfers between devices with their start and end apart: 14 -> 14, of which waited for: 4 -> 4; matrix products, arithmetic and copies ran while one was open for 0% -> 0% of each run, Pallas kernels for 47% -> 49%
where the time goes in v14:
time: 44 us; the launch traced here: 43.7 us
  Pallas kernels  24 us (55%)
  starting transfers between devices  16.6 us (38%)
  waiting for transfers between devices  1.42 us (3%)
  other arithmetic  0.86 us (2%)
  between operations  0.82 us (2%)
    pallas_call x17, Pallas kernels, run(): pl.pallas_call(body, out_shape=shapes, in_specs=specs or [whole] * len(ar...  14.7 us
    pallas_call x3, Pallas kernels, outer(): pl.pallas_call(functools.partial(outer_body, most, first_of), out_shape=l...  9.25 us
    ppermute x6, starting transfers between devices, across(): return lax.ppermute(array, 'nout', [(i, i ^ shift) for i in range(nn)])  9.18 us
    ppermute x2, starting transfers between devices, on_device(): got = lax.ppermute(sent, 'tok', swap)  4.55 us
    ppermute x1, starting transfers between devices, on_device(): other_pre = lax.ppermute(own_pre, 'tok', swap)  1.55 us
    ppermute x6, waiting for transfers between devices, across(): return lax.ppermute(array, 'nout', [(i, i ^ shift) for i in range(nn)])  0.88 us
  transfers between devices with their start and end apart: 14, of which 4 were waited for; matrix products, arithmetic and copies ran while one was open for 0% of the time, Pallas kernels for 49%

profile of v14, /device:TPU:0, one launch (start us, length us, event | category | flops | bytes accessed | tf_op | source)
XLA Modules:
  0.0 43.7 jit_solution(5881182055273217250)
XLA Ops:
  0.6 0.9 %fusion = (bf16[8,1536]{1,0:T(8,128)(2,1)S(1)}, bf16[8,1536]{1,0:T(8,128)(2,1)S(1)}) fusion(s32[]{:T(128)S(6)} %select_n.7, bf16[4,3072]{1,0:T(4,128)(2,1)} %param.6, bf16[4,3072]{1,0:T(4,128)(2,1)} %param.11, s32[]{:T(128)S(6)} %select_n.6), kind=kLoop, calls=%fused_computation.4 | loop fusion | flops 98304 | bytes 98312 | tf_op jit(solution)/shard_map/concatenate | solution.py:354
  1.5 3.0 %collective-permute-start = (bf16[8,1536]{1,0:T(8,128)(2,1)S(1)}, bf16[8,1536]{1,0:T(8,128)(2,1)S(1)}, u32[]{:S(2)}, u32[]{:S(2)}) collective-permute-start(bf16[8,1536]{1,0:T(8,128)(2,1)S(1)} %get-tuple-element.52.after_ref), channel_id=1, source_target_pairs={{0,8},{8,0},{1,9},{9,1},{2,10},{10,2},{3,11},{11,3},{4,12},{12,4},... | collective-permute-start | bytes 73736 | tf_op jit(solution)/shard_map/ppermute | solution.py:358
  4.5 1.9 %load_far.1.after_ref.far_ref.refs_4_ = bf16[1536,1024]{1,0:T(8,128)(2,1)S(1)} custom-call(bf16[1536,3072]{1,0:T(8,128)(2,1)} %hbm_ref.3, bf16[8,1536]{1,0:T(8,128)(2,1)S(1)} %get-tuple-element.52.after_ref), custom_call_target="tpu_custom_call" | custom-call | tf_op jit(solution)/shard_map/load_far/pallas_call | solution.py:55
  6.4 0.0 collective-permute-done.got_ref
  6.4 4.1 %collective-permute-start.1 = (bf16[16,1664]{1,0:T(8,128)(2,1)S(1)}, bf16[16,1664]{1,0:T(8,128)(2,1)S(1)}, u32[]{:S(2)}, u32[]{:S(2)}) collective-permute-start(bf16[16,1664]{1,0:T(8,128)(2,1)S(1)} %get-tuple-element.29), channel_id=1, source_target_pairs={{0,3},{1,2},{2,1},{3,0},{4,7},{5,6},{6,5},{7,4},{8,11},{9,10},{10,... | collective-permute-start | bytes 159752 | tf_op jit(solution)/shard_map/ppermute | solution.py:344
  10.5 0.0 collective-permute-start.3
  10.5 0.6 %collective-permute-start.2 = (bf16[16,1536]{1,0:T(8,128)(2,1)S(1)}, bf16[16,1536]{1,0:T(8,128)(2,1)S(1)}, u32[]{:S(2)}, u32[]{:S(2)}) collective-permute-start(bf16[16,1536]{1,0:T(8,128)(2,1)S(1)} %get-tuple-element.30.after_ref.refs_3_), channel_id=1, source_target_pairs={{0,2},{1,3},{2,0},{3,1},{4,6},{5,7},{6,4},{7,5},{8,10},{9,11},{10,... | collective-permute-start | bytes 147464 | tf_op jit(solution)/shard_map/ppermute | solution.py:344
  11.2 0.0 slice-start
  11.2 0.0 slice-start.1
  11.2 3.6 %load_own.1 = (bf16[1536,1536]{1,0:T(8,128)(2,1)S(1)}, bf16[1536,512]{1,0:T(8,128)(2,1)S(1)}, bf16[1536,1536]{1,0:T(8,128)(2,1)S(1)}, bf16[1536,1536]{1,0:T(8,128)(2,1)S(1)}) custom-call(bf16[1536,3072]{1,0:T(8,128)(2,1)} %hbm_ref.3, bf16[16,1536]{1,0:T(8,128)(2,1)S(1)} %get-tuple-element.30.after_ref.refs_3_, ...), custom_call_target="tpu_custom_call" | custom-call | tf_op jit(solution)/shard_map/load_own/pallas_call | solution.py:55
  14.7 0.0 collective-permute-done.3.refs_2_
  14.8 0.8 %collective-permute-done.2.refs_1_ = bf16[16,1536]{1,0:T(8,128)(2,1)S(1)} collective-permute-done((bf16[16,1536]{1,0:T(8,128)(2,1)S(1)}, bf16[16,1536]{1,0:T(8,128)(2,1)S(1)}, u32[]{:S(2)}, u32[]{:S(2)}) %collective-permute-start.2) | collective-permute-done | bytes 49184 | tf_op jit(solution)/shard_map/ppermute | solution.py:344
  15.5 0.0 collective-permute-done.1.refs_0_
  15.5 0.0 slice-start.2
  15.5 0.9 %far_pre.1 = (bf16[32,1536]{1,0:T(8,128)(2,1)S(1)}, bf16[32,1536]{1,0:T(8,128)(2,1)S(1)}, bf16[32,1536]{1,0:T(8,128)(2,1)S(1)}, f32[1,1536]{1,0:T(1,128)S(1)}) custom-call(bf16[16,1664]{1,0:T(8,128)(2,1)S(1)} %collective-permute-done.1.refs_0_, bf16[16,1536]{1,0:T(8,128)(2,1)S(1)} %collective-permute-done.2.refs_1_, ...), custom_call_target="tpu_custom_call" | custom-call | tf_op jit(solution)/shard_map/far_pre/pallas_call | solution.py:55
  16.4 0.0 collective-permute-start.4
  16.5 0.9 %own_pre.1.own_ref = f32[32,1536]{1,0:T(8,128)S(1)} custom-call(bf16[32,1536]{1,0:T(8,128)(2,1)S(1)} %get-tuple-element.33.x_ref.left_ref, bf16[1536,1536]{1,0:T(8,128)(2,1)S(1)} %get-tuple-element.32.refs_6_.w_in_ref, bf16[32,1536]{1,0:T(8,128)(2,1)S(1)} %get-tuple-element.34.after_ref), custom_call_target="tpu_custom_call" | custom-call | tf_op jit(solution)/shard_map/own_pre/pallas_call | solution.py:55
  17.4 0.4 collective-permute-done.4.got_ref
  17.8 1.6 %collective-permute-start.5 = (bf16[32,1664]{1,0:T(8,128)(2,1)S(1)}, bf16[32,1664]{1,0:T(8,128)(2,1)S(1)}, u32[]{:S(2)}, u32[]{:S(2)}) collective-permute-start(bf16[32,1664]{1,0:T(8,128)(2,1)S(1)} %add_pre.1.after_ref.own_ref), channel_id=1, source_target_pairs={{0,8},{8,0},{1,9},{9,1},{2,10},{10,2},{3,11},{11,3},{4,12},{12,4},... | collective-permute-start | bytes 319496 | tf_op jit(solution)/shard_map/ppermute | solution.py:402
  19.4 0.0 slice-done
  19.4 0.0 slice-done.1
  19.4 0.0 slice-done.2
  19.4 0.0 copy-start.1
  19.4 1.4 %far_grad.1 = bf16[32,1536]{1,0:T(8,128)(2,1)S(1)} custom-call(bf16[32,1536]{1,0:T(8,128)(2,1)S(1)} %get-tuple-element.36.dy_ref.right_ref, bf16[3072,1536]{1,0:T(8,128)(2,1)S(1)} %bitcast.5, bf16[32,1664]{1,0:T(8,128)(2,1)S(1)} %add_pre.1.after_ref.own_ref), custom_call_target="tpu_custom_call" | custom-call | tf_op jit(solution)/shard_map/far_grad/pallas_call | solution.py:55
  20.8 0.0 collective-permute-start.6
  20.8 1.5 %own_grad.1.own_ref = f32[32,1536]{1,0:T(8,128)S(1)} custom-call(bf16[32,1536]{1,0:T(8,128)(2,1)S(1)} %get-tuple-element.36.dy_ref.right_ref, bf16[3072,1536]{1,0:T(8,128)(2,1)S(1)} %bitcast.5), custom_call_target="tpu_custom_call" | custom-call | tf_op jit(solution)/shard_map/own_grad/pallas_call | solution.py:55
  22.3 0.0 collective-permute-done.6.got_ref
  22.4 0.6 %collective-permute-start.7 = (bf16[32,1664]{1,0:T(8,128)(2,1)S(1)}, bf16[32,1664]{1,0:T(8,128)(2,1)S(1)}, u32[]{:S(2)}, u32[]{:S(2)}) collective-permute-start(bf16[32,1664]{1,0:T(8,128)(2,1)S(1)} %add_grad.1.after_ref.own_ref), channel_id=1, source_target_pairs={{0,8},{8,0},{1,9},{9,1},{2,10},{10,2},{3,11},{11,3},{4,12},{12,4},... | collective-permute-start | bytes 319496 | tf_op jit(solution)/shard_map/ppermute | solution.py:407
  23.0 0.0 collective-permute-done.5.other_ref
  23.0 0.0 copy-done.1
  23.0 0.1 gelu.1
  23.1 0.3 collective-permute-start.8
  23.4 0.9 %own_forward.1.terms_ref = f32[32,1536]{1,0:T(8,128)S(1)} custom-call(bf16[32,1536]{1,0:T(8,128)(2,1)S(1)} %get-tuple-element.38.act_ref.left_ref, bf16[3072,1536]{1,0:T(8,128)(2,1)S(1)} %bitcast.5), custom_call_target="tpu_custom_call" | custom-call | tf_op jit(solution)/shard_map/own_forward/pallas_call | solution.py:55
  24.2 2.6 %weight_out_grad_own.1.later_ref.refs_0_ = bf16[3072,1536]{1,0:T(8,128)(2,1)} custom-call(bf16[32,1536]{1,0:T(8,128)(2,1)S(1)} %get-tuple-element.38.act_ref.left_ref, bf16[32,1536]{1,0:T(8,128)(2,1)S(1)} %get-tuple-element.36.dy_ref.right_ref), custom_call_target="tpu_custom_call" | custom-call | tf_op jit(solution)/shard_map/weight_out_grad_own/pallas_call | solution.py:295
  26.8 0.0 collective-permute-done.8.far_ref.left_ref
  26.8 0.9 %far_forward.1.after_ref.forward_ref = f32[32,1536]{1,0:T(8,128)S(1)} custom-call(bf16[32,1536]{1,0:T(8,128)(2,1)S(1)} %collective-permute-done.8.far_ref.left_ref, bf16[3072,1536]{1,0:T(8,128)(2,1)S(1)} %bitcast.5, f32[32,1536]{1,0:T(8,128)S(1)} %own_forward.1.terms_ref), custom_call_target="tpu_custom_call" | custom-call | tf_op jit(solution)/shard_map/far_forward/pallas_call | solution.py:55
  27.8 0.0 collective-permute-done.7.other_ref
  27.8 0.4 collective-permute-start.9
  28.2 0.0 copy-start
  28.2 0.9 %own_backward.1.backward_ref = f32[32,1536]{1,0:T(8,128)S(1)} custom-call(bf16[32,1536]{1,0:T(8,128)(2,1)S(1)} %grad_pre.1.grad_ref.own_ref, bf16[1536,1536]{1,0:T(8,128)(2,1)S(1)} %get-tuple-element.39.turned_ref), custom_call_target="tpu_custom_call" | custom-call | tf_op jit(solution)/shard_map/own_backward/pallas_call | solution.py:55
  29.1 0.1 collective-permute-done.9.far_ref
  29.2 0.9 %output_blocks.1 = (bf16[32,3072]{1,0:T(8,128)(2,1)S(1)}, bf16[16,1536]{1,0:T(8,128)(2,1)S(1)}, bf16[16,1536]{1,0:T(8,128)(2,1)S(1)}, bf16[16,1536]{1,0:T(8,128)(2,1)S(1)}, bf16[16,1536]{1,0:T(8,128)(2,1)S(1)}) custom-call(bf16[32,1536]{1,0:T(8,128)(2,1)S(1)} %grad_pre.1.grad_ref.own_ref, bf16[32,1536]{1,0:T(8,128)(2,1)S(1)} %collective-permute-done.9.far_ref, ...), custom_call_target="tpu_custom_call" | custom-call | tf_op jit(solution)/shard_map/output_blocks/pallas_call | solution.py:55
  30.1 3.1 %collective-permute-start.10 = (bf16[16,1536]{1,0:T(8,128)(2,1)S(1)}, bf16[16,1536]{1,0:T(8,128)(2,1)S(1)}, u32[]{:S(2)}, u32[]{:S(2)}) collective-permute-start(bf16[16,1536]{1,0:T(8,128)(2,1)S(1)} %get-tuple-element.41), channel_id=1, source_target_pairs={{0,3},{1,2},{2,1},{3,0},{4,7},{5,6},{6,5},{7,4},{8,11},{9,10},{10,... | collective-permute-start | bytes 147464 | tf_op jit(solution)/shard_map/ppermute | solution.py:344
  33.2 0.5 %collective-permute-start.11 = (bf16[16,1536]{1,0:T(8,128)(2,1)S(1)}, bf16[16,1536]{1,0:T(8,128)(2,1)S(1)}, u32[]{:S(2)}, u32[]{:S(2)}) collective-permute-start(bf16[16,1536]{1,0:T(8,128)(2,1)S(1)} %get-tuple-element.42), channel_id=1, source_target_pairs={{0,2},{1,3},{2,0},{3,1},{4,6},{5,7},{6,4},{7,5},{8,10},{9,11},{10,... | collective-permute-start | bytes 147464 | tf_op jit(solution)/shard_map/ppermute | solution.py:344
  33.7 0.9 %collective-permute-start.12 = (bf16[16,1536]{1,0:T(8,128)(2,1)S(1)}, bf16[16,1536]{1,0:T(8,128)(2,1)S(1)}, u32[]{:S(2)}, u32[]{:S(2)}) collective-permute-start(bf16[16,1536]{1,0:T(8,128)(2,1)S(1)} %get-tuple-element.43), channel_id=1, source_target_pairs={{0,1},{1,0},{2,3},{3,2},{4,5},{5,4},{6,7},{7,6},{8,9},{9,8},{10,11... | collective-permute-start | bytes 147464 | tf_op jit(solution)/shard_map/ppermute | solution.py:344
  34.6 4.1 %weight_in_grad.1.refs_4_ = bf16[1536,3072]{1,0:T(8,128)(2,1)} custom-call(bf16[32,1536]{1,0:T(8,128)(2,1)S(1)} %get-tuple-element.33.x_ref.left_ref, bf16[32,3072]{1,0:T(8,128)(2,1)S(1)} %get-tuple-element.45.right_ref.hidden_ref), custom_call_target="tpu_custom_call" | custom-call | tf_op jit(solution)/shard_map/weight_in_grad/pallas_call | solution.py:295
  38.7 0.0 collective-permute-done.10.refs_0_
  38.7 0.1 collective-permute-done.11.refs_1_
  38.8 0.0 collective-permute-done.12.refs_2_
  38.8 0.0 copy-done
  38.9 1.6 %collective-permute-start.13 = (bf16[8,1536]{1,0:T(8,128)(2,1)S(1)}, bf16[8,1536]{1,0:T(8,128)(2,1)S(1)}, u32[]{:S(2)}, u32[]{:S(2)}) collective-permute-start(bf16[8,1536]{1,0:T(8,128)(2,1)S(1)} %get-tuple-element.47), channel_id=1, source_target_pairs={{0,8},{8,0},{1,9},{9,1},{2,10},{10,2},{3,11},{11,3},{4,12},{12,4},... | collective-permute-start | bytes 73736 | tf_op jit(solution)/shard_map/ppermute | solution.py:455
  40.4 2.6 %weight_out_grad_far.1 = bf16[3072,1536]{1,0:T(8,128)(2,1)} custom-call(bf16[32,1536]{1,0:T(8,128)(2,1)S(1)} %collective-permute-done.8.far_ref.left_ref, bf16[32,1536]{1,0:T(8,128)(2,1)S(1)} %get-tuple-element.36.dy_ref.right_ref, bf16[3072,1536]{1,0:T(8,128)(2,1)} %weight_out_grad_own.1.later_ref.refs_0_), custom_call_target="tpu_custom_call", output_to_operand_aliasing={{}: (2, {})} | custom-call | tf_op jit(solution)/shard_map/weight_out_grad_far/pallas_call | solution.py:295
  43.0 0.0 collective-permute-done.13.got_ref
  43.0 0.7 %final_rows.1 = (bf16[4,3072]{1,0:T(4,128)(2,1)}, bf16[4,3072]{1,0:T(4,128)(2,1)}, f32[1,3072]{1,0:T(1,128)}, f32[1,3072]{1,0:T(1,128)}) custom-call(bf16[8,1536]{1,0:T(8,128)(2,1)S(1)} %get-tuple-element.46.own_ref, bf16[8,1536]{1,0:T(8,128)(2,1)S(1)} %collective-permute-done.13.got_ref, f32[1,1536]{1,0:T(1,128)S(1)} %get-tuple-element.35.sums_ref, ...), custom_call_target="tpu_custom_call" | custom-call | tf_op jit(solution)/shard_map/final_rows/pallas_call | solution.py:55
  (6 shorter events, 0.2 us)
Async XLA Ops:
  1.5 4.9 %collective-permute-start = (bf16[8,1536]{1,0:T(8,128)(2,1)S(1)}, bf16[8,1536]{1,0:T(8,128)(2,1)S(1)}, u32[]{:S(2)}, u32[]{:S(2)}) collective-permute-start(bf16[8,1536]{1,0:T(8,128)(2,1)S(1)} %get-tuple-element.52.after_ref), channel_id=1, source_target_pairs={{0,8},{8,0},{1,9},{9,1},{2,10},{10,2},{3,11},{11,3},{4,12},{12,4},... | collective-permute-start | bytes 73736 | tf_op jit(solution)/shard_map/ppermute | solution.py:358
  6.4 9.1 %collective-permute-start.1 = (bf16[16,1664]{1,0:T(8,128)(2,1)S(1)}, bf16[16,1664]{1,0:T(8,128)(2,1)S(1)}, u32[]{:S(2)}, u32[]{:S(2)}) collective-permute-start(bf16[16,1664]{1,0:T(8,128)(2,1)S(1)} %get-tuple-element.29), channel_id=1, source_target_pairs={{0,3},{1,2},{2,1},{3,0},{4,7},{5,6},{6,5},{7,4},{8,11},{9,10},{10,... | collective-permute-start | bytes 159752 | tf_op jit(solution)/shard_map/ppermute | solution.py:344
  10.5 4.2 %collective-permute-start.3 = (bf16[16,1536]{1,0:T(8,128)(2,1)S(1)}, bf16[16,1536]{1,0:T(8,128)(2,1)S(1)}, u32[]{:S(2)}, u32[]{:S(2)}) collective-permute-start(bf16[16,1536]{1,0:T(8,128)(2,1)S(1)} %get-tuple-element.30.after_ref.refs_3_), channel_id=1, source_target_pairs={{0,1},{1,0},{2,3},{3,2},{4,5},{5,4},{6,7},{7,6},{8,9},{9,8},{10,11... | collective-permute-start | bytes 147464 | tf_op jit(solution)/shard_map/ppermute | solution.py:344
  10.5 5.0 %collective-permute-start.2 = (bf16[16,1536]{1,0:T(8,128)(2,1)S(1)}, bf16[16,1536]{1,0:T(8,128)(2,1)S(1)}, u32[]{:S(2)}, u32[]{:S(2)}) collective-permute-start(bf16[16,1536]{1,0:T(8,128)(2,1)S(1)} %get-tuple-element.30.after_ref.refs_3_), channel_id=1, source_target_pairs={{0,2},{1,3},{2,0},{3,1},{4,6},{5,7},{6,4},{7,5},{8,10},{9,11},{10,... | collective-permute-start | bytes 147464 | tf_op jit(solution)/shard_map/ppermute | solution.py:344
  11.2 8.2 %slice-start = ((s8[9437184]{0:T(1024)(128)(4,1)}), s8[1048576]{0:T(1024)(128)(4,1)S(1)}, s32[]{:S(2)}) async-start(s8[9437184]{0:T(1024)(128)(4,1)} %bitcast.4), calls=%async_computation | async-start | bytes 2097152
  11.2 8.2 %slice-start.1 = ((s8[9437184]{0:T(1024)(128)(4,1)}), s8[4194304]{0:T(1024)(128)(4,1)S(1)}, s32[]{:S(2)}) async-start(s8[9437184]{0:T(1024)(128)(4,1)} %bitcast.4), calls=%async_computation.1 | async-start | bytes 8388608
  15.5 3.8 %slice-start.2 = ((s8[9437184]{0:T(1024)(128)(4,1)}), s8[4194304]{0:T(1024)(128)(4,1)S(1)}, s32[]{:S(2)}) async-start(s8[9437184]{0:T(1024)(128)(4,1)} %bitcast.4), calls=%async_computation.2 | async-start | bytes 8388608
  16.4 1.3 %collective-permute-start.4 = (bf16[32,1536]{1,0:T(8,128)(2,1)S(1)}, bf16[32,1536]{1,0:T(8,128)(2,1)S(1)}, u32[]{:S(2)}, u32[]{:S(2)}) collective-permute-start(bf16[32,1536]{1,0:T(8,128)(2,1)S(1)} %get-tuple-element.34.after_ref), channel_id=1, source_target_pairs={{0,4},{4,0},{1,5},{5,1},{2,6},{6,2},{3,7},{7,3},{8,12},{12,8},{9,1... | collective-permute-start | bytes 294920 | tf_op jit(solution)/shard_map/ppermute | solution.py:399
  17.8 5.2 %collective-permute-start.5 = (bf16[32,1664]{1,0:T(8,128)(2,1)S(1)}, bf16[32,1664]{1,0:T(8,128)(2,1)S(1)}, u32[]{:S(2)}, u32[]{:S(2)}) collective-permute-start(bf16[32,1664]{1,0:T(8,128)(2,1)S(1)} %add_pre.1.after_ref.own_ref), channel_id=1, source_target_pairs={{0,8},{8,0},{1,9},{9,1},{2,10},{10,2},{3,11},{11,3},{4,12},{12,4},... | collective-permute-start | bytes 319496 | tf_op jit(solution)/shard_map/ppermute | solution.py:402
  19.4 3.6 %copy-start.1 = (f32[3072]{0:T(1024)S(1)}, f32[3072]{0:T(1024)}, u32[]{:S(2)}) copy-start(f32[3072]{0:T(1024)} %param.8) | copy-start | bytes 36868
  20.8 1.5 %collective-permute-start.6 = (bf16[32,1536]{1,0:T(8,128)(2,1)S(1)}, bf16[32,1536]{1,0:T(8,128)(2,1)S(1)}, u32[]{:S(2)}, u32[]{:S(2)}) collective-permute-start(bf16[32,1536]{1,0:T(8,128)(2,1)S(1)} %far_grad.1), channel_id=1, source_target_pairs={{0,4},{4,0},{1,5},{5,1},{2,6},{6,2},{3,7},{7,3},{8,12},{12,8},{9,1... | collective-permute-start | bytes 294920 | tf_op jit(solution)/shard_map/ppermute | solution.py:404
  22.4 5.4 %collective-permute-start.7 = (bf16[32,1664]{1,0:T(8,128)(2,1)S(1)}, bf16[32,1664]{1,0:T(8,128)(2,1)S(1)}, u32[]{:S(2)}, u32[]{:S(2)}) collective-permute-start(bf16[32,1664]{1,0:T(8,128)(2,1)S(1)} %add_grad.1.after_ref.own_ref), channel_id=1, source_target_pairs={{0,8},{8,0},{1,9},{9,1},{2,10},{10,2},{3,11},{11,3},{4,12},{12,4},... | collective-permute-start | bytes 319496 | tf_op jit(solution)/shard_map/ppermute | solution.py:407
  23.1 3.7 %collective-permute-start.8 = (bf16[32,1536]{1,0:T(8,128)(2,1)S(1)}, bf16[32,1536]{1,0:T(8,128)(2,1)S(1)}, u32[]{:S(2)}, u32[]{:S(2)}) collective-permute-start(bf16[32,1536]{1,0:T(8,128)(2,1)S(1)} %get-tuple-element.38.act_ref.left_ref), channel_id=1, source_target_pairs={{0,4},{4,0},{1,5},{5,1},{2,6},{6,2},{3,7},{7,3},{8,12},{12,8},{9,1... | collective-permute-start | bytes 294920 | tf_op jit(solution)/shard_map/ppermute | solution.py:411
  27.8 1.4 %collective-permute-start.9 = (bf16[32,1536]{1,0:T(8,128)(2,1)S(1)}, bf16[32,1536]{1,0:T(8,128)(2,1)S(1)}, u32[]{:S(2)}, u32[]{:S(2)}) collective-permute-start(bf16[32,1536]{1,0:T(8,128)(2,1)S(1)} %grad_pre.1.grad_ref.own_ref), channel_id=1, source_target_pairs={{0,4},{4,0},{1,5},{5,1},{2,6},{6,2},{3,7},{7,3},{8,12},{12,8},{9,1... | collective-permute-start | bytes 294920 | tf_op jit(solution)/shard_map/ppermute | solution.py:426
  28.2 10.6 %copy-start = (f32[3072]{0:T(1024)S(1)}, f32[3072]{0:T(1024)}, u32[]{:S(2)}) copy-start(f32[3072]{0:T(1024)} %param.10) | copy-start | bytes 36868
  30.1 8.6 %collective-permute-start.10 = (bf16[16,1536]{1,0:T(8,128)(2,1)S(1)}, bf16[16,1536]{1,0:T(8,128)(2,1)S(1)}, u32[]{:S(2)}, u32[]{:S(2)}) collective-permute-start(bf16[16,1536]{1,0:T(8,128)(2,1)S(1)} %get-tuple-element.41), channel_id=1, source_target_pairs={{0,3},{1,2},{2,1},{3,0},{4,7},{5,6},{6,5},{7,4},{8,11},{9,10},{10,... | collective-permute-start | bytes 147464 | tf_op jit(solution)/shard_map/ppermute | solution.py:344
  33.2 5.6 %collective-permute-start.11 = (bf16[16,1536]{1,0:T(8,128)(2,1)S(1)}, bf16[16,1536]{1,0:T(8,128)(2,1)S(1)}, u32[]{:S(2)}, u32[]{:S(2)}) collective-permute-start(bf16[16,1536]{1,0:T(8,128)(2,1)S(1)} %get-tuple-element.42), channel_id=1, source_target_pairs={{0,2},{1,3},{2,0},{3,1},{4,6},{5,7},{6,4},{7,5},{8,10},{9,11},{10,... | collective-permute-start | bytes 147464 | tf_op jit(solution)/shard_map/ppermute | solution.py:344
  33.7 5.1 %collective-permute-start.12 = (bf16[16,1536]{1,0:T(8,128)(2,1)S(1)}, bf16[16,1536]{1,0:T(8,128)(2,1)S(1)}, u32[]{:S(2)}, u32[]{:S(2)}) collective-permute-start(bf16[16,1536]{1,0:T(8,128)(2,1)S(1)} %get-tuple-element.43), channel_id=1, source_target_pairs={{0,1},{1,0},{2,3},{3,2},{4,5},{5,4},{6,7},{7,6},{8,9},{9,8},{10,11... | collective-permute-start | bytes 147464 | tf_op jit(solution)/shard_map/ppermute | solution.py:344
  38.9 4.1 %collective-permute-start.13 = (bf16[8,1536]{1,0:T(8,128)(2,1)S(1)}, bf16[8,1536]{1,0:T(8,128)(2,1)S(1)}, u32[]{:S(2)}, u32[]{:S(2)}) collective-permute-start(bf16[8,1536]{1,0:T(8,128)(2,1)S(1)} %get-tuple-element.47), channel_id=1, source_target_pairs={{0,8},{8,0},{1,9},{9,1},{2,10},{10,2},{3,11},{11,3},{4,12},{12,4},... | collective-permute-start | bytes 73736 | tf_op jit(solution)/shard_map/ppermute | solution.py:455

commit v15 on v14

--- a/solution.py
+++ b/solution.py
@@ -32,10 +32,6 @@
 
 def exchange(chunks, axes):
     return lax.all_to_all(chunks, axes, split_axis=0, concat_axis=0, tiled=True)
-
-
-def dot_turned(rows, weight):
-    return dot(weight, rows, 1, 1).T
 
 
 def tile_of(size, most):
@@ -113,9 +109,9 @@
     return (1 - lax.axis_index("kin")) * half
 
 
-def half_tiles(half, mine, most):
+def half_tiles(half, mine):
     first = own_rows(half) if mine else far_rows(half)
-    tile = tile_of(half, most)
+    tile = tile_of(half, 512)
     return [
         (pl.ds(i * tile, tile), pl.ds(pl.multiple_of(first + i * tile, tile), tile))
         for i in range(half // tile)
@@ -138,7 +134,8 @@
         copy.wait()
 
 
-def load_and_turn_body(hbm_ref, after_ref, far_ref, own_ref, last_ref, own_turned, far_turned, sems):
+def load_and_turn_body(hbm_ref, after_ref, far_ref, w_out_ref, *refs):
+    own_ref, last_ref, own_turned, far_turned, out_turned, sems = refs
     wide, half = own_ref.shape
     first, last = far_ref.shape[1], last_ref.shape[1]
     size = wide // 4
@@ -154,6 +151,8 @@
     ]
     for copy in copies[0] + copies[1]:
         copy.start()
+    for part in tiles_of(w_out_ref.shape[0]):
+        out_turned[:, part] = w_out_ref[part, :].T
     for part in parts:
         far_turned[:first, part] = far_ref[part, :].T
     for part, copy in zip(parts, copies[0]):
@@ -194,16 +193,16 @@
         own_ref[:, at] = dot(x_cols, w_in_ref[:, at], 1, 0)
 
 
-def far_grad_body(dy_ref, w_out_ref, after_ref, sent_ref):
+def far_grad_body(dy_ref, turned_ref, after_ref, sent_ref):
     dy_cols = dy_ref[...]
-    for at, there in half_tiles(sent_ref.shape[1], False, 1536):
-        sent_ref[:, at] = dot_turned(dy_cols, w_out_ref[there, :]).astype(bf16)
-
-
-def own_grad_body(dy_ref, w_out_ref, own_ref):
+    for at, there in half_tiles(sent_ref.shape[1], False):
+        sent_ref[:, at] = dot(dy_cols, turned_ref[:, there], 1, 0).astype(bf16)
+
+
+def own_grad_body(dy_ref, turned_ref, own_ref):
     dy_cols = dy_ref[...]
-    for at, there in half_tiles(own_ref.shape[1], True, 1536):
-        own_ref[:, at] = dot(dy_cols, w_out_ref[there, :], 1, 1)
+    for at, there in half_tiles(own_ref.shape[1], True):
+        own_ref[:, at] = dot(dy_cols, turned_ref[:, there], 1, 0)
 
 
 def add_body(own_ref, got_ref, out_ref):
@@ -250,7 +249,7 @@
 def far_forward_body(far_ref, w_out_ref, terms_ref, out_ref):
     act = far_ref[...]
     part = half_of(act.shape[1], False)
-    for at in tiles_of(out_ref.shape[1], 1536):
+    for at in tiles_of(out_ref.shape[1]):
         out_ref[:, at] = terms_ref[:, at] + dot(act, w_out_ref[part, at], 1, 0)
 
 
@@ -373,14 +372,16 @@
         )
         pieces = [across(tiles, shift) for shift in range(1, nn - 1)]
         pieces = [across(farthest, nn - 1)] + pieces[::-1] + [tiles]
-        in_own, in_last, own_turned, far_turned = call(
+        in_own, in_last, own_turned, far_turned, out_turned = call(
             load_and_turn_body,
             "load_own",
-            [like((wide, half), bf16), like((wide, last), bf16)] + [like((half, wide), bf16)] * 2,
+            [like((wide, half), bf16), like((wide, last), bf16)]
+            + [like((half, wide), bf16)] * 2
+            + [like((wide, hid), bf16)],
             grant=8 * MIB,
             scratch=[sem((2, 4))],
-            specs=[hbm, pl.BlockSpec(memory_space=pl.ANY), whole],
-        )(in_hbm(weight_in), tiles, kept(in_far))
+            specs=[hbm, pl.BlockSpec(memory_space=pl.ANY), whole, whole],
+        )(in_hbm(weight_in), tiles, kept(in_far), kept(weight_out))
 
         def product(body, name, outs, *args):
             return call(body, name, outs, grant=8 * MIB)(*map(kept, args))
@@ -400,9 +401,9 @@
         (own,) = product(own_pre_body, "own_pre", [like((count, half), f32)], x_cols, in_own, sent)
         (own_pre,) = product(add_pre_body, "add_pre", [crossing], own, got, sums)
         other_pre = lax.ppermute(own_pre, "tok", swap)
-        (sent,) = product(far_grad_body, "far_grad", [side], dy_cols, weight_out, own_pre)
+        (sent,) = product(far_grad_body, "far_grad", [side], dy_cols, out_turned, own_pre)
         got = lax.ppermute(sent, "kin", swap)
-        (own,) = product(own_grad_body, "own_grad", [like((count, half), f32)], dy_cols, weight_out)
+        (own,) = product(own_grad_body, "own_grad", [like((count, half), f32)], dy_cols, out_turned)
         (own_grad,) = product(add_body, "add_grad", [crossing], own, got)
         other_grad = lax.ppermute(own_grad, "tok", swap)
         slopes, act_own = call(gelu_body, "gelu", [like((count, half), f32), side])(

time: 44 us -> 46.1 us (1.048)
  Pallas kernels: 24 us -> 25.5 us
    pallas_call x17, Pallas kernels: 14.7 us -> 16.3 us  [run(): pl.pallas_call(body, out_shape=shapes, in_specs=specs or [whole] * len(ar...]
    ppermute x1, waiting for transfers between devices: 0.01 us -> 0.67 us  [on_device(): other_pre = lax.ppermute(own_pre, 'tok', swap)]
    ppermute x6, waiting for transfers between devices: 0.88 us -> 0.37 us  [across(): return lax.ppermute(array, 'nout', [(i, i ^ shift) for i in range(nn)])]
  transfers between devices with their start and end apart: 14 -> 14, of which waited for: 4 -> 5; matrix products, arithmetic and copies ran while one was open for 0% -> 0% of each run, Pallas kernels for 49% -> 50%
where the time goes in v15:
time: 46.1 us; the launch traced here: 45.8 us
  Pallas kernels  25.5 us (55%)
  starting transfers between devices  16.6 us (36%)
  waiting for transfers between devices  1.87 us (4%)
  other arithmetic  1.01 us (2%)
  between operations  0.83 us (2%)
    pallas_call x17, Pallas kernels, run(): pl.pallas_call(body, out_shape=shapes, in_specs=specs or [whole] * len(ar...  16.3 us
    pallas_call x3, Pallas kernels, outer(): pl.pallas_call(functools.partial(outer_body, most, first_of), out_shape=l...  9.23 us
    ppermute x6, starting transfers between devices, across(): return lax.ppermute(array, 'nout', [(i, i ^ shift) for i in range(nn)])  9.19 us
    ppermute x2, starting transfers between devices, on_device(): got = lax.ppermute(sent, 'tok', swap)  4.57 us
    ppermute x1, starting transfers between devices, on_device(): other_pre = lax.ppermute(own_pre, 'tok', swap)  1.7 us
    concatenate x1, other arithmetic, on_device(): mine = jnp.concatenate([tokens, grad_out], axis=0)  1.01 us
  transfers between devices with their start and end apart: 14, of which 5 were waited for; matrix products, arithmetic and copies ran while one was open for 0% of the time, Pallas kernels for 50%

profile of v15, /device:TPU:0, one launch (start us, length us, event | category | flops | bytes accessed | tf_op | source)
XLA Modules:
  0.0 45.8 jit_solution(15437188899850220009)
XLA Ops:
  0.6 0.0 copy-start
  0.6 1.0 %fusion = (bf16[8,1536]{1,0:T(8,128)(2,1)S(1)}, bf16[8,1536]{1,0:T(8,128)(2,1)S(1)}) fusion(s32[]{:T(128)S(6)} %select_n.7, bf16[4,3072]{1,0:T(4,128)(2,1)} %param.6, bf16[4,3072]{1,0:T(4,128)(2,1)} %param.11, s32[]{:T(128)S(6)} %select_n.6), kind=kLoop, calls=%fused_computation.4 | loop fusion | flops 98304 | bytes 98312 | tf_op jit(solution)/shard_map/concatenate | solution.py:353
  1.7 3.0 %collective-permute-start = (bf16[8,1536]{1,0:T(8,128)(2,1)S(1)}, bf16[8,1536]{1,0:T(8,128)(2,1)S(1)}, u32[]{:S(2)}, u32[]{:S(2)}) collective-permute-start(bf16[8,1536]{1,0:T(8,128)(2,1)S(1)} %get-tuple-element.54.after_ref), channel_id=1, source_target_pairs={{0,8},{8,0},{1,9},{9,1},{2,10},{10,2},{3,11},{11,3},{4,12},{12,4},... | collective-permute-start | bytes 73736 | tf_op jit(solution)/shard_map/ppermute | solution.py:357
  4.7 1.9 %load_far.1.after_ref.far_ref.refs_4_ = bf16[1536,1024]{1,0:T(8,128)(2,1)S(1)} custom-call(bf16[1536,3072]{1,0:T(8,128)(2,1)} %hbm_ref.3, bf16[8,1536]{1,0:T(8,128)(2,1)S(1)} %get-tuple-element.54.after_ref), custom_call_target="tpu_custom_call" | custom-call | tf_op jit(solution)/shard_map/load_far/pallas_call | solution.py:51
  6.6 0.0 collective-permute-done.got_ref
  6.6 4.1 %collective-permute-start.1 = (bf16[16,1664]{1,0:T(8,128)(2,1)S(1)}, bf16[16,1664]{1,0:T(8,128)(2,1)S(1)}, u32[]{:S(2)}, u32[]{:S(2)}) collective-permute-start(bf16[16,1664]{1,0:T(8,128)(2,1)S(1)} %get-tuple-element.30), channel_id=1, source_target_pairs={{0,3},{1,2},{2,1},{3,0},{4,7},{5,6},{6,5},{7,4},{8,11},{9,10},{10,... | collective-permute-start | bytes 159752 | tf_op jit(solution)/shard_map/ppermute | solution.py:343
  10.7 0.0 collective-permute-start.3
  10.7 0.6 %collective-permute-start.2 = (bf16[16,1536]{1,0:T(8,128)(2,1)S(1)}, bf16[16,1536]{1,0:T(8,128)(2,1)S(1)}, u32[]{:S(2)}, u32[]{:S(2)}) collective-permute-start(bf16[16,1536]{1,0:T(8,128)(2,1)S(1)} %get-tuple-element.31.after_ref.refs_3_), channel_id=1, source_target_pairs={{0,2},{1,3},{2,0},{3,1},{4,6},{5,7},{6,4},{7,5},{8,10},{9,11},{10,... | collective-permute-start | bytes 147464 | tf_op jit(solution)/shard_map/ppermute | solution.py:343
  11.3 0.0 copy-done
  11.3 6.2 %load_own.1 = (bf16[1536,1536]{1,0:T(8,128)(2,1)S(1)}, bf16[1536,512]{1,0:T(8,128)(2,1)S(1)}, bf16[1536,1536]{1,0:T(8,128)(2,1)S(1)}, bf16[1536,1536]{1,0:T(8,128)(2,1)S(1)}, bf16[1536,3072]{1,0:T(8,128)(2,1)S(1)}) custom-call(bf16[1536,3072]{1,0:T(8,128)(2,1)} %hbm_ref.3, bf16[16,1536]{1,0:T(8,128)(2,1)S(1)} %get-tuple-element.31.after_ref.refs_3_, ...), custom_call_target="tpu_custom_call" | custom-call | tf_op jit(solution)/shard_map/load_own/pallas_call | solution.py:51
  17.5 0.0 collective-permute-done.3.refs_2_
  17.5 0.0 collective-permute-done.2.refs_1_
  17.5 0.0 collective-permute-done.1.refs_0_
  17.5 0.9 %far_pre.1 = (bf16[32,1536]{1,0:T(8,128)(2,1)S(1)}, bf16[32,1536]{1,0:T(8,128)(2,1)S(1)}, bf16[32,1536]{1,0:T(8,128)(2,1)S(1)}, f32[1,1536]{1,0:T(1,128)S(1)}) custom-call(bf16[16,1664]{1,0:T(8,128)(2,1)S(1)} %collective-permute-done.1.refs_0_, bf16[16,1536]{1,0:T(8,128)(2,1)S(1)} %collective-permute-done.2.refs_1_, ...), custom_call_target="tpu_custom_call" | custom-call | tf_op jit(solution)/shard_map/far_pre/pallas_call | solution.py:51
  18.4 0.0 collective-permute-start.4
  18.5 0.9 %own_pre.1.own_ref = f32[32,1536]{1,0:T(8,128)S(1)} custom-call(bf16[32,1536]{1,0:T(8,128)(2,1)S(1)} %get-tuple-element.34.x_ref.left_ref, bf16[1536,1536]{1,0:T(8,128)(2,1)S(1)} %get-tuple-element.33.refs_6_.w_in_ref, bf16[32,1536]{1,0:T(8,128)(2,1)S(1)} %get-tuple-element.35.after_ref), custom_call_target="tpu_custom_call" | custom-call | tf_op jit(solution)/shard_map/own_pre/pallas_call | solution.py:51
  19.4 0.4 collective-permute-done.4.got_ref
  19.8 1.7 %collective-permute-start.5 = (bf16[32,1664]{1,0:T(8,128)(2,1)S(1)}, bf16[32,1664]{1,0:T(8,128)(2,1)S(1)}, u32[]{:S(2)}, u32[]{:S(2)}) collective-permute-start(bf16[32,1664]{1,0:T(8,128)(2,1)S(1)} %add_pre.1.after_ref.own_ref), channel_id=1, source_target_pairs={{0,8},{8,0},{1,9},{9,1},{2,10},{10,2},{3,11},{11,3},{4,12},{12,4},... | collective-permute-start | bytes 319496 | tf_op jit(solution)/shard_map/ppermute | solution.py:403
  21.5 0.0 copy-start.2
  21.5 0.9 %far_grad.1 = bf16[32,1536]{1,0:T(8,128)(2,1)S(1)} custom-call(bf16[32,1536]{1,0:T(8,128)(2,1)S(1)} %get-tuple-element.37.dy_ref.right_ref, bf16[1536,3072]{1,0:T(8,128)(2,1)S(1)} %get-tuple-element.38.turned_ref, bf16[32,1664]{1,0:T(8,128)(2,1)S(1)} %add_pre.1.after_ref.own_ref), custom_call_target="tpu_custom_call" | custom-call | tf_op jit(solution)/shard_map/far_grad/pallas_call | solution.py:51
  22.4 0.0 collective-permute-start.6
  22.4 0.9 %own_grad.1.own_ref = f32[32,1536]{1,0:T(8,128)S(1)} custom-call(bf16[32,1536]{1,0:T(8,128)(2,1)S(1)} %get-tuple-element.37.dy_ref.right_ref, bf16[1536,3072]{1,0:T(8,128)(2,1)S(1)} %get-tuple-element.38.turned_ref), custom_call_target="tpu_custom_call" | custom-call | tf_op jit(solution)/shard_map/own_grad/pallas_call | solution.py:51
  23.4 0.4 collective-permute-done.6.got_ref
  23.8 0.5 collective-permute-start.7
  24.2 0.7 %collective-permute-done.5.other_ref = bf16[32,1664]{1,0:T(8,128)(2,1)S(1)} collective-permute-done((bf16[32,1664]{1,0:T(8,128)(2,1)S(1)}, bf16[32,1664]{1,0:T(8,128)(2,1)S(1)}, u32[]{:S(2)}, u32[]{:S(2)}) %collective-permute-start.5) | collective-permute-done | bytes 106528 | tf_op jit(solution)/shard_map/ppermute | solution.py:403
  24.9 0.0 copy-done.2
  24.9 0.1 gelu.1
  25.0 0.1 collective-permute-start.8
  25.1 0.9 %own_forward.1.terms_ref = f32[32,1536]{1,0:T(8,128)S(1)} custom-call(bf16[32,1536]{1,0:T(8,128)(2,1)S(1)} %get-tuple-element.40.act_ref.left_ref, bf16[3072,1536]{1,0:T(8,128)(2,1)S(1)} %copy-done), custom_call_target="tpu_custom_call" | custom-call | tf_op jit(solution)/shard_map/own_forward/pallas_call | solution.py:51
  26.0 2.6 %weight_out_grad_own.1.later_ref.refs_0_ = bf16[3072,1536]{1,0:T(8,128)(2,1)} custom-call(bf16[32,1536]{1,0:T(8,128)(2,1)S(1)} %get-tuple-element.40.act_ref.left_ref, bf16[32,1536]{1,0:T(8,128)(2,1)S(1)} %get-tuple-element.37.dy_ref.right_ref), custom_call_target="tpu_custom_call" | custom-call | tf_op jit(solution)/shard_map/weight_out_grad_own/pallas_call | solution.py:294
  28.6 0.0 collective-permute-done.8.far_ref.left_ref
  28.6 0.9 %far_forward.1.after_ref.forward_ref = f32[32,1536]{1,0:T(8,128)S(1)} custom-call(bf16[32,1536]{1,0:T(8,128)(2,1)S(1)} %collective-permute-done.8.far_ref.left_ref, bf16[3072,1536]{1,0:T(8,128)(2,1)S(1)} %copy-done, f32[32,1536]{1,0:T(8,128)S(1)} %own_forward.1.terms_ref), custom_call_target="tpu_custom_call" | custom-call | tf_op jit(solution)/shard_map/far_forward/pallas_call | solution.py:51
  29.5 0.0 collective-permute-done.7.other_ref
  29.6 0.6 %collective-permute-start.9 = (bf16[32,1536]{1,0:T(8,128)(2,1)S(1)}, bf16[32,1536]{1,0:T(8,128)(2,1)S(1)}, u32[]{:S(2)}, u32[]{:S(2)}) collective-permute-start(bf16[32,1536]{1,0:T(8,128)(2,1)S(1)} %grad_pre.1.grad_ref.own_ref), channel_id=1, source_target_pairs={{0,4},{4,0},{1,5},{5,1},{2,6},{6,2},{3,7},{7,3},{8,12},{12,8},{9,1... | collective-permute-start | bytes 294920 | tf_op jit(solution)/shard_map/ppermute | solution.py:427
  30.1 0.0 copy-start.1
  30.1 0.9 %own_backward.1.backward_ref = f32[32,1536]{1,0:T(8,128)S(1)} custom-call(bf16[32,1536]{1,0:T(8,128)(2,1)S(1)} %grad_pre.1.grad_ref.own_ref, bf16[1536,1536]{1,0:T(8,128)(2,1)S(1)} %get-tuple-element.41.turned_ref), custom_call_target="tpu_custom_call" | custom-call | tf_op jit(solution)/shard_map/own_backward/pallas_call | solution.py:51
  31.0 0.0 collective-permute-done.9.far_ref
  31.1 0.9 %output_blocks.1 = (bf16[32,3072]{1,0:T(8,128)(2,1)S(1)}, bf16[16,1536]{1,0:T(8,128)(2,1)S(1)}, bf16[16,1536]{1,0:T(8,128)(2,1)S(1)}, bf16[16,1536]{1,0:T(8,128)(2,1)S(1)}, bf16[16,1536]{1,0:T(8,128)(2,1)S(1)}) custom-call(bf16[32,1536]{1,0:T(8,128)(2,1)S(1)} %grad_pre.1.grad_ref.own_ref, bf16[32,1536]{1,0:T(8,128)(2,1)S(1)} %collective-permute-done.9.far_ref, ...), custom_call_target="tpu_custom_call" | custom-call | tf_op jit(solution)/shard_map/output_blocks/pallas_call | solution.py:51
  32.0 3.8 %collective-permute-start.10 = (bf16[16,1536]{1,0:T(8,128)(2,1)S(1)}, bf16[16,1536]{1,0:T(8,128)(2,1)S(1)}, u32[]{:S(2)}, u32[]{:S(2)}) collective-permute-start(bf16[16,1536]{1,0:T(8,128)(2,1)S(1)} %get-tuple-element.43), channel_id=1, source_target_pairs={{0,3},{1,2},{2,1},{3,0},{4,7},{5,6},{6,5},{7,4},{8,11},{9,10},{10,... | collective-permute-start | bytes 147464 | tf_op jit(solution)/shard_map/ppermute | solution.py:343
  35.8 0.0 collective-permute-start.11
  35.8 0.7 %collective-permute-start.12 = (bf16[16,1536]{1,0:T(8,128)(2,1)S(1)}, bf16[16,1536]{1,0:T(8,128)(2,1)S(1)}, u32[]{:S(2)}, u32[]{:S(2)}) collective-permute-start(bf16[16,1536]{1,0:T(8,128)(2,1)S(1)} %get-tuple-element.45), channel_id=1, source_target_pairs={{0,1},{1,0},{2,3},{3,2},{4,5},{5,4},{6,7},{7,6},{8,9},{9,8},{10,11... | collective-permute-start | bytes 147464 | tf_op jit(solution)/shard_map/ppermute | solution.py:343
  36.5 4.1 %weight_in_grad.1.refs_4_ = bf16[1536,3072]{1,0:T(8,128)(2,1)} custom-call(bf16[32,1536]{1,0:T(8,128)(2,1)S(1)} %get-tuple-element.34.x_ref.left_ref, bf16[32,3072]{1,0:T(8,128)(2,1)S(1)} %get-tuple-element.47.right_ref.hidden_ref), custom_call_target="tpu_custom_call" | custom-call | tf_op jit(solution)/shard_map/weight_in_grad/pallas_call | solution.py:294
  40.6 0.0 collective-permute-done.10.refs_0_
  40.6 0.3 collective-permute-done.11.refs_1_
  40.9 0.1 collective-permute-done.12.refs_2_
  40.9 0.0 copy-done.1
  41.0 1.6 %collective-permute-start.13 = (bf16[8,1536]{1,0:T(8,128)(2,1)S(1)}, bf16[8,1536]{1,0:T(8,128)(2,1)S(1)}, u32[]{:S(2)}, u32[]{:S(2)}) collective-permute-start(bf16[8,1536]{1,0:T(8,128)(2,1)S(1)} %get-tuple-element.49), channel_id=1, source_target_pairs={{0,8},{8,0},{1,9},{9,1},{2,10},{10,2},{3,11},{11,3},{4,12},{12,4},... | collective-permute-start | bytes 73736 | tf_op jit(solution)/shard_map/ppermute | solution.py:456
  42.6 2.6 %weight_out_grad_far.1 = bf16[3072,1536]{1,0:T(8,128)(2,1)} custom-call(bf16[32,1536]{1,0:T(8,128)(2,1)S(1)} %collective-permute-done.8.far_ref.left_ref, bf16[32,1536]{1,0:T(8,128)(2,1)S(1)} %get-tuple-element.37.dy_ref.right_ref, bf16[3072,1536]{1,0:T(8,128)(2,1)} %weight_out_grad_own.1.later_ref.refs_0_), custom_call_target="tpu_custom_call", output_to_operand_aliasing={{}: (2, {})} | custom-call | tf_op jit(solution)/shard_map/weight_out_grad_far/pallas_call | solution.py:294
  45.1 0.0 collective-permute-done.13.got_ref
  45.1 0.7 %final_rows.1 = (bf16[4,3072]{1,0:T(4,128)(2,1)}, bf16[4,3072]{1,0:T(4,128)(2,1)}, f32[1,3072]{1,0:T(1,128)}, f32[1,3072]{1,0:T(1,128)}) custom-call(bf16[8,1536]{1,0:T(8,128)(2,1)S(1)} %get-tuple-element.48.own_ref, bf16[8,1536]{1,0:T(8,128)(2,1)S(1)} %collective-permute-done.13.got_ref, f32[1,1536]{1,0:T(1,128)S(1)} %get-tuple-element.36.sums_ref, ...), custom_call_target="tpu_custom_call" | custom-call | tf_op jit(solution)/shard_map/final_rows/pallas_call | solution.py:51
  (5 shorter events, 0.2 us)
Async XLA Ops:
  0.6 10.7 %copy-start = (bf16[3072,1536]{1,0:T(8,128)(2,1)S(1)}, bf16[3072,1536]{1,0:T(8,128)(2,1)}, u32[]{:S(2)}) copy-start(bf16[3072,1536]{1,0:T(8,128)(2,1)} %w_out_ref.5) | copy-start | bytes 28311556
  1.7 4.9 %collective-permute-start = (bf16[8,1536]{1,0:T(8,128)(2,1)S(1)}, bf16[8,1536]{1,0:T(8,128)(2,1)S(1)}, u32[]{:S(2)}, u32[]{:S(2)}) collective-permute-start(bf16[8,1536]{1,0:T(8,128)(2,1)S(1)} %get-tuple-element.54.after_ref), channel_id=1, source_target_pairs={{0,8},{8,0},{1,9},{9,1},{2,10},{10,2},{3,11},{11,3},{4,12},{12,4},... | collective-permute-start | bytes 73736 | tf_op jit(solution)/shard_map/ppermute | solution.py:357
  6.6 10.9 %collective-permute-start.1 = (bf16[16,1664]{1,0:T(8,128)(2,1)S(1)}, bf16[16,1664]{1,0:T(8,128)(2,1)S(1)}, u32[]{:S(2)}, u32[]{:S(2)}) collective-permute-start(bf16[16,1664]{1,0:T(8,128)(2,1)S(1)} %get-tuple-element.30), channel_id=1, source_target_pairs={{0,3},{1,2},{2,1},{3,0},{4,7},{5,6},{6,5},{7,4},{8,11},{9,10},{10,... | collective-permute-start | bytes 159752 | tf_op jit(solution)/shard_map/ppermute | solution.py:343
  10.7 6.8 %collective-permute-start.3 = (bf16[16,1536]{1,0:T(8,128)(2,1)S(1)}, bf16[16,1536]{1,0:T(8,128)(2,1)S(1)}, u32[]{:S(2)}, u32[]{:S(2)}) collective-permute-start(bf16[16,1536]{1,0:T(8,128)(2,1)S(1)} %get-tuple-element.31.after_ref.refs_3_), channel_id=1, source_target_pairs={{0,1},{1,0},{2,3},{3,2},{4,5},{5,4},{6,7},{7,6},{8,9},{9,8},{10,11... | collective-permute-start | bytes 147464 | tf_op jit(solution)/shard_map/ppermute | solution.py:343
  10.7 6.8 %collective-permute-start.2 = (bf16[16,1536]{1,0:T(8,128)(2,1)S(1)}, bf16[16,1536]{1,0:T(8,128)(2,1)S(1)}, u32[]{:S(2)}, u32[]{:S(2)}) collective-permute-start(bf16[16,1536]{1,0:T(8,128)(2,1)S(1)} %get-tuple-element.31.after_ref.refs_3_), channel_id=1, source_target_pairs={{0,2},{1,3},{2,0},{3,1},{4,6},{5,7},{6,4},{7,5},{8,10},{9,11},{10,... | collective-permute-start | bytes 147464 | tf_op jit(solution)/shard_map/ppermute | solution.py:343
  18.4 1.3 %collective-permute-start.4 = (bf16[32,1536]{1,0:T(8,128)(2,1)S(1)}, bf16[32,1536]{1,0:T(8,128)(2,1)S(1)}, u32[]{:S(2)}, u32[]{:S(2)}) collective-permute-start(bf16[32,1536]{1,0:T(8,128)(2,1)S(1)} %get-tuple-element.35.after_ref), channel_id=1, source_target_pairs={{0,4},{4,0},{1,5},{5,1},{2,6},{6,2},{3,7},{7,3},{8,12},{12,8},{9,1... | collective-permute-start | bytes 294920 | tf_op jit(solution)/shard_map/ppermute | solution.py:400
  19.8 5.1 %collective-permute-start.5 = (bf16[32,1664]{1,0:T(8,128)(2,1)S(1)}, bf16[32,1664]{1,0:T(8,128)(2,1)S(1)}, u32[]{:S(2)}, u32[]{:S(2)}) collective-permute-start(bf16[32,1664]{1,0:T(8,128)(2,1)S(1)} %add_pre.1.after_ref.own_ref), channel_id=1, source_target_pairs={{0,8},{8,0},{1,9},{9,1},{2,10},{10,2},{3,11},{11,3},{4,12},{12,4},... | collective-permute-start | bytes 319496 | tf_op jit(solution)/shard_map/ppermute | solution.py:403
  21.5 3.4 %copy-start.2 = (f32[3072]{0:T(1024)S(1)}, f32[3072]{0:T(1024)}, u32[]{:S(2)}) copy-start(f32[3072]{0:T(1024)} %param.8) | copy-start | bytes 36868
  22.4 1.3 %collective-permute-start.6 = (bf16[32,1536]{1,0:T(8,128)(2,1)S(1)}, bf16[32,1536]{1,0:T(8,128)(2,1)S(1)}, u32[]{:S(2)}, u32[]{:S(2)}) collective-permute-start(bf16[32,1536]{1,0:T(8,128)(2,1)S(1)} %far_grad.1), channel_id=1, source_target_pairs={{0,4},{4,0},{1,5},{5,1},{2,6},{6,2},{3,7},{7,3},{8,12},{12,8},{9,1... | collective-permute-start | bytes 294920 | tf_op jit(solution)/shard_map/ppermute | solution.py:405
  23.8 5.8 %collective-permute-start.7 = (bf16[32,1664]{1,0:T(8,128)(2,1)S(1)}, bf16[32,1664]{1,0:T(8,128)(2,1)S(1)}, u32[]{:S(2)}, u32[]{:S(2)}) collective-permute-start(bf16[32,1664]{1,0:T(8,128)(2,1)S(1)} %add_grad.1.after_ref.own_ref), channel_id=1, source_target_pairs={{0,8},{8,0},{1,9},{9,1},{2,10},{10,2},{3,11},{11,3},{4,12},{12,4},... | collective-permute-start | bytes 319496 | tf_op jit(solution)/shard_map/ppermute | solution.py:408
  25.0 3.6 %collective-permute-start.8 = (bf16[32,1536]{1,0:T(8,128)(2,1)S(1)}, bf16[32,1536]{1,0:T(8,128)(2,1)S(1)}, u32[]{:S(2)}, u32[]{:S(2)}) collective-permute-start(bf16[32,1536]{1,0:T(8,128)(2,1)S(1)} %get-tuple-element.40.act_ref.left_ref), channel_id=1, source_target_pairs={{0,4},{4,0},{1,5},{5,1},{2,6},{6,2},{3,7},{7,3},{8,12},{12,8},{9,1... | collective-permute-start | bytes 294920 | tf_op jit(solution)/shard_map/ppermute | solution.py:412
  29.6 1.5 %collective-permute-start.9 = (bf16[32,1536]{1,0:T(8,128)(2,1)S(1)}, bf16[32,1536]{1,0:T(8,128)(2,1)S(1)}, u32[]{:S(2)}, u32[]{:S(2)}) collective-permute-start(bf16[32,1536]{1,0:T(8,128)(2,1)S(1)} %grad_pre.1.grad_ref.own_ref), channel_id=1, source_target_pairs={{0,4},{4,0},{1,5},{5,1},{2,6},{6,2},{3,7},{7,3},{8,12},{12,8},{9,1... | collective-permute-start | bytes 294920 | tf_op jit(solution)/shard_map/ppermute | solution.py:427
  30.1 10.8 %copy-start.1 = (f32[3072]{0:T(1024)S(1)}, f32[3072]{0:T(1024)}, u32[]{:S(2)}) copy-start(f32[3072]{0:T(1024)} %param.10) | copy-start | bytes 36868
  32.0 8.6 %collective-permute-start.10 = (bf16[16,1536]{1,0:T(8,128)(2,1)S(1)}, bf16[16,1536]{1,0:T(8,128)(2,1)S(1)}, u32[]{:S(2)}, u32[]{:S(2)}) collective-permute-start(bf16[16,1536]{1,0:T(8,128)(2,1)S(1)} %get-tuple-element.43), channel_id=1, source_target_pairs={{0,3},{1,2},{2,1},{3,0},{4,7},{5,6},{6,5},{7,4},{8,11},{9,10},{10,... | collective-permute-start | bytes 147464 | tf_op jit(solution)/shard_map/ppermute | solution.py:343
  35.8 5.0 %collective-permute-start.11 = (bf16[16,1536]{1,0:T(8,128)(2,1)S(1)}, bf16[16,1536]{1,0:T(8,128)(2,1)S(1)}, u32[]{:S(2)}, u32[]{:S(2)}) collective-permute-start(bf16[16,1536]{1,0:T(8,128)(2,1)S(1)} %get-tuple-element.44), channel_id=1, source_target_pairs={{0,2},{1,3},{2,0},{3,1},{4,6},{5,7},{6,4},{7,5},{8,10},{9,11},{10,... | collective-permute-start | bytes 147464 | tf_op jit(solution)/shard_map/ppermute | solution.py:343
  35.8 5.1 %collective-permute-start.12 = (bf16[16,1536]{1,0:T(8,128)(2,1)S(1)}, bf16[16,1536]{1,0:T(8,128)(2,1)S(1)}, u32[]{:S(2)}, u32[]{:S(2)}) collective-permute-start(bf16[16,1536]{1,0:T(8,128)(2,1)S(1)} %get-tuple-element.45), channel_id=1, source_target_pairs={{0,1},{1,0},{2,3},{3,2},{4,5},{5,4},{6,7},{7,6},{8,9},{9,8},{10,11... | collective-permute-start | bytes 147464 | tf_op jit(solution)/shard_map/ppermute | solution.py:343
  41.0 4.1 %collective-permute-start.13 = (bf16[8,1536]{1,0:T(8,128)(2,1)S(1)}, bf16[8,1536]{1,0:T(8,128)(2,1)S(1)}, u32[]{:S(2)}, u32[]{:S(2)}) collective-permute-start(bf16[8,1536]{1,0:T(8,128)(2,1)S(1)} %get-tuple-element.49), channel_id=1, source_target_pairs={{0,8},{8,0},{1,9},{9,1},{2,10},{10,2},{3,11},{11,3},{4,12},{12,4},... | collective-permute-start | bytes 73736 | tf_op jit(solution)/shard_map/ppermute | solution.py:456

commit v16 on v14

--- a/solution.py
+++ b/solution.py
@@ -240,13 +240,6 @@
     grad_ref[...] = (grad_act * slopes_ref[...]).astype(bf16)
 
 
-def own_forward_body(act_ref, w_out_ref, out_ref):
-    act = act_ref[...]
-    part = half_of(act.shape[1], True)
-    for at in tiles_of(out_ref.shape[1]):
-        out_ref[:, at] = dot(act, w_out_ref[part, at], 1, 0)
-
-
 def far_forward_body(far_ref, w_out_ref, terms_ref, out_ref):
     act = far_ref[...]
     part = half_of(act.shape[1], False)
@@ -272,7 +265,12 @@
 
 
 def outer_body(most, first_of, left_ref, right_ref, *refs):
-    out_hbm, block_ref, sems = refs[-3:]
+    copies = start_outer(most, first_of, left_ref, right_ref, *refs[-3:])
+    for copy in copies:
+        copy.wait()
+
+
+def start_outer(most, first_of, left_ref, right_ref, out_hbm, block_ref, sems):
     first = first_of(left_ref.shape[1])
     copies = []
     for i, at in enumerate(tiles_of(left_ref.shape[1], most)):
@@ -284,8 +282,34 @@
             pltpu.make_async_copy(block_ref.at[at, :], out_hbm.at[there, :], sems.at[i])
         )
         copies[-1].start()
+    return copies
+
+
+def own_forward_body(act_ref, dy_ref, w_out_ref, terms_ref, out_hbm, block_ref, sems):
+    copies = start_outer(128, own_rows, act_ref, dy_ref, out_hbm, block_ref, sems)
+    act = act_ref[...]
+    part = half_of(act.shape[1], True)
+    for at in tiles_of(terms_ref.shape[1]):
+        terms_ref[:, at] = dot(act, w_out_ref[part, at], 1, 0)
     for copy in copies:
         copy.wait()
+
+
+def own_forward(act, dy_cols, weight_out):
+    count, half = act.shape
+    hid, wide = weight_out.shape
+    return pl.pallas_call(
+        own_forward_body,
+        out_shape=[pltpu.VMEM((count, wide), f32), like((hid, wide), bf16)],
+        in_specs=[whole] * 3,
+        out_specs=[whole, pl.BlockSpec(memory_space=pl.ANY)],
+        scratch_shapes=[
+            pltpu.VMEM((half, wide), bf16),
+            pltpu.SemaphoreType.DMA((len(tiles_of(half, 128)),)),
+        ],
+        compiler_params=pltpu.CompilerParams(vmem_limit_bytes=16 * MIB),
+        name="own_forward",
+    )(kept(act), kept(dy_cols), kept(weight_out))
 
 
 def outer(left, right, high, name, first_of, into=None, most=128):
@@ -409,11 +433,10 @@
             bias_in.reshape(1, hid), kept(own_pre), kept(other_pre), kept(own_grad)
         )
         act_far = lax.ppermute(act_own, "kin", swap)
-        (forward,) = product(own_forward_body, "own_forward", [ends], act_own, weight_out)
+        forward, weight_out_grad = own_forward(act_own, dy_cols, weight_out)
         (forward,) = product(
             far_forward_body, "far_forward", [ends], act_far, weight_out, forward
         )
-        weight_out_grad = outer(act_own, dy_cols, hid, "weight_out_grad_own", own_rows)
         (grad_own,) = call(
             grad_pre_body, "grad_pre", [side], specs=[whole] * 4 + [hbm]
         )(

time: 44 us -> 43.7 us (level)
  waiting for transfers between devices: 1.42 us -> 2.59 us
  starting transfers between devices: 16.6 us -> 15.7 us
  Pallas kernels: 24 us -> 23.4 us
    pallas_call x0 -> x1, Pallas kernels: none -> 2.86 us  [own_forward(): pl.pallas_call(own_forward_body, out_shape=[pltpu.VMEM((count, wide), f32...]
    pallas_call x3 -> x2, Pallas kernels: 9.25 us -> 6.67 us  [outer(): pl.pallas_call(functools.partial(outer_body, most, first_of), out_shape=l...]
    pallas_call x17 -> x16, Pallas kernels: 14.7 us -> 13.8 us  [run(): pl.pallas_call(body, out_shape=shapes, in_specs=specs or [whole] * len(ar...]
    ppermute x1, waiting for transfers between devices: 0.03 us -> 0.64 us  [on_device(): other_grad = lax.ppermute(own_grad, 'tok', swap)]
    ppermute x2, starting transfers between devices: 4.55 us -> 3.99 us  [on_device(): got = lax.ppermute(sent, 'tok', swap)]
  transfers between devices with their start and end apart: 14 -> 14, of which waited for: 4 -> 6; matrix products, arithmetic and copies ran while one was open for 0% -> 0% of each run, Pallas kernels for 49% -> 48%
where the time goes in v16:
time: 43.7 us; the launch traced here: 43.4 us
  Pallas kernels  23.4 us (54%)
  starting transfers between devices  15.7 us (36%)
  waiting for transfers between devices  2.59 us (6%)
  other arithmetic  0.86 us (2%)
  between operations  0.82 us (2%)
    pallas_call x16, Pallas kernels, run(): pl.pallas_call(body, out_shape=shapes, in_specs=specs or [whole] * len(ar...  13.8 us
    ppermute x6, starting transfers between devices, across(): return lax.ppermute(array, 'nout', [(i, i ^ shift) for i in range(nn)])  9.18 us
    pallas_call x2, Pallas kernels, outer(): pl.pallas_call(functools.partial(outer_body, most, first_of), out_shape=l...  6.67 us
    ppermute x2, starting transfers between devices, on_device(): got = lax.ppermute(sent, 'tok', swap)  3.99 us
    pallas_call x1, Pallas kernels, own_forward(): pl.pallas_call(own_forward_body, out_shape=[pltpu.VMEM((count, wide), f32...  2.86 us
    ppermute x1, starting transfers between devices, on_device(): other_pre = lax.ppermute(own_pre, 'tok', swap)  1.56 us
  transfers between devices with their start and end apart: 14, of which 6 were waited for; matrix products, arithmetic and copies ran while one was open for 0% of the time, Pallas kernels for 48%

profile of v16, /device:TPU:0, one launch (start us, length us, event | category | flops | bytes accessed | tf_op | source)
XLA Modules:
  0.0 43.4 jit_solution(3464003268749800927)
XLA Ops:
  0.6 0.9 %fusion = (bf16[8,1536]{1,0:T(8,128)(2,1)S(1)}, bf16[8,1536]{1,0:T(8,128)(2,1)S(1)}) fusion(s32[]{:T(128)S(6)} %select_n.7, bf16[4,3072]{1,0:T(4,128)(2,1)} %param.6, bf16[4,3072]{1,0:T(4,128)(2,1)} %param.11, s32[]{:T(128)S(6)} %select_n.6), kind=kLoop, calls=%fused_computation.4 | loop fusion | flops 98304 | bytes 98312 | tf_op jit(solution)/shard_map/concatenate | solution.py:378
  1.5 3.0 %collective-permute-start = (bf16[8,1536]{1,0:T(8,128)(2,1)S(1)}, bf16[8,1536]{1,0:T(8,128)(2,1)S(1)}, u32[]{:S(2)}, u32[]{:S(2)}) collective-permute-start(bf16[8,1536]{1,0:T(8,128)(2,1)S(1)} %get-tuple-element.56.after_ref), channel_id=1, source_target_pairs={{0,8},{8,0},{1,9},{9,1},{2,10},{10,2},{3,11},{11,3},{4,12},{12,4},... | collective-permute-start | bytes 73736 | tf_op jit(solution)/shard_map/ppermute | solution.py:382
  4.5 1.9 %load_far.1.after_ref.far_ref.refs_4_ = bf16[1536,1024]{1,0:T(8,128)(2,1)S(1)} custom-call(bf16[1536,3072]{1,0:T(8,128)(2,1)} %hbm_ref.3, bf16[8,1536]{1,0:T(8,128)(2,1)S(1)} %get-tuple-element.56.after_ref), custom_call_target="tpu_custom_call" | custom-call | tf_op jit(solution)/shard_map/load_far/pallas_call | solution.py:55
  6.4 0.0 collective-permute-done.got_ref
  6.4 4.1 %collective-permute-start.1 = (bf16[16,1664]{1,0:T(8,128)(2,1)S(1)}, bf16[16,1664]{1,0:T(8,128)(2,1)S(1)}, u32[]{:S(2)}, u32[]{:S(2)}) collective-permute-start(bf16[16,1664]{1,0:T(8,128)(2,1)S(1)} %get-tuple-element.31), channel_id=1, source_target_pairs={{0,3},{1,2},{2,1},{3,0},{4,7},{5,6},{6,5},{7,4},{8,11},{9,10},{10,... | collective-permute-start | bytes 159752 | tf_op jit(solution)/shard_map/ppermute | solution.py:368
  10.5 0.0 collective-permute-start.3
  10.5 0.6 %collective-permute-start.2 = (bf16[16,1536]{1,0:T(8,128)(2,1)S(1)}, bf16[16,1536]{1,0:T(8,128)(2,1)S(1)}, u32[]{:S(2)}, u32[]{:S(2)}) collective-permute-start(bf16[16,1536]{1,0:T(8,128)(2,1)S(1)} %get-tuple-element.32.after_ref.refs_3_), channel_id=1, source_target_pairs={{0,2},{1,3},{2,0},{3,1},{4,6},{5,7},{6,4},{7,5},{8,10},{9,11},{10,... | collective-permute-start | bytes 147464 | tf_op jit(solution)/shard_map/ppermute | solution.py:368
  11.2 0.0 slice-start
  11.2 0.0 slice-start.1
  11.2 3.6 %load_own.1 = (bf16[1536,1536]{1,0:T(8,128)(2,1)S(1)}, bf16[1536,512]{1,0:T(8,128)(2,1)S(1)}, bf16[1536,1536]{1,0:T(8,128)(2,1)S(1)}, bf16[1536,1536]{1,0:T(8,128)(2,1)S(1)}) custom-call(bf16[1536,3072]{1,0:T(8,128)(2,1)} %hbm_ref.3, bf16[16,1536]{1,0:T(8,128)(2,1)S(1)} %get-tuple-element.32.after_ref.refs_3_, ...), custom_call_target="tpu_custom_call" | custom-call | tf_op jit(solution)/shard_map/load_own/pallas_call | solution.py:55
  14.7 0.0 collective-permute-done.3.refs_2_
  14.8 0.8 %collective-permute-done.2.refs_1_ = bf16[16,1536]{1,0:T(8,128)(2,1)S(1)} collective-permute-done((bf16[16,1536]{1,0:T(8,128)(2,1)S(1)}, bf16[16,1536]{1,0:T(8,128)(2,1)S(1)}, u32[]{:S(2)}, u32[]{:S(2)}) %collective-permute-start.2) | collective-permute-done | bytes 49184 | tf_op jit(solution)/shard_map/ppermute | solution.py:368
  15.5 0.0 collective-permute-done.1.refs_0_
  15.5 0.0 slice-start.2
  15.5 0.9 %far_pre.1 = (bf16[32,1536]{1,0:T(8,128)(2,1)S(1)}, bf16[32,1536]{1,0:T(8,128)(2,1)S(1)}, bf16[32,1536]{1,0:T(8,128)(2,1)S(1)}, f32[1,1536]{1,0:T(1,128)S(1)}) custom-call(bf16[16,1664]{1,0:T(8,128)(2,1)S(1)} %collective-permute-done.1.refs_0_, bf16[16,1536]{1,0:T(8,128)(2,1)S(1)} %collective-permute-done.2.refs_1_, ...), custom_call_target="tpu_custom_call" | custom-call | tf_op jit(solution)/shard_map/far_pre/pallas_call | solution.py:55
  16.4 0.0 collective-permute-start.4
  16.5 0.9 %own_pre.1.own_ref = f32[32,1536]{1,0:T(8,128)S(1)} custom-call(bf16[32,1536]{1,0:T(8,128)(2,1)S(1)} %get-tuple-element.35.x_ref.left_ref, bf16[1536,1536]{1,0:T(8,128)(2,1)S(1)} %get-tuple-element.34.refs_6_.w_in_ref, bf16[32,1536]{1,0:T(8,128)(2,1)S(1)} %get-tuple-element.36.after_ref), custom_call_target="tpu_custom_call" | custom-call | tf_op jit(solution)/shard_map/own_pre/pallas_call | solution.py:55
  17.4 0.4 collective-permute-done.4.got_ref
  17.8 1.6 %collective-permute-start.5 = (bf16[32,1664]{1,0:T(8,128)(2,1)S(1)}, bf16[32,1664]{1,0:T(8,128)(2,1)S(1)}, u32[]{:S(2)}, u32[]{:S(2)}) collective-permute-start(bf16[32,1664]{1,0:T(8,128)(2,1)S(1)} %add_pre.1.after_ref.own_ref), channel_id=1, source_target_pairs={{0,8},{8,0},{1,9},{9,1},{2,10},{10,2},{3,11},{11,3},{4,12},{12,4},... | collective-permute-start | bytes 319496 | tf_op jit(solution)/shard_map/ppermute | solution.py:426
  19.4 0.0 slice-done
  19.4 0.0 slice-done.1
  19.4 0.0 slice-done.2
  19.4 0.0 copy-start.1
  19.4 1.4 %far_grad.1 = bf16[32,1536]{1,0:T(8,128)(2,1)S(1)} custom-call(bf16[32,1536]{1,0:T(8,128)(2,1)S(1)} %get-tuple-element.38.dy_ref.right_ref, bf16[3072,1536]{1,0:T(8,128)(2,1)S(1)} %bitcast.5, bf16[32,1664]{1,0:T(8,128)(2,1)S(1)} %add_pre.1.after_ref.own_ref), custom_call_target="tpu_custom_call" | custom-call | tf_op jit(solution)/shard_map/far_grad/pallas_call | solution.py:55
  20.8 0.0 collective-permute-start.6
  20.8 1.5 %own_grad.1.own_ref = f32[32,1536]{1,0:T(8,128)S(1)} custom-call(bf16[32,1536]{1,0:T(8,128)(2,1)S(1)} %get-tuple-element.38.dy_ref.right_ref, bf16[3072,1536]{1,0:T(8,128)(2,1)S(1)} %bitcast.5), custom_call_target="tpu_custom_call" | custom-call | tf_op jit(solution)/shard_map/own_grad/pallas_call | solution.py:55
  22.3 0.0 collective-permute-done.6.got_ref
  22.4 0.6 %collective-permute-start.7 = (bf16[32,1664]{1,0:T(8,128)(2,1)S(1)}, bf16[32,1664]{1,0:T(8,128)(2,1)S(1)}, u32[]{:S(2)}, u32[]{:S(2)}) collective-permute-start(bf16[32,1664]{1,0:T(8,128)(2,1)S(1)} %add_grad.1.after_ref.own_ref), channel_id=1, source_target_pairs={{0,8},{8,0},{1,9},{9,1},{2,10},{10,2},{3,11},{11,3},{4,12},{12,4},... | collective-permute-start | bytes 319496 | tf_op jit(solution)/shard_map/ppermute | solution.py:431
  23.0 0.0 collective-permute-done.5.other_ref
  23.0 0.0 copy-done.1
  23.0 0.1 gelu.1
  23.1 0.3 collective-permute-start.8
  23.3 2.9 %own_forward.1 = (f32[32,1536]{1,0:T(8,128)S(1)}, bf16[3072,1536]{1,0:T(8,128)(2,1)}) custom-call(bf16[32,1536]{1,0:T(8,128)(2,1)S(1)} %get-tuple-element.40.act_ref, bf16[32,1536]{1,0:T(8,128)(2,1)S(1)} %get-tuple-element.38.dy_ref.right_ref, bf16[3072,1536]{1,0:T(8,128)(2,1)S(1)} %bitcast.5), custom_call_target="tpu_custom_call" | custom-call | tf_op jit(solution)/shard_map/own_forward/pallas_call | solution.py:301
  26.2 0.0 collective-permute-done.8.far_ref.left_ref
  26.2 0.9 %far_forward.1.after_ref.forward_ref = f32[32,1536]{1,0:T(8,128)S(1)} custom-call(bf16[32,1536]{1,0:T(8,128)(2,1)S(1)} %collective-permute-done.8.far_ref.left_ref, bf16[3072,1536]{1,0:T(8,128)(2,1)S(1)} %bitcast.5, f32[32,1536]{1,0:T(8,128)S(1)} %get-tuple-element.41.terms_ref), custom_call_target="tpu_custom_call" | custom-call | tf_op jit(solution)/shard_map/far_forward/pallas_call | solution.py:55
  27.1 0.6 %collective-permute-done.7.other_ref = bf16[32,1664]{1,0:T(8,128)(2,1)S(1)} collective-permute-done((bf16[32,1664]{1,0:T(8,128)(2,1)S(1)}, bf16[32,1664]{1,0:T(8,128)(2,1)S(1)}, u32[]{:S(2)}, u32[]{:S(2)}) %collective-permute-start.7) | collective-permute-done | bytes 106528 | tf_op jit(solution)/shard_map/ppermute | solution.py:431
  27.8 0.1 collective-permute-start.9
  27.9 0.0 copy-start
  27.9 0.9 %own_backward.1.backward_ref = f32[32,1536]{1,0:T(8,128)S(1)} custom-call(bf16[32,1536]{1,0:T(8,128)(2,1)S(1)} %grad_pre.1.grad_ref.own_ref, bf16[1536,1536]{1,0:T(8,128)(2,1)S(1)} %get-tuple-element.43.turned_ref), custom_call_target="tpu_custom_call" | custom-call | tf_op jit(solution)/shard_map/own_backward/pallas_call | solution.py:55
  28.8 0.4 collective-permute-done.9.far_ref
  29.2 0.9 %output_blocks.1 = (bf16[32,3072]{1,0:T(8,128)(2,1)S(1)}, bf16[16,1536]{1,0:T(8,128)(2,1)S(1)}, bf16[16,1536]{1,0:T(8,128)(2,1)S(1)}, bf16[16,1536]{1,0:T(8,128)(2,1)S(1)}, bf16[16,1536]{1,0:T(8,128)(2,1)S(1)}) custom-call(bf16[32,1536]{1,0:T(8,128)(2,1)S(1)} %grad_pre.1.grad_ref.own_ref, bf16[32,1536]{1,0:T(8,128)(2,1)S(1)} %collective-permute-done.9.far_ref, ...), custom_call_target="tpu_custom_call" | custom-call | tf_op jit(solution)/shard_map/output_blocks/pallas_call | solution.py:55
  30.1 3.1 %collective-permute-start.10 = (bf16[16,1536]{1,0:T(8,128)(2,1)S(1)}, bf16[16,1536]{1,0:T(8,128)(2,1)S(1)}, u32[]{:S(2)}, u32[]{:S(2)}) collective-permute-start(bf16[16,1536]{1,0:T(8,128)(2,1)S(1)} %get-tuple-element.45), channel_id=1, source_target_pairs={{0,3},{1,2},{2,1},{3,0},{4,7},{5,6},{6,5},{7,4},{8,11},{9,10},{10,... | collective-permute-start | bytes 147464 | tf_op jit(solution)/shard_map/ppermute | solution.py:368
  33.2 0.5 %collective-permute-start.11 = (bf16[16,1536]{1,0:T(8,128)(2,1)S(1)}, bf16[16,1536]{1,0:T(8,128)(2,1)S(1)}, u32[]{:S(2)}, u32[]{:S(2)}) collective-permute-start(bf16[16,1536]{1,0:T(8,128)(2,1)S(1)} %get-tuple-element.46), channel_id=1, source_target_pairs={{0,2},{1,3},{2,0},{3,1},{4,6},{5,7},{6,4},{7,5},{8,10},{9,11},{10,... | collective-permute-start | bytes 147464 | tf_op jit(solution)/shard_map/ppermute | solution.py:368
  33.7 0.9 %collective-permute-start.12 = (bf16[16,1536]{1,0:T(8,128)(2,1)S(1)}, bf16[16,1536]{1,0:T(8,128)(2,1)S(1)}, u32[]{:S(2)}, u32[]{:S(2)}) collective-permute-start(bf16[16,1536]{1,0:T(8,128)(2,1)S(1)} %get-tuple-element.47), channel_id=1, source_target_pairs={{0,1},{1,0},{2,3},{3,2},{4,5},{5,4},{6,7},{7,6},{8,9},{9,8},{10,11... | collective-permute-start | bytes 147464 | tf_op jit(solution)/shard_map/ppermute | solution.py:368
  34.6 4.1 %weight_in_grad.1.refs_4_ = bf16[1536,3072]{1,0:T(8,128)(2,1)} custom-call(bf16[32,1536]{1,0:T(8,128)(2,1)S(1)} %get-tuple-element.35.x_ref.left_ref, bf16[32,3072]{1,0:T(8,128)(2,1)S(1)} %get-tuple-element.49.right_ref.hidden_ref), custom_call_target="tpu_custom_call" | custom-call | tf_op jit(solution)/shard_map/weight_in_grad/pallas_call | solution.py:319
  38.7 0.0 collective-permute-done.10.refs_0_
  38.7 0.0 collective-permute-done.11.refs_1_
  38.7 0.1 collective-permute-done.12.refs_2_
  38.8 0.0 copy-done
  38.8 1.0 %collective-permute-start.13 = (bf16[8,1536]{1,0:T(8,128)(2,1)S(1)}, bf16[8,1536]{1,0:T(8,128)(2,1)S(1)}, u32[]{:S(2)}, u32[]{:S(2)}) collective-permute-start(bf16[8,1536]{1,0:T(8,128)(2,1)S(1)} %get-tuple-element.51), channel_id=1, source_target_pairs={{0,8},{8,0},{1,9},{9,1},{2,10},{10,2},{3,11},{11,3},{4,12},{12,4},... | collective-permute-start | bytes 73736 | tf_op jit(solution)/shard_map/ppermute | solution.py:478
  39.8 2.6 %weight_out_grad_far.1 = bf16[3072,1536]{1,0:T(8,128)(2,1)} custom-call(bf16[32,1536]{1,0:T(8,128)(2,1)S(1)} %collective-permute-done.8.far_ref.left_ref, bf16[32,1536]{1,0:T(8,128)(2,1)S(1)} %get-tuple-element.38.dy_ref.right_ref, bf16[3072,1536]{1,0:T(8,128)(2,1)} %get-tuple-element.42.later_ref.refs_0_), custom_call_target="tpu_custom_call", output_to_operand_aliasing={{}: (2, {})} | custom-call | tf_op jit(solution)/shard_map/weight_out_grad_far/pallas_call | solution.py:319
  42.4 0.3 collective-permute-done.13.got_ref
  42.7 0.7 %final_rows.1 = (bf16[4,3072]{1,0:T(4,128)(2,1)}, bf16[4,3072]{1,0:T(4,128)(2,1)}, f32[1,3072]{1,0:T(1,128)}, f32[1,3072]{1,0:T(1,128)}) custom-call(bf16[8,1536]{1,0:T(8,128)(2,1)S(1)} %get-tuple-element.50.own_ref, bf16[8,1536]{1,0:T(8,128)(2,1)S(1)} %collective-permute-done.13.got_ref, f32[1,1536]{1,0:T(1,128)S(1)} %get-tuple-element.37.sums_ref, ...), custom_call_target="tpu_custom_call" | custom-call | tf_op jit(solution)/shard_map/final_rows/pallas_call | solution.py:55
  (6 shorter events, 0.2 us)
Async XLA Ops:
  1.5 4.9 %collective-permute-start = (bf16[8,1536]{1,0:T(8,128)(2,1)S(1)}, bf16[8,1536]{1,0:T(8,128)(2,1)S(1)}, u32[]{:S(2)}, u32[]{:S(2)}) collective-permute-start(bf16[8,1536]{1,0:T(8,128)(2,1)S(1)} %get-tuple-element.56.after_ref), channel_id=1, source_target_pairs={{0,8},{8,0},{1,9},{9,1},{2,10},{10,2},{3,11},{11,3},{4,12},{12,4},... | collective-permute-start | bytes 73736 | tf_op jit(solution)/shard_map/ppermute | solution.py:382
  6.4 9.1 %collective-permute-start.1 = (bf16[16,1664]{1,0:T(8,128)(2,1)S(1)}, bf16[16,1664]{1,0:T(8,128)(2,1)S(1)}, u32[]{:S(2)}, u32[]{:S(2)}) collective-permute-start(bf16[16,1664]{1,0:T(8,128)(2,1)S(1)} %get-tuple-element.31), channel_id=1, source_target_pairs={{0,3},{1,2},{2,1},{3,0},{4,7},{5,6},{6,5},{7,4},{8,11},{9,10},{10,... | collective-permute-start | bytes 159752 | tf_op jit(solution)/shard_map/ppermute | solution.py:368
  10.5 4.2 %collective-permute-start.3 = (bf16[16,1536]{1,0:T(8,128)(2,1)S(1)}, bf16[16,1536]{1,0:T(8,128)(2,1)S(1)}, u32[]{:S(2)}, u32[]{:S(2)}) collective-permute-start(bf16[16,1536]{1,0:T(8,128)(2,1)S(1)} %get-tuple-element.32.after_ref.refs_3_), channel_id=1, source_target_pairs={{0,1},{1,0},{2,3},{3,2},{4,5},{5,4},{6,7},{7,6},{8,9},{9,8},{10,11... | collective-permute-start | bytes 147464 | tf_op jit(solution)/shard_map/ppermute | solution.py:368
  10.5 5.0 %collective-permute-start.2 = (bf16[16,1536]{1,0:T(8,128)(2,1)S(1)}, bf16[16,1536]{1,0:T(8,128)(2,1)S(1)}, u32[]{:S(2)}, u32[]{:S(2)}) collective-permute-start(bf16[16,1536]{1,0:T(8,128)(2,1)S(1)} %get-tuple-element.32.after_ref.refs_3_), channel_id=1, source_target_pairs={{0,2},{1,3},{2,0},{3,1},{4,6},{5,7},{6,4},{7,5},{8,10},{9,11},{10,... | collective-permute-start | bytes 147464 | tf_op jit(solution)/shard_map/ppermute | solution.py:368
  11.2 8.2 %slice-start = ((s8[9437184]{0:T(1024)(128)(4,1)}), s8[1048576]{0:T(1024)(128)(4,1)S(1)}, s32[]{:S(2)}) async-start(s8[9437184]{0:T(1024)(128)(4,1)} %bitcast.4), calls=%async_computation | async-start | bytes 2097152
  11.2 8.2 %slice-start.1 = ((s8[9437184]{0:T(1024)(128)(4,1)}), s8[4194304]{0:T(1024)(128)(4,1)S(1)}, s32[]{:S(2)}) async-start(s8[9437184]{0:T(1024)(128)(4,1)} %bitcast.4), calls=%async_computation.1 | async-start | bytes 8388608
  15.5 3.8 %slice-start.2 = ((s8[9437184]{0:T(1024)(128)(4,1)}), s8[4194304]{0:T(1024)(128)(4,1)S(1)}, s32[]{:S(2)}) async-start(s8[9437184]{0:T(1024)(128)(4,1)} %bitcast.4), calls=%async_computation.2 | async-start | bytes 8388608
  16.4 1.3 %collective-permute-start.4 = (bf16[32,1536]{1,0:T(8,128)(2,1)S(1)}, bf16[32,1536]{1,0:T(8,128)(2,1)S(1)}, u32[]{:S(2)}, u32[]{:S(2)}) collective-permute-start(bf16[32,1536]{1,0:T(8,128)(2,1)S(1)} %get-tuple-element.36.after_ref), channel_id=1, source_target_pairs={{0,4},{4,0},{1,5},{5,1},{2,6},{6,2},{3,7},{7,3},{8,12},{12,8},{9,1... | collective-permute-start | bytes 294920 | tf_op jit(solution)/shard_map/ppermute | solution.py:423
  17.8 5.2 %collective-permute-start.5 = (bf16[32,1664]{1,0:T(8,128)(2,1)S(1)}, bf16[32,1664]{1,0:T(8,128)(2,1)S(1)}, u32[]{:S(2)}, u32[]{:S(2)}) collective-permute-start(bf16[32,1664]{1,0:T(8,128)(2,1)S(1)} %add_pre.1.after_ref.own_ref), channel_id=1, source_target_pairs={{0,8},{8,0},{1,9},{9,1},{2,10},{10,2},{3,11},{11,3},{4,12},{12,4},... | collective-permute-start | bytes 319496 | tf_op jit(solution)/shard_map/ppermute | solution.py:426
  19.4 3.6 %copy-start.1 = (f32[3072]{0:T(1024)S(1)}, f32[3072]{0:T(1024)}, u32[]{:S(2)}) copy-start(f32[3072]{0:T(1024)} %param.8) | copy-start | bytes 36868
  20.8 1.5 %collective-permute-start.6 = (bf16[32,1536]{1,0:T(8,128)(2,1)S(1)}, bf16[32,1536]{1,0:T(8,128)(2,1)S(1)}, u32[]{:S(2)}, u32[]{:S(2)}) collective-permute-start(bf16[32,1536]{1,0:T(8,128)(2,1)S(1)} %far_grad.1), channel_id=1, source_target_pairs={{0,4},{4,0},{1,5},{5,1},{2,6},{6,2},{3,7},{7,3},{8,12},{12,8},{9,1... | collective-permute-start | bytes 294920 | tf_op jit(solution)/shard_map/ppermute | solution.py:428
  22.4 5.4 %collective-permute-start.7 = (bf16[32,1664]{1,0:T(8,128)(2,1)S(1)}, bf16[32,1664]{1,0:T(8,128)(2,1)S(1)}, u32[]{:S(2)}, u32[]{:S(2)}) collective-permute-start(bf16[32,1664]{1,0:T(8,128)(2,1)S(1)} %add_grad.1.after_ref.own_ref), channel_id=1, source_target_pairs={{0,8},{8,0},{1,9},{9,1},{2,10},{10,2},{3,11},{11,3},{4,12},{12,4},... | collective-permute-start | bytes 319496 | tf_op jit(solution)/shard_map/ppermute | solution.py:431
  23.1 3.1 %collective-permute-start.8 = (bf16[32,1536]{1,0:T(8,128)(2,1)S(1)}, bf16[32,1536]{1,0:T(8,128)(2,1)S(1)}, u32[]{:S(2)}, u32[]{:S(2)}) collective-permute-start(bf16[32,1536]{1,0:T(8,128)(2,1)S(1)} %get-tuple-element.40.act_ref), channel_id=1, source_target_pairs={{0,4},{4,0},{1,5},{5,1},{2,6},{6,2},{3,7},{7,3},{8,12},{12,8},{9,1... | collective-permute-start | bytes 294920 | tf_op jit(solution)/shard_map/ppermute | solution.py:435
  27.8 1.4 %collective-permute-start.9 = (bf16[32,1536]{1,0:T(8,128)(2,1)S(1)}, bf16[32,1536]{1,0:T(8,128)(2,1)S(1)}, u32[]{:S(2)}, u32[]{:S(2)}) collective-permute-start(bf16[32,1536]{1,0:T(8,128)(2,1)S(1)} %grad_pre.1.grad_ref.own_ref), channel_id=1, source_target_pairs={{0,4},{4,0},{1,5},{5,1},{2,6},{6,2},{3,7},{7,3},{8,12},{12,8},{9,1... | collective-permute-start | bytes 294920 | tf_op jit(solution)/shard_map/ppermute | solution.py:449
  27.9 10.9 %copy-start = (f32[3072]{0:T(1024)S(1)}, f32[3072]{0:T(1024)}, u32[]{:S(2)}) copy-start(f32[3072]{0:T(1024)} %param.10) | copy-start | bytes 36868
  30.1 8.6 %collective-permute-start.10 = (bf16[16,1536]{1,0:T(8,128)(2,1)S(1)}, bf16[16,1536]{1,0:T(8,128)(2,1)S(1)}, u32[]{:S(2)}, u32[]{:S(2)}) collective-permute-start(bf16[16,1536]{1,0:T(8,128)(2,1)S(1)} %get-tuple-element.45), channel_id=1, source_target_pairs={{0,3},{1,2},{2,1},{3,0},{4,7},{5,6},{6,5},{7,4},{8,11},{9,10},{10,... | collective-permute-start | bytes 147464 | tf_op jit(solution)/shard_map/ppermute | solution.py:368
  33.2 5.5 %collective-permute-start.11 = (bf16[16,1536]{1,0:T(8,128)(2,1)S(1)}, bf16[16,1536]{1,0:T(8,128)(2,1)S(1)}, u32[]{:S(2)}, u32[]{:S(2)}) collective-permute-start(bf16[16,1536]{1,0:T(8,128)(2,1)S(1)} %get-tuple-element.46), channel_id=1, source_target_pairs={{0,2},{1,3},{2,0},{3,1},{4,6},{5,7},{6,4},{7,5},{8,10},{9,11},{10,... | collective-permute-start | bytes 147464 | tf_op jit(solution)/shard_map/ppermute | solution.py:368
  33.7 5.1 %collective-permute-start.12 = (bf16[16,1536]{1,0:T(8,128)(2,1)S(1)}, bf16[16,1536]{1,0:T(8,128)(2,1)S(1)}, u32[]{:S(2)}, u32[]{:S(2)}) collective-permute-start(bf16[16,1536]{1,0:T(8,128)(2,1)S(1)} %get-tuple-element.47), channel_id=1, source_target_pairs={{0,1},{1,0},{2,3},{3,2},{4,5},{5,4},{6,7},{7,6},{8,9},{9,8},{10,11... | collective-permute-start | bytes 147464 | tf_op jit(solution)/shard_map/ppermute | solution.py:368
  38.8 3.9 %collective-permute-start.13 = (bf16[8,1536]{1,0:T(8,128)(2,1)S(1)}, bf16[8,1536]{1,0:T(8,128)(2,1)S(1)}, u32[]{:S(2)}, u32[]{:S(2)}) collective-permute-start(bf16[8,1536]{1,0:T(8,128)(2,1)S(1)} %get-tuple-element.51), channel_id=1, source_target_pairs={{0,8},{8,0},{1,9},{9,1},{2,10},{10,2},{3,11},{11,3},{4,12},{12,4},... | collective-permute-start | bytes 73736 | tf_op jit(solution)/shard_map/ppermute | solution.py:478

commit v17 on v16

--- a/solution.py
+++ b/solution.py
@@ -32,10 +32,6 @@
 
 def exchange(chunks, axes):
     return lax.all_to_all(chunks, axes, split_axis=0, concat_axis=0, tiled=True)
-
-
-def dot_turned(rows, weight):
-    return dot(weight, rows, 1, 1).T
 
 
 def tile_of(size, most):
@@ -113,9 +109,9 @@
     return (1 - lax.axis_index("kin")) * half
 
 
-def half_tiles(half, mine, most):
+def half_tiles(half, mine):
     first = own_rows(half) if mine else far_rows(half)
-    tile = tile_of(half, most)
+    tile = tile_of(half, 512)
     return [
         (pl.ds(i * tile, tile), pl.ds(pl.multiple_of(first + i * tile, tile), tile))
         for i in range(half // tile)
@@ -138,7 +134,8 @@
         copy.wait()
 
 
-def load_and_turn_body(hbm_ref, after_ref, far_ref, own_ref, last_ref, own_turned, far_turned, sems):
+def load_and_turn_body(hbm_ref, after_ref, far_ref, w_out_ref, *refs):
+    own_ref, last_ref, own_turned, far_turned, sems = refs
     wide, half = own_ref.shape
     first, last = far_ref.shape[1], last_ref.shape[1]
     size = wide // 4
@@ -188,21 +185,25 @@
     sent_ref[:, first:] = dot(x_cols, w_last_ref[...], 1, 0).astype(bf16)
 
 
-def own_pre_body(x_ref, w_in_ref, after_ref, own_ref):
+def own_pre_body(x_ref, w_in_ref, dy_ref, w_out_ref, after_ref, own_ref, first_ref):
     x_cols = x_ref[...]
     for at in tiles_of(own_ref.shape[1]):
         own_ref[:, at] = dot(x_cols, w_in_ref[:, at], 1, 0)
-
-
-def far_grad_body(dy_ref, w_out_ref, after_ref, sent_ref):
+    there = half_tiles(own_ref.shape[1], False)[0][1]
+    first_ref[...] = dot(dy_ref[...], w_out_ref[there, :], 1, 1).astype(bf16)
+
+
+def far_grad_body(dy_ref, w_out_ref, first_ref, after_ref, sent_ref):
     dy_cols = dy_ref[...]
-    for at, there in half_tiles(sent_ref.shape[1], False, 1536):
-        sent_ref[:, at] = dot_turned(dy_cols, w_out_ref[there, :]).astype(bf16)
+    tiles = half_tiles(sent_ref.shape[1], False)
+    sent_ref[:, tiles[0][0]] = first_ref[...]
+    for at, there in tiles[1:]:
+        sent_ref[:, at] = dot(dy_cols, w_out_ref[there, :], 1, 1).astype(bf16)
 
 
 def own_grad_body(dy_ref, w_out_ref, own_ref):
     dy_cols = dy_ref[...]
-    for at, there in half_tiles(own_ref.shape[1], True, 1536):
+    for at, there in half_tiles(own_ref.shape[1], True):
         own_ref[:, at] = dot(dy_cols, w_out_ref[there, :], 1, 1)
 
 
@@ -243,7 +244,7 @@
 def far_forward_body(far_ref, w_out_ref, terms_ref, out_ref):
     act = far_ref[...]
     part = half_of(act.shape[1], False)
-    for at in tiles_of(out_ref.shape[1], 1536):
+    for at in tiles_of(out_ref.shape[1]):
         out_ref[:, at] = terms_ref[:, at] + dot(act, w_out_ref[part, at], 1, 0)
 
 
@@ -396,15 +397,15 @@
             kept(own), kept(got), kept(in_far)
         )
         pieces = [across(tiles, shift) for shift in range(1, nn - 1)]
-        pieces = [across(farthest, nn - 1)] + pieces[::-1] + [tiles]
+        pieces = [across(farthest, nn - 1)] + pieces + [tiles]
         in_own, in_last, own_turned, far_turned = call(
             load_and_turn_body,
             "load_own",
             [like((wide, half), bf16), like((wide, last), bf16)] + [like((half, wide), bf16)] * 2,
             grant=8 * MIB,
             scratch=[sem((2, 4))],
-            specs=[hbm, pl.BlockSpec(memory_space=pl.ANY), whole],
-        )(in_hbm(weight_in), tiles, kept(in_far))
+            specs=[hbm, pl.BlockSpec(memory_space=pl.ANY), whole, whole],
+        )(in_hbm(weight_in), tiles, kept(in_far), kept(weight_out))
 
         def product(body, name, outs, *args):
             return call(body, name, outs, grant=8 * MIB)(*map(kept, args))
@@ -421,10 +422,21 @@
             in_own,
         )
         got = lax.ppermute(sent, "kin", swap)
-        (own,) = product(own_pre_body, "own_pre", [like((count, half), f32)], x_cols, in_own, sent)
+        own, first = product(
+            own_pre_body,
+            "own_pre",
+            [like((count, half), f32), like((count, tile_of(half, 512)), bf16)],
+            x_cols,
+            in_own,
+            dy_cols,
+            weight_out,
+            sent,
+        )
         (own_pre,) = product(add_pre_body, "add_pre", [crossing], own, got, sums)
         other_pre = lax.ppermute(own_pre, "tok", swap)
-        (sent,) = product(far_grad_body, "far_grad", [side], dy_cols, weight_out, own_pre)
+        (sent,) = product(
+            far_grad_body, "far_grad", [side], dy_cols, weight_out, first, own_pre
+        )
         got = lax.ppermute(sent, "kin", swap)
         (own,) = product(own_grad_body, "own_grad", [like((count, half), f32)], dy_cols, weight_out)
         (own_grad,) = product(add_body, "add_grad", [crossing], own, got)
@@ -464,7 +476,8 @@
             act_far, dy_cols, hid, "weight_out_grad_far", far_rows, into=weight_out_grad
         )
 
-        terms = [across(blocks[i], nn - 1 - i) for i in range(nn - 1)] + [blocks[-1]]
+        terms = [across(blocks[0], nn - 1)]
+        terms += [across(blocks[shift], shift) for shift in reversed(range(1, nn - 1))] + [blocks[-1]]
         own, sent = call(
             functools.partial(sum_body, rows),
             "sum_blocks",

time: 43.7 us -> 43.7 us (level)
  starting transfers between devices: 15.7 us -> 16.7 us
  waiting for transfers between devices: 2.59 us -> 1.64 us
    ppermute x2, starting transfers between devices: 3.99 us -> 4.58 us  [on_device(): got = lax.ppermute(sent, 'tok', swap)]
    ppermute x1, waiting for transfers between devices: 0.01 us -> 0.52 us  [on_device(): other_pre = lax.ppermute(own_pre, 'tok', swap)]
    ppermute x1, waiting for transfers between devices: 0.64 us -> 0.13 us  [on_device(): other_grad = lax.ppermute(own_grad, 'tok', swap)]
  transfers between devices with their start and end apart: 14 -> 14, of which waited for: 6 -> 3; matrix products, arithmetic and copies ran while one was open for 0% -> 0% of each run, Pallas kernels for 48% -> 47%
where the time goes in v17:
time: 43.7 us; the launch traced here: 43.4 us
  Pallas kernels  23.2 us (53%)
  starting transfers between devices  16.7 us (38%)
  waiting for transfers between devices  1.64 us (4%)
  other arithmetic  1.01 us (2%)
  between operations  0.86 us (2%)
    pallas_call x16, Pallas kernels, run(): pl.pallas_call(body, out_shape=shapes, in_specs=specs or [whole] * len(ar...  13.7 us
    ppermute x6, starting transfers between devices, across(): return lax.ppermute(array, 'nout', [(i, i ^ shift) for i in range(nn)])  9.18 us
    pallas_call x2, Pallas kernels, outer(): pl.pallas_call(functools.partial(outer_body, most, first_of), out_shape=l...  6.66 us
    ppermute x2, starting transfers between devices, on_device(): got = lax.ppermute(sent, 'tok', swap)  4.58 us
    pallas_call x1, Pallas kernels, own_forward(): pl.pallas_call(own_forward_body, out_shape=[pltpu.VMEM((count, wide), f32...  2.86 us
    ppermute x1, starting transfers between devices, on_device(): other_pre = lax.ppermute(own_pre, 'tok', swap)  1.56 us
    concatenate x1, other arithmetic, on_device(): mine = jnp.concatenate([tokens, grad_out], axis=0)  1.01 us
    ppermute x6, waiting for transfers between devices, across(): return lax.ppermute(array, 'nout', [(i, i ^ shift) for i in range(nn)])  0.93 us
  transfers between devices with their start and end apart: 14, of which 3 were waited for; matrix products, arithmetic and copies ran while one was open for 0% of the time, Pallas kernels for 47%

profile of v17, /device:TPU:0, one launch (start us, length us, event | category | flops | bytes accessed | tf_op | source)
XLA Modules:
  0.0 43.4 jit_solution(1125981557538189564)
XLA Ops:
  0.6 0.0 copy-start
  0.6 1.0 %fusion = (bf16[8,1536]{1,0:T(8,128)(2,1)S(1)}, bf16[8,1536]{1,0:T(8,128)(2,1)S(1)}) fusion(s32[]{:T(128)S(6)} %select_n.7, bf16[4,3072]{1,0:T(4,128)(2,1)} %param.6, bf16[4,3072]{1,0:T(4,128)(2,1)} %param.11, s32[]{:T(128)S(6)} %select_n.6), kind=kLoop, calls=%fused_computation.4 | loop fusion | flops 98304 | bytes 98312 | tf_op jit(solution)/shard_map/concatenate | solution.py:379
  1.7 3.0 %collective-permute-start = (bf16[8,1536]{1,0:T(8,128)(2,1)S(1)}, bf16[8,1536]{1,0:T(8,128)(2,1)S(1)}, u32[]{:S(2)}, u32[]{:S(2)}) collective-permute-start(bf16[8,1536]{1,0:T(8,128)(2,1)S(1)} %get-tuple-element.60.after_ref), channel_id=1, source_target_pairs={{0,8},{8,0},{1,9},{9,1},{2,10},{10,2},{3,11},{11,3},{4,12},{12,4},... | collective-permute-start | bytes 73736 | tf_op jit(solution)/shard_map/ppermute | solution.py:383
  4.7 1.9 %load_far.1.after_ref.far_ref.refs_4_ = bf16[1536,1024]{1,0:T(8,128)(2,1)S(1)} custom-call(bf16[1536,3072]{1,0:T(8,128)(2,1)} %hbm_ref.3, bf16[8,1536]{1,0:T(8,128)(2,1)S(1)} %get-tuple-element.60.after_ref), custom_call_target="tpu_custom_call" | custom-call | tf_op jit(solution)/shard_map/load_far/pallas_call | solution.py:51
  6.6 0.0 collective-permute-done.got_ref
  6.6 4.1 %collective-permute-start.1 = (bf16[16,1664]{1,0:T(8,128)(2,1)S(1)}, bf16[16,1664]{1,0:T(8,128)(2,1)S(1)}, u32[]{:S(2)}, u32[]{:S(2)}) collective-permute-start(bf16[16,1664]{1,0:T(8,128)(2,1)S(1)} %get-tuple-element.33), channel_id=1, source_target_pairs={{0,3},{1,2},{2,1},{3,0},{4,7},{5,6},{6,5},{7,4},{8,11},{9,10},{10,... | collective-permute-start | bytes 159752 | tf_op jit(solution)/shard_map/ppermute | solution.py:369
  10.7 0.0 collective-permute-start.3
  10.7 0.6 %collective-permute-start.2 = (bf16[16,1536]{1,0:T(8,128)(2,1)S(1)}, bf16[16,1536]{1,0:T(8,128)(2,1)S(1)}, u32[]{:S(2)}, u32[]{:S(2)}) collective-permute-start(bf16[16,1536]{1,0:T(8,128)(2,1)S(1)} %get-tuple-element.34.after_ref.refs_3_), channel_id=1, source_target_pairs={{0,1},{1,0},{2,3},{3,2},{4,5},{5,4},{6,7},{7,6},{8,9},{9,8},{10,11... | collective-permute-start | bytes 147464 | tf_op jit(solution)/shard_map/ppermute | solution.py:369
  11.3 0.0 copy-done
  11.3 3.4 %load_own.1 = (bf16[1536,1536]{1,0:T(8,128)(2,1)S(1)}, bf16[1536,512]{1,0:T(8,128)(2,1)S(1)}, bf16[1536,1536]{1,0:T(8,128)(2,1)S(1)}, bf16[1536,1536]{1,0:T(8,128)(2,1)S(1)}) custom-call(bf16[1536,3072]{1,0:T(8,128)(2,1)} %hbm_ref.3, bf16[16,1536]{1,0:T(8,128)(2,1)S(1)} %get-tuple-element.34.after_ref.refs_3_, ...), custom_call_target="tpu_custom_call" | custom-call | tf_op jit(solution)/shard_map/load_own/pallas_call | solution.py:51
  14.8 0.9 %collective-permute-done.3.refs_2_ = bf16[16,1536]{1,0:T(8,128)(2,1)S(1)} collective-permute-done((bf16[16,1536]{1,0:T(8,128)(2,1)S(1)}, bf16[16,1536]{1,0:T(8,128)(2,1)S(1)}, u32[]{:S(2)}, u32[]{:S(2)}) %collective-permute-start.3) | collective-permute-done | bytes 49184 | tf_op jit(solution)/shard_map/ppermute | solution.py:369
  15.7 0.0 collective-permute-done.2.refs_1_
  15.7 0.0 collective-permute-done.1.refs_0_
  15.7 0.9 %far_pre.1 = (bf16[32,1536]{1,0:T(8,128)(2,1)S(1)}, bf16[32,1536]{1,0:T(8,128)(2,1)S(1)}, bf16[32,1536]{1,0:T(8,128)(2,1)S(1)}, f32[1,1536]{1,0:T(1,128)S(1)}) custom-call(bf16[16,1664]{1,0:T(8,128)(2,1)S(1)} %collective-permute-done.1.refs_0_, bf16[16,1536]{1,0:T(8,128)(2,1)S(1)} %collective-permute-done.2.refs_1_, ...), custom_call_target="tpu_custom_call" | custom-call | tf_op jit(solution)/shard_map/far_pre/pallas_call | solution.py:51
  16.6 0.0 collective-permute-start.4
  16.6 1.3 %own_pre.1 = (f32[32,1536]{1,0:T(8,128)S(1)}, bf16[32,512]{1,0:T(8,128)(2,1)S(1)}) custom-call(bf16[32,1536]{1,0:T(8,128)(2,1)S(1)} %get-tuple-element.37.x_ref.left_ref, bf16[1536,1536]{1,0:T(8,128)(2,1)S(1)} %get-tuple-element.36.refs_6_.w_in_ref, bf16[32,1536]{1,0:T(8,128)(2,1)S(1)} %get-tuple-element.38.dy_ref.right_ref, bf16[3072,1536]{1,0:T(8,128)(2,1)S(1)} %copy-done, ...), custom_call_target="tpu_custom_call" | custom-call | tf_op jit(solution)/shard_map/own_pre/pallas_call | solution.py:51
  18.0 0.0 collective-permute-done.4.got_ref
  18.0 1.6 %collective-permute-start.5 = (bf16[32,1664]{1,0:T(8,128)(2,1)S(1)}, bf16[32,1664]{1,0:T(8,128)(2,1)S(1)}, u32[]{:S(2)}, u32[]{:S(2)}) collective-permute-start(bf16[32,1664]{1,0:T(8,128)(2,1)S(1)} %add_pre.1.after_ref.own_ref), channel_id=1, source_target_pairs={{0,8},{8,0},{1,9},{9,1},{2,10},{10,2},{3,11},{11,3},{4,12},{12,4},... | collective-permute-start | bytes 319496 | tf_op jit(solution)/shard_map/ppermute | solution.py:436
  19.6 0.0 copy-start.2
  19.6 1.0 %far_grad.1 = bf16[32,1536]{1,0:T(8,128)(2,1)S(1)} custom-call(bf16[32,1536]{1,0:T(8,128)(2,1)S(1)} %get-tuple-element.38.dy_ref.right_ref, bf16[3072,1536]{1,0:T(8,128)(2,1)S(1)} %copy-done, bf16[32,512]{1,0:T(8,128)(2,1)S(1)} %get-tuple-element.42.first_ref, bf16[32,1664]{1,0:T(8,128)(2,1)S(1)} %add_pre.1.after_ref.own_ref), custom_call_target="tpu_custom_call" | custom-call | tf_op jit(solution)/shard_map/far_grad/pallas_call | solution.py:51
  20.6 0.2 collective-permute-start.6
  20.8 1.5 %own_grad.1.own_ref = f32[32,1536]{1,0:T(8,128)S(1)} custom-call(bf16[32,1536]{1,0:T(8,128)(2,1)S(1)} %get-tuple-element.38.dy_ref.right_ref, bf16[3072,1536]{1,0:T(8,128)(2,1)S(1)} %copy-done), custom_call_target="tpu_custom_call" | custom-call | tf_op jit(solution)/shard_map/own_grad/pallas_call | solution.py:51
  22.3 0.0 collective-permute-done.6.got_ref
  22.3 0.6 %collective-permute-start.7 = (bf16[32,1664]{1,0:T(8,128)(2,1)S(1)}, bf16[32,1664]{1,0:T(8,128)(2,1)S(1)}, u32[]{:S(2)}, u32[]{:S(2)}) collective-permute-start(bf16[32,1664]{1,0:T(8,128)(2,1)S(1)} %add_grad.1.after_ref.own_ref), channel_id=1, source_target_pairs={{0,8},{8,0},{1,9},{9,1},{2,10},{10,2},{3,11},{11,3},{4,12},{12,4},... | collective-permute-start | bytes 319496 | tf_op jit(solution)/shard_map/ppermute | solution.py:443
  22.9 0.5 %collective-permute-done.5.other_ref = bf16[32,1664]{1,0:T(8,128)(2,1)S(1)} collective-permute-done((bf16[32,1664]{1,0:T(8,128)(2,1)S(1)}, bf16[32,1664]{1,0:T(8,128)(2,1)S(1)}, u32[]{:S(2)}, u32[]{:S(2)}) %collective-permute-start.5) | collective-permute-done | bytes 106528 | tf_op jit(solution)/shard_map/ppermute | solution.py:436
  23.5 0.0 copy-done.2
  23.5 0.1 gelu.1
  23.6 0.1 collective-permute-start.8
  23.7 2.9 %own_forward.1 = (f32[32,1536]{1,0:T(8,128)S(1)}, bf16[3072,1536]{1,0:T(8,128)(2,1)}) custom-call(bf16[32,1536]{1,0:T(8,128)(2,1)S(1)} %get-tuple-element.44.act_ref, bf16[32,1536]{1,0:T(8,128)(2,1)S(1)} %get-tuple-element.38.dy_ref.right_ref, bf16[3072,1536]{1,0:T(8,128)(2,1)S(1)} %copy-done), custom_call_target="tpu_custom_call" | custom-call | tf_op jit(solution)/shard_map/own_forward/pallas_call | solution.py:302
  26.5 0.0 collective-permute-done.8.far_ref.left_ref
  26.5 0.9 %far_forward.1.after_ref.forward_ref = f32[32,1536]{1,0:T(8,128)S(1)} custom-call(bf16[32,1536]{1,0:T(8,128)(2,1)S(1)} %collective-permute-done.8.far_ref.left_ref, bf16[3072,1536]{1,0:T(8,128)(2,1)S(1)} %copy-done, f32[32,1536]{1,0:T(8,128)S(1)} %get-tuple-element.45.terms_ref), custom_call_target="tpu_custom_call" | custom-call | tf_op jit(solution)/shard_map/far_forward/pallas_call | solution.py:51
  27.5 0.1 collective-permute-done.7.other_ref
  27.6 0.5 %collective-permute-start.9 = (bf16[32,1536]{1,0:T(8,128)(2,1)S(1)}, bf16[32,1536]{1,0:T(8,128)(2,1)S(1)}, u32[]{:S(2)}, u32[]{:S(2)}) collective-permute-start(bf16[32,1536]{1,0:T(8,128)(2,1)S(1)} %grad_pre.1.grad_ref.own_ref), channel_id=1, source_target_pairs={{0,4},{4,0},{1,5},{5,1},{2,6},{6,2},{3,7},{7,3},{8,12},{12,8},{9,1... | collective-permute-start | bytes 294920 | tf_op jit(solution)/shard_map/ppermute | solution.py:461
  28.1 0.0 copy-start.1
  28.1 0.9 %own_backward.1.backward_ref = f32[32,1536]{1,0:T(8,128)S(1)} custom-call(bf16[32,1536]{1,0:T(8,128)(2,1)S(1)} %grad_pre.1.grad_ref.own_ref, bf16[1536,1536]{1,0:T(8,128)(2,1)S(1)} %get-tuple-element.47.turned_ref), custom_call_target="tpu_custom_call" | custom-call | tf_op jit(solution)/shard_map/own_backward/pallas_call | solution.py:51
  29.0 0.0 collective-permute-done.9.far_ref
  29.0 0.9 %output_blocks.1 = (bf16[32,3072]{1,0:T(8,128)(2,1)S(1)}, bf16[16,1536]{1,0:T(8,128)(2,1)S(1)}, bf16[16,1536]{1,0:T(8,128)(2,1)S(1)}, bf16[16,1536]{1,0:T(8,128)(2,1)S(1)}, bf16[16,1536]{1,0:T(8,128)(2,1)S(1)}) custom-call(bf16[32,1536]{1,0:T(8,128)(2,1)S(1)} %grad_pre.1.grad_ref.own_ref, bf16[32,1536]{1,0:T(8,128)(2,1)S(1)} %collective-permute-done.9.far_ref, ...), custom_call_target="tpu_custom_call" | custom-call | tf_op jit(solution)/shard_map/output_blocks/pallas_call | solution.py:51
  30.0 2.9 %collective-permute-start.10 = (bf16[16,1536]{1,0:T(8,128)(2,1)S(1)}, bf16[16,1536]{1,0:T(8,128)(2,1)S(1)}, u32[]{:S(2)}, u32[]{:S(2)}) collective-permute-start(bf16[16,1536]{1,0:T(8,128)(2,1)S(1)} %get-tuple-element.49), channel_id=1, source_target_pairs={{0,3},{1,2},{2,1},{3,0},{4,7},{5,6},{6,5},{7,4},{8,11},{9,10},{10,... | collective-permute-start | bytes 147464 | tf_op jit(solution)/shard_map/ppermute | solution.py:369
  32.9 0.0 collective-permute-start.11
  32.9 1.5 %collective-permute-start.12 = (bf16[16,1536]{1,0:T(8,128)(2,1)S(1)}, bf16[16,1536]{1,0:T(8,128)(2,1)S(1)}, u32[]{:S(2)}, u32[]{:S(2)}) collective-permute-start(bf16[16,1536]{1,0:T(8,128)(2,1)S(1)} %get-tuple-element.51), channel_id=1, source_target_pairs={{0,1},{1,0},{2,3},{3,2},{4,5},{5,4},{6,7},{7,6},{8,9},{9,8},{10,11... | collective-permute-start | bytes 147464 | tf_op jit(solution)/shard_map/ppermute | solution.py:369
  34.4 4.1 %weight_in_grad.1.refs_4_ = bf16[1536,3072]{1,0:T(8,128)(2,1)} custom-call(bf16[32,1536]{1,0:T(8,128)(2,1)S(1)} %get-tuple-element.37.x_ref.left_ref, bf16[32,3072]{1,0:T(8,128)(2,1)S(1)} %get-tuple-element.53.right_ref.hidden_ref), custom_call_target="tpu_custom_call" | custom-call | tf_op jit(solution)/shard_map/weight_in_grad/pallas_call | solution.py:320
  38.5 0.0 collective-permute-done.10.refs_0_
  38.5 0.0 collective-permute-done.11.refs_1_
  38.5 0.0 collective-permute-done.12.refs_2_
  38.6 0.0 copy-done.1
  38.6 1.6 %collective-permute-start.13 = (bf16[8,1536]{1,0:T(8,128)(2,1)S(1)}, bf16[8,1536]{1,0:T(8,128)(2,1)S(1)}, u32[]{:S(2)}, u32[]{:S(2)}) collective-permute-start(bf16[8,1536]{1,0:T(8,128)(2,1)S(1)} %get-tuple-element.55), channel_id=1, source_target_pairs={{0,8},{8,0},{1,9},{9,1},{2,10},{10,2},{3,11},{11,3},{4,12},{12,4},... | collective-permute-start | bytes 73736 | tf_op jit(solution)/shard_map/ppermute | solution.py:491
  40.2 2.6 %weight_out_grad_far.1 = bf16[3072,1536]{1,0:T(8,128)(2,1)} custom-call(bf16[32,1536]{1,0:T(8,128)(2,1)S(1)} %collective-permute-done.8.far_ref.left_ref, bf16[32,1536]{1,0:T(8,128)(2,1)S(1)} %get-tuple-element.38.dy_ref.right_ref, bf16[3072,1536]{1,0:T(8,128)(2,1)} %get-tuple-element.46.later_ref.refs_0_), custom_call_target="tpu_custom_call", output_to_operand_aliasing={{}: (2, {})} | custom-call | tf_op jit(solution)/shard_map/weight_out_grad_far/pallas_call | solution.py:320
  42.8 0.0 collective-permute-done.13.got_ref
  42.8 0.7 %final_rows.1 = (bf16[4,3072]{1,0:T(4,128)(2,1)}, bf16[4,3072]{1,0:T(4,128)(2,1)}, f32[1,3072]{1,0:T(1,128)}, f32[1,3072]{1,0:T(1,128)}) custom-call(bf16[8,1536]{1,0:T(8,128)(2,1)S(1)} %get-tuple-element.54.own_ref, bf16[8,1536]{1,0:T(8,128)(2,1)S(1)} %collective-permute-done.13.got_ref, f32[1,1536]{1,0:T(1,128)S(1)} %get-tuple-element.41.sums_ref, ...), custom_call_target="tpu_custom_call" | custom-call | tf_op jit(solution)/shard_map/final_rows/pallas_call | solution.py:51
  (5 shorter events, 0.2 us)
Async XLA Ops:
  0.6 10.7 %copy-start = (bf16[3072,1536]{1,0:T(8,128)(2,1)S(1)}, bf16[3072,1536]{1,0:T(8,128)(2,1)}, u32[]{:S(2)}) copy-start(bf16[3072,1536]{1,0:T(8,128)(2,1)} %w_out_ref.11) | copy-start | bytes 28311556
  1.7 4.9 %collective-permute-start = (bf16[8,1536]{1,0:T(8,128)(2,1)S(1)}, bf16[8,1536]{1,0:T(8,128)(2,1)S(1)}, u32[]{:S(2)}, u32[]{:S(2)}) collective-permute-start(bf16[8,1536]{1,0:T(8,128)(2,1)S(1)} %get-tuple-element.60.after_ref), channel_id=1, source_target_pairs={{0,8},{8,0},{1,9},{9,1},{2,10},{10,2},{3,11},{11,3},{4,12},{12,4},... | collective-permute-start | bytes 73736 | tf_op jit(solution)/shard_map/ppermute | solution.py:383
  6.6 9.1 %collective-permute-start.1 = (bf16[16,1664]{1,0:T(8,128)(2,1)S(1)}, bf16[16,1664]{1,0:T(8,128)(2,1)S(1)}, u32[]{:S(2)}, u32[]{:S(2)}) collective-permute-start(bf16[16,1664]{1,0:T(8,128)(2,1)S(1)} %get-tuple-element.33), channel_id=1, source_target_pairs={{0,3},{1,2},{2,1},{3,0},{4,7},{5,6},{6,5},{7,4},{8,11},{9,10},{10,... | collective-permute-start | bytes 159752 | tf_op jit(solution)/shard_map/ppermute | solution.py:369
  10.7 5.0 %collective-permute-start.3 = (bf16[16,1536]{1,0:T(8,128)(2,1)S(1)}, bf16[16,1536]{1,0:T(8,128)(2,1)S(1)}, u32[]{:S(2)}, u32[]{:S(2)}) collective-permute-start(bf16[16,1536]{1,0:T(8,128)(2,1)S(1)} %get-tuple-element.34.after_ref.refs_3_), channel_id=1, source_target_pairs={{0,2},{1,3},{2,0},{3,1},{4,6},{5,7},{6,4},{7,5},{8,10},{9,11},{10,... | collective-permute-start | bytes 147464 | tf_op jit(solution)/shard_map/ppermute | solution.py:369
  10.7 5.0 %collective-permute-start.2 = (bf16[16,1536]{1,0:T(8,128)(2,1)S(1)}, bf16[16,1536]{1,0:T(8,128)(2,1)S(1)}, u32[]{:S(2)}, u32[]{:S(2)}) collective-permute-start(bf16[16,1536]{1,0:T(8,128)(2,1)S(1)} %get-tuple-element.34.after_ref.refs_3_), channel_id=1, source_target_pairs={{0,1},{1,0},{2,3},{3,2},{4,5},{5,4},{6,7},{7,6},{8,9},{9,8},{10,11... | collective-permute-start | bytes 147464 | tf_op jit(solution)/shard_map/ppermute | solution.py:369
  16.6 1.4 %collective-permute-start.4 = (bf16[32,1536]{1,0:T(8,128)(2,1)S(1)}, bf16[32,1536]{1,0:T(8,128)(2,1)S(1)}, u32[]{:S(2)}, u32[]{:S(2)}) collective-permute-start(bf16[32,1536]{1,0:T(8,128)(2,1)S(1)} %get-tuple-element.39.after_ref), channel_id=1, source_target_pairs={{0,4},{4,0},{1,5},{5,1},{2,6},{6,2},{3,7},{7,3},{8,12},{12,8},{9,1... | collective-permute-start | bytes 294920 | tf_op jit(solution)/shard_map/ppermute | solution.py:424
  18.0 5.4 %collective-permute-start.5 = (bf16[32,1664]{1,0:T(8,128)(2,1)S(1)}, bf16[32,1664]{1,0:T(8,128)(2,1)S(1)}, u32[]{:S(2)}, u32[]{:S(2)}) collective-permute-start(bf16[32,1664]{1,0:T(8,128)(2,1)S(1)} %add_pre.1.after_ref.own_ref), channel_id=1, source_target_pairs={{0,8},{8,0},{1,9},{9,1},{2,10},{10,2},{3,11},{11,3},{4,12},{12,4},... | collective-permute-start | bytes 319496 | tf_op jit(solution)/shard_map/ppermute | solution.py:436
  19.6 3.9 %copy-start.2 = (f32[3072]{0:T(1024)S(1)}, f32[3072]{0:T(1024)}, u32[]{:S(2)}) copy-start(f32[3072]{0:T(1024)} %param.8) | copy-start | bytes 36868
  20.6 1.7 %collective-permute-start.6 = (bf16[32,1536]{1,0:T(8,128)(2,1)S(1)}, bf16[32,1536]{1,0:T(8,128)(2,1)S(1)}, u32[]{:S(2)}, u32[]{:S(2)}) collective-permute-start(bf16[32,1536]{1,0:T(8,128)(2,1)S(1)} %far_grad.1), channel_id=1, source_target_pairs={{0,4},{4,0},{1,5},{5,1},{2,6},{6,2},{3,7},{7,3},{8,12},{12,8},{9,1... | collective-permute-start | bytes 294920 | tf_op jit(solution)/shard_map/ppermute | solution.py:440
  22.3 5.2 %collective-permute-start.7 = (bf16[32,1664]{1,0:T(8,128)(2,1)S(1)}, bf16[32,1664]{1,0:T(8,128)(2,1)S(1)}, u32[]{:S(2)}, u32[]{:S(2)}) collective-permute-start(bf16[32,1664]{1,0:T(8,128)(2,1)S(1)} %add_grad.1.after_ref.own_ref), channel_id=1, source_target_pairs={{0,8},{8,0},{1,9},{9,1},{2,10},{10,2},{3,11},{11,3},{4,12},{12,4},... | collective-permute-start | bytes 319496 | tf_op jit(solution)/shard_map/ppermute | solution.py:443
  23.6 2.9 %collective-permute-start.8 = (bf16[32,1536]{1,0:T(8,128)(2,1)S(1)}, bf16[32,1536]{1,0:T(8,128)(2,1)S(1)}, u32[]{:S(2)}, u32[]{:S(2)}) collective-permute-start(bf16[32,1536]{1,0:T(8,128)(2,1)S(1)} %get-tuple-element.44.act_ref), channel_id=1, source_target_pairs={{0,4},{4,0},{1,5},{5,1},{2,6},{6,2},{3,7},{7,3},{8,12},{12,8},{9,1... | collective-permute-start | bytes 294920 | tf_op jit(solution)/shard_map/ppermute | solution.py:447
  27.6 1.4 %collective-permute-start.9 = (bf16[32,1536]{1,0:T(8,128)(2,1)S(1)}, bf16[32,1536]{1,0:T(8,128)(2,1)S(1)}, u32[]{:S(2)}, u32[]{:S(2)}) collective-permute-start(bf16[32,1536]{1,0:T(8,128)(2,1)S(1)} %grad_pre.1.grad_ref.own_ref), channel_id=1, source_target_pairs={{0,4},{4,0},{1,5},{5,1},{2,6},{6,2},{3,7},{7,3},{8,12},{12,8},{9,1... | collective-permute-start | bytes 294920 | tf_op jit(solution)/shard_map/ppermute | solution.py:461
  28.1 10.5 %copy-start.1 = (f32[3072]{0:T(1024)S(1)}, f32[3072]{0:T(1024)}, u32[]{:S(2)}) copy-start(f32[3072]{0:T(1024)} %param.10) | copy-start | bytes 36868
  30.0 8.6 %collective-permute-start.10 = (bf16[16,1536]{1,0:T(8,128)(2,1)S(1)}, bf16[16,1536]{1,0:T(8,128)(2,1)S(1)}, u32[]{:S(2)}, u32[]{:S(2)}) collective-permute-start(bf16[16,1536]{1,0:T(8,128)(2,1)S(1)} %get-tuple-element.49), channel_id=1, source_target_pairs={{0,3},{1,2},{2,1},{3,0},{4,7},{5,6},{6,5},{7,4},{8,11},{9,10},{10,... | collective-permute-start | bytes 147464 | tf_op jit(solution)/shard_map/ppermute | solution.py:369
  32.9 5.7 %collective-permute-start.11 = (bf16[16,1536]{1,0:T(8,128)(2,1)S(1)}, bf16[16,1536]{1,0:T(8,128)(2,1)S(1)}, u32[]{:S(2)}, u32[]{:S(2)}) collective-permute-start(bf16[16,1536]{1,0:T(8,128)(2,1)S(1)} %get-tuple-element.50), channel_id=1, source_target_pairs={{0,2},{1,3},{2,0},{3,1},{4,6},{5,7},{6,4},{7,5},{8,10},{9,11},{10,... | collective-permute-start | bytes 147464 | tf_op jit(solution)/shard_map/ppermute | solution.py:369
  32.9 5.7 %collective-permute-start.12 = (bf16[16,1536]{1,0:T(8,128)(2,1)S(1)}, bf16[16,1536]{1,0:T(8,128)(2,1)S(1)}, u32[]{:S(2)}, u32[]{:S(2)}) collective-permute-start(bf16[16,1536]{1,0:T(8,128)(2,1)S(1)} %get-tuple-element.51), channel_id=1, source_target_pairs={{0,1},{1,0},{2,3},{3,2},{4,5},{5,4},{6,7},{7,6},{8,9},{9,8},{10,11... | collective-permute-start | bytes 147464 | tf_op jit(solution)/shard_map/ppermute | solution.py:369
  38.6 4.1 %collective-permute-start.13 = (bf16[8,1536]{1,0:T(8,128)(2,1)S(1)}, bf16[8,1536]{1,0:T(8,128)(2,1)S(1)}, u32[]{:S(2)}, u32[]{:S(2)}) collective-permute-start(bf16[8,1536]{1,0:T(8,128)(2,1)S(1)} %get-tuple-element.55), channel_id=1, source_target_pairs={{0,8},{8,0},{1,9},{9,1},{2,10},{10,2},{3,11},{11,3},{4,12},{12,4},... | collective-permute-start | bytes 73736 | tf_op jit(solution)/shard_map/ppermute | solution.py:491

commit v18 on v16

--- a/solution.py
+++ b/solution.py
@@ -164,6 +164,21 @@
         far_turned[first:, part] = last_ref[part, :].T
 
 
+def cut_body(tokens_hbm, grad_hbm, own_ref, sent_ref, tokens_ref, grad_ref, sems):
+    me = lax.axis_index("tok")
+    first = pltpu.make_async_copy(tokens_hbm, tokens_ref, sems.at[0])
+    second = pltpu.make_async_copy(grad_hbm, grad_ref, sems.at[1])
+    first.start()
+    second.start()
+    first.wait()
+    second.wait()
+    mine = jnp.concatenate([tokens_ref[...].astype(f32), grad_ref[...].astype(f32)], axis=0)
+    wide = own_ref.shape[1]
+    low, high = mine[:, :wide], mine[:, wide:]
+    own_ref[...] = jnp.where(me == 0, low, high).astype(bf16)
+    sent_ref[...] = jnp.where(me == 0, high, low).astype(bf16)
+
+
 def pair_body(own_ref, got_ref, after_ref, *out_refs):
     tiles = ordered(lax.axis_index("tok"), own_ref[...], got_ref[...])
     count, wide = tiles.shape
@@ -375,10 +390,13 @@
         count = 2 * nn * rows
         sem = pltpu.SemaphoreType.DMA
 
-        mine = jnp.concatenate([tokens, grad_out], axis=0)
-        me = lax.axis_index("tok")
-        own = lax.dynamic_slice_in_dim(mine, me * wide, wide, 1)
-        sent = lax.dynamic_slice_in_dim(mine, (1 - me) * wide, wide, 1)
+        own, sent = call(
+            cut_body,
+            "cut_tiles",
+            [like((pair, wide), bf16)] * 2,
+            scratch=[pltpu.VMEM((rows, cols), bf16)] * 2 + [pltpu.SemaphoreType.DMA((2,))],
+            specs=[hbm] * 2,
+        )(in_hbm(tokens), in_hbm(grad_out))
         got = lax.ppermute(sent, "tok", swap)
 
         last = tile_of(half, 512)
@@ -396,7 +414,7 @@
             kept(own), kept(got), kept(in_far)
         )
         pieces = [across(tiles, shift) for shift in range(1, nn - 1)]
-        pieces = [across(farthest, nn - 1)] + pieces[::-1] + [tiles]
+        pieces = [across(farthest, nn - 1)] + pieces + [tiles]
         in_own, in_last, own_turned, far_turned = call(
             load_and_turn_body,
             "load_own",
@@ -464,7 +482,8 @@
             act_far, dy_cols, hid, "weight_out_grad_far", far_rows, into=weight_out_grad
         )
 
-        terms = [across(blocks[i], nn - 1 - i) for i in range(nn - 1)] + [blocks[-1]]
+        terms = [across(blocks[0], nn - 1)]
+        terms += [across(blocks[shift], shift) for shift in reversed(range(1, nn - 1))] + [blocks[-1]]
         own, sent = call(
             functools.partial(sum_body, rows),
             "sum_blocks",

time: 43.7 us -> 43.5 us (level)
  other arithmetic: 0.86 us -> 0.01 us
  Pallas kernels: 23.4 us -> 24.2 us
    concatenate x1 -> x0, other arithmetic: 0.86 us -> none  [on_device(): mine = jnp.concatenate([tokens, grad_out], axis=0)]
    pallas_call x16 -> x17, Pallas kernels: 13.8 us -> 14.6 us  [run(): pl.pallas_call(body, out_shape=shapes, in_specs=specs or [whole] * len(ar...]
  transfers between devices with their start and end apart: 14 -> 14, of which waited for: 6 -> 5; matrix products, arithmetic and copies ran while one was open for 0% -> 0% of each run, Pallas kernels for 48% -> 48%
where the time goes in v18:
time: 43.5 us; the launch traced here: 43.3 us
  Pallas kernels  24.2 us (56%)
  starting transfers between devices  15.7 us (36%)
  waiting for transfers between devices  2.61 us (6%)
  between operations  0.84 us (2%)
    pallas_call x17, Pallas kernels, run(): pl.pallas_call(body, out_shape=shapes, in_specs=specs or [whole] * len(ar...  14.6 us
    ppermute x6, starting transfers between devices, across(): return lax.ppermute(array, 'nout', [(i, i ^ shift) for i in range(nn)])  9.18 us
    pallas_call x2, Pallas kernels, outer(): pl.pallas_call(functools.partial(outer_body, most, first_of), out_shape=l...  6.67 us
    ppermute x2, starting transfers between devices, on_device(): got = lax.ppermute(sent, 'tok', swap)  3.93 us
    pallas_call x1, Pallas kernels, own_forward(): pl.pallas_call(own_forward_body, out_shape=[pltpu.VMEM((count, wide), f32...  2.86 us
    ppermute x1, starting transfers between devices, on_device(): other_pre = lax.ppermute(own_pre, 'tok', swap)  1.56 us
  transfers between devices with their start and end apart: 14, of which 5 were waited for; matrix products, arithmetic and copies ran while one was open for 0% of the time, Pallas kernels for 48%

profile of v18, /device:TPU:0, one launch (start us, length us, event | category | flops | bytes accessed | tf_op | source)
XLA Modules:
  0.0 43.3 jit_solution(14640299915512534947)
XLA Ops:
  0.6 0.8 %cut_tiles.1 = (bf16[8,1536]{1,0:T(8,128)(2,1)S(1)}, bf16[8,1536]{1,0:T(8,128)(2,1)S(1)}) custom-call(bf16[4,3072]{1,0:T(4,128)(2,1)} %tokens_hbm.1, bf16[4,3072]{1,0:T(4,128)(2,1)} %grad_hbm.1), custom_call_target="tpu_custom_call" | custom-call | tf_op jit(solution)/shard_map/cut_tiles/pallas_call | solution.py:55
  1.4 3.0 %collective-permute-start = (bf16[8,1536]{1,0:T(8,128)(2,1)S(1)}, bf16[8,1536]{1,0:T(8,128)(2,1)S(1)}, u32[]{:S(2)}, u32[]{:S(2)}) collective-permute-start(bf16[8,1536]{1,0:T(8,128)(2,1)S(1)} %get-tuple-element.34.after_ref), channel_id=1, source_target_pairs={{0,8},{8,0},{1,9},{9,1},{2,10},{10,2},{3,11},{11,3},{4,12},{12,4},... | collective-permute-start | bytes 73736 | tf_op jit(solution)/shard_map/ppermute | solution.py:400
  4.4 1.9 %load_far.1.after_ref.far_ref.refs_4_ = bf16[1536,1024]{1,0:T(8,128)(2,1)S(1)} custom-call(bf16[1536,3072]{1,0:T(8,128)(2,1)} %hbm_ref.3, bf16[8,1536]{1,0:T(8,128)(2,1)S(1)} %get-tuple-element.34.after_ref), custom_call_target="tpu_custom_call" | custom-call | tf_op jit(solution)/shard_map/load_far/pallas_call | solution.py:55
  6.3 0.0 collective-permute-done.got_ref
  6.4 4.1 %collective-permute-start.1 = (bf16[16,1664]{1,0:T(8,128)(2,1)S(1)}, bf16[16,1664]{1,0:T(8,128)(2,1)S(1)}, u32[]{:S(2)}, u32[]{:S(2)}) collective-permute-start(bf16[16,1664]{1,0:T(8,128)(2,1)S(1)} %get-tuple-element.35), channel_id=1, source_target_pairs={{0,3},{1,2},{2,1},{3,0},{4,7},{5,6},{6,5},{7,4},{8,11},{9,10},{10,... | collective-permute-start | bytes 159752 | tf_op jit(solution)/shard_map/ppermute | solution.py:383
  10.5 0.0 collective-permute-start.3
  10.5 0.6 %collective-permute-start.2 = (bf16[16,1536]{1,0:T(8,128)(2,1)S(1)}, bf16[16,1536]{1,0:T(8,128)(2,1)S(1)}, u32[]{:S(2)}, u32[]{:S(2)}) collective-permute-start(bf16[16,1536]{1,0:T(8,128)(2,1)S(1)} %get-tuple-element.36.after_ref.refs_3_), channel_id=1, source_target_pairs={{0,1},{1,0},{2,3},{3,2},{4,5},{5,4},{6,7},{7,6},{8,9},{9,8},{10,11... | collective-permute-start | bytes 147464 | tf_op jit(solution)/shard_map/ppermute | solution.py:383
  11.1 0.0 slice-start
  11.1 0.0 slice-start.1
  11.1 3.6 %load_own.1 = (bf16[1536,1536]{1,0:T(8,128)(2,1)S(1)}, bf16[1536,512]{1,0:T(8,128)(2,1)S(1)}, bf16[1536,1536]{1,0:T(8,128)(2,1)S(1)}, bf16[1536,1536]{1,0:T(8,128)(2,1)S(1)}) custom-call(bf16[1536,3072]{1,0:T(8,128)(2,1)} %hbm_ref.3, bf16[16,1536]{1,0:T(8,128)(2,1)S(1)} %get-tuple-element.36.after_ref.refs_3_, ...), custom_call_target="tpu_custom_call" | custom-call | tf_op jit(solution)/shard_map/load_own/pallas_call | solution.py:55
  14.7 0.8 %collective-permute-done.3.refs_2_ = bf16[16,1536]{1,0:T(8,128)(2,1)S(1)} collective-permute-done((bf16[16,1536]{1,0:T(8,128)(2,1)S(1)}, bf16[16,1536]{1,0:T(8,128)(2,1)S(1)}, u32[]{:S(2)}, u32[]{:S(2)}) %collective-permute-start.3) | collective-permute-done | bytes 49184 | tf_op jit(solution)/shard_map/ppermute | solution.py:383
  15.4 0.0 collective-permute-done.2.refs_1_
  15.4 0.0 collective-permute-done.1.refs_0_
  15.5 0.0 slice-start.2
  15.5 0.9 %far_pre.1 = (bf16[32,1536]{1,0:T(8,128)(2,1)S(1)}, bf16[32,1536]{1,0:T(8,128)(2,1)S(1)}, bf16[32,1536]{1,0:T(8,128)(2,1)S(1)}, f32[1,1536]{1,0:T(1,128)S(1)}) custom-call(bf16[16,1664]{1,0:T(8,128)(2,1)S(1)} %collective-permute-done.1.refs_0_, bf16[16,1536]{1,0:T(8,128)(2,1)S(1)} %collective-permute-done.2.refs_1_, ...), custom_call_target="tpu_custom_call" | custom-call | tf_op jit(solution)/shard_map/far_pre/pallas_call | solution.py:55
  16.4 0.0 collective-permute-start.4
  16.4 0.9 %own_pre.1.own_ref = f32[32,1536]{1,0:T(8,128)S(1)} custom-call(bf16[32,1536]{1,0:T(8,128)(2,1)S(1)} %get-tuple-element.39.x_ref.left_ref, bf16[1536,1536]{1,0:T(8,128)(2,1)S(1)} %get-tuple-element.38.refs_6_.w_in_ref, bf16[32,1536]{1,0:T(8,128)(2,1)S(1)} %get-tuple-element.40.after_ref), custom_call_target="tpu_custom_call" | custom-call | tf_op jit(solution)/shard_map/own_pre/pallas_call | solution.py:55
  17.3 0.4 collective-permute-done.4.got_ref
  17.7 1.6 %collective-permute-start.5 = (bf16[32,1664]{1,0:T(8,128)(2,1)S(1)}, bf16[32,1664]{1,0:T(8,128)(2,1)S(1)}, u32[]{:S(2)}, u32[]{:S(2)}) collective-permute-start(bf16[32,1664]{1,0:T(8,128)(2,1)S(1)} %add_pre.1.after_ref.own_ref), channel_id=1, source_target_pairs={{0,8},{8,0},{1,9},{9,1},{2,10},{10,2},{3,11},{11,3},{4,12},{12,4},... | collective-permute-start | bytes 319496 | tf_op jit(solution)/shard_map/ppermute | solution.py:444
  19.3 0.0 slice-done
  19.3 0.0 slice-done.1
  19.3 0.0 slice-done.2
  19.3 0.0 copy-start.1
  19.3 1.4 %far_grad.1 = bf16[32,1536]{1,0:T(8,128)(2,1)S(1)} custom-call(bf16[32,1536]{1,0:T(8,128)(2,1)S(1)} %get-tuple-element.42.dy_ref.right_ref, bf16[3072,1536]{1,0:T(8,128)(2,1)S(1)} %bitcast.5, bf16[32,1664]{1,0:T(8,128)(2,1)S(1)} %add_pre.1.after_ref.own_ref), custom_call_target="tpu_custom_call" | custom-call | tf_op jit(solution)/shard_map/far_grad/pallas_call | solution.py:55
  20.7 0.0 collective-permute-start.6
  20.8 1.5 %own_grad.1.own_ref = f32[32,1536]{1,0:T(8,128)S(1)} custom-call(bf16[32,1536]{1,0:T(8,128)(2,1)S(1)} %get-tuple-element.42.dy_ref.right_ref, bf16[3072,1536]{1,0:T(8,128)(2,1)S(1)} %bitcast.5), custom_call_target="tpu_custom_call" | custom-call | tf_op jit(solution)/shard_map/own_grad/pallas_call | solution.py:55
  22.2 0.0 collective-permute-done.6.got_ref
  22.3 0.6 %collective-permute-start.7 = (bf16[32,1664]{1,0:T(8,128)(2,1)S(1)}, bf16[32,1664]{1,0:T(8,128)(2,1)S(1)}, u32[]{:S(2)}, u32[]{:S(2)}) collective-permute-start(bf16[32,1664]{1,0:T(8,128)(2,1)S(1)} %add_grad.1.after_ref.own_ref), channel_id=1, source_target_pairs={{0,8},{8,0},{1,9},{9,1},{2,10},{10,2},{3,11},{11,3},{4,12},{12,4},... | collective-permute-start | bytes 319496 | tf_op jit(solution)/shard_map/ppermute | solution.py:449
  22.9 0.0 collective-permute-done.5.other_ref
  22.9 0.0 copy-done.1
  22.9 0.1 gelu.1
  23.0 0.3 collective-permute-start.8
  23.3 2.9 %own_forward.1 = (f32[32,1536]{1,0:T(8,128)S(1)}, bf16[3072,1536]{1,0:T(8,128)(2,1)}) custom-call(bf16[32,1536]{1,0:T(8,128)(2,1)S(1)} %get-tuple-element.44.act_ref, bf16[32,1536]{1,0:T(8,128)(2,1)S(1)} %get-tuple-element.42.dy_ref.right_ref, bf16[3072,1536]{1,0:T(8,128)(2,1)S(1)} %bitcast.5), custom_call_target="tpu_custom_call" | custom-call | tf_op jit(solution)/shard_map/own_forward/pallas_call | solution.py:316
  26.2 0.0 collective-permute-done.8.far_ref.left_ref
  26.2 0.9 %far_forward.1.after_ref.forward_ref = f32[32,1536]{1,0:T(8,128)S(1)} custom-call(bf16[32,1536]{1,0:T(8,128)(2,1)S(1)} %collective-permute-done.8.far_ref.left_ref, bf16[3072,1536]{1,0:T(8,128)(2,1)S(1)} %bitcast.5, f32[32,1536]{1,0:T(8,128)S(1)} %get-tuple-element.45.terms_ref), custom_call_target="tpu_custom_call" | custom-call | tf_op jit(solution)/shard_map/far_forward/pallas_call | solution.py:55
  27.1 0.6 %collective-permute-done.7.other_ref = bf16[32,1664]{1,0:T(8,128)(2,1)S(1)} collective-permute-done((bf16[32,1664]{1,0:T(8,128)(2,1)S(1)}, bf16[32,1664]{1,0:T(8,128)(2,1)S(1)}, u32[]{:S(2)}, u32[]{:S(2)}) %collective-permute-start.7) | collective-permute-done | bytes 106528 | tf_op jit(solution)/shard_map/ppermute | solution.py:449
  27.8 0.1 collective-permute-start.9
  27.8 0.0 copy-start
  27.9 0.9 %own_backward.1.backward_ref = f32[32,1536]{1,0:T(8,128)S(1)} custom-call(bf16[32,1536]{1,0:T(8,128)(2,1)S(1)} %grad_pre.1.grad_ref.own_ref, bf16[1536,1536]{1,0:T(8,128)(2,1)S(1)} %get-tuple-element.47.turned_ref), custom_call_target="tpu_custom_call" | custom-call | tf_op jit(solution)/shard_map/own_backward/pallas_call | solution.py:55
  28.8 0.4 collective-permute-done.9.far_ref
  29.1 0.9 %output_blocks.1 = (bf16[32,3072]{1,0:T(8,128)(2,1)S(1)}, bf16[16,1536]{1,0:T(8,128)(2,1)S(1)}, bf16[16,1536]{1,0:T(8,128)(2,1)S(1)}, bf16[16,1536]{1,0:T(8,128)(2,1)S(1)}, bf16[16,1536]{1,0:T(8,128)(2,1)S(1)}) custom-call(bf16[32,1536]{1,0:T(8,128)(2,1)S(1)} %grad_pre.1.grad_ref.own_ref, bf16[32,1536]{1,0:T(8,128)(2,1)S(1)} %collective-permute-done.9.far_ref, ...), custom_call_target="tpu_custom_call" | custom-call | tf_op jit(solution)/shard_map/output_blocks/pallas_call | solution.py:55
  30.1 3.1 %collective-permute-start.10 = (bf16[16,1536]{1,0:T(8,128)(2,1)S(1)}, bf16[16,1536]{1,0:T(8,128)(2,1)S(1)}, u32[]{:S(2)}, u32[]{:S(2)}) collective-permute-start(bf16[16,1536]{1,0:T(8,128)(2,1)S(1)} %get-tuple-element.49), channel_id=1, source_target_pairs={{0,3},{1,2},{2,1},{3,0},{4,7},{5,6},{6,5},{7,4},{8,11},{9,10},{10,... | collective-permute-start | bytes 147464 | tf_op jit(solution)/shard_map/ppermute | solution.py:383
  33.1 0.0 collective-permute-start.11
  33.1 1.4 %collective-permute-start.12 = (bf16[16,1536]{1,0:T(8,128)(2,1)S(1)}, bf16[16,1536]{1,0:T(8,128)(2,1)S(1)}, u32[]{:S(2)}, u32[]{:S(2)}) collective-permute-start(bf16[16,1536]{1,0:T(8,128)(2,1)S(1)} %get-tuple-element.51), channel_id=1, source_target_pairs={{0,1},{1,0},{2,3},{3,2},{4,5},{5,4},{6,7},{7,6},{8,9},{9,8},{10,11... | collective-permute-start | bytes 147464 | tf_op jit(solution)/shard_map/ppermute | solution.py:383
  34.5 4.1 %weight_in_grad.1.refs_4_ = bf16[1536,3072]{1,0:T(8,128)(2,1)} custom-call(bf16[32,1536]{1,0:T(8,128)(2,1)S(1)} %get-tuple-element.39.x_ref.left_ref, bf16[32,3072]{1,0:T(8,128)(2,1)S(1)} %get-tuple-element.53.right_ref.hidden_ref), custom_call_target="tpu_custom_call" | custom-call | tf_op jit(solution)/shard_map/weight_in_grad/pallas_call | solution.py:334
  38.6 0.0 collective-permute-done.10.refs_0_
  38.7 0.0 collective-permute-done.11.refs_1_
  38.7 0.0 collective-permute-done.12.refs_2_
  38.7 0.0 copy-done
  38.7 0.9 %collective-permute-start.13 = (bf16[8,1536]{1,0:T(8,128)(2,1)S(1)}, bf16[8,1536]{1,0:T(8,128)(2,1)S(1)}, u32[]{:S(2)}, u32[]{:S(2)}) collective-permute-start(bf16[8,1536]{1,0:T(8,128)(2,1)S(1)} %get-tuple-element.55), channel_id=1, source_target_pairs={{0,8},{8,0},{1,9},{9,1},{2,10},{10,2},{3,11},{11,3},{4,12},{12,4},... | collective-permute-start | bytes 73736 | tf_op jit(solution)/shard_map/ppermute | solution.py:497
  39.7 2.6 %weight_out_grad_far.1 = bf16[3072,1536]{1,0:T(8,128)(2,1)} custom-call(bf16[32,1536]{1,0:T(8,128)(2,1)S(1)} %collective-permute-done.8.far_ref.left_ref, bf16[32,1536]{1,0:T(8,128)(2,1)S(1)} %get-tuple-element.42.dy_ref.right_ref, bf16[3072,1536]{1,0:T(8,128)(2,1)} %get-tuple-element.46.later_ref.refs_0_), custom_call_target="tpu_custom_call", output_to_operand_aliasing={{}: (2, {})} | custom-call | tf_op jit(solution)/shard_map/weight_out_grad_far/pallas_call | solution.py:334
  42.2 0.4 collective-permute-done.13.got_ref
  42.6 0.7 %final_rows.1 = (bf16[4,3072]{1,0:T(4,128)(2,1)}, bf16[4,3072]{1,0:T(4,128)(2,1)}, f32[1,3072]{1,0:T(1,128)}, f32[1,3072]{1,0:T(1,128)}) custom-call(bf16[8,1536]{1,0:T(8,128)(2,1)S(1)} %get-tuple-element.54.own_ref, bf16[8,1536]{1,0:T(8,128)(2,1)S(1)} %collective-permute-done.13.got_ref, f32[1,1536]{1,0:T(1,128)S(1)} %get-tuple-element.41.sums_ref, ...), custom_call_target="tpu_custom_call" | custom-call | tf_op jit(solution)/shard_map/final_rows/pallas_call | solution.py:55
  (6 shorter events, 0.2 us)
Async XLA Ops:
  1.4 4.9 %collective-permute-start = (bf16[8,1536]{1,0:T(8,128)(2,1)S(1)}, bf16[8,1536]{1,0:T(8,128)(2,1)S(1)}, u32[]{:S(2)}, u32[]{:S(2)}) collective-permute-start(bf16[8,1536]{1,0:T(8,128)(2,1)S(1)} %get-tuple-element.34.after_ref), channel_id=1, source_target_pairs={{0,8},{8,0},{1,9},{9,1},{2,10},{10,2},{3,11},{11,3},{4,12},{12,4},... | collective-permute-start | bytes 73736 | tf_op jit(solution)/shard_map/ppermute | solution.py:400
  6.4 9.1 %collective-permute-start.1 = (bf16[16,1664]{1,0:T(8,128)(2,1)S(1)}, bf16[16,1664]{1,0:T(8,128)(2,1)S(1)}, u32[]{:S(2)}, u32[]{:S(2)}) collective-permute-start(bf16[16,1664]{1,0:T(8,128)(2,1)S(1)} %get-tuple-element.35), channel_id=1, source_target_pairs={{0,3},{1,2},{2,1},{3,0},{4,7},{5,6},{6,5},{7,4},{8,11},{9,10},{10,... | collective-permute-start | bytes 159752 | tf_op jit(solution)/shard_map/ppermute | solution.py:383
  10.5 5.0 %collective-permute-start.3 = (bf16[16,1536]{1,0:T(8,128)(2,1)S(1)}, bf16[16,1536]{1,0:T(8,128)(2,1)S(1)}, u32[]{:S(2)}, u32[]{:S(2)}) collective-permute-start(bf16[16,1536]{1,0:T(8,128)(2,1)S(1)} %get-tuple-element.36.after_ref.refs_3_), channel_id=1, source_target_pairs={{0,2},{1,3},{2,0},{3,1},{4,6},{5,7},{6,4},{7,5},{8,10},{9,11},{10,... | collective-permute-start | bytes 147464 | tf_op jit(solution)/shard_map/ppermute | solution.py:383
  10.5 5.0 %collective-permute-start.2 = (bf16[16,1536]{1,0:T(8,128)(2,1)S(1)}, bf16[16,1536]{1,0:T(8,128)(2,1)S(1)}, u32[]{:S(2)}, u32[]{:S(2)}) collective-permute-start(bf16[16,1536]{1,0:T(8,128)(2,1)S(1)} %get-tuple-element.36.after_ref.refs_3_), channel_id=1, source_target_pairs={{0,1},{1,0},{2,3},{3,2},{4,5},{5,4},{6,7},{7,6},{8,9},{9,8},{10,11... | collective-permute-start | bytes 147464 | tf_op jit(solution)/shard_map/ppermute | solution.py:383
  11.1 8.2 %slice-start = ((s8[9437184]{0:T(1024)(128)(4,1)}), s8[1048576]{0:T(1024)(128)(4,1)S(1)}, s32[]{:S(2)}) async-start(s8[9437184]{0:T(1024)(128)(4,1)} %bitcast.4), calls=%async_computation | async-start | bytes 2097152
  11.1 8.2 %slice-start.1 = ((s8[9437184]{0:T(1024)(128)(4,1)}), s8[4194304]{0:T(1024)(128)(4,1)S(1)}, s32[]{:S(2)}) async-start(s8[9437184]{0:T(1024)(128)(4,1)} %bitcast.4), calls=%async_computation.1 | async-start | bytes 8388608
  15.5 3.8 %slice-start.2 = ((s8[9437184]{0:T(1024)(128)(4,1)}), s8[4194304]{0:T(1024)(128)(4,1)S(1)}, s32[]{:S(2)}) async-start(s8[9437184]{0:T(1024)(128)(4,1)} %bitcast.4), calls=%async_computation.2 | async-start | bytes 8388608
  16.4 1.3 %collective-permute-start.4 = (bf16[32,1536]{1,0:T(8,128)(2,1)S(1)}, bf16[32,1536]{1,0:T(8,128)(2,1)S(1)}, u32[]{:S(2)}, u32[]{:S(2)}) collective-permute-start(bf16[32,1536]{1,0:T(8,128)(2,1)S(1)} %get-tuple-element.40.after_ref), channel_id=1, source_target_pairs={{0,4},{4,0},{1,5},{5,1},{2,6},{6,2},{3,7},{7,3},{8,12},{12,8},{9,1... | collective-permute-start | bytes 294920 | tf_op jit(solution)/shard_map/ppermute | solution.py:441
  17.7 5.2 %collective-permute-start.5 = (bf16[32,1664]{1,0:T(8,128)(2,1)S(1)}, bf16[32,1664]{1,0:T(8,128)(2,1)S(1)}, u32[]{:S(2)}, u32[]{:S(2)}) collective-permute-start(bf16[32,1664]{1,0:T(8,128)(2,1)S(1)} %add_pre.1.after_ref.own_ref), channel_id=1, source_target_pairs={{0,8},{8,0},{1,9},{9,1},{2,10},{10,2},{3,11},{11,3},{4,12},{12,4},... | collective-permute-start | bytes 319496 | tf_op jit(solution)/shard_map/ppermute | solution.py:444
  19.3 3.6 %copy-start.1 = (f32[3072]{0:T(1024)S(1)}, f32[3072]{0:T(1024)}, u32[]{:S(2)}) copy-start(f32[3072]{0:T(1024)} %param.8) | copy-start | bytes 36868
  20.7 1.5 %collective-permute-start.6 = (bf16[32,1536]{1,0:T(8,128)(2,1)S(1)}, bf16[32,1536]{1,0:T(8,128)(2,1)S(1)}, u32[]{:S(2)}, u32[]{:S(2)}) collective-permute-start(bf16[32,1536]{1,0:T(8,128)(2,1)S(1)} %far_grad.1), channel_id=1, source_target_pairs={{0,4},{4,0},{1,5},{5,1},{2,6},{6,2},{3,7},{7,3},{8,12},{12,8},{9,1... | collective-permute-start | bytes 294920 | tf_op jit(solution)/shard_map/ppermute | solution.py:446
  22.3 5.4 %collective-permute-start.7 = (bf16[32,1664]{1,0:T(8,128)(2,1)S(1)}, bf16[32,1664]{1,0:T(8,128)(2,1)S(1)}, u32[]{:S(2)}, u32[]{:S(2)}) collective-permute-start(bf16[32,1664]{1,0:T(8,128)(2,1)S(1)} %add_grad.1.after_ref.own_ref), channel_id=1, source_target_pairs={{0,8},{8,0},{1,9},{9,1},{2,10},{10,2},{3,11},{11,3},{4,12},{12,4},... | collective-permute-start | bytes 319496 | tf_op jit(solution)/shard_map/ppermute | solution.py:449
  23.0 3.1 %collective-permute-start.8 = (bf16[32,1536]{1,0:T(8,128)(2,1)S(1)}, bf16[32,1536]{1,0:T(8,128)(2,1)S(1)}, u32[]{:S(2)}, u32[]{:S(2)}) collective-permute-start(bf16[32,1536]{1,0:T(8,128)(2,1)S(1)} %get-tuple-element.44.act_ref), channel_id=1, source_target_pairs={{0,4},{4,0},{1,5},{5,1},{2,6},{6,2},{3,7},{7,3},{8,12},{12,8},{9,1... | collective-permute-start | bytes 294920 | tf_op jit(solution)/shard_map/ppermute | solution.py:453
  27.8 1.4 %collective-permute-start.9 = (bf16[32,1536]{1,0:T(8,128)(2,1)S(1)}, bf16[32,1536]{1,0:T(8,128)(2,1)S(1)}, u32[]{:S(2)}, u32[]{:S(2)}) collective-permute-start(bf16[32,1536]{1,0:T(8,128)(2,1)S(1)} %grad_pre.1.grad_ref.own_ref), channel_id=1, source_target_pairs={{0,4},{4,0},{1,5},{5,1},{2,6},{6,2},{3,7},{7,3},{8,12},{12,8},{9,1... | collective-permute-start | bytes 294920 | tf_op jit(solution)/shard_map/ppermute | solution.py:467
  27.8 10.8 %copy-start = (f32[3072]{0:T(1024)S(1)}, f32[3072]{0:T(1024)}, u32[]{:S(2)}) copy-start(f32[3072]{0:T(1024)} %param.10) | copy-start | bytes 36868
  30.1 8.6 %collective-permute-start.10 = (bf16[16,1536]{1,0:T(8,128)(2,1)S(1)}, bf16[16,1536]{1,0:T(8,128)(2,1)S(1)}, u32[]{:S(2)}, u32[]{:S(2)}) collective-permute-start(bf16[16,1536]{1,0:T(8,128)(2,1)S(1)} %get-tuple-element.49), channel_id=1, source_target_pairs={{0,3},{1,2},{2,1},{3,0},{4,7},{5,6},{6,5},{7,4},{8,11},{9,10},{10,... | collective-permute-start | bytes 147464 | tf_op jit(solution)/shard_map/ppermute | solution.py:383
  33.1 5.5 %collective-permute-start.11 = (bf16[16,1536]{1,0:T(8,128)(2,1)S(1)}, bf16[16,1536]{1,0:T(8,128)(2,1)S(1)}, u32[]{:S(2)}, u32[]{:S(2)}) collective-permute-start(bf16[16,1536]{1,0:T(8,128)(2,1)S(1)} %get-tuple-element.50), channel_id=1, source_target_pairs={{0,2},{1,3},{2,0},{3,1},{4,6},{5,7},{6,4},{7,5},{8,10},{9,11},{10,... | collective-permute-start | bytes 147464 | tf_op jit(solution)/shard_map/ppermute | solution.py:383
  33.1 5.5 %collective-permute-start.12 = (bf16[16,1536]{1,0:T(8,128)(2,1)S(1)}, bf16[16,1536]{1,0:T(8,128)(2,1)S(1)}, u32[]{:S(2)}, u32[]{:S(2)}) collective-permute-start(bf16[16,1536]{1,0:T(8,128)(2,1)S(1)} %get-tuple-element.51), channel_id=1, source_target_pairs={{0,1},{1,0},{2,3},{3,2},{4,5},{5,4},{6,7},{7,6},{8,9},{9,8},{10,11... | collective-permute-start | bytes 147464 | tf_op jit(solution)/shard_map/ppermute | solution.py:383
  38.7 3.9 %collective-permute-start.13 = (bf16[8,1536]{1,0:T(8,128)(2,1)S(1)}, bf16[8,1536]{1,0:T(8,128)(2,1)S(1)}, u32[]{:S(2)}, u32[]{:S(2)}) collective-permute-start(bf16[8,1536]{1,0:T(8,128)(2,1)S(1)} %get-tuple-element.55), channel_id=1, source_target_pairs={{0,8},{8,0},{1,9},{9,1},{2,10},{10,2},{3,11},{11,3},{4,12},{12,4},... | collective-permute-start | bytes 73736 | tf_op jit(solution)/shard_map/ppermute | solution.py:497

commit v19 on v18

--- a/solution.py
+++ b/solution.py
@@ -179,13 +179,8 @@
     sent_ref[...] = jnp.where(me == 0, high, low).astype(bf16)
 
 
-def pair_body(own_ref, got_ref, after_ref, *out_refs):
-    tiles = ordered(lax.axis_index("tok"), own_ref[...], got_ref[...])
-    count, wide = tiles.shape
-    for out_ref in out_refs:
-        out_ref[:, :wide] = tiles
-        if out_ref.shape[1] > wide:
-            out_ref[:, wide:] = jnp.zeros((count, out_ref.shape[1] - wide), bf16)
+def pair_body(own_ref, got_ref, after_ref, out_ref):
+    out_ref[...] = ordered(lax.axis_index("tok"), own_ref[...], got_ref[...])
 
 
 def far_pre_body(rows, count, *refs):
@@ -408,13 +403,10 @@
             scratch=[sem((4,))],
             specs=[hbm, pl.BlockSpec(memory_space=pl.ANY)],
         )(in_hbm(weight_in), sent)
-        tiles, farthest = call(
-            pair_body, "pair_tiles", [like((2 * pair, wide + more), bf16) for more in (0, 128)]
-        )(
+        (tiles,) = call(pair_body, "pair_tiles", [like((2 * pair, wide), bf16)])(
             kept(own), kept(got), kept(in_far)
         )
-        pieces = [across(tiles, shift) for shift in range(1, nn - 1)]
-        pieces = [across(farthest, nn - 1)] + pieces + [tiles]
+        pieces = [across(tiles, shift) for shift in range(1, nn)] + [tiles]
         in_own, in_last, own_turned, far_turned = call(
             load_and_turn_body,
             "load_own",
@@ -482,8 +474,7 @@
             act_far, dy_cols, hid, "weight_out_grad_far", far_rows, into=weight_out_grad
         )
 
-        terms = [across(blocks[0], nn - 1)]
-        terms += [across(blocks[shift], shift) for shift in reversed(range(1, nn - 1))] + [blocks[-1]]
+        terms = [across(blocks[shift - 1], shift) for shift in reversed(range(1, nn))] + [blocks[-1]]
         own, sent = call(
             functools.partial(sum_body, rows),
             "sum_blocks",

time: 43.5 us -> 43.5 us (level)
  no operation moved by 1% of the time
where the time goes in v19:
time: 43.5 us; the launch traced here: 43.3 us
  Pallas kernels  24.1 us (55%)
  starting transfers between devices  15.7 us (36%)
  waiting for transfers between devices  2.59 us (6%)
  between operations  0.85 us (2%)
    pallas_call x17, Pallas kernels, run(): pl.pallas_call(body, out_shape=shapes, in_specs=specs or [whole] * len(ar...  14.6 us
    ppermute x6, starting transfers between devices, across(): return lax.ppermute(array, 'nout', [(i, i ^ shift) for i in range(nn)])  9.18 us
    pallas_call x2, Pallas kernels, outer(): pl.pallas_call(functools.partial(outer_body, most, first_of), out_shape=l...  6.66 us
    ppermute x2, starting transfers between devices, on_device(): got = lax.ppermute(sent, 'tok', swap)  3.94 us
    pallas_call x1, Pallas kernels, own_forward(): pl.pallas_call(own_forward_body, out_shape=[pltpu.VMEM((count, wide), f32...  2.86 us
    ppermute x1, starting transfers between devices, on_device(): other_pre = lax.ppermute(own_pre, 'tok', swap)  1.56 us
  transfers between devices with their start and end apart: 14, of which 5 were waited for; matrix products, arithmetic and copies ran while one was open for 0% of the time, Pallas kernels for 48%

profile of v19, /device:TPU:0, one launch (start us, length us, event | category | flops | bytes accessed | tf_op | source)
XLA Modules:
  0.0 43.3 jit_solution(5781496287556150229)
XLA Ops:
  0.6 0.8 %cut_tiles.1 = (bf16[8,1536]{1,0:T(8,128)(2,1)S(1)}, bf16[8,1536]{1,0:T(8,128)(2,1)S(1)}) custom-call(bf16[4,3072]{1,0:T(4,128)(2,1)} %tokens_hbm.1, bf16[4,3072]{1,0:T(4,128)(2,1)} %grad_hbm.1), custom_call_target="tpu_custom_call" | custom-call | tf_op jit(solution)/shard_map/cut_tiles/pallas_call | solution.py:55
  1.4 3.0 %collective-permute-start = (bf16[8,1536]{1,0:T(8,128)(2,1)S(1)}, bf16[8,1536]{1,0:T(8,128)(2,1)S(1)}, u32[]{:S(2)}, u32[]{:S(2)}) collective-permute-start(bf16[8,1536]{1,0:T(8,128)(2,1)S(1)} %get-tuple-element.32.after_ref), channel_id=1, source_target_pairs={{0,8},{8,0},{1,9},{9,1},{2,10},{10,2},{3,11},{11,3},{4,12},{12,4},... | collective-permute-start | bytes 73736 | tf_op jit(solution)/shard_map/ppermute | solution.py:395
  4.4 1.9 %load_far.1.after_ref.far_ref.refs_4_ = bf16[1536,1024]{1,0:T(8,128)(2,1)S(1)} custom-call(bf16[1536,3072]{1,0:T(8,128)(2,1)} %hbm_ref.3, bf16[8,1536]{1,0:T(8,128)(2,1)S(1)} %get-tuple-element.32.after_ref), custom_call_target="tpu_custom_call" | custom-call | tf_op jit(solution)/shard_map/load_far/pallas_call | solution.py:55
  6.3 0.0 collective-permute-done.got_ref
  6.4 4.1 %collective-permute-start.3 = (bf16[16,1536]{1,0:T(8,128)(2,1)S(1)}, bf16[16,1536]{1,0:T(8,128)(2,1)S(1)}, u32[]{:S(2)}, u32[]{:S(2)}) collective-permute-start(bf16[16,1536]{1,0:T(8,128)(2,1)S(1)} %pair_tiles.1.after_ref.refs_3_), channel_id=1, source_target_pairs={{0,3},{1,2},{2,1},{3,0},{4,7},{5,6},{6,5},{7,4},{8,11},{9,10},{10,... | collective-permute-start | bytes 147464 | tf_op jit(solution)/shard_map/ppermute | solution.py:378
  10.5 0.0 collective-permute-start.2
  10.5 0.6 %collective-permute-start.1 = (bf16[16,1536]{1,0:T(8,128)(2,1)S(1)}, bf16[16,1536]{1,0:T(8,128)(2,1)S(1)}, u32[]{:S(2)}, u32[]{:S(2)}) collective-permute-start(bf16[16,1536]{1,0:T(8,128)(2,1)S(1)} %pair_tiles.1.after_ref.refs_3_), channel_id=1, source_target_pairs={{0,1},{1,0},{2,3},{3,2},{4,5},{5,4},{6,7},{7,6},{8,9},{9,8},{10,11... | collective-permute-start | bytes 147464 | tf_op jit(solution)/shard_map/ppermute | solution.py:378
  11.1 0.0 slice-start
  11.1 0.0 slice-start.1
  11.1 3.6 %load_own.1 = (bf16[1536,1536]{1,0:T(8,128)(2,1)S(1)}, bf16[1536,512]{1,0:T(8,128)(2,1)S(1)}, bf16[1536,1536]{1,0:T(8,128)(2,1)S(1)}, bf16[1536,1536]{1,0:T(8,128)(2,1)S(1)}) custom-call(bf16[1536,3072]{1,0:T(8,128)(2,1)} %hbm_ref.3, bf16[16,1536]{1,0:T(8,128)(2,1)S(1)} %pair_tiles.1.after_ref.refs_3_, bf16[1536,1024]{1,0:T(8,128)(2,1)S(1)} %load_far.1.after_ref.far_ref.refs_4_), custom_call_target="tpu_custom_call" | custom-call | tf_op jit(solution)/shard_map/load_own/pallas_call | solution.py:55
  14.7 0.0 collective-permute-done.3.refs_2_
  14.7 0.8 %collective-permute-done.2.refs_1_ = bf16[16,1536]{1,0:T(8,128)(2,1)S(1)} collective-permute-done((bf16[16,1536]{1,0:T(8,128)(2,1)S(1)}, bf16[16,1536]{1,0:T(8,128)(2,1)S(1)}, u32[]{:S(2)}, u32[]{:S(2)}) %collective-permute-start.2) | collective-permute-done | bytes 49184 | tf_op jit(solution)/shard_map/ppermute | solution.py:378
  15.4 0.0 collective-permute-done.1.refs_0_
  15.4 0.0 slice-start.2
  15.4 0.9 %far_pre.1 = (bf16[32,1536]{1,0:T(8,128)(2,1)S(1)}, bf16[32,1536]{1,0:T(8,128)(2,1)S(1)}, bf16[32,1536]{1,0:T(8,128)(2,1)S(1)}, f32[1,1536]{1,0:T(1,128)S(1)}) custom-call(bf16[16,1536]{1,0:T(8,128)(2,1)S(1)} %collective-permute-done.1.refs_0_, bf16[16,1536]{1,0:T(8,128)(2,1)S(1)} %collective-permute-done.2.refs_1_, ...), custom_call_target="tpu_custom_call" | custom-call | tf_op jit(solution)/shard_map/far_pre/pallas_call | solution.py:55
  16.4 0.0 collective-permute-start.4
  16.4 0.9 %own_pre.1.own_ref = f32[32,1536]{1,0:T(8,128)S(1)} custom-call(bf16[32,1536]{1,0:T(8,128)(2,1)S(1)} %get-tuple-element.35.x_ref.left_ref, bf16[1536,1536]{1,0:T(8,128)(2,1)S(1)} %get-tuple-element.34.refs_6_.w_in_ref, bf16[32,1536]{1,0:T(8,128)(2,1)S(1)} %get-tuple-element.36.after_ref), custom_call_target="tpu_custom_call" | custom-call | tf_op jit(solution)/shard_map/own_pre/pallas_call | solution.py:55
  17.3 0.4 collective-permute-done.4.got_ref
  17.7 1.6 %collective-permute-start.5 = (bf16[32,1664]{1,0:T(8,128)(2,1)S(1)}, bf16[32,1664]{1,0:T(8,128)(2,1)S(1)}, u32[]{:S(2)}, u32[]{:S(2)}) collective-permute-start(bf16[32,1664]{1,0:T(8,128)(2,1)S(1)} %add_pre.1.after_ref.own_ref), channel_id=1, source_target_pairs={{0,8},{8,0},{1,9},{9,1},{2,10},{10,2},{3,11},{11,3},{4,12},{12,4},... | collective-permute-start | bytes 319496 | tf_op jit(solution)/shard_map/ppermute | solution.py:436
  19.3 0.0 slice-done
  19.3 0.0 slice-done.1
  19.3 0.0 slice-done.2
  19.3 0.0 copy-start.1
  19.3 1.4 %far_grad.1 = bf16[32,1536]{1,0:T(8,128)(2,1)S(1)} custom-call(bf16[32,1536]{1,0:T(8,128)(2,1)S(1)} %get-tuple-element.38.dy_ref.right_ref, bf16[3072,1536]{1,0:T(8,128)(2,1)S(1)} %bitcast.5, bf16[32,1664]{1,0:T(8,128)(2,1)S(1)} %add_pre.1.after_ref.own_ref), custom_call_target="tpu_custom_call" | custom-call | tf_op jit(solution)/shard_map/far_grad/pallas_call | solution.py:55
  20.7 0.0 collective-permute-start.6
  20.8 1.5 %own_grad.1.own_ref = f32[32,1536]{1,0:T(8,128)S(1)} custom-call(bf16[32,1536]{1,0:T(8,128)(2,1)S(1)} %get-tuple-element.38.dy_ref.right_ref, bf16[3072,1536]{1,0:T(8,128)(2,1)S(1)} %bitcast.5), custom_call_target="tpu_custom_call" | custom-call | tf_op jit(solution)/shard_map/own_grad/pallas_call | solution.py:55
  22.2 0.0 collective-permute-done.6.got_ref
  22.3 0.6 %collective-permute-start.7 = (bf16[32,1664]{1,0:T(8,128)(2,1)S(1)}, bf16[32,1664]{1,0:T(8,128)(2,1)S(1)}, u32[]{:S(2)}, u32[]{:S(2)}) collective-permute-start(bf16[32,1664]{1,0:T(8,128)(2,1)S(1)} %add_grad.1.after_ref.own_ref), channel_id=1, source_target_pairs={{0,8},{8,0},{1,9},{9,1},{2,10},{10,2},{3,11},{11,3},{4,12},{12,4},... | collective-permute-start | bytes 319496 | tf_op jit(solution)/shard_map/ppermute | solution.py:441
  22.9 0.0 collective-permute-done.5.other_ref
  22.9 0.0 copy-done.1
  22.9 0.1 gelu.1
  23.0 0.3 collective-permute-start.8
  23.3 2.9 %own_forward.1 = (f32[32,1536]{1,0:T(8,128)S(1)}, bf16[3072,1536]{1,0:T(8,128)(2,1)}) custom-call(bf16[32,1536]{1,0:T(8,128)(2,1)S(1)} %get-tuple-element.40.act_ref, bf16[32,1536]{1,0:T(8,128)(2,1)S(1)} %get-tuple-element.38.dy_ref.right_ref, bf16[3072,1536]{1,0:T(8,128)(2,1)S(1)} %bitcast.5), custom_call_target="tpu_custom_call" | custom-call | tf_op jit(solution)/shard_map/own_forward/pallas_call | solution.py:311
  26.1 0.0 collective-permute-done.8.far_ref.left_ref
  26.1 0.9 %far_forward.1.after_ref.forward_ref = f32[32,1536]{1,0:T(8,128)S(1)} custom-call(bf16[32,1536]{1,0:T(8,128)(2,1)S(1)} %collective-permute-done.8.far_ref.left_ref, bf16[3072,1536]{1,0:T(8,128)(2,1)S(1)} %bitcast.5, f32[32,1536]{1,0:T(8,128)S(1)} %get-tuple-element.41.terms_ref), custom_call_target="tpu_custom_call" | custom-call | tf_op jit(solution)/shard_map/far_forward/pallas_call | solution.py:55
  27.1 0.6 %collective-permute-done.7.other_ref = bf16[32,1664]{1,0:T(8,128)(2,1)S(1)} collective-permute-done((bf16[32,1664]{1,0:T(8,128)(2,1)S(1)}, bf16[32,1664]{1,0:T(8,128)(2,1)S(1)}, u32[]{:S(2)}, u32[]{:S(2)}) %collective-permute-start.7) | collective-permute-done | bytes 106528 | tf_op jit(solution)/shard_map/ppermute | solution.py:441
  27.8 0.1 collective-permute-start.9
  27.8 0.0 copy-start
  27.8 0.9 %own_backward.1.backward_ref = f32[32,1536]{1,0:T(8,128)S(1)} custom-call(bf16[32,1536]{1,0:T(8,128)(2,1)S(1)} %grad_pre.1.grad_ref.own_ref, bf16[1536,1536]{1,0:T(8,128)(2,1)S(1)} %get-tuple-element.43.turned_ref), custom_call_target="tpu_custom_call" | custom-call | tf_op jit(solution)/shard_map/own_backward/pallas_call | solution.py:55
  28.7 0.4 collective-permute-done.9.far_ref
  29.1 0.9 %output_blocks.1 = (bf16[32,3072]{1,0:T(8,128)(2,1)S(1)}, bf16[16,1536]{1,0:T(8,128)(2,1)S(1)}, bf16[16,1536]{1,0:T(8,128)(2,1)S(1)}, bf16[16,1536]{1,0:T(8,128)(2,1)S(1)}, bf16[16,1536]{1,0:T(8,128)(2,1)S(1)}) custom-call(bf16[32,1536]{1,0:T(8,128)(2,1)S(1)} %grad_pre.1.grad_ref.own_ref, bf16[32,1536]{1,0:T(8,128)(2,1)S(1)} %collective-permute-done.9.far_ref, ...), custom_call_target="tpu_custom_call" | custom-call | tf_op jit(solution)/shard_map/output_blocks/pallas_call | solution.py:55
  30.0 3.1 %collective-permute-start.10 = (bf16[16,1536]{1,0:T(8,128)(2,1)S(1)}, bf16[16,1536]{1,0:T(8,128)(2,1)S(1)}, u32[]{:S(2)}, u32[]{:S(2)}) collective-permute-start(bf16[16,1536]{1,0:T(8,128)(2,1)S(1)} %get-tuple-element.45), channel_id=1, source_target_pairs={{0,3},{1,2},{2,1},{3,0},{4,7},{5,6},{6,5},{7,4},{8,11},{9,10},{10,... | collective-permute-start | bytes 147464 | tf_op jit(solution)/shard_map/ppermute | solution.py:378
  33.1 0.0 collective-permute-start.11
  33.1 1.4 %collective-permute-start.12 = (bf16[16,1536]{1,0:T(8,128)(2,1)S(1)}, bf16[16,1536]{1,0:T(8,128)(2,1)S(1)}, u32[]{:S(2)}, u32[]{:S(2)}) collective-permute-start(bf16[16,1536]{1,0:T(8,128)(2,1)S(1)} %get-tuple-element.47), channel_id=1, source_target_pairs={{0,1},{1,0},{2,3},{3,2},{4,5},{5,4},{6,7},{7,6},{8,9},{9,8},{10,11... | collective-permute-start | bytes 147464 | tf_op jit(solution)/shard_map/ppermute | solution.py:378
  34.5 4.1 %weight_in_grad.1.refs_4_ = bf16[1536,3072]{1,0:T(8,128)(2,1)} custom-call(bf16[32,1536]{1,0:T(8,128)(2,1)S(1)} %get-tuple-element.35.x_ref.left_ref, bf16[32,3072]{1,0:T(8,128)(2,1)S(1)} %get-tuple-element.49.right_ref.hidden_ref), custom_call_target="tpu_custom_call" | custom-call | tf_op jit(solution)/shard_map/weight_in_grad/pallas_call | solution.py:329
  38.6 0.0 collective-permute-done.10.refs_0_
  38.6 0.0 collective-permute-done.11.refs_1_
  38.6 0.0 collective-permute-done.12.refs_2_
  38.6 0.0 copy-done
  38.7 0.9 %collective-permute-start.13 = (bf16[8,1536]{1,0:T(8,128)(2,1)S(1)}, bf16[8,1536]{1,0:T(8,128)(2,1)S(1)}, u32[]{:S(2)}, u32[]{:S(2)}) collective-permute-start(bf16[8,1536]{1,0:T(8,128)(2,1)S(1)} %get-tuple-element.51), channel_id=1, source_target_pairs={{0,8},{8,0},{1,9},{9,1},{2,10},{10,2},{3,11},{11,3},{4,12},{12,4},... | collective-permute-start | bytes 73736 | tf_op jit(solution)/shard_map/ppermute | solution.py:488
  39.6 2.6 %weight_out_grad_far.1 = bf16[3072,1536]{1,0:T(8,128)(2,1)} custom-call(bf16[32,1536]{1,0:T(8,128)(2,1)S(1)} %collective-permute-done.8.far_ref.left_ref, bf16[32,1536]{1,0:T(8,128)(2,1)S(1)} %get-tuple-element.38.dy_ref.right_ref, bf16[3072,1536]{1,0:T(8,128)(2,1)} %get-tuple-element.42.later_ref.refs_0_), custom_call_target="tpu_custom_call", output_to_operand_aliasing={{}: (2, {})} | custom-call | tf_op jit(solution)/shard_map/weight_out_grad_far/pallas_call | solution.py:329
  42.2 0.4 collective-permute-done.13.got_ref
  42.6 0.7 %final_rows.1 = (bf16[4,3072]{1,0:T(4,128)(2,1)}, bf16[4,3072]{1,0:T(4,128)(2,1)}, f32[1,3072]{1,0:T(1,128)}, f32[1,3072]{1,0:T(1,128)}) custom-call(bf16[8,1536]{1,0:T(8,128)(2,1)S(1)} %get-tuple-element.50.own_ref, bf16[8,1536]{1,0:T(8,128)(2,1)S(1)} %collective-permute-done.13.got_ref, f32[1,1536]{1,0:T(1,128)S(1)} %get-tuple-element.37.sums_ref, ...), custom_call_target="tpu_custom_call" | custom-call | tf_op jit(solution)/shard_map/final_rows/pallas_call | solution.py:55
  (6 shorter events, 0.2 us)
Async XLA Ops:
  1.4 4.9 %collective-permute-start = (bf16[8,1536]{1,0:T(8,128)(2,1)S(1)}, bf16[8,1536]{1,0:T(8,128)(2,1)S(1)}, u32[]{:S(2)}, u32[]{:S(2)}) collective-permute-start(bf16[8,1536]{1,0:T(8,128)(2,1)S(1)} %get-tuple-element.32.after_ref), channel_id=1, source_target_pairs={{0,8},{8,0},{1,9},{9,1},{2,10},{10,2},{3,11},{11,3},{4,12},{12,4},... | collective-permute-start | bytes 73736 | tf_op jit(solution)/shard_map/ppermute | solution.py:395
  6.4 8.3 %collective-permute-start.3 = (bf16[16,1536]{1,0:T(8,128)(2,1)S(1)}, bf16[16,1536]{1,0:T(8,128)(2,1)S(1)}, u32[]{:S(2)}, u32[]{:S(2)}) collective-permute-start(bf16[16,1536]{1,0:T(8,128)(2,1)S(1)} %pair_tiles.1.after_ref.refs_3_), channel_id=1, source_target_pairs={{0,3},{1,2},{2,1},{3,0},{4,7},{5,6},{6,5},{7,4},{8,11},{9,10},{10,... | collective-permute-start | bytes 147464 | tf_op jit(solution)/shard_map/ppermute | solution.py:378
  10.5 5.0 %collective-permute-start.2 = (bf16[16,1536]{1,0:T(8,128)(2,1)S(1)}, bf16[16,1536]{1,0:T(8,128)(2,1)S(1)}, u32[]{:S(2)}, u32[]{:S(2)}) collective-permute-start(bf16[16,1536]{1,0:T(8,128)(2,1)S(1)} %pair_tiles.1.after_ref.refs_3_), channel_id=1, source_target_pairs={{0,2},{1,3},{2,0},{3,1},{4,6},{5,7},{6,4},{7,5},{8,10},{9,11},{10,... | collective-permute-start | bytes 147464 | tf_op jit(solution)/shard_map/ppermute | solution.py:378
  10.5 5.0 %collective-permute-start.1 = (bf16[16,1536]{1,0:T(8,128)(2,1)S(1)}, bf16[16,1536]{1,0:T(8,128)(2,1)S(1)}, u32[]{:S(2)}, u32[]{:S(2)}) collective-permute-start(bf16[16,1536]{1,0:T(8,128)(2,1)S(1)} %pair_tiles.1.after_ref.refs_3_), channel_id=1, source_target_pairs={{0,1},{1,0},{2,3},{3,2},{4,5},{5,4},{6,7},{7,6},{8,9},{9,8},{10,11... | collective-permute-start | bytes 147464 | tf_op jit(solution)/shard_map/ppermute | solution.py:378
  11.1 8.2 %slice-start = ((s8[9437184]{0:T(1024)(128)(4,1)}), s8[1048576]{0:T(1024)(128)(4,1)S(1)}, s32[]{:S(2)}) async-start(s8[9437184]{0:T(1024)(128)(4,1)} %bitcast.4), calls=%async_computation | async-start | bytes 2097152
  11.1 8.2 %slice-start.1 = ((s8[9437184]{0:T(1024)(128)(4,1)}), s8[4194304]{0:T(1024)(128)(4,1)S(1)}, s32[]{:S(2)}) async-start(s8[9437184]{0:T(1024)(128)(4,1)} %bitcast.4), calls=%async_computation.1 | async-start | bytes 8388608
  15.4 3.8 %slice-start.2 = ((s8[9437184]{0:T(1024)(128)(4,1)}), s8[4194304]{0:T(1024)(128)(4,1)S(1)}, s32[]{:S(2)}) async-start(s8[9437184]{0:T(1024)(128)(4,1)} %bitcast.4), calls=%async_computation.2 | async-start | bytes 8388608
  16.4 1.3 %collective-permute-start.4 = (bf16[32,1536]{1,0:T(8,128)(2,1)S(1)}, bf16[32,1536]{1,0:T(8,128)(2,1)S(1)}, u32[]{:S(2)}, u32[]{:S(2)}) collective-permute-start(bf16[32,1536]{1,0:T(8,128)(2,1)S(1)} %get-tuple-element.36.after_ref), channel_id=1, source_target_pairs={{0,4},{4,0},{1,5},{5,1},{2,6},{6,2},{3,7},{7,3},{8,12},{12,8},{9,1... | collective-permute-start | bytes 294920 | tf_op jit(solution)/shard_map/ppermute | solution.py:433
  17.7 5.2 %collective-permute-start.5 = (bf16[32,1664]{1,0:T(8,128)(2,1)S(1)}, bf16[32,1664]{1,0:T(8,128)(2,1)S(1)}, u32[]{:S(2)}, u32[]{:S(2)}) collective-permute-start(bf16[32,1664]{1,0:T(8,128)(2,1)S(1)} %add_pre.1.after_ref.own_ref), channel_id=1, source_target_pairs={{0,8},{8,0},{1,9},{9,1},{2,10},{10,2},{3,11},{11,3},{4,12},{12,4},... | collective-permute-start | bytes 319496 | tf_op jit(solution)/shard_map/ppermute | solution.py:436
  19.3 3.6 %copy-start.1 = (f32[3072]{0:T(1024)S(1)}, f32[3072]{0:T(1024)}, u32[]{:S(2)}) copy-start(f32[3072]{0:T(1024)} %param.8) | copy-start | bytes 36868
  20.7 1.5 %collective-permute-start.6 = (bf16[32,1536]{1,0:T(8,128)(2,1)S(1)}, bf16[32,1536]{1,0:T(8,128)(2,1)S(1)}, u32[]{:S(2)}, u32[]{:S(2)}) collective-permute-start(bf16[32,1536]{1,0:T(8,128)(2,1)S(1)} %far_grad.1), channel_id=1, source_target_pairs={{0,4},{4,0},{1,5},{5,1},{2,6},{6,2},{3,7},{7,3},{8,12},{12,8},{9,1... | collective-permute-start | bytes 294920 | tf_op jit(solution)/shard_map/ppermute | solution.py:438
  22.3 5.4 %collective-permute-start.7 = (bf16[32,1664]{1,0:T(8,128)(2,1)S(1)}, bf16[32,1664]{1,0:T(8,128)(2,1)S(1)}, u32[]{:S(2)}, u32[]{:S(2)}) collective-permute-start(bf16[32,1664]{1,0:T(8,128)(2,1)S(1)} %add_grad.1.after_ref.own_ref), channel_id=1, source_target_pairs={{0,8},{8,0},{1,9},{9,1},{2,10},{10,2},{3,11},{11,3},{4,12},{12,4},... | collective-permute-start | bytes 319496 | tf_op jit(solution)/shard_map/ppermute | solution.py:441
  23.0 3.1 %collective-permute-start.8 = (bf16[32,1536]{1,0:T(8,128)(2,1)S(1)}, bf16[32,1536]{1,0:T(8,128)(2,1)S(1)}, u32[]{:S(2)}, u32[]{:S(2)}) collective-permute-start(bf16[32,1536]{1,0:T(8,128)(2,1)S(1)} %get-tuple-element.40.act_ref), channel_id=1, source_target_pairs={{0,4},{4,0},{1,5},{5,1},{2,6},{6,2},{3,7},{7,3},{8,12},{12,8},{9,1... | collective-permute-start | bytes 294920 | tf_op jit(solution)/shard_map/ppermute | solution.py:445
  27.8 1.4 %collective-permute-start.9 = (bf16[32,1536]{1,0:T(8,128)(2,1)S(1)}, bf16[32,1536]{1,0:T(8,128)(2,1)S(1)}, u32[]{:S(2)}, u32[]{:S(2)}) collective-permute-start(bf16[32,1536]{1,0:T(8,128)(2,1)S(1)} %grad_pre.1.grad_ref.own_ref), channel_id=1, source_target_pairs={{0,4},{4,0},{1,5},{5,1},{2,6},{6,2},{3,7},{7,3},{8,12},{12,8},{9,1... | collective-permute-start | bytes 294920 | tf_op jit(solution)/shard_map/ppermute | solution.py:459
  27.8 10.8 %copy-start = (f32[3072]{0:T(1024)S(1)}, f32[3072]{0:T(1024)}, u32[]{:S(2)}) copy-start(f32[3072]{0:T(1024)} %param.10) | copy-start | bytes 36868
  30.0 8.6 %collective-permute-start.10 = (bf16[16,1536]{1,0:T(8,128)(2,1)S(1)}, bf16[16,1536]{1,0:T(8,128)(2,1)S(1)}, u32[]{:S(2)}, u32[]{:S(2)}) collective-permute-start(bf16[16,1536]{1,0:T(8,128)(2,1)S(1)} %get-tuple-element.45), channel_id=1, source_target_pairs={{0,3},{1,2},{2,1},{3,0},{4,7},{5,6},{6,5},{7,4},{8,11},{9,10},{10,... | collective-permute-start | bytes 147464 | tf_op jit(solution)/shard_map/ppermute | solution.py:378
  33.1 5.5 %collective-permute-start.11 = (bf16[16,1536]{1,0:T(8,128)(2,1)S(1)}, bf16[16,1536]{1,0:T(8,128)(2,1)S(1)}, u32[]{:S(2)}, u32[]{:S(2)}) collective-permute-start(bf16[16,1536]{1,0:T(8,128)(2,1)S(1)} %get-tuple-element.46), channel_id=1, source_target_pairs={{0,2},{1,3},{2,0},{3,1},{4,6},{5,7},{6,4},{7,5},{8,10},{9,11},{10,... | collective-permute-start | bytes 147464 | tf_op jit(solution)/shard_map/ppermute | solution.py:378
  33.1 5.5 %collective-permute-start.12 = (bf16[16,1536]{1,0:T(8,128)(2,1)S(1)}, bf16[16,1536]{1,0:T(8,128)(2,1)S(1)}, u32[]{:S(2)}, u32[]{:S(2)}) collective-permute-start(bf16[16,1536]{1,0:T(8,128)(2,1)S(1)} %get-tuple-element.47), channel_id=1, source_target_pairs={{0,1},{1,0},{2,3},{3,2},{4,5},{5,4},{6,7},{7,6},{8,9},{9,8},{10,11... | collective-permute-start | bytes 147464 | tf_op jit(solution)/shard_map/ppermute | solution.py:378
  38.7 3.9 %collective-permute-start.13 = (bf16[8,1536]{1,0:T(8,128)(2,1)S(1)}, bf16[8,1536]{1,0:T(8,128)(2,1)S(1)}, u32[]{:S(2)}, u32[]{:S(2)}) collective-permute-start(bf16[8,1536]{1,0:T(8,128)(2,1)S(1)} %get-tuple-element.51), channel_id=1, source_target_pairs={{0,8},{8,0},{1,9},{9,1},{2,10},{10,2},{3,11},{11,3},{4,12},{12,4},... | collective-permute-start | bytes 73736 | tf_op jit(solution)/shard_map/ppermute | solution.py:488

commit v20 on v16

--- a/solution.py
+++ b/solution.py
@@ -275,7 +275,7 @@
     copies = []
     for i, at in enumerate(tiles_of(left_ref.shape[1], most)):
         left = left_ref[:, at].T
-        for part in tiles_of(out_hbm.shape[1], 512):
+        for part in tiles_of(out_hbm.shape[1], 1536):
             block_ref[at, part] = dot(left, right_ref[:, part], 1, 0).astype(bf16)
         there = pl.ds(pl.multiple_of(first + at.start, at.size), at.size)
         copies.append(

time: 43.7 us -> 43.7 us (level)
  no operation moved by 1% of the time
where the time goes in v20:
time: 43.7 us; the launch traced here: 43.4 us
  Pallas kernels  23.4 us (54%)
  starting transfers between devices  15.7 us (36%)
  waiting for transfers between devices  2.59 us (6%)
  other arithmetic  0.86 us (2%)
  between operations  0.82 us (2%)
    pallas_call x16, Pallas kernels, run(): pl.pallas_call(body, out_shape=shapes, in_specs=specs or [whole] * len(ar...  13.8 us
    ppermute x6, starting transfers between devices, across(): return lax.ppermute(array, 'nout', [(i, i ^ shift) for i in range(nn)])  9.18 us
    pallas_call x2, Pallas kernels, outer(): pl.pallas_call(functools.partial(outer_body, most, first_of), out_shape=l...  6.67 us
    ppermute x2, starting transfers between devices, on_device(): got = lax.ppermute(sent, 'tok', swap)  3.99 us
    pallas_call x1, Pallas kernels, own_forward(): pl.pallas_call(own_forward_body, out_shape=[pltpu.VMEM((count, wide), f32...  2.86 us
    ppermute x1, starting transfers between devices, on_device(): other_pre = lax.ppermute(own_pre, 'tok', swap)  1.56 us
  transfers between devices with their start and end apart: 14, of which 6 were waited for; matrix products, arithmetic and copies ran while one was open for 0% of the time, Pallas kernels for 48%

profile of v20, /device:TPU:0, one launch (start us, length us, event | category | flops | bytes accessed | tf_op | source)
XLA Modules:
  0.0 43.4 jit_solution(3464003268749800927)
XLA Ops:
  0.6 0.9 %fusion = (bf16[8,1536]{1,0:T(8,128)(2,1)S(1)}, bf16[8,1536]{1,0:T(8,128)(2,1)S(1)}) fusion(s32[]{:T(128)S(6)} %select_n.7, bf16[4,3072]{1,0:T(4,128)(2,1)} %param.6, bf16[4,3072]{1,0:T(4,128)(2,1)} %param.11, s32[]{:T(128)S(6)} %select_n.6), kind=kLoop, calls=%fused_computation.4 | loop fusion | flops 98304 | bytes 98312 | tf_op jit(solution)/shard_map/concatenate | solution.py:378
  1.5 3.0 %collective-permute-start = (bf16[8,1536]{1,0:T(8,128)(2,1)S(1)}, bf16[8,1536]{1,0:T(8,128)(2,1)S(1)}, u32[]{:S(2)}, u32[]{:S(2)}) collective-permute-start(bf16[8,1536]{1,0:T(8,128)(2,1)S(1)} %get-tuple-element.56.after_ref), channel_id=1, source_target_pairs={{0,8},{8,0},{1,9},{9,1},{2,10},{10,2},{3,11},{11,3},{4,12},{12,4},... | collective-permute-start | bytes 73736 | tf_op jit(solution)/shard_map/ppermute | solution.py:382
  4.5 1.9 %load_far.1.after_ref.far_ref.refs_4_ = bf16[1536,1024]{1,0:T(8,128)(2,1)S(1)} custom-call(bf16[1536,3072]{1,0:T(8,128)(2,1)} %hbm_ref.3, bf16[8,1536]{1,0:T(8,128)(2,1)S(1)} %get-tuple-element.56.after_ref), custom_call_target="tpu_custom_call" | custom-call | tf_op jit(solution)/shard_map/load_far/pallas_call | solution.py:55
  6.4 0.0 collective-permute-done.got_ref
  6.4 4.1 %collective-permute-start.1 = (bf16[16,1664]{1,0:T(8,128)(2,1)S(1)}, bf16[16,1664]{1,0:T(8,128)(2,1)S(1)}, u32[]{:S(2)}, u32[]{:S(2)}) collective-permute-start(bf16[16,1664]{1,0:T(8,128)(2,1)S(1)} %get-tuple-element.31), channel_id=1, source_target_pairs={{0,3},{1,2},{2,1},{3,0},{4,7},{5,6},{6,5},{7,4},{8,11},{9,10},{10,... | collective-permute-start | bytes 159752 | tf_op jit(solution)/shard_map/ppermute | solution.py:368
  10.5 0.0 collective-permute-start.3
  10.5 0.6 %collective-permute-start.2 = (bf16[16,1536]{1,0:T(8,128)(2,1)S(1)}, bf16[16,1536]{1,0:T(8,128)(2,1)S(1)}, u32[]{:S(2)}, u32[]{:S(2)}) collective-permute-start(bf16[16,1536]{1,0:T(8,128)(2,1)S(1)} %get-tuple-element.32.after_ref.refs_3_), channel_id=1, source_target_pairs={{0,2},{1,3},{2,0},{3,1},{4,6},{5,7},{6,4},{7,5},{8,10},{9,11},{10,... | collective-permute-start | bytes 147464 | tf_op jit(solution)/shard_map/ppermute | solution.py:368
  11.2 0.0 slice-start
  11.2 0.0 slice-start.1
  11.2 3.6 %load_own.1 = (bf16[1536,1536]{1,0:T(8,128)(2,1)S(1)}, bf16[1536,512]{1,0:T(8,128)(2,1)S(1)}, bf16[1536,1536]{1,0:T(8,128)(2,1)S(1)}, bf16[1536,1536]{1,0:T(8,128)(2,1)S(1)}) custom-call(bf16[1536,3072]{1,0:T(8,128)(2,1)} %hbm_ref.3, bf16[16,1536]{1,0:T(8,128)(2,1)S(1)} %get-tuple-element.32.after_ref.refs_3_, ...), custom_call_target="tpu_custom_call" | custom-call | tf_op jit(solution)/shard_map/load_own/pallas_call | solution.py:55
  14.7 0.0 collective-permute-done.3.refs_2_
  14.8 0.8 %collective-permute-done.2.refs_1_ = bf16[16,1536]{1,0:T(8,128)(2,1)S(1)} collective-permute-done((bf16[16,1536]{1,0:T(8,128)(2,1)S(1)}, bf16[16,1536]{1,0:T(8,128)(2,1)S(1)}, u32[]{:S(2)}, u32[]{:S(2)}) %collective-permute-start.2) | collective-permute-done | bytes 49184 | tf_op jit(solution)/shard_map/ppermute | solution.py:368
  15.5 0.0 collective-permute-done.1.refs_0_
  15.5 0.0 slice-start.2
  15.5 0.9 %far_pre.1 = (bf16[32,1536]{1,0:T(8,128)(2,1)S(1)}, bf16[32,1536]{1,0:T(8,128)(2,1)S(1)}, bf16[32,1536]{1,0:T(8,128)(2,1)S(1)}, f32[1,1536]{1,0:T(1,128)S(1)}) custom-call(bf16[16,1664]{1,0:T(8,128)(2,1)S(1)} %collective-permute-done.1.refs_0_, bf16[16,1536]{1,0:T(8,128)(2,1)S(1)} %collective-permute-done.2.refs_1_, ...), custom_call_target="tpu_custom_call" | custom-call | tf_op jit(solution)/shard_map/far_pre/pallas_call | solution.py:55
  16.4 0.0 collective-permute-start.4
  16.5 0.9 %own_pre.1.own_ref = f32[32,1536]{1,0:T(8,128)S(1)} custom-call(bf16[32,1536]{1,0:T(8,128)(2,1)S(1)} %get-tuple-element.35.x_ref.left_ref, bf16[1536,1536]{1,0:T(8,128)(2,1)S(1)} %get-tuple-element.34.refs_6_.w_in_ref, bf16[32,1536]{1,0:T(8,128)(2,1)S(1)} %get-tuple-element.36.after_ref), custom_call_target="tpu_custom_call" | custom-call | tf_op jit(solution)/shard_map/own_pre/pallas_call | solution.py:55
  17.4 0.4 collective-permute-done.4.got_ref
  17.8 1.6 %collective-permute-start.5 = (bf16[32,1664]{1,0:T(8,128)(2,1)S(1)}, bf16[32,1664]{1,0:T(8,128)(2,1)S(1)}, u32[]{:S(2)}, u32[]{:S(2)}) collective-permute-start(bf16[32,1664]{1,0:T(8,128)(2,1)S(1)} %add_pre.1.after_ref.own_ref), channel_id=1, source_target_pairs={{0,8},{8,0},{1,9},{9,1},{2,10},{10,2},{3,11},{11,3},{4,12},{12,4},... | collective-permute-start | bytes 319496 | tf_op jit(solution)/shard_map/ppermute | solution.py:426
  19.4 0.0 slice-done
  19.4 0.0 slice-done.1
  19.4 0.0 slice-done.2
  19.4 0.0 copy-start.1
  19.4 1.4 %far_grad.1 = bf16[32,1536]{1,0:T(8,128)(2,1)S(1)} custom-call(bf16[32,1536]{1,0:T(8,128)(2,1)S(1)} %get-tuple-element.38.dy_ref.right_ref, bf16[3072,1536]{1,0:T(8,128)(2,1)S(1)} %bitcast.5, bf16[32,1664]{1,0:T(8,128)(2,1)S(1)} %add_pre.1.after_ref.own_ref), custom_call_target="tpu_custom_call" | custom-call | tf_op jit(solution)/shard_map/far_grad/pallas_call | solution.py:55
  20.8 0.0 collective-permute-start.6
  20.8 1.5 %own_grad.1.own_ref = f32[32,1536]{1,0:T(8,128)S(1)} custom-call(bf16[32,1536]{1,0:T(8,128)(2,1)S(1)} %get-tuple-element.38.dy_ref.right_ref, bf16[3072,1536]{1,0:T(8,128)(2,1)S(1)} %bitcast.5), custom_call_target="tpu_custom_call" | custom-call | tf_op jit(solution)/shard_map/own_grad/pallas_call | solution.py:55
  22.3 0.0 collective-permute-done.6.got_ref
  22.4 0.6 %collective-permute-start.7 = (bf16[32,1664]{1,0:T(8,128)(2,1)S(1)}, bf16[32,1664]{1,0:T(8,128)(2,1)S(1)}, u32[]{:S(2)}, u32[]{:S(2)}) collective-permute-start(bf16[32,1664]{1,0:T(8,128)(2,1)S(1)} %add_grad.1.after_ref.own_ref), channel_id=1, source_target_pairs={{0,8},{8,0},{1,9},{9,1},{2,10},{10,2},{3,11},{11,3},{4,12},{12,4},... | collective-permute-start | bytes 319496 | tf_op jit(solution)/shard_map/ppermute | solution.py:431
  23.0 0.0 collective-permute-done.5.other_ref
  23.0 0.0 copy-done.1
  23.0 0.1 gelu.1
  23.1 0.3 collective-permute-start.8
  23.3 2.9 %own_forward.1 = (f32[32,1536]{1,0:T(8,128)S(1)}, bf16[3072,1536]{1,0:T(8,128)(2,1)}) custom-call(bf16[32,1536]{1,0:T(8,128)(2,1)S(1)} %get-tuple-element.40.act_ref, bf16[32,1536]{1,0:T(8,128)(2,1)S(1)} %get-tuple-element.38.dy_ref.right_ref, bf16[3072,1536]{1,0:T(8,128)(2,1)S(1)} %bitcast.5), custom_call_target="tpu_custom_call" | custom-call | tf_op jit(solution)/shard_map/own_forward/pallas_call | solution.py:301
  26.2 0.0 collective-permute-done.8.far_ref.left_ref
  26.2 0.9 %far_forward.1.after_ref.forward_ref = f32[32,1536]{1,0:T(8,128)S(1)} custom-call(bf16[32,1536]{1,0:T(8,128)(2,1)S(1)} %collective-permute-done.8.far_ref.left_ref, bf16[3072,1536]{1,0:T(8,128)(2,1)S(1)} %bitcast.5, f32[32,1536]{1,0:T(8,128)S(1)} %get-tuple-element.41.terms_ref), custom_call_target="tpu_custom_call" | custom-call | tf_op jit(solution)/shard_map/far_forward/pallas_call | solution.py:55
  27.1 0.6 %collective-permute-done.7.other_ref = bf16[32,1664]{1,0:T(8,128)(2,1)S(1)} collective-permute-done((bf16[32,1664]{1,0:T(8,128)(2,1)S(1)}, bf16[32,1664]{1,0:T(8,128)(2,1)S(1)}, u32[]{:S(2)}, u32[]{:S(2)}) %collective-permute-start.7) | collective-permute-done | bytes 106528 | tf_op jit(solution)/shard_map/ppermute | solution.py:431
  27.8 0.1 collective-permute-start.9
  27.9 0.0 copy-start
  27.9 0.9 %own_backward.1.backward_ref = f32[32,1536]{1,0:T(8,128)S(1)} custom-call(bf16[32,1536]{1,0:T(8,128)(2,1)S(1)} %grad_pre.1.grad_ref.own_ref, bf16[1536,1536]{1,0:T(8,128)(2,1)S(1)} %get-tuple-element.43.turned_ref), custom_call_target="tpu_custom_call" | custom-call | tf_op jit(solution)/shard_map/own_backward/pallas_call | solution.py:55
  28.8 0.4 collective-permute-done.9.far_ref
  29.2 0.9 %output_blocks.1 = (bf16[32,3072]{1,0:T(8,128)(2,1)S(1)}, bf16[16,1536]{1,0:T(8,128)(2,1)S(1)}, bf16[16,1536]{1,0:T(8,128)(2,1)S(1)}, bf16[16,1536]{1,0:T(8,128)(2,1)S(1)}, bf16[16,1536]{1,0:T(8,128)(2,1)S(1)}) custom-call(bf16[32,1536]{1,0:T(8,128)(2,1)S(1)} %grad_pre.1.grad_ref.own_ref, bf16[32,1536]{1,0:T(8,128)(2,1)S(1)} %collective-permute-done.9.far_ref, ...), custom_call_target="tpu_custom_call" | custom-call | tf_op jit(solution)/shard_map/output_blocks/pallas_call | solution.py:55
  30.1 3.1 %collective-permute-start.10 = (bf16[16,1536]{1,0:T(8,128)(2,1)S(1)}, bf16[16,1536]{1,0:T(8,128)(2,1)S(1)}, u32[]{:S(2)}, u32[]{:S(2)}) collective-permute-start(bf16[16,1536]{1,0:T(8,128)(2,1)S(1)} %get-tuple-element.45), channel_id=1, source_target_pairs={{0,3},{1,2},{2,1},{3,0},{4,7},{5,6},{6,5},{7,4},{8,11},{9,10},{10,... | collective-permute-start | bytes 147464 | tf_op jit(solution)/shard_map/ppermute | solution.py:368
  33.2 0.5 %collective-permute-start.11 = (bf16[16,1536]{1,0:T(8,128)(2,1)S(1)}, bf16[16,1536]{1,0:T(8,128)(2,1)S(1)}, u32[]{:S(2)}, u32[]{:S(2)}) collective-permute-start(bf16[16,1536]{1,0:T(8,128)(2,1)S(1)} %get-tuple-element.46), channel_id=1, source_target_pairs={{0,2},{1,3},{2,0},{3,1},{4,6},{5,7},{6,4},{7,5},{8,10},{9,11},{10,... | collective-permute-start | bytes 147464 | tf_op jit(solution)/shard_map/ppermute | solution.py:368
  33.7 0.9 %collective-permute-start.12 = (bf16[16,1536]{1,0:T(8,128)(2,1)S(1)}, bf16[16,1536]{1,0:T(8,128)(2,1)S(1)}, u32[]{:S(2)}, u32[]{:S(2)}) collective-permute-start(bf16[16,1536]{1,0:T(8,128)(2,1)S(1)} %get-tuple-element.47), channel_id=1, source_target_pairs={{0,1},{1,0},{2,3},{3,2},{4,5},{5,4},{6,7},{7,6},{8,9},{9,8},{10,11... | collective-permute-start | bytes 147464 | tf_op jit(solution)/shard_map/ppermute | solution.py:368
  34.6 4.1 %weight_in_grad.1.refs_4_ = bf16[1536,3072]{1,0:T(8,128)(2,1)} custom-call(bf16[32,1536]{1,0:T(8,128)(2,1)S(1)} %get-tuple-element.35.x_ref.left_ref, bf16[32,3072]{1,0:T(8,128)(2,1)S(1)} %get-tuple-element.49.right_ref.hidden_ref), custom_call_target="tpu_custom_call" | custom-call | tf_op jit(solution)/shard_map/weight_in_grad/pallas_call | solution.py:319
  38.7 0.0 collective-permute-done.10.refs_0_
  38.7 0.0 collective-permute-done.11.refs_1_
  38.7 0.1 collective-permute-done.12.refs_2_
  38.8 0.0 copy-done
  38.8 1.0 %collective-permute-start.13 = (bf16[8,1536]{1,0:T(8,128)(2,1)S(1)}, bf16[8,1536]{1,0:T(8,128)(2,1)S(1)}, u32[]{:S(2)}, u32[]{:S(2)}) collective-permute-start(bf16[8,1536]{1,0:T(8,128)(2,1)S(1)} %get-tuple-element.51), channel_id=1, source_target_pairs={{0,8},{8,0},{1,9},{9,1},{2,10},{10,2},{3,11},{11,3},{4,12},{12,4},... | collective-permute-start | bytes 73736 | tf_op jit(solution)/shard_map/ppermute | solution.py:478
  39.8 2.6 %weight_out_grad_far.1 = bf16[3072,1536]{1,0:T(8,128)(2,1)} custom-call(bf16[32,1536]{1,0:T(8,128)(2,1)S(1)} %collective-permute-done.8.far_ref.left_ref, bf16[32,1536]{1,0:T(8,128)(2,1)S(1)} %get-tuple-element.38.dy_ref.right_ref, bf16[3072,1536]{1,0:T(8,128)(2,1)} %get-tuple-element.42.later_ref.refs_0_), custom_call_target="tpu_custom_call", output_to_operand_aliasing={{}: (2, {})} | custom-call | tf_op jit(solution)/shard_map/weight_out_grad_far/pallas_call | solution.py:319
  42.4 0.3 collective-permute-done.13.got_ref
  42.7 0.7 %final_rows.1 = (bf16[4,3072]{1,0:T(4,128)(2,1)}, bf16[4,3072]{1,0:T(4,128)(2,1)}, f32[1,3072]{1,0:T(1,128)}, f32[1,3072]{1,0:T(1,128)}) custom-call(bf16[8,1536]{1,0:T(8,128)(2,1)S(1)} %get-tuple-element.50.own_ref, bf16[8,1536]{1,0:T(8,128)(2,1)S(1)} %collective-permute-done.13.got_ref, f32[1,1536]{1,0:T(1,128)S(1)} %get-tuple-element.37.sums_ref, ...), custom_call_target="tpu_custom_call" | custom-call | tf_op jit(solution)/shard_map/final_rows/pallas_call | solution.py:55
  (6 shorter events, 0.2 us)
Async XLA Ops:
  1.5 4.9 %collective-permute-start = (bf16[8,1536]{1,0:T(8,128)(2,1)S(1)}, bf16[8,1536]{1,0:T(8,128)(2,1)S(1)}, u32[]{:S(2)}, u32[]{:S(2)}) collective-permute-start(bf16[8,1536]{1,0:T(8,128)(2,1)S(1)} %get-tuple-element.56.after_ref), channel_id=1, source_target_pairs={{0,8},{8,0},{1,9},{9,1},{2,10},{10,2},{3,11},{11,3},{4,12},{12,4},... | collective-permute-start | bytes 73736 | tf_op jit(solution)/shard_map/ppermute | solution.py:382
  6.4 9.1 %collective-permute-start.1 = (bf16[16,1664]{1,0:T(8,128)(2,1)S(1)}, bf16[16,1664]{1,0:T(8,128)(2,1)S(1)}, u32[]{:S(2)}, u32[]{:S(2)}) collective-permute-start(bf16[16,1664]{1,0:T(8,128)(2,1)S(1)} %get-tuple-element.31), channel_id=1, source_target_pairs={{0,3},{1,2},{2,1},{3,0},{4,7},{5,6},{6,5},{7,4},{8,11},{9,10},{10,... | collective-permute-start | bytes 159752 | tf_op jit(solution)/shard_map/ppermute | solution.py:368
  10.5 4.2 %collective-permute-start.3 = (bf16[16,1536]{1,0:T(8,128)(2,1)S(1)}, bf16[16,1536]{1,0:T(8,128)(2,1)S(1)}, u32[]{:S(2)}, u32[]{:S(2)}) collective-permute-start(bf16[16,1536]{1,0:T(8,128)(2,1)S(1)} %get-tuple-element.32.after_ref.refs_3_), channel_id=1, source_target_pairs={{0,1},{1,0},{2,3},{3,2},{4,5},{5,4},{6,7},{7,6},{8,9},{9,8},{10,11... | collective-permute-start | bytes 147464 | tf_op jit(solution)/shard_map/ppermute | solution.py:368
  10.5 5.0 %collective-permute-start.2 = (bf16[16,1536]{1,0:T(8,128)(2,1)S(1)}, bf16[16,1536]{1,0:T(8,128)(2,1)S(1)}, u32[]{:S(2)}, u32[]{:S(2)}) collective-permute-start(bf16[16,1536]{1,0:T(8,128)(2,1)S(1)} %get-tuple-element.32.after_ref.refs_3_), channel_id=1, source_target_pairs={{0,2},{1,3},{2,0},{3,1},{4,6},{5,7},{6,4},{7,5},{8,10},{9,11},{10,... | collective-permute-start | bytes 147464 | tf_op jit(solution)/shard_map/ppermute | solution.py:368
  11.2 8.2 %slice-start = ((s8[9437184]{0:T(1024)(128)(4,1)}), s8[1048576]{0:T(1024)(128)(4,1)S(1)}, s32[]{:S(2)}) async-start(s8[9437184]{0:T(1024)(128)(4,1)} %bitcast.4), calls=%async_computation | async-start | bytes 2097152
  11.2 8.2 %slice-start.1 = ((s8[9437184]{0:T(1024)(128)(4,1)}), s8[4194304]{0:T(1024)(128)(4,1)S(1)}, s32[]{:S(2)}) async-start(s8[9437184]{0:T(1024)(128)(4,1)} %bitcast.4), calls=%async_computation.1 | async-start | bytes 8388608
  15.5 3.8 %slice-start.2 = ((s8[9437184]{0:T(1024)(128)(4,1)}), s8[4194304]{0:T(1024)(128)(4,1)S(1)}, s32[]{:S(2)}) async-start(s8[9437184]{0:T(1024)(128)(4,1)} %bitcast.4), calls=%async_computation.2 | async-start | bytes 8388608
  16.4 1.3 %collective-permute-start.4 = (bf16[32,1536]{1,0:T(8,128)(2,1)S(1)}, bf16[32,1536]{1,0:T(8,128)(2,1)S(1)}, u32[]{:S(2)}, u32[]{:S(2)}) collective-permute-start(bf16[32,1536]{1,0:T(8,128)(2,1)S(1)} %get-tuple-element.36.after_ref), channel_id=1, source_target_pairs={{0,4},{4,0},{1,5},{5,1},{2,6},{6,2},{3,7},{7,3},{8,12},{12,8},{9,1... | collective-permute-start | bytes 294920 | tf_op jit(solution)/shard_map/ppermute | solution.py:423
  17.8 5.2 %collective-permute-start.5 = (bf16[32,1664]{1,0:T(8,128)(2,1)S(1)}, bf16[32,1664]{1,0:T(8,128)(2,1)S(1)}, u32[]{:S(2)}, u32[]{:S(2)}) collective-permute-start(bf16[32,1664]{1,0:T(8,128)(2,1)S(1)} %add_pre.1.after_ref.own_ref), channel_id=1, source_target_pairs={{0,8},{8,0},{1,9},{9,1},{2,10},{10,2},{3,11},{11,3},{4,12},{12,4},... | collective-permute-start | bytes 319496 | tf_op jit(solution)/shard_map/ppermute | solution.py:426
  19.4 3.6 %copy-start.1 = (f32[3072]{0:T(1024)S(1)}, f32[3072]{0:T(1024)}, u32[]{:S(2)}) copy-start(f32[3072]{0:T(1024)} %param.8) | copy-start | bytes 36868
  20.8 1.5 %collective-permute-start.6 = (bf16[32,1536]{1,0:T(8,128)(2,1)S(1)}, bf16[32,1536]{1,0:T(8,128)(2,1)S(1)}, u32[]{:S(2)}, u32[]{:S(2)}) collective-permute-start(bf16[32,1536]{1,0:T(8,128)(2,1)S(1)} %far_grad.1), channel_id=1, source_target_pairs={{0,4},{4,0},{1,5},{5,1},{2,6},{6,2},{3,7},{7,3},{8,12},{12,8},{9,1... | collective-permute-start | bytes 294920 | tf_op jit(solution)/shard_map/ppermute | solution.py:428
  22.4 5.4 %collective-permute-start.7 = (bf16[32,1664]{1,0:T(8,128)(2,1)S(1)}, bf16[32,1664]{1,0:T(8,128)(2,1)S(1)}, u32[]{:S(2)}, u32[]{:S(2)}) collective-permute-start(bf16[32,1664]{1,0:T(8,128)(2,1)S(1)} %add_grad.1.after_ref.own_ref), channel_id=1, source_target_pairs={{0,8},{8,0},{1,9},{9,1},{2,10},{10,2},{3,11},{11,3},{4,12},{12,4},... | collective-permute-start | bytes 319496 | tf_op jit(solution)/shard_map/ppermute | solution.py:431
  23.1 3.1 %collective-permute-start.8 = (bf16[32,1536]{1,0:T(8,128)(2,1)S(1)}, bf16[32,1536]{1,0:T(8,128)(2,1)S(1)}, u32[]{:S(2)}, u32[]{:S(2)}) collective-permute-start(bf16[32,1536]{1,0:T(8,128)(2,1)S(1)} %get-tuple-element.40.act_ref), channel_id=1, source_target_pairs={{0,4},{4,0},{1,5},{5,1},{2,6},{6,2},{3,7},{7,3},{8,12},{12,8},{9,1... | collective-permute-start | bytes 294920 | tf_op jit(solution)/shard_map/ppermute | solution.py:435
  27.8 1.4 %collective-permute-start.9 = (bf16[32,1536]{1,0:T(8,128)(2,1)S(1)}, bf16[32,1536]{1,0:T(8,128)(2,1)S(1)}, u32[]{:S(2)}, u32[]{:S(2)}) collective-permute-start(bf16[32,1536]{1,0:T(8,128)(2,1)S(1)} %grad_pre.1.grad_ref.own_ref), channel_id=1, source_target_pairs={{0,4},{4,0},{1,5},{5,1},{2,6},{6,2},{3,7},{7,3},{8,12},{12,8},{9,1... | collective-permute-start | bytes 294920 | tf_op jit(solution)/shard_map/ppermute | solution.py:449
  27.9 10.9 %copy-start = (f32[3072]{0:T(1024)S(1)}, f32[3072]{0:T(1024)}, u32[]{:S(2)}) copy-start(f32[3072]{0:T(1024)} %param.10) | copy-start | bytes 36868
  30.1 8.6 %collective-permute-start.10 = (bf16[16,1536]{1,0:T(8,128)(2,1)S(1)}, bf16[16,1536]{1,0:T(8,128)(2,1)S(1)}, u32[]{:S(2)}, u32[]{:S(2)}) collective-permute-start(bf16[16,1536]{1,0:T(8,128)(2,1)S(1)} %get-tuple-element.45), channel_id=1, source_target_pairs={{0,3},{1,2},{2,1},{3,0},{4,7},{5,6},{6,5},{7,4},{8,11},{9,10},{10,... | collective-permute-start | bytes 147464 | tf_op jit(solution)/shard_map/ppermute | solution.py:368
  33.2 5.5 %collective-permute-start.11 = (bf16[16,1536]{1,0:T(8,128)(2,1)S(1)}, bf16[16,1536]{1,0:T(8,128)(2,1)S(1)}, u32[]{:S(2)}, u32[]{:S(2)}) collective-permute-start(bf16[16,1536]{1,0:T(8,128)(2,1)S(1)} %get-tuple-element.46), channel_id=1, source_target_pairs={{0,2},{1,3},{2,0},{3,1},{4,6},{5,7},{6,4},{7,5},{8,10},{9,11},{10,... | collective-permute-start | bytes 147464 | tf_op jit(solution)/shard_map/ppermute | solution.py:368
  33.7 5.1 %collective-permute-start.12 = (bf16[16,1536]{1,0:T(8,128)(2,1)S(1)}, bf16[16,1536]{1,0:T(8,128)(2,1)S(1)}, u32[]{:S(2)}, u32[]{:S(2)}) collective-permute-start(bf16[16,1536]{1,0:T(8,128)(2,1)S(1)} %get-tuple-element.47), channel_id=1, source_target_pairs={{0,1},{1,0},{2,3},{3,2},{4,5},{5,4},{6,7},{7,6},{8,9},{9,8},{10,11... | collective-permute-start | bytes 147464 | tf_op jit(solution)/shard_map/ppermute | solution.py:368
  38.8 3.9 %collective-permute-start.13 = (bf16[8,1536]{1,0:T(8,128)(2,1)S(1)}, bf16[8,1536]{1,0:T(8,128)(2,1)S(1)}, u32[]{:S(2)}, u32[]{:S(2)}) collective-permute-start(bf16[8,1536]{1,0:T(8,128)(2,1)S(1)} %get-tuple-element.51), channel_id=1, source_target_pairs={{0,8},{8,0},{1,9},{9,1},{2,10},{10,2},{3,11},{11,3},{4,12},{12,4},... | collective-permute-start | bytes 73736 | tf_op jit(solution)/shard_map/ppermute | solution.py:478
